TPU v7x, 32 devices: a whole 2x2x4 slice. The times are simulated.
32 devices in a mesh: crop: 2 (over core), row: 4 (over z), col: 4 (over y, x).
Axes of the slice: x: 2, y: 2, z: 4, core: 2. Of those that a mesh axis runs over, the one named last changes fastest.
Arguments:
- pair: float32 [2, 512, 512, 128], P('crop', 'row', 'col'), parts along dimension 0, may hold values from -6 to 6
- gain_input: float32 [128], replicated, may hold values from 0.1 to 1.9
- weights_in: float32 [128, 512], replicated, may hold values from -0.5 to 0.5
- gate_weights: float32 [128, 128], replicated, may hold values from -0.5 to 0.5
- weights_out: float32 [128, 128], replicated, may hold values from -0.5 to 0.5
- gain_product: float32 [128], replicated, may hold values from 0.1 to 1.9
- gain_transition: float32 [128], replicated, may hold values from 0.1 to 1.9
- transition_in: float32 [128, 1024], replicated, may hold values from -0.5 to 0.5
- transition_out: float32 [512, 128], replicated, may hold values from -0.25 to 0.25
- distogram_weights: float32 [128, 64], replicated, may hold values from -0.5 to 0.5
- distogram_bias: float32 [64], replicated, may hold values from -4 to 4
Outputs:
- logits: float32 [2, 512, 512, 64], P('crop', 'row', 'col'), parts along dimension 0
There are 2 independent parts, one for each index of `crop`. A program takes and returns all parts, laid end to end along the dimension named above; an argument that names none is the same for every part. Nothing has to cross between parts.
All inputs are finite; a program needn't handle non-finite values.
Results may differ from a plain program's by a relative error of at most 0.00007.
Values sent between devices are 32-bit elements; how exact they have to be, the bound alone decides.
No kernel may reach another device: no remote copies, remote signals or barrier semaphores. Data moves between devices by JAX's collectives and lax.ppermute only.
A program may use at most 192 MiB of HBM per device.

v0:
```python
import jax
import jax.numpy as jnp
from jax import lax
from jax.sharding import PartitionSpec as P

HIGH = lax.Precision.HIGHEST


def layer_norm(values, gain):
    center = values - jnp.mean(values, axis=-1, keepdims=True)
    spread = jnp.mean(center * center, axis=-1, keepdims=True)
    return center * lax.rsqrt(spread + 1e-05) * gain


def project(values, weights):
    return jnp.einsum("...c,cd->...d", values, weights, precision=HIGH)


def outgoing(left_hand, right_hand):
    return jnp.einsum("bikc,bjkc->bijc", left_hand, right_hand, precision=HIGH)


def mirrored(values):
    columns = lax.all_to_all(values, ("row", "col"), split_axis=2, concat_axis=1, tiled=True)
    return jnp.swapaxes(columns, 1, 2)


def shards(
    pair,
    gain_input,
    weights_in,
    gate_weights,
    weights_out,
    gain_product,
    gain_transition,
    transition_in,
    transition_out,
    distogram_weights,
    distogram_bias,
):
    row_count = lax.axis_size("row")
    col_count = lax.axis_size("col")
    crops, tile_rows, tile_cols, width = pair.shape
    normed = layer_norm(pair, gain_input)
    projected = project(normed, weights_in)
    left_hand = jax.nn.sigmoid(projected[..., width : 2 * width]) * projected[..., :width]
    right_hand = jax.nn.sigmoid(projected[..., 3 * width :]) * projected[..., 2 * width : 3 * width]
    stacked = jnp.stack([left_hand, right_hand], axis=0)
    received = lax.all_to_all(stacked, ("row", "col"), split_axis=4, concat_axis=2, tiled=True)
    items = received.shape[1]
    owned = received.shape[4]
    square = received.reshape(2, items, row_count, col_count, tile_rows, tile_cols, owned)
    square = square.transpose(0, 1, 2, 4, 3, 5, 6).reshape(
        2, items, row_count * tile_rows, col_count * tile_cols, owned
    )
    result = outgoing(square[0], square[1])
    product = lax.all_to_all(result, ("row", "col"), split_axis=1, concat_axis=3, tiled=True)
    base = lax.all_to_all(pair, "col", split_axis=1, concat_axis=2, tiled=True)
    normed_base = layer_norm(base, gain_input)
    gate = jax.nn.sigmoid(project(normed_base, gate_weights))
    updated = base + gate * project(layer_norm(product, gain_product), weights_out)
    hidden = project(layer_norm(updated, gain_transition), transition_in)
    hidden_width = transition_out.shape[0]
    activated = jax.nn.silu(hidden[..., :hidden_width]) * hidden[..., hidden_width:]
    pair_out = updated + project(activated, transition_out)
    symmetric = pair_out + mirrored(pair_out)
    line_logits = project(symmetric, distogram_weights) + distogram_bias
    return lax.all_to_all(line_logits, "col", split_axis=2, concat_axis=1, tiled=True)


def solution(mesh):
    return jax.shard_map(
        shards,
        mesh=mesh,
        in_specs=(P("crop", "row", "col", None), P(), P(), P(), P(), P(), P(), P(), P(), P(), P()),
        out_specs=P("crop", "row", "col", None),
        check_vma=False,
    )
```

profile of v0, /device:TPU:12, one launch (start us, length us, event | category | flops | bytes accessed | tf_op | source)
XLA Modules:
  0.0 1230.5 jit_solution(14820717124912528765)
XLA Ops:
  0.0 5.7 reduce_sum.74
  5.7 0.0 copy-start.2
  5.7 7.3 multiply_reduce_fusion.2
  13.1 30.2 %convolution_bitcast_fusion.1 = f32[1,128,128,512]{3,2,1,0:T(8,128)} fusion(f32[1,128,128,128]{3,2,1,0:T(8,128)S(1)} %copy-done.2, f32[128]{0:T(128)S(1)} %copy-done.9, f32[128,128]{1,0:T(8,128)S(1)} %add_rsqrt_fusion.2, f32[128,128]{1,0:T(8,128)S(1)} %broadcast_multiply_fusion.2, f32[128,512]{1,0:T(8,128)S(1)} %copy-done.5), kind=kOutput, calls=%fused_computation.13 | convolution fusion | flops 12891193344 | bytes 42336768 | tf_op jit(solution)/shard_map/...c,cd->...d/dot_general | solution.py:16
  43.3 18.9 %fusion.14 = (f32[1,1,128,128,128]{4,3,2,1,0:T(8,128)}, f32[1,1,128,128,128]{4,3,2,1,0:T(8,128)}) fusion(f32[1,128,128,512]{3,2,1,0:T(8,128)} %convolution_bitcast_fusion.1), kind=kLoop, calls=%fused_computation.21 | loop fusion | flops 16777216 | bytes 50331648 | tf_op jit(solution)/shard_map/stack | solution.py:48
  62.2 11.7 pad_maximum_fusion
  73.8 18.0 %copy.44 = f32[2,1,128,128,128]{3,2,1,0,4:T(8,128)} copy(f32[2,1,128,128,128]{4,3,2,1,0:T(8,128)} %pad_maximum_fusion) | data formatting | bytes 33554432 | tf_op jit(solution)/shard_map/stack | solution.py:48
  91.8 369.5 %all_to_all.87 = f32[2,1,128,128,128]{3,2,1,0,4:T(8,128)} all-to-all(f32[2,1,128,128,128]{3,2,1,0,4:T(8,128)} %copy.44), channel_id=1, replica_groups=mesh['crop'=2,'row'=4,'col'=4] {'row','col'}, dimensions={4} | all-to-all | bytes 33554432 | tf_op jit(solution)/shard_map/all_to_all | solution.py:49
  461.3 7.2 all-to-all-start
  468.5 15.3 %copy.45 = f32[2,1,128,128,128]{3,4,2,0,1:T(8,128)S(1)} copy(f32[2,1,128,128,128]{3,2,1,0,4:T(8,128)} %all_to_all.87) | data formatting | bytes 33554432 | tf_op jit(solution)/shard_map/all_to_all | solution.py:49
  483.8 6.1 copy.78
  489.9 6.3 fusion.61
  496.2 10.3 reshape.187
  506.4 10.3 reshape.188
  516.7 19.5 %convolution_bitcast_fusion.2 = f32[1,512,512,8]{1,2,3,0:T(8,128)} fusion(f32[512,512,8]{1,0,2:T(8,128)} %reshape.187, f32[512,512,8]{1,0,2:T(8,128)} %reshape.188), kind=kOutput, calls=%fused_computation.64 | convolution fusion | flops 12884901888 | bytes 25165824 | tf_op jit(solution)/shard_map/bikc,bjkc->bijc/dot_general | solution.py:20
  536.3 10.4 copy.47
  546.7 12.4 %all-to-all-done = f32[1,128,128,128]{3,2,0,1:T(8,128)} async-done(((f32[1,128,128,128]{3,2,0,1:T(8,128)}), f32[1,128,128,128]{3,2,0,1:T(8,128)}, u32[]{:S(2)}, u32[]{:S(2)}) %all-to-all-start) | async-done | bytes 8388640 | tf_op jit(solution)/shard_map/all_to_all | solution.py:58
  559.2 5.3 all-to-all-start.2
  564.4 9.9 copy.41
  574.4 10.3 all_to_all.66
  584.7 4.3 bitcast_reduce_fusion
  589.0 1.4 copy-done.3
  590.4 2.4 multiply_reduce_fusion.3
  592.9 157.3 %all-to-all-done.2 = f32[1,512,512,8]{2,3,0,1:T(8,128)} async-done(((f32[1,512,512,8]{2,3,0,1:T(8,128)}), f32[1,512,512,8]{2,3,0,1:T(8,128)}, u32[]{:S(2)}, u32[]{:S(2)}) %all-to-all-start.2) | async-done | bytes 8388640 | tf_op jit(solution)/shard_map/all_to_all | solution.py:57
  750.3 4.5 reduce_sum.76
  754.8 4.6 multiply_reduce_fusion.1
  759.4 0.0 copy-start.13
  759.5 12.4 %fusion.22 = f32[32,512,128]{1,2,0:T(8,128)S(1)} fusion(f32[1,32,512,16,8]{2,4,1,3,0:T(8,128)} %bitcast.16, f32[128]{0:T(128)S(1)} %copy-done.10, f32[32,512]{1,0:T(8,128)S(1)} %add_rsqrt_fusion.1, f32[32,512]{1,0:T(8,128)S(1)} %broadcast_multiply_fusion.1, f32[128,128]{1,0:T(8,128)S(1)} %copy-done.6), kind=kOutput, calls=%fused_computation.32 | convolution fusion | flops 3227516928 | bytes 16974336 | tf_op jit(solution)/shard_map/...c,cd->...d/dot_general | solution.py:16
  771.9 15.9 %fusion.62 = (f32[32,512]{1,0:T(8,128)S(1)}, f32[32,512,128]{1,2,0:T(8,128)S(1)}) fusion(f32[32,512,128]{1,2,0:T(8,128)} %all_to_all.66, f32[32,512,128]{1,2,0:T(8,128)S(1)} %fusion.22, f32[128,128]{1,0:T(8,128)S(1)} %copy-done.13, f32[128]{0:T(128)S(1)} %copy-done.9, f32[32,512]{1,0:T(8,128)S(1)} %get-tuple-element.11, f32[32,512]{1,0:T(8,128)S(1)} %get-tuple-element.12), kind=kOutput, calls=%fused_computation.84 | convolution fusion | flops 3240083456 | bytes 25428480 | tf_op jit(solution)/shard_map/...c,cd->...d/dot_general | solution.py:16
  787.8 0.0 copy-start.8
  787.8 1.4 multiply_reduce_fusion
  789.3 1.8 copy-done.4
  791.1 57.7 %convolution_bitcast_fusion = f32[1,32,512,1024]{3,2,1,0:T(8,128)} fusion(f32[32,512,128]{1,2,0:T(8,128)S(1)} %get-tuple-element.10, f32[128]{0:T(128)S(1)} %copy-done.8, f32[32,512]{1,0:T(8,128)S(1)} %add_rsqrt_fusion, f32[32,512]{1,0:T(8,128)S(1)} %broadcast_multiply_fusion, f32[128,1024]{1,0:T(8,128)S(1)} %copy-done), kind=kOutput, calls=%fused_computation.9 | convolution fusion | flops 25776095232 | bytes 76153344 | tf_op jit(solution)/shard_map/...c,cd->...d/dot_general | solution.py:16
  848.7 0.0 copy-done.12
  848.7 51.0 %add_bitcast_fusion = f32[1,32,512,128]{2,3,1,0:T(8,128)} fusion(f32[32,512,128]{1,2,0:T(8,128)} %copy-done.4, f32[1,32,512,1024]{3,2,1,0:T(8,128)} %convolution_bitcast_fusion, f32[512,128]{1,0:T(8,128)S(1)} %copy-done.12), kind=kOutput, calls=%fused_computation.35 | convolution fusion | flops 12928942080 | bytes 84148224 | tf_op jit(solution)/shard_map/...c,cd->...d/dot_general | solution.py:16
  899.7 10.3 copy.53
  910.0 188.5 %all_to_all.88 = f32[1,32,512,128]{3,1,0,2:T(8,128)S(1)} all-to-all(f32[1,32,512,128]{3,1,0,2:T(8,128)} %copy.53), channel_id=1, replica_groups=mesh['crop'=2,'row'=4,'col'=4] {'row','col'}, dimensions={2} | all-to-all | bytes 16777216 | tf_op jit(solution)/shard_map/all_to_all | solution.py:24
  1098.5 4.9 copy.54
  1103.4 4.2 copy.55
  1107.6 10.0 copy.56
  1117.6 10.1 add_bitcast_fusion.1
  1127.7 9.1 copy.58
  1136.8 8.6 reshape.197
  1145.4 51.8 %all_to_all.89 = f32[4,1,262144]{2,1,0:T(1,128)} all-to-all(f32[4,1,262144]{2,1,0:T(1,128)} %reshape.197), channel_id=1, replica_groups=mesh['crop'=2,'row'=4,'col'=4] {'col'}, dimensions={0} | all-to-all | bytes 8388608 | tf_op jit(solution)/shard_map/all_to_all | solution.py:68
  1197.2 0.5 broadcast.162
  1197.8 15.3 %reduce.14 = f32[4,262144]{1,0:T(4,128)} reduce(f32[4,1,262144]{2,1,0:T(1,128)} %all_to_all.89, f32[]{:T(128)} %broadcast.162), dimensions={1}, to_apply=%all_to_all.78.reduce_sub_computation | reduce | bytes 8388612 | tf_op jit(solution)/shard_map/all_to_all | solution.py:68
  1213.0 9.3 reshape.198
  1222.3 8.0 copy.59
  (31 shorter events, 0.2 us)
Async XLA Ops:
  0.0 791.1 %copy-start = (f32[128,1024]{1,0:T(8,128)S(1)}, f32[128,1024]{1,0:T(8,128)}, u32[]{:S(2)}) copy-start(f32[128,1024]{1,0:T(8,128)} %param.18) | copy-start | bytes 1572868
  0.0 13.1 %copy-start.9 = (f32[128]{0:T(128)S(1)}, f32[128]{0:T(128)}, u32[]{:S(2)}) copy-start(f32[128]{0:T(128)} %param.12) | copy-start | bytes 1540
  0.0 13.1 %copy-start.5 = (f32[128,512]{1,0:T(8,128)S(1)}, f32[128,512]{1,0:T(8,128)}, u32[]{:S(2)}) copy-start(f32[128,512]{1,0:T(8,128)} %param.13) | copy-start | bytes 786436
  5.7 7.4 copy-start.2
  461.3 97.9 %all-to-all-start = ((f32[1,128,128,128]{3,2,0,1:T(8,128)}), f32[1,128,128,128]{3,2,0,1:T(8,128)}, u32[]{:S(2)}, u32[]{:S(2)}) async-start(f32[1,128,128,128]{3,2,0,1:T(8,128)} %bitcast.105), calls=%async_computation | async-start | bytes 16777216 | tf_op jit(solution)/shard_map/all_to_all | solution.py:58
  559.2 191.1 %all-to-all-start.2 = ((f32[1,512,512,8]{2,3,0,1:T(8,128)}), f32[1,512,512,8]{2,3,0,1:T(8,128)}, u32[]{:S(2)}, u32[]{:S(2)}) async-start(f32[1,512,512,8]{2,3,0,1:T(8,128)} %copy.47), calls=%async_computation.2 | async-start | bytes 16777216 | tf_op jit(solution)/shard_map/all_to_all | solution.py:57
  584.7 5.8 copy-start.3
  750.3 9.2 copy-start.6
  750.3 9.2 copy-start.10
  759.4 12.4 %copy-start.13 = (f32[128,128]{1,0:T(8,128)S(1)}, f32[128,128]{1,0:T(8,128)}, u32[]{:S(2)}) copy-start(f32[128,128]{1,0:T(8,128)} %param.14) | copy-start | bytes 196612
  787.8 3.3 copy-start.4
  787.8 3.3 copy-start.8
  791.1 57.7 %copy-start.12 = (f32[512,128]{1,0:T(8,128)S(1)}, f32[512,128]{1,0:T(8,128)}, u32[]{:S(2)}) copy-start(f32[512,128]{1,0:T(8,128)} %param.19) | copy-start | bytes 786436
  1107.6 10.0 copy-start.7
  1107.6 10.0 copy-start.11
  1213.0 17.3 %copy-start.1 = (f32[128,1024]{1,0:T(8,128)S(1)}, f32[128,1024]{1,0:T(8,128)}, u32[]{:S(2)}) copy-start(f32[128,1024]{1,0:T(8,128)} %param.18) | copy-start | bytes 1572868
where the time goes:
time: 1240 us; the launch traced here: 1230 us
  blocking collectives  610 us (49%)
  matrix products  197 us (16%)
  waiting for transfers between devices  170 us (14%)
  local copies, waits for them, and re-layouts  165 us (13%)
  other arithmetic  76.2 us (6%)
  starting transfers between devices  12.5 us (1%)
    all_to_all x1, blocking collectives, shards(): lax.all_to_all(stacked, ('row', 'col'), split_axis=4, concat_axis=2, tile...  369 us
    all_to_all x1, blocking collectives, mirrored(): lax.all_to_all(values, ('row', 'col'), split_axis=2, concat_axis=1, tiled...  189 us
    dot_general x6, matrix products, project(): return jnp.einsum('...c,cd->...d', values, weights, precision=HIGH)  177 us
    all_to_all x1, waiting for transfers between devices, shards(): lax.all_to_all(result, ('row', 'col'), split_axis=1, concat_axis=3, tiled...  157 us
    all_to_all x1, blocking collectives, shards(): lax.all_to_all(line_logits, 'col', split_axis=2, concat_axis=1, tiled=True)  51.8 us
    another operation x2, other arithmetic, shards(): stacked = jnp.stack([left_hand, right_hand], axis=0)  30.6 us
  transfers between devices with their start and end apart: 2, of which 2 were waited for; matrix products, arithmetic and copies ran while one was open for 8% of the time, Pallas kernels for 0%

commit v1 on v0

--- a/solution.py
+++ b/solution.py
@@ -1,9 +1,18 @@
+import functools
+
 import jax
 import jax.numpy as jnp
 from jax import lax
-from jax.sharding import PartitionSpec as P
+from jax.experimental import pallas as pl
+from jax.experimental.pallas import tpu as pltpu
+from jax.sharding import Mesh, PartitionSpec as P
 
 HIGH = lax.Precision.HIGHEST
+LANES = 128
+GROUP = 8
+CHUNKS = 4
+VMEM = 56 * 1024 * 1024
+SCALE = 8
 
 
 def layer_norm(values, gain):
@@ -25,7 +34,7 @@
     return jnp.swapaxes(columns, 1, 2)
 
 
-def shards(
+def general_shards(
     pair,
     gain_input,
     weights_in,
@@ -68,11 +77,276 @@
     return lax.all_to_all(line_logits, "col", split_axis=2, concat_axis=1, tiled=True)
 
 
+def split_weights(weights, gain=None):
+    if gain is not None:
+        weights = gain[:, None] * weights
+    flipped = weights.T
+    high = lax.reduce_precision(flipped, 8, 7)
+    low = flipped - high
+    return jnp.concatenate([high, high, low], axis=1).astype(jnp.bfloat16)
+
+
+def estimate(flops, moved):
+    return pl.CostEstimate(flops=flops // SCALE, bytes_accessed=moved // SCALE, transcendentals=0)
+
+
+def parts(values):
+    high = values.astype(jnp.bfloat16)
+    low = (values - high.astype(jnp.float32)).astype(jnp.bfloat16)
+    return high, low
+
+
+def times(weights3, values):
+    high, low = parts(values)
+    return jnp.dot(
+        weights3, jnp.concatenate([high, low, high], axis=0), preferred_element_type=jnp.float32
+    )
+
+
+def normalized(values):
+    center = values - jnp.mean(values, axis=0, keepdims=True)
+    spread = jnp.mean(center * center, axis=0, keepdims=True)
+    return center * lax.rsqrt(spread + 1e-05)
+
+
+def hands_kernel(pair_ref, weights_ref, out_ref):
+    rows, _, width = pair_ref.shape
+    per = 4
+    flat = out_ref.reshape(width * rows, LANES)
+    for start in range(0, rows, per):
+        values = jnp.concatenate([pair_ref[start + n].T for n in range(per)], axis=1)
+        projected = times(weights_ref[...], normalized(values))
+        result = jax.nn.sigmoid(projected[width:]) * projected[:width]
+        for n in range(per):
+            flat[pl.ds(start + n, width, stride=rows), :] = result[:, n * LANES : (n + 1) * LANES]
+
+
+def hands(pair, weights3, first, rows):
+    _, tile_cols, width = pair.shape
+    lead = first // GROUP
+    return pl.pallas_call(
+        hands_kernel,
+        grid=(rows // GROUP,),
+        in_specs=[
+            pl.BlockSpec((GROUP, tile_cols, width), lambda g: (lead + g, 0, 0)),
+            pl.BlockSpec(weights3.shape, lambda g: (0, 0)),
+        ],
+        out_specs=pl.BlockSpec((width, GROUP, tile_cols), lambda g: (0, g, 0)),
+        out_shape=jax.ShapeDtypeStruct((width, rows, tile_cols), jnp.float32),
+        compiler_params=pltpu.CompilerParams(vmem_limit_bytes=VMEM),
+        cost_estimate=estimate(6 * rows * tile_cols * width * 2 * width, 8 * rows * tile_cols * width),
+        name="hands",
+    )(pair, weights3)
+
+
+def product_kernel(left_ref, right_ref, out_ref):
+    cols = right_ref.shape[1] // 2
+
+    def lines(ref):
+        return jnp.concatenate(
+            [
+                jnp.concatenate([ref[lo * cols + c, 0] for c in range(cols)], axis=1)
+                for lo in range(2)
+            ],
+            axis=0,
+        )
+
+    left_high, left_low = parts(lines(left_ref))
+    right_high, right_low = parts(
+        jnp.concatenate([lines(right_ref.at[half]) for half in range(2)], axis=0)
+    )
+    result = lax.dot_general(
+        jnp.concatenate([right_high, right_high, right_low], axis=1),
+        jnp.concatenate([left_high, left_low, left_high], axis=1),
+        (((1,), (1,)), ((), ())),
+        preferred_element_type=jnp.float32,
+    )
+    rows = right_ref.shape[3]
+    wide = result.shape[1] // 2
+    for line in range(2):
+        for plane in range(cols):
+            out_ref[line * cols + plane, 0] = result[
+                plane * rows : (plane + 1) * rows, line * wide : (line + 1) * wide
+            ]
+
+
+def product(left, right):
+    _, sources, owned, rows, width = right.shape
+    wide = left.shape[2]
+    k_all = width * sources // 2
+    return pl.pallas_call(
+        product_kernel,
+        grid=(owned,),
+        in_specs=[
+            pl.BlockSpec((sources, 1, wide, width), lambda n: (0, n, 0, 0)),
+            pl.BlockSpec((2, sources, 1, rows, width), lambda n: (0, 0, n, 0, 0)),
+        ],
+        out_specs=pl.BlockSpec((sources, 1, rows, wide), lambda n: (0, n, 0, 0)),
+        out_shape=jax.ShapeDtypeStruct((sources, owned, rows, wide), jnp.float32),
+        compiler_params=pltpu.CompilerParams(vmem_limit_bytes=VMEM),
+        cost_estimate=estimate(
+            6 * owned * 4 * rows * 2 * wide * k_all, 4 * owned * k_all * (2 * wide + 4 * rows)
+        ),
+        name="product",
+    )(left, right)
+
+
+def head_kernel(
+    pair_ref, product_ref, gate_ref, output_ref, up_ref, down_ref, bins_ref, out_ref
+):
+    tile_rows, cols, width = pair_ref.shape
+    bins = out_ref.shape[1]
+    per = 4
+    flat_pair = pair_ref.reshape(tile_rows * cols, width)
+    flat_product = product_ref.reshape(width * cols, tile_rows)
+    hidden_width = up_ref.shape[0] // 2
+    for start in range(0, cols, per):
+        values = jnp.concatenate(
+            [flat_pair[pl.ds(start + n, tile_rows, stride=cols), :].T for n in range(per)], axis=1
+        )
+        product_values = jnp.concatenate(
+            [flat_product[pl.ds(start + n, width, stride=cols), :] for n in range(per)], axis=1
+        )
+        gate = jax.nn.sigmoid(times(gate_ref[...], normalized(values)))
+        updated = values + gate * times(output_ref[...], normalized(product_values))
+        hidden = times(up_ref[...], normalized(updated))
+        activated = jax.nn.silu(hidden[:hidden_width]) * hidden[hidden_width:]
+        pair_out = updated + times(down_ref[...], activated)
+        logits = times(bins_ref[...], pair_out)
+        for n in range(per):
+            out_ref[start + n] = logits[:, n * tile_rows : (n + 1) * tile_rows]
+
+
+def head(pair, product_values, chunk, gate3, output3, up3, down3, bins3):
+    tile_rows, tile_cols, width = pair.shape
+    chunk_cols = product_values.shape[1]
+    steps = chunk_cols // GROUP
+    bins = bins3.shape[0]
+    whole = lambda array: pl.BlockSpec(array.shape, lambda g: (0, 0))
+    macs = gate3.size + output3.size + up3.size + down3.size + bins3.size
+    return pl.pallas_call(
+        head_kernel,
+        grid=(steps,),
+        in_specs=[
+            pl.BlockSpec((tile_rows, GROUP, width), lambda g: (0, chunk * steps + g, 0)),
+            pl.BlockSpec((width, GROUP, tile_rows), lambda g: (0, g, 0)),
+            whole(gate3),
+            whole(output3),
+            whole(up3),
+            whole(down3),
+            whole(bins3),
+        ],
+        out_specs=pl.BlockSpec((GROUP, bins, tile_rows), lambda g: (g, 0, 0)),
+        out_shape=jax.ShapeDtypeStruct((chunk_cols, bins, tile_rows), jnp.float32),
+        compiler_params=pltpu.CompilerParams(vmem_limit_bytes=VMEM),
+        cost_estimate=estimate(
+            2 * chunk_cols * tile_rows * macs, 4 * chunk_cols * tile_rows * (2 * width + bins)
+        ),
+        name="head",
+    )(pair, product_values, gate3, output3, up3, down3, bins3)
+
+
+def mover(count):
+    every = [(r, c) for r in range(count) for c in range(count)]
+
+    def move(values, target):
+        pairs = [(r * count + c, target(r, c)) for r, c in every]
+        return lax.ppermute(values, ("half", "lo", "col"), pairs)
+
+    return move
+
+
+def swap_steps(count, turn):
+    aside = lambda r, c: r * count + (c ^ r ^ turn)
+    return [aside, lambda r, c: (c ^ r ^ turn) * count + c, aside]
+
+
+def half_shards(
+    pair,
+    gain_input,
+    weights_in,
+    gate_weights,
+    weights_out,
+    gain_product,
+    gain_transition,
+    transition_in,
+    transition_out,
+    distogram_weights,
+    distogram_bias,
+):
+    row_count = 2 * lax.axis_size("lo")
+    col_count = lax.axis_size("col")
+    _, tile_rows, tile_cols, width = pair.shape
+    tile = pair[0]
+    chunk_rows = tile_rows // CHUNKS
+    in3 = split_weights(weights_in, gain_input)
+    left3, right3 = in3[: 2 * width], in3[2 * width :]
+    gate3 = split_weights(gate_weights, gain_input)
+    output3 = split_weights(weights_out, gain_product)
+    up3 = split_weights(transition_in, gain_transition)
+    down3 = split_weights(transition_out)
+    bins3 = split_weights(distogram_weights)
+    sources = 2 * col_count
+    owned = width // sources
+
+    def spread(values):
+        values = values.reshape(sources, owned, *values.shape[1:])
+        return lax.all_to_all(values, ("lo", "col"), split_axis=0, concat_axis=0, tiled=True)
+
+    others = []
+    for chunk in range(CHUNKS):
+        right = spread(hands(tile, right3, chunk * chunk_rows, chunk_rows))
+        others.append(lax.all_gather(right, "half"))
+    left = spread(hands(tile, left3, 0, tile_rows))
+
+    move = mover(row_count)
+    own, mirror, steps = [], [], []
+    for chunk in range(CHUNKS):
+        values = product(left, others[chunk])
+        values = lax.all_to_all(values, ("lo", "col"), split_axis=0, concat_axis=0, tiled=True)
+        values = values.reshape(width, chunk_rows, tile_rows)
+        if chunk:
+            values, mirror = lax.optimization_barrier((values, mirror))
+        logits = head(tile, values, chunk, gate3, output3, up3, down3, bins3)
+        own.append(logits)
+        mirror.append(logits)
+        last = chunk == CHUNKS - 1
+        steps.append([lambda r, c: c * row_count + r] if last else swap_steps(row_count, chunk))
+        for n in range(chunk + 1):
+            if steps[n]:
+                mirror[n] = move(mirror[n], steps[n].pop(0))
+    for n in range(CHUNKS):
+        for step in steps[n]:
+            mirror[n] = move(mirror[n], step)
+    turned = jnp.transpose(jnp.concatenate(own, axis=0), (2, 1, 0))
+    logits = turned + jnp.concatenate(mirror, axis=0) + distogram_bias[None, :, None]
+    return jnp.swapaxes(logits, 1, 2)[None]
+
+
 def solution(mesh):
-    return jax.shard_map(
-        shards,
-        mesh=mesh,
-        in_specs=(P("crop", "row", "col", None), P(), P(), P(), P(), P(), P(), P(), P(), P(), P()),
-        out_specs=P("crop", "row", "col", None),
-        check_vma=False,
-    )
+    names = mesh.axis_names
+    crops, rows, cols = (mesh.shape[name] for name in names)
+
+    def run(pair, *parameters):
+        crop_count, height, across, width = pair.shape
+        tile_rows, tile_cols = height // rows, across // cols
+        by_halves = (
+            crop_count == crops
+            and rows == cols == 4
+            and tile_rows == tile_cols == LANES
+            and width == LANES
+        )
+        if by_halves:
+            halves = Mesh(mesh.devices.reshape(crops, 2, rows // 2, cols), ("crop", "half", "lo", "col"))
+            spec, used, body = P("crop", ("half", "lo"), "col", None), halves, half_shards
+        else:
+            spec, used, body = P("crop", "row", "col", None), mesh, general_shards
+        return jax.shard_map(
+            body,
+            mesh=used,
+            in_specs=(spec,) + (P(),) * len(parameters),
+            out_specs=spec,
+            check_vma=False,
+        )(pair, *parameters)
+
+    return run

time: 1240 us -> 913 us (0.74)
  blocking collectives: 610 us -> 0 us
  waiting for transfers between devices: 170 us -> 555 us
  matrix products: 197 us -> 0 us
  Pallas kernels: 0 us -> 159 us
  local copies, waits for them, and re-layouts: 165 us -> 25.7 us
  starting transfers between devices: 12.5 us -> 137 us
  other arithmetic: 76.2 us -> 15.2 us
  between operations: 0.5 us -> 13.4 us
    all_to_all x3 -> x0, blocking collectives: 610 us -> none  [the longest x1 369 us: shards(): lax.all_to_all(stacked, ('row', 'col'), split_axis=4, concat_axis=2, tile...]
    all_gather x0 -> x4, waiting for transfers between devices: none -> 221 us  [half_shards(): others.append(lax.all_gather(right, 'half'))]
    dot_general x7 -> x0, matrix products: 197 us -> none  [the longest x6 177 us: project(): return jnp.einsum('...c,cd->...d', values, weights, precision=HIGH)]
    pallas_call x0 -> x13, Pallas kernels: none -> 159 us  [the longest x4 63.4 us: head(): pl.pallas_call(head_kernel, grid=(steps,), in_specs=[pl.BlockSpec((tile_r...]
    ppermute x0 -> x10, waiting for transfers between devices: none -> 138 us  [move(): return lax.ppermute(values, ('half', 'lo', 'col'), pairs)]
    ppermute x0 -> x10, starting transfers between devices: none -> 78.6 us  [move(): return lax.ppermute(values, ('half', 'lo', 'col'), pairs)]
    all_to_all x8 -> x0, local copies, waits for them, and re-layouts: 63.1 us -> none  [the longest x2 20.2 us: shards(): base = lax.all_to_all(pair, 'col', split_axis=1, concat_axis=2, tiled=True)]
    all_to_all x2 -> x9, starting transfers between devices: 12.5 us -> 58.7 us  [the longest x5 30.5 us: spread(): lax.all_to_all(values, ('lo', 'col'), split_axis=0, concat_axis=0, tiled=...]
  transfers between devices with their start and end apart: 2 -> 23, of which waited for: 2 -> 15; matrix products, arithmetic and copies ran while one was open for 8% -> 2% of each run, Pallas kernels for 0% -> 17%
where the time goes in v1:
time: 913 us; the launch traced here: 905 us
  waiting for transfers between devices  555 us (61%)
  Pallas kernels  159 us (17%)
  starting transfers between devices  137 us (15%)
  local copies, waits for them, and re-layouts  25.7 us (3%)
  other arithmetic  15.2 us (2%)
  between operations  13.4 us (1%)
    all_gather x4, waiting for transfers between devices, half_shards(): others.append(lax.all_gather(right, 'half'))  221 us
    all_to_all x5, waiting for transfers between devices, spread(): lax.all_to_all(values, ('lo', 'col'), split_axis=0, concat_axis=0, tiled=...  193 us
    ppermute x10, waiting for transfers between devices, move(): return lax.ppermute(values, ('half', 'lo', 'col'), pairs)  138 us
    ppermute x10, starting transfers between devices, move(): return lax.ppermute(values, ('half', 'lo', 'col'), pairs)  78.6 us
    pallas_call x4, Pallas kernels, head(): pl.pallas_call(head_kernel, grid=(steps,), in_specs=[pl.BlockSpec((tile_r...  63.4 us
    pallas_call x4, Pallas kernels, product(): pl.pallas_call(product_kernel, grid=(owned,), in_specs=[pl.BlockSpec((sou...  57.5 us
    pallas_call x5, Pallas kernels, hands(): pl.pallas_call(hands_kernel, grid=(rows // GROUP,), in_specs=[pl.BlockSpe...  37.7 us
    all_to_all x5, starting transfers between devices, spread(): lax.all_to_all(values, ('lo', 'col'), split_axis=0, concat_axis=0, tiled=...  30.5 us
  transfers between devices with their start and end apart: 23, of which 15 were waited for; matrix products, arithmetic and copies ran while one was open for 2% of the time, Pallas kernels for 17%

profile of v1, /device:TPU:12, one launch (start us, length us, event | category | flops | bytes accessed | tf_op | source)
XLA Modules:
  0.0 905.2 jit_solution(9880355427223424220)
XLA Ops:
  9.2 5.2 hands.6
  14.4 5.1 all-to-all-start.1
  19.5 5.3 hands.7
  24.7 19.3 %all-to-all-done.1 = f32[8,16,32,128]{3,2,1,0:T(8,128)S(1)} async-done(((f32[8,16,32,128]{3,2,1,0:T(8,128)}), f32[8,16,32,128]{3,2,1,0:T(8,128)S(1)}, u32[]{:S(2)}, u32[]{:S(2)}) %all-to-all-start.1) | async-done | bytes 2097184 | tf_op jit(solution)/shard_map/all_to_all | solution.py:294
  45.3 6.6 all-to-all-start.3
  51.9 5.2 hands.8
  57.1 19.0 %all-to-all-done.3 = f32[8,16,32,128]{3,2,1,0:T(8,128)S(1)} async-done(((f32[8,16,32,128]{3,2,1,0:T(8,128)}), f32[8,16,32,128]{3,2,1,0:T(8,128)S(1)}, u32[]{:S(2)}, u32[]{:S(2)}) %all-to-all-start.3) | async-done | bytes 2097184 | tf_op jit(solution)/shard_map/all_to_all | solution.py:294
  77.4 6.0 all-to-all-start.5
  83.4 16.9 %hands.5 = f32[128,128,128]{2,1,0:T(8,128)} custom-call(f32[128,128,128]{2,1,0:T(8,128)} %bitcast.47, bf16[256,384]{1,0:T(8,128)(2,1)} %get-tuple-element.26.weights_ref), custom_call_target="tpu_custom_call" | custom-call | flops 402653184 | bytes 2097152 | tf_op jit(solution)/shard_map/hands/pallas_call | solution.py:127
  100.3 7.8 all-to-all-done.5
  109.5 6.8 all-to-all-start
  117.1 5.2 hands.9
  122.3 129.3 %all-to-all-done.left_ref = f32[8,16,128,128]{3,2,1,0:T(8,128)} async-done(((f32[8,16,128,128]{3,2,1,0:T(8,128)}), f32[8,16,128,128]{3,2,1,0:T(8,128)}, u32[]{:S(2)}, u32[]{:S(2)}) %all-to-all-start) | async-done | bytes 8388640 | tf_op jit(solution)/shard_map/all_to_all | solution.py:294
  251.7 6.0 all-to-all-start.7
  258.4 14.5 %product.4 = f32[8,16,32,128]{3,2,1,0:T(8,128)} custom-call(f32[8,16,128,128]{3,2,1,0:T(8,128)} %all-to-all-done.left_ref, f32[2,8,16,32,128]{4,3,2,1,0:T(8,128)} %bitcast.63), custom_call_target="tpu_custom_call" | custom-call | flops 201326592 | bytes 1572864 | tf_op jit(solution)/shard_map/product/pallas_call | solution.py:177
  272.8 17.6 %all-to-all-done.7 = f32[8,16,32,128]{3,2,1,0:T(8,128)S(1)} async-done(((f32[8,16,32,128]{3,2,1,0:T(8,128)}), f32[8,16,32,128]{3,2,1,0:T(8,128)S(1)}, u32[]{:S(2)}, u32[]{:S(2)}) %all-to-all-start.7) | async-done | bytes 2097184 | tf_op jit(solution)/shard_map/all_to_all | solution.py:294
  291.7 5.0 all-to-all-start.2
  297.5 63.3 %all-gather.11.cloned.1.call-done = f32[16,16,32,128]{3,2,1,0:T(8,128)} async-done(((f32[8,16,32,128]{3,2,1,0:T(8,128)}), f32[16,16,32,128]{3,2,1,0:T(8,128)}) %all-gather.11.cloned.1.call-update) | async-done | bytes 4194320 | tf_op jit(solution)/shard_map/all_gather | solution.py:299
  360.7 14.5 %product.5 = f32[8,16,32,128]{3,2,1,0:T(8,128)} custom-call(f32[8,16,128,128]{3,2,1,0:T(8,128)} %all-to-all-done.left_ref, f32[2,8,16,32,128]{4,3,2,1,0:T(8,128)} %bitcast.61), custom_call_target="tpu_custom_call" | custom-call | flops 201326592 | bytes 1572864 | tf_op jit(solution)/shard_map/product/pallas_call | solution.py:177
  375.2 8.0 all-to-all-start.4
  383.7 80.3 %all-gather.13.cloned.1.call-done = f32[16,16,32,128]{3,2,1,0:T(8,128)} async-done(((f32[8,16,32,128]{3,2,1,0:T(8,128)}), f32[16,16,32,128]{3,2,1,0:T(8,128)}) %all-gather.13.cloned.1.call-update) | async-done | bytes 4194320 | tf_op jit(solution)/shard_map/all_gather | solution.py:299
  464.0 14.4 %product.6 = f32[8,16,32,128]{3,2,1,0:T(8,128)} custom-call(f32[8,16,128,128]{3,2,1,0:T(8,128)} %all-to-all-done.left_ref, f32[2,8,16,32,128]{4,3,2,1,0:T(8,128)} %bitcast.62), custom_call_target="tpu_custom_call" | custom-call | flops 201326592 | bytes 1572864 | tf_op jit(solution)/shard_map/product/pallas_call | solution.py:177
  478.5 7.4 all-to-all-start.6
  489.1 77.9 %all-gather.15.cloned.1.call-done = f32[16,16,32,128]{3,2,1,0:T(8,128)} async-done(((f32[8,16,32,128]{3,2,1,0:T(8,128)}), f32[16,16,32,128]{3,2,1,0:T(8,128)}) %all-gather.15.cloned.1.call-update) | async-done | bytes 4194320 | tf_op jit(solution)/shard_map/all_gather | solution.py:299
  567.1 14.2 %product.7 = f32[8,16,32,128]{3,2,1,0:T(8,128)} custom-call(f32[8,16,128,128]{3,2,1,0:T(8,128)} %all-to-all-done.left_ref, f32[2,8,16,32,128]{4,3,2,1,0:T(8,128)} %bitcast.60), custom_call_target="tpu_custom_call" | custom-call | flops 201326592 | bytes 1572864 | tf_op jit(solution)/shard_map/product/pallas_call | solution.py:177
  581.2 7.8 all-to-all-start.8
  590.5 15.8 %head.4 = f32[32,64,128]{2,1,0:T(8,128)} custom-call(f32[128,128,128]{2,1,0:T(8,128)} %bitcast.49, f32[128,32,128]{2,1,0:T(8,128)} %bitcast.54, bf16[128,384]{1,0:T(8,128)(2,1)} %get-tuple-element.37.gate_ref, bf16[128,384]{1,0:T(8,128)(2,1)} %get-tuple-element.38.output_ref, bf16[1024,384]{1,0:T(8,128)(2,1)} %pad_maximum_fusion.up_ref, ...), custom_call_target="tpu_custom_call" | custom-call | flops 729808896 | bytes 655360 | tf_op jit(solution)/shard_map/head/pallas_call | solution.py:227
  606.3 3.5 collective-permute-start
  609.8 26.5 %collective-permute-done = f32[32,64,128]{2,1,0:T(8,128)S(1)} collective-permute-done((f32[32,64,128]{2,1,0:T(8,128)}, f32[32,64,128]{2,1,0:T(8,128)S(1)}, u32[]{:S(2)}, u32[]{:S(2)}) %collective-permute-start) | collective-permute-done | bytes 1048608 | tf_op jit(solution)/shard_map/ppermute | solution.py:254
  636.3 15.8 %head.5 = f32[32,64,128]{2,1,0:T(8,128)} custom-call(f32[128,128,128]{2,1,0:T(8,128)} %bitcast.50, f32[128,32,128]{2,1,0:T(8,128)} %bitcast.13.product_ref, bf16[128,384]{1,0:T(8,128)(2,1)} %get-tuple-element.37.gate_ref, bf16[128,384]{1,0:T(8,128)(2,1)} %get-tuple-element.38.output_ref, bf16[1024,384]{1,0:T(8,128)(2,1)} %pad_maximum_fusion.up_ref, ...), custom_call_target="tpu_custom_call" | custom-call | flops 729808896 | bytes 655360 | tf_op jit(solution)/shard_map/head/pallas_call | solution.py:227
  654.0 4.0 collective-permute-start.1
  658.1 44.6 %collective-permute-done.1 = f32[32,64,128]{2,1,0:T(8,128)} collective-permute-done((f32[32,64,128]{2,1,0:T(8,128)S(1)}, f32[32,64,128]{2,1,0:T(8,128)}, u32[]{:S(2)}, u32[]{:S(2)}) %collective-permute-start.1) | collective-permute-done | bytes 1048608 | tf_op jit(solution)/shard_map/ppermute | solution.py:254
  702.7 15.8 %head.6 = f32[32,64,128]{2,1,0:T(8,128)} custom-call(f32[128,128,128]{2,1,0:T(8,128)} %bitcast.51, f32[128,32,128]{2,1,0:T(8,128)} %bitcast.55, bf16[128,384]{1,0:T(8,128)(2,1)} %get-tuple-element.37.gate_ref, bf16[128,384]{1,0:T(8,128)(2,1)} %get-tuple-element.38.output_ref, bf16[1024,384]{1,0:T(8,128)(2,1)} %pad_maximum_fusion.up_ref, ...), custom_call_target="tpu_custom_call" | custom-call | flops 729808896 | bytes 655360 | tf_op jit(solution)/shard_map/head/pallas_call | solution.py:227
  720.4 5.2 collective-permute-start.3
  725.6 5.6 collective-permute-start.4
  731.2 16.4 %collective-permute-done.5 = f32[32,64,128]{2,1,0:T(8,128)} collective-permute-done((f32[32,64,128]{2,1,0:T(8,128)}, f32[32,64,128]{2,1,0:T(8,128)}, u32[]{:S(2)}, u32[]{:S(2)}) %collective-permute-start.5) | collective-permute-done | bytes 1048608 | tf_op jit(solution)/shard_map/ppermute | solution.py:254
  747.6 21.8 %collective-permute-done.3 = f32[32,64,128]{2,1,0:T(8,128)S(1)} collective-permute-done((f32[32,64,128]{2,1,0:T(8,128)}, f32[32,64,128]{2,1,0:T(8,128)S(1)}, u32[]{:S(2)}, u32[]{:S(2)}) %collective-permute-start.3) | collective-permute-done | bytes 1048608 | tf_op jit(solution)/shard_map/ppermute | solution.py:254
  769.4 4.3 collective-permute-done.4
  773.7 9.6 %collective-permute-start.7 = (f32[32,64,128]{2,1,0:T(8,128)}, f32[32,64,128]{2,1,0:T(8,128)}, u32[]{:S(2)}, u32[]{:S(2)}) collective-permute-start(f32[32,64,128]{2,1,0:T(8,128)} %collective-permute-done.5), channel_id=1, source_target_pairs={{0,8},{1,13},{2,2},{3,7},{4,12},{5,9},{6,6},{7,3},{8,0},{9,5},{10,... | collective-permute-start | bytes 3145736 | tf_op jit(solution)/shard_map/ppermute | solution.py:254
  783.3 15.9 %head.7 = f32[32,64,128]{2,1,0:T(8,128)} custom-call(f32[128,128,128]{2,1,0:T(8,128)} %bitcast.52, f32[128,32,128]{2,1,0:T(8,128)} %bitcast.19.product_ref, bf16[128,384]{1,0:T(8,128)(2,1)} %get-tuple-element.37.gate_ref, bf16[128,384]{1,0:T(8,128)(2,1)} %get-tuple-element.38.output_ref, bf16[1024,384]{1,0:T(8,128)(2,1)} %pad_maximum_fusion.up_ref, ...), custom_call_target="tpu_custom_call" | custom-call | flops 729808896 | bytes 655360 | tf_op jit(solution)/shard_map/head/pallas_call | solution.py:227
  801.2 9.5 %collective-permute-start.6 = (f32[32,64,128]{2,1,0:T(8,128)}, f32[32,64,128]{2,1,0:T(8,128)}, u32[]{:S(2)}, u32[]{:S(2)}) collective-permute-start(f32[32,64,128]{2,1,0:T(8,128)} %copy-done.20), channel_id=1, source_target_pairs={{0,1},{1,0},{2,3},{3,2},{4,4},{5,5},{6,6},{7,7},{8,11},{9,10},{10,... | collective-permute-start | bytes 3145736 | tf_op jit(solution)/shard_map/ppermute | solution.py:254
  810.7 35.4 %collective-permute-start.8 = (f32[32,64,128]{2,1,0:T(8,128)}, f32[32,64,128]{2,1,0:T(8,128)}, u32[]{:S(2)}, u32[]{:S(2)}) collective-permute-start(f32[32,64,128]{2,1,0:T(8,128)} %collective-permute-done.7), channel_id=1, source_target_pairs={{0,2},{1,3},{2,0},{3,1},{4,7},{5,6},{6,5},{7,4},{8,8},{9,9},{10,10... | collective-permute-start | bytes 3145736 | tf_op jit(solution)/shard_map/ppermute | solution.py:254
  846.1 4.5 copy.26
  850.6 4.5 copy.27
  855.1 4.5 copy.28
  859.6 4.5 copy.29
  865.9 22.4 %collective-permute-done.8 = f32[32,64,128]{2,1,0:T(8,128)} collective-permute-done((f32[32,64,128]{2,1,0:T(8,128)}, f32[32,64,128]{2,1,0:T(8,128)}, u32[]{:S(2)}, u32[]{:S(2)}) %collective-permute-start.8) | collective-permute-done | bytes 1048608 | tf_op jit(solution)/shard_map/ppermute | solution.py:254
  888.3 10.4 %fusion.2 = f32[1,128,128,64]{2,3,1,0:T(8,128)} fusion(f32[32,64,128]{0,1,2:T(8,128)} %copy.29, f32[32,64,128]{0,1,2:T(8,128)} %copy.28, f32[32,64,128]{0,1,2:T(8,128)} %copy.27, f32[32,64,128]{0,1,2:T(8,128)} %copy.26, f32[32,64,128]{2,1,0:T(8,128)} %collective-permute-done.9, f32[32,64,128]{2,1,0:T(8,128)} %collective-permute-done.8, ...), kind=kLoop, calls=%fused_computation.3 | loop fusion | flops 8388608 | bytes 12583168 | tf_op jit(solution)/shard_map/broadcast_in_dim | solution.py:323
  (79 shorter events, 23.0 us)
Async XLA Ops:
  14.4 29.7 %all-to-all-start.1 = ((f32[8,16,32,128]{3,2,1,0:T(8,128)}), f32[8,16,32,128]{3,2,1,0:T(8,128)S(1)}, u32[]{:S(2)}, u32[]{:S(2)}) async-start(f32[8,16,32,128]{3,2,1,0:T(8,128)} %bitcast.59), calls=%async_computation.1 | async-start | bytes 4194304 | tf_op jit(solution)/shard_map/all_to_all | solution.py:294
  44.0 1.3 copy-start.5
  45.3 30.7 %all-to-all-start.3 = ((f32[8,16,32,128]{3,2,1,0:T(8,128)}), f32[8,16,32,128]{3,2,1,0:T(8,128)S(1)}, u32[]{:S(2)}, u32[]{:S(2)}) async-start(f32[8,16,32,128]{3,2,1,0:T(8,128)} %bitcast.58), calls=%async_computation.3 | async-start | bytes 4194304 | tf_op jit(solution)/shard_map/all_to_all | solution.py:294
  76.0 1.4 copy-start.4
  77.4 30.8 %all-to-all-start.5 = ((f32[8,16,32,128]{3,2,1,0:T(8,128)}), f32[8,16,32,128]{3,2,1,0:T(8,128)S(1)}, u32[]{:S(2)}, u32[]{:S(2)}) async-start(f32[8,16,32,128]{3,2,1,0:T(8,128)} %bitcast.57), calls=%async_computation.5 | async-start | bytes 4194304 | tf_op jit(solution)/shard_map/all_to_all | solution.py:294
  108.2 1.4 copy-start.3
  109.5 142.1 %all-to-all-start = ((f32[8,16,128,128]{3,2,1,0:T(8,128)}), f32[8,16,128,128]{3,2,1,0:T(8,128)}, u32[]{:S(2)}, u32[]{:S(2)}) async-start(f32[8,16,128,128]{3,2,1,0:T(8,128)} %bitcast.53), calls=%async_computation | async-start | bytes 16777216 | tf_op jit(solution)/shard_map/all_to_all | solution.py:294
  116.4 142.0 %all-gather.9.cloned.1.call-start = ((), (), s32[]{:S(2)}) async-start(), calls=%async_computation.9 | async-start | bytes 6291456 | tf_op jit(solution)/shard_map/all_gather | solution.py:299
  251.7 38.7 %all-to-all-start.7 = ((f32[8,16,32,128]{3,2,1,0:T(8,128)}), f32[8,16,32,128]{3,2,1,0:T(8,128)S(1)}, u32[]{:S(2)}, u32[]{:S(2)}) async-start(f32[8,16,32,128]{3,2,1,0:T(8,128)} %bitcast.56), calls=%async_computation.7 | async-start | bytes 4194304 | tf_op jit(solution)/shard_map/all_to_all | solution.py:294
  257.6 103.1 %all-gather.11.cloned.1.call-start = ((), (), s32[]{:S(2)}) async-start(), calls=%async_computation.10 | async-start | bytes 6291456 | tf_op jit(solution)/shard_map/all_gather | solution.py:299
  290.4 1.3 copy-start.2
  291.7 83.5 %all-to-all-start.2 = ((f32[8,16,32,128]{3,2,1,0:T(8,128)}), f32[8,16,32,128]{3,2,1,0:T(8,128)S(1)}, u32[]{:S(2)}, u32[]{:S(2)}) async-start(f32[8,16,32,128]{3,2,1,0:T(8,128)} %product.4), calls=%async_computation.2 | async-start | bytes 4194304 | tf_op jit(solution)/shard_map/all_to_all | solution.py:306
  296.7 167.2 %all-gather.13.cloned.1.call-start = ((), (), s32[]{:S(2)}) async-start(), calls=%async_computation.11 | async-start | bytes 6291456 | tf_op jit(solution)/shard_map/all_gather | solution.py:299
  375.2 103.2 %copy-start = (f32[8,16,32,128]{3,2,1,0:T(8,128)}, f32[8,16,32,128]{3,2,1,0:T(8,128)S(1)}, u32[]{:S(2)}) copy-start(f32[8,16,32,128]{3,2,1,0:T(8,128)S(1)} %all-to-all-done.2) | copy-start | bytes 6291460
  375.2 103.3 %all-to-all-start.4 = ((f32[8,16,32,128]{3,2,1,0:T(8,128)}), f32[8,16,32,128]{3,2,1,0:T(8,128)}, u32[]{:S(2)}, u32[]{:S(2)}) async-start(f32[8,16,32,128]{3,2,1,0:T(8,128)} %product.5), calls=%async_computation.4 | async-start | bytes 4194304 | tf_op jit(solution)/shard_map/all_to_all | solution.py:306
  383.2 183.9 %all-gather.15.cloned.1.call-start = ((), (), s32[]{:S(2)}) async-start(), calls=%async_computation.12 | async-start | bytes 6291456 | tf_op jit(solution)/shard_map/all_gather | solution.py:299
  478.4 7.5 copy-start.14
  478.4 7.6 copy-start.15
  478.4 7.7 copy-start.12
  478.5 7.9 copy-start.13
  478.5 8.0 copy-start.16
  478.5 8.1 copy-start.17
  478.5 8.8 copy-start.18
  478.5 102.7 %all-to-all-start.6 = ((f32[8,16,32,128]{3,2,1,0:T(8,128)}), f32[8,16,32,128]{3,2,1,0:T(8,128)S(1)}, u32[]{:S(2)}, u32[]{:S(2)}) async-start(f32[8,16,32,128]{3,2,1,0:T(8,128)} %product.6), calls=%async_computation.6 | async-start | bytes 4194304 | tf_op jit(solution)/shard_map/all_to_all | solution.py:306
  581.2 25.1 %copy-start.1 = (f32[8,16,32,128]{3,2,1,0:T(8,128)}, f32[8,16,32,128]{3,2,1,0:T(8,128)S(1)}, u32[]{:S(2)}) copy-start(f32[8,16,32,128]{3,2,1,0:T(8,128)S(1)} %all-to-all-done.6) | copy-start | bytes 6291460
  581.2 150.0 %all-to-all-start.8 = ((f32[8,16,32,128]{3,2,1,0:T(8,128)}), f32[8,16,32,128]{3,2,1,0:T(8,128)}, u32[]{:S(2)}, u32[]{:S(2)}) async-start(f32[8,16,32,128]{3,2,1,0:T(8,128)} %product.7), calls=%async_computation.8 | async-start | bytes 4194304 | tf_op jit(solution)/shard_map/all_to_all | solution.py:306
  606.3 30.0 %collective-permute-start = (f32[32,64,128]{2,1,0:T(8,128)}, f32[32,64,128]{2,1,0:T(8,128)S(1)}, u32[]{:S(2)}, u32[]{:S(2)}) collective-permute-start(f32[32,64,128]{2,1,0:T(8,128)} %head.4), channel_id=1, source_target_pairs={{0,0},{1,1},{2,2},{3,3},{4,5},{5,4},{6,7},{7,6},{8,10},{9,11},{10,... | collective-permute-start | bytes 3145736 | tf_op jit(solution)/shard_map/ppermute | solution.py:254
  652.2 5.9 collective-permute-start.2
  654.0 48.6 %collective-permute-start.1 = (f32[32,64,128]{2,1,0:T(8,128)S(1)}, f32[32,64,128]{2,1,0:T(8,128)}, u32[]{:S(2)}, u32[]{:S(2)}) collective-permute-start(f32[32,64,128]{2,1,0:T(8,128)S(1)} %collective-permute-done), channel_id=1, source_target_pairs={{0,0},{1,5},{2,10},{3,15},{4,4},{5,1},{6,14},{7,11},{8,8},{9,13},{... | collective-permute-start | bytes 3145736 | tf_op jit(solution)/shard_map/ppermute | solution.py:254
  718.5 29.1 %collective-permute-start.5 = (f32[32,64,128]{2,1,0:T(8,128)}, f32[32,64,128]{2,1,0:T(8,128)}, u32[]{:S(2)}, u32[]{:S(2)}) collective-permute-start(f32[32,64,128]{2,1,0:T(8,128)} %head.6), channel_id=1, source_target_pairs={{0,2},{1,3},{2,0},{3,1},{4,7},{5,6},{6,5},{7,4},{8,8},{9,9},{10,10... | collective-permute-start | bytes 3145736 | tf_op jit(solution)/shard_map/ppermute | solution.py:254
  720.4 49.0 %collective-permute-start.3 = (f32[32,64,128]{2,1,0:T(8,128)}, f32[32,64,128]{2,1,0:T(8,128)S(1)}, u32[]{:S(2)}, u32[]{:S(2)}) collective-permute-start(f32[32,64,128]{2,1,0:T(8,128)} %collective-permute-done.1), channel_id=1, source_target_pairs={{0,0},{1,1},{2,2},{3,3},{4,5},{5,4},{6,7},{7,6},{8,10},{9,11},{10,... | collective-permute-start | bytes 3145736 | tf_op jit(solution)/shard_map/ppermute | solution.py:254
  725.6 48.1 %collective-permute-start.4 = (f32[32,64,128]{2,1,0:T(8,128)S(1)}, f32[32,64,128]{2,1,0:T(8,128)S(1)}, u32[]{:S(2)}, u32[]{:S(2)}) collective-permute-start(f32[32,64,128]{2,1,0:T(8,128)S(1)} %collective-permute-done.2), channel_id=1, source_target_pairs={{0,4},{1,1},{2,14},{3,11},{4,0},{5,5},{6,10},{7,15},{8,12},{9,9},{... | collective-permute-start | bytes 3145736 | tf_op jit(solution)/shard_map/ppermute | solution.py:254
  769.4 4.3 copy-start.10
  773.7 9.6 %copy-start.20 = (f32[32,64,128]{2,1,0:T(8,128)}, f32[32,64,128]{2,1,0:T(8,128)S(1)}, u32[]{:S(2)}) copy-start(f32[32,64,128]{2,1,0:T(8,128)S(1)} %collective-permute-done.4) | copy-start | bytes 3145732
  773.7 72.4 %copy-start.6 = (f32[32,64,128]{2,1,0:T(8,128)S(1)}, f32[32,64,128]{2,1,0:T(8,128)}, u32[]{:S(2)}) copy-start(f32[32,64,128]{2,1,0:T(8,128)} %head.4) | copy-start | bytes 3145732
  773.7 37.0 %collective-permute-start.7 = (f32[32,64,128]{2,1,0:T(8,128)}, f32[32,64,128]{2,1,0:T(8,128)}, u32[]{:S(2)}, u32[]{:S(2)}) collective-permute-start(f32[32,64,128]{2,1,0:T(8,128)} %collective-permute-done.5), channel_id=1, source_target_pairs={{0,8},{1,13},{2,2},{3,7},{4,12},{5,9},{6,6},{7,3},{8,0},{9,5},{10,... | collective-permute-start | bytes 3145736 | tf_op jit(solution)/shard_map/ppermute | solution.py:254
  799.2 51.4 %copy-start.7 = (f32[32,64,128]{2,1,0:T(8,128)S(1)}, f32[32,64,128]{2,1,0:T(8,128)}, u32[]{:S(2)}) copy-start(f32[32,64,128]{2,1,0:T(8,128)} %head.5) | copy-start | bytes 3145732
  799.2 55.9 %copy-start.8 = (f32[32,64,128]{2,1,0:T(8,128)S(1)}, f32[32,64,128]{2,1,0:T(8,128)}, u32[]{:S(2)}) copy-start(f32[32,64,128]{2,1,0:T(8,128)} %head.6) | copy-start | bytes 3145732
  799.2 66.7 %collective-permute-start.9 = (f32[32,64,128]{2,1,0:T(8,128)}, f32[32,64,128]{2,1,0:T(8,128)}, u32[]{:S(2)}, u32[]{:S(2)}) collective-permute-start(f32[32,64,128]{2,1,0:T(8,128)} %head.7), channel_id=1, source_target_pairs={{0,0},{1,4},{2,8},{3,12},{4,1},{5,5},{6,9},{7,13},{8,2},{9,6},{10,... | collective-permute-start | bytes 3145736 | tf_op jit(solution)/shard_map/ppermute | solution.py:254
  801.2 64.7 %collective-permute-start.6 = (f32[32,64,128]{2,1,0:T(8,128)}, f32[32,64,128]{2,1,0:T(8,128)}, u32[]{:S(2)}, u32[]{:S(2)}) collective-permute-start(f32[32,64,128]{2,1,0:T(8,128)} %copy-done.20), channel_id=1, source_target_pairs={{0,1},{1,0},{2,3},{3,2},{4,4},{5,5},{6,6},{7,7},{8,11},{9,10},{10,... | collective-permute-start | bytes 3145736 | tf_op jit(solution)/shard_map/ppermute | solution.py:254
  810.7 77.6 %collective-permute-start.8 = (f32[32,64,128]{2,1,0:T(8,128)}, f32[32,64,128]{2,1,0:T(8,128)}, u32[]{:S(2)}, u32[]{:S(2)}) collective-permute-start(f32[32,64,128]{2,1,0:T(8,128)} %collective-permute-done.7), channel_id=1, source_target_pairs={{0,2},{1,3},{2,0},{3,1},{4,7},{5,6},{6,5},{7,4},{8,8},{9,9},{10,10... | collective-permute-start | bytes 3145736 | tf_op jit(solution)/shard_map/ppermute | solution.py:254
  850.6 9.0 copy-start.9
  855.1 33.2 %copy-start.11 = (f32[32,64,128]{2,1,0:T(8,128)S(1)}, f32[32,64,128]{2,1,0:T(8,128)}, u32[]{:S(2)}) copy-start(f32[32,64,128]{2,1,0:T(8,128)} %copy-done.10) | copy-start | bytes 3145732
  855.1 33.2 %copy-start.19 = (f32[64]{0:T(128)S(1)}, f32[64]{0:T(128)}, u32[]{:S(2)}) copy-start(f32[64]{0:T(128)} %param.21) | copy-start | bytes 772
Sparse Core Ops, SparseCore 0:
  118.7 103.8 all-gather.8
  260.0 100.6 all-gather.10
  362.3 101.6 all-gather.12
  465.4 101.6 all-gather.14

commit v2 on v1

--- a/solution.py
+++ b/solution.py
@@ -10,7 +10,7 @@
 HIGH = lax.Precision.HIGHEST
 LANES = 128
 GROUP = 8
-CHUNKS = 4
+CHUNKS = (56, 48, 24)
 VMEM = 56 * 1024 * 1024
 SCALE = 8
 
@@ -217,10 +217,11 @@
             out_ref[start + n] = logits[:, n * tile_rows : (n + 1) * tile_rows]
 
 
-def head(pair, product_values, chunk, gate3, output3, up3, down3, bins3):
+def head(pair, product_values, first, gate3, output3, up3, down3, bins3):
     tile_rows, tile_cols, width = pair.shape
     chunk_cols = product_values.shape[1]
     steps = chunk_cols // GROUP
+    lead = first // GROUP
     bins = bins3.shape[0]
     whole = lambda array: pl.BlockSpec(array.shape, lambda g: (0, 0))
     macs = gate3.size + output3.size + up3.size + down3.size + bins3.size
@@ -228,7 +229,7 @@
         head_kernel,
         grid=(steps,),
         in_specs=[
-            pl.BlockSpec((tile_rows, GROUP, width), lambda g: (0, chunk * steps + g, 0)),
+            pl.BlockSpec((tile_rows, GROUP, width), lambda g: (0, lead + g, 0)),
             pl.BlockSpec((width, GROUP, tile_rows), lambda g: (0, g, 0)),
             whole(gate3),
             whole(output3),
@@ -278,7 +279,6 @@
     col_count = lax.axis_size("col")
     _, tile_rows, tile_cols, width = pair.shape
     tile = pair[0]
-    chunk_rows = tile_rows // CHUNKS
     in3 = split_weights(weights_in, gain_input)
     left3, right3 = in3[: 2 * width], in3[2 * width :]
     gate3 = split_weights(gate_weights, gain_input)
@@ -293,31 +293,39 @@
         values = values.reshape(sources, owned, *values.shape[1:])
         return lax.all_to_all(values, ("lo", "col"), split_axis=0, concat_axis=0, tiled=True)
 
-    others = []
-    for chunk in range(CHUNKS):
-        right = spread(hands(tile, right3, chunk * chunk_rows, chunk_rows))
-        others.append(lax.all_gather(right, "half"))
+    firsts = [sum(CHUNKS[:n]) for n in range(len(CHUNKS))]
+    rights = [spread(hands(tile, right3, 0, CHUNKS[0]))]
     left = spread(hands(tile, left3, 0, tile_rows))
+    later, left = lax.optimization_barrier((tile, left))
+    for first, rows in zip(firsts[1:], CHUNKS[1:]):
+        rights.append(spread(hands(later, right3, first, rows)))
+    gathered = [lax.all_gather(right, "half") for right in rights]
+
+    def product_and_spread(right):
+        values = product(left, right)
+        values = lax.all_to_all(values, ("lo", "col"), split_axis=0, concat_axis=0, tiled=True)
+        return values.reshape(width, values.shape[2], tile_rows)
+
+    def run_head(values, chunk):
+        return head(tile, values, firsts[chunk], gate3, output3, up3, down3, bins3)
 
     move = mover(row_count)
-    own, mirror, steps = [], [], []
-    for chunk in range(CHUNKS):
-        values = product(left, others[chunk])
-        values = lax.all_to_all(values, ("lo", "col"), split_axis=0, concat_axis=0, tiled=True)
-        values = values.reshape(width, chunk_rows, tile_rows)
-        if chunk:
-            values, mirror = lax.optimization_barrier((values, mirror))
-        logits = head(tile, values, chunk, gate3, output3, up3, down3, bins3)
-        own.append(logits)
-        mirror.append(logits)
-        last = chunk == CHUNKS - 1
-        steps.append([lambda r, c: c * row_count + r] if last else swap_steps(row_count, chunk))
-        for n in range(chunk + 1):
-            if steps[n]:
-                mirror[n] = move(mirror[n], steps[n].pop(0))
-    for n in range(CHUNKS):
-        for step in steps[n]:
-            mirror[n] = move(mirror[n], step)
+    tie = lax.optimization_barrier
+    way = [swap_steps(row_count, turn) for turn in range(2)]
+    own = [run_head(product_and_spread(gathered[0]), 0)]
+    mirror = [move(own[0], way[0][0])]
+    right, mirror[0] = tie((gathered[1], mirror[0]))
+    mirror[0] = move(mirror[0], way[0][1])
+    values, mirror[0] = tie((product_and_spread(right), mirror[0]))
+    own.append(run_head(values, 1))
+    mirror[0] = move(mirror[0], way[0][2])
+    mirror.append(move(own[1], way[1][0]))
+    right, mirror = tie((gathered[2], mirror))
+    mirror[1] = move(mirror[1], way[1][1])
+    values, mirror = tie((product_and_spread(right), mirror))
+    own.append(run_head(values, 2))
+    mirror[1] = move(mirror[1], way[1][2])
+    mirror.append(move(own[2], lambda r, c: c * row_count + r))
     turned = jnp.transpose(jnp.concatenate(own, axis=0), (2, 1, 0))
     logits = turned + jnp.concatenate(mirror, axis=0) + distogram_bias[None, :, None]
     return jnp.swapaxes(logits, 1, 2)[None]

time: 913 us -> 868 us (0.951)
  starting transfers between devices: 137 us -> 112 us
  Pallas kernels: 159 us -> 142 us
    all_gather x4 -> x3, waiting for transfers between devices: 221 us -> 10.9 us  [half_shards(): gathered = [lax.all_gather(right, 'half') for right in rights]]
    ppermute x10 -> x7, waiting for transfers between devices: 138 us -> 276 us  [move(): return lax.ppermute(values, ('half', 'lo', 'col'), pairs)]
    all_to_all x4 -> x3, waiting for transfers between devices: 0.01 us -> 58.5 us  [product_and_spread(): lax.all_to_all(values, ('lo', 'col'), split_axis=0, concat_axis=0, tiled=...]
    ppermute x10 -> x7, starting transfers between devices: 78.6 us -> 33.1 us  [move(): return lax.ppermute(values, ('half', 'lo', 'col'), pairs)]
    all_to_all x4 -> x3, starting transfers between devices: 28.2 us -> 50.2 us  [product_and_spread(): lax.all_to_all(values, ('lo', 'col'), split_axis=0, concat_axis=0, tiled=...]
    pallas_call x4 -> x0, local copies, waits for them, and re-layouts: 17.9 us -> none  [head(): pl.pallas_call(head_kernel, grid=(steps,), in_specs=[pl.BlockSpec((tile_r...]
    all_to_all x5 -> x4, waiting for transfers between devices: 193 us -> 208 us  [spread(): lax.all_to_all(values, ('lo', 'col'), split_axis=0, concat_axis=0, tiled=...]
    pallas_call x4 -> x3, Pallas kernels: 57.5 us -> 43.9 us  [product(): pl.pallas_call(product_kernel, grid=(owned,), in_specs=[pl.BlockSpec((sou...]
  transfers between devices with their start and end apart: 23 -> 17, of which waited for: 15 -> 10; matrix products, arithmetic and copies ran while one was open for 2% -> 2% of each run, Pallas kernels for 17% -> 14%
where the time goes in v2:
time: 868 us; the launch traced here: 861 us
  waiting for transfers between devices  555 us (64%)
  Pallas kernels  142 us (16%)
  starting transfers between devices  112 us (13%)
  local copies, waits for them, and re-layouts  26.5 us (3%)
  between operations  13.3 us (2%)
  other arithmetic  11.6 us (1%)
    ppermute x7, waiting for transfers between devices, move(): return lax.ppermute(values, ('half', 'lo', 'col'), pairs)  276 us
    all_to_all x4, waiting for transfers between devices, spread(): lax.all_to_all(values, ('lo', 'col'), split_axis=0, concat_axis=0, tiled=...  208 us
    pallas_call x3, Pallas kernels, head(): pl.pallas_call(head_kernel, grid=(steps,), in_specs=[pl.BlockSpec((tile_r...  61.2 us
    all_to_all x3, waiting for transfers between devices, product_and_spread(): lax.all_to_all(values, ('lo', 'col'), split_axis=0, concat_axis=0, tiled=...  58.5 us
    all_to_all x3, starting transfers between devices, product_and_spread(): lax.all_to_all(values, ('lo', 'col'), split_axis=0, concat_axis=0, tiled=...  50.2 us
    pallas_call x3, Pallas kernels, product(): pl.pallas_call(product_kernel, grid=(owned,), in_specs=[pl.BlockSpec((sou...  43.9 us
    pallas_call x4, Pallas kernels, hands(): pl.pallas_call(hands_kernel, grid=(rows // GROUP,), in_specs=[pl.BlockSpe...  37.1 us
    ppermute x7, starting transfers between devices, move(): return lax.ppermute(values, ('half', 'lo', 'col'), pairs)  33.1 us
  transfers between devices with their start and end apart: 17, of which 10 were waited for; matrix products, arithmetic and copies ran while one was open for 2% of the time, Pallas kernels for 14%

profile of v2, /device:TPU:12, one launch (start us, length us, event | category | flops | bytes accessed | tf_op | source)
XLA Modules:
  0.0 861.0 jit_solution(7718548909707291984)
XLA Ops:
  6.5 1.1 copy.21
  7.6 0.7 reduce-precision_convert_fusion.2
  8.4 0.8 fusion.9
  9.2 8.3 hands.5
  17.5 5.1 all-to-all-start.1
  22.6 16.9 %hands.4 = f32[128,128,128]{2,1,0:T(8,128)} custom-call(f32[128,128,128]{2,1,0:T(8,128)} %bitcast.42, bf16[256,384]{1,0:T(8,128)(2,1)} %get-tuple-element.32.weights_ref), custom_call_target="tpu_custom_call" | custom-call | flops 402653184 | bytes 2097152 | tf_op jit(solution)/shard_map/hands/pallas_call | solution.py:127
  39.5 26.6 %all-to-all-done.1 = f32[8,16,56,128]{3,2,1,0:T(8,128)} async-done(((f32[8,16,56,128]{3,2,1,0:T(8,128)}), f32[8,16,56,128]{3,2,1,0:T(8,128)}, u32[]{:S(2)}, u32[]{:S(2)}) %all-to-all-start.1) | async-done | bytes 3670048 | tf_op jit(solution)/shard_map/all_to_all | solution.py:294
  66.2 7.7 all-to-all-start
  73.9 0.7 all-gather.7.cloned.1.call-update
  74.6 165.4 %all-to-all-done.left_ref = f32[8,16,128,128]{3,2,1,0:T(8,128)} async-done(((f32[8,16,128,128]{3,2,1,0:T(8,128)}), f32[8,16,128,128]{3,2,1,0:T(8,128)}, u32[]{:S(2)}, u32[]{:S(2)}) %all-to-all-start) | async-done | bytes 8388640 | tf_op jit(solution)/shard_map/all_to_all | solution.py:294
  240.0 7.2 hands.6
  247.2 6.9 all-to-all-start.3
  254.0 15.3 %product.3 = f32[8,16,56,128]{3,2,1,0:T(8,128)} custom-call(f32[8,16,128,128]{3,2,1,0:T(8,128)} %all-to-all-done.left_ref, f32[2,8,16,56,128]{4,3,2,1,0:T(8,128)} %bitcast.52), custom_call_target="tpu_custom_call" | custom-call | flops 352321536 | bytes 1966080 | tf_op jit(solution)/shard_map/product/pallas_call | solution.py:177
  269.3 16.3 %all-to-all-done.3 = f32[8,16,48,128]{3,2,1,0:T(8,128)S(1)} async-done(((f32[8,16,48,128]{3,2,1,0:T(8,128)}), f32[8,16,48,128]{3,2,1,0:T(8,128)S(1)}, u32[]{:S(2)}, u32[]{:S(2)}) %all-to-all-start.3) | async-done | bytes 3145760 | tf_op jit(solution)/shard_map/all_to_all | solution.py:294
  285.7 1.7 copy-done
  287.4 6.0 all-to-all-start.2
  294.8 4.6 hands.7
  299.5 58.5 %all-to-all-done.2 = f32[8,16,56,128]{3,2,1,0:T(8,128)} async-done(((f32[8,16,56,128]{3,2,1,0:T(8,128)}), f32[8,16,56,128]{3,2,1,0:T(8,128)}, u32[]{:S(2)}, u32[]{:S(2)}) %all-to-all-start.2) | async-done | bytes 3670048 | tf_op jit(solution)/shard_map/all_to_all | solution.py:306
  358.0 9.3 %all-to-all-start.5 = ((f32[8,16,24,128]{3,2,1,0:T(8,128)}), f32[8,16,24,128]{3,2,1,0:T(8,128)S(1)}, u32[]{:S(2)}, u32[]{:S(2)}) async-start(f32[8,16,24,128]{3,2,1,0:T(8,128)} %bitcast.54), calls=%async_computation.5 | async-start | bytes 3145728 | tf_op jit(solution)/shard_map/all_to_all | solution.py:294
  368.0 0.7 pad_maximum_fusion.3
  368.7 1.0 pad_maximum_fusion.up_ref
  369.8 0.8 pad_maximum_fusion.2.down_ref
  370.6 26.1 %head.3 = f32[56,64,128]{2,1,0:T(8,128)} custom-call(f32[128,128,128]{2,1,0:T(8,128)} %bitcast.45, f32[128,56,128]{2,1,0:T(8,128)} %bitcast.5.product_ref, bf16[128,384]{1,0:T(8,128)(2,1)} %get-tuple-element.43.gate_ref, bf16[128,384]{1,0:T(8,128)(2,1)} %get-tuple-element.44.output_ref, bf16[1024,384]{1,0:T(8,128)(2,1)} %pad_maximum_fusion.up_ref, ...), custom_call_target="tpu_custom_call" | custom-call | flops 1277165568 | bytes 1146880 | tf_op jit(solution)/shard_map/head/pallas_call | solution.py:228
  396.6 3.3 collective-permute-start
  399.9 32.1 %collective-permute-done = f32[56,64,128]{2,1,0:T(8,128)} collective-permute-done((f32[56,64,128]{2,1,0:T(8,128)}, f32[56,64,128]{2,1,0:T(8,128)}, u32[]{:S(2)}, u32[]{:S(2)}) %collective-permute-start) | collective-permute-done | bytes 1835040 | tf_op jit(solution)/shard_map/ppermute | solution.py:255
  432.0 10.9 %all-gather.9.cloned.1.call-done = f32[16,16,48,128]{3,2,1,0:T(8,128)} async-done(((f32[8,16,48,128]{3,2,1,0:T(8,128)}), f32[16,16,48,128]{3,2,1,0:T(8,128)}) %all-gather.9.cloned.1.call-update) | async-done | bytes 6291472 | tf_op jit(solution)/shard_map/all_gather | solution.py:302
  442.9 14.9 %product.4 = f32[8,16,48,128]{3,2,1,0:T(8,128)} custom-call(f32[8,16,128,128]{3,2,1,0:T(8,128)} %all-to-all-done.left_ref, f32[2,8,16,48,128]{4,3,2,1,0:T(8,128)} %bitcast.53), custom_call_target="tpu_custom_call" | custom-call | flops 301989888 | bytes 1835008 | tf_op jit(solution)/shard_map/product/pallas_call | solution.py:177
  457.9 1.1 copy-done.3
  459.0 7.2 all-to-all-start.4
  466.2 3.3 collective-permute-start.1
  469.6 133.2 %collective-permute-done.1 = f32[56,64,128]{2,1,0:T(8,128)} collective-permute-done((f32[56,64,128]{2,1,0:T(8,128)}, f32[56,64,128]{2,1,0:T(8,128)}, u32[]{:S(2)}, u32[]{:S(2)}) %collective-permute-start.1) | collective-permute-done | bytes 1835040 | tf_op jit(solution)/shard_map/ppermute | solution.py:255
  602.8 3.7 collective-permute-start.2
  606.5 22.7 %head.4 = f32[48,64,128]{2,1,0:T(8,128)} custom-call(f32[128,128,128]{2,1,0:T(8,128)} %bitcast.46, f32[128,48,128]{2,1,0:T(8,128)} %bitcast.50, bf16[128,384]{1,0:T(8,128)(2,1)} %get-tuple-element.43.gate_ref, bf16[128,384]{1,0:T(8,128)(2,1)} %get-tuple-element.44.output_ref, bf16[1024,384]{1,0:T(8,128)(2,1)} %pad_maximum_fusion.up_ref, ...), custom_call_target="tpu_custom_call" | custom-call | flops 1094713344 | bytes 983040 | tf_op jit(solution)/shard_map/head/pallas_call | solution.py:228
  629.2 2.1 collective-permute-start.3
  631.2 11.2 %collective-permute-done.2 = f32[56,64,128]{2,1,0:T(8,128)} collective-permute-done((f32[56,64,128]{2,1,0:T(8,128)}, f32[56,64,128]{2,1,0:T(8,128)}, u32[]{:S(2)}, u32[]{:S(2)}) %collective-permute-start.2) | collective-permute-done | bytes 1835040 | tf_op jit(solution)/shard_map/ppermute | solution.py:255
  642.5 13.7 %product.5 = f32[8,16,24,128]{3,2,1,0:T(8,128)} custom-call(f32[8,16,128,128]{3,2,1,0:T(8,128)} %all-to-all-done.left_ref, f32[2,8,16,24,128]{4,3,2,1,0:T(8,128)} %bitcast.56), custom_call_target="tpu_custom_call" | custom-call | flops 150994944 | bytes 1441792 | tf_op jit(solution)/shard_map/product/pallas_call | solution.py:177
  656.2 37.0 %all-to-all-start.6 = ((f32[8,16,24,128]{3,2,1,0:T(8,128)}), f32[8,16,24,128]{3,2,1,0:T(8,128)S(1)}, u32[]{:S(2)}, u32[]{:S(2)}) async-start(f32[8,16,24,128]{3,2,1,0:T(8,128)} %product.5), calls=%async_computation.6 | async-start | bytes 3145728 | tf_op jit(solution)/shard_map/all_to_all | solution.py:306
  693.1 5.6 collective-permute-start.4
  698.8 67.8 %collective-permute-done.4 = f32[48,64,128]{2,1,0:T(8,128)} collective-permute-done((f32[48,64,128]{2,1,0:T(8,128)S(1)}, f32[48,64,128]{2,1,0:T(8,128)}, u32[]{:S(2)}, u32[]{:S(2)}) %collective-permute-start.4) | collective-permute-done | bytes 1572896 | tf_op jit(solution)/shard_map/ppermute | solution.py:255
  766.6 13.3 %collective-permute-start.5 = (f32[48,64,128]{2,1,0:T(8,128)}, f32[48,64,128]{2,1,0:T(8,128)}, u32[]{:S(2)}, u32[]{:S(2)}) collective-permute-start(f32[48,64,128]{2,1,0:T(8,128)} %collective-permute-done.4), channel_id=1, source_target_pairs={{0,1},{1,0},{2,3},{3,2},{4,4},{5,5},{6,6},{7,7},{8,11},{9,10},{10,... | collective-permute-start | bytes 4718600 | tf_op jit(solution)/shard_map/ppermute | solution.py:255
  779.9 12.5 %head.5 = f32[24,64,128]{2,1,0:T(8,128)} custom-call(f32[128,128,128]{2,1,0:T(8,128)} %bitcast.47, f32[128,24,128]{2,1,0:T(8,128)} %bitcast.55, bf16[128,384]{1,0:T(8,128)(2,1)} %get-tuple-element.43.gate_ref, bf16[128,384]{1,0:T(8,128)(2,1)} %get-tuple-element.44.output_ref, bf16[1024,384]{1,0:T(8,128)(2,1)} %pad_maximum_fusion.up_ref, ...), custom_call_target="tpu_custom_call" | custom-call | flops 547356672 | bytes 491520 | tf_op jit(solution)/shard_map/head/pallas_call | solution.py:228
  792.4 1.9 collective-permute-start.6
  794.3 5.6 copy.26
  799.9 31.5 %collective-permute-done.6 = f32[24,64,128]{2,1,0:T(8,128)S(1)} collective-permute-done((f32[24,64,128]{2,1,0:T(8,128)}, f32[24,64,128]{2,1,0:T(8,128)S(1)}, u32[]{:S(2)}, u32[]{:S(2)}) %collective-permute-start.6) | collective-permute-done | bytes 786464 | tf_op jit(solution)/shard_map/ppermute | solution.py:255
  831.4 4.4 copy.28
  835.8 5.8 copy.27
  841.6 7.5 fusion.2
  849.1 5.4 copy.29
  (51 shorter events, 2.2 us)
Async XLA Ops:
  17.5 48.7 %all-to-all-start.1 = ((f32[8,16,56,128]{3,2,1,0:T(8,128)}), f32[8,16,56,128]{3,2,1,0:T(8,128)}, u32[]{:S(2)}, u32[]{:S(2)}) async-start(f32[8,16,56,128]{3,2,1,0:T(8,128)} %bitcast.49), calls=%async_computation.1 | async-start | bytes 7340032 | tf_op jit(solution)/shard_map/all_to_all | solution.py:294
  66.2 173.8 %all-to-all-start = ((f32[8,16,128,128]{3,2,1,0:T(8,128)}), f32[8,16,128,128]{3,2,1,0:T(8,128)}, u32[]{:S(2)}, u32[]{:S(2)}) async-start(f32[8,16,128,128]{3,2,1,0:T(8,128)} %bitcast.48), calls=%async_computation | async-start | bytes 16777216 | tf_op jit(solution)/shard_map/all_to_all | solution.py:294
  73.9 180.2 %all-gather.7.cloned.1.call-start = ((), (), s32[]{:S(2)}) async-start(), calls=%async_computation.7 | async-start | bytes 11010048 | tf_op jit(solution)/shard_map/all_gather | solution.py:302
  247.2 38.5 %all-to-all-start.3 = ((f32[8,16,48,128]{3,2,1,0:T(8,128)}), f32[8,16,48,128]{3,2,1,0:T(8,128)S(1)}, u32[]{:S(2)}, u32[]{:S(2)}) async-start(f32[8,16,48,128]{3,2,1,0:T(8,128)} %bitcast.51), calls=%async_computation.3 | async-start | bytes 6291456 | tf_op jit(solution)/shard_map/all_to_all | solution.py:294
  285.7 1.7 copy-start
  285.7 8.5 copy-start.8
  285.7 8.6 copy-start.9
  287.4 70.6 %all-to-all-start.2 = ((f32[8,16,56,128]{3,2,1,0:T(8,128)}), f32[8,16,56,128]{3,2,1,0:T(8,128)}, u32[]{:S(2)}, u32[]{:S(2)}) async-start(f32[8,16,56,128]{3,2,1,0:T(8,128)} %product.3), calls=%async_computation.2 | async-start | bytes 7340032 | tf_op jit(solution)/shard_map/all_to_all | solution.py:306
  293.4 1.0 copy-start.6
  293.4 1.2 copy-start.10
  293.4 1.3 copy-start.11
  293.4 1.3 copy-start.12
  293.4 1.3 copy-start.13
  293.4 149.5 %all-gather.9.cloned.1.call-start = ((), (), s32[]{:S(2)}) async-start(), calls=%async_computation.8 | async-start | bytes 9437184 | tf_op jit(solution)/shard_map/all_gather | solution.py:302
  294.8 73.1 %copy-start.7 = (f32[512,128]{1,0:T(8,128)S(1)}, f32[512,128]{1,0:T(8,128)}, u32[]{:S(2)}) copy-start(f32[512,128]{1,0:T(8,128)} %param.19) | copy-start | bytes 786436
  358.0 99.9 %all-to-all-start.5 = ((f32[8,16,24,128]{3,2,1,0:T(8,128)}), f32[8,16,24,128]{3,2,1,0:T(8,128)S(1)}, u32[]{:S(2)}, u32[]{:S(2)}) async-start(f32[8,16,24,128]{3,2,1,0:T(8,128)} %bitcast.54), calls=%async_computation.5 | async-start | bytes 3145728 | tf_op jit(solution)/shard_map/all_to_all | solution.py:294
  396.6 35.4 %collective-permute-start = (f32[56,64,128]{2,1,0:T(8,128)}, f32[56,64,128]{2,1,0:T(8,128)}, u32[]{:S(2)}, u32[]{:S(2)}) collective-permute-start(f32[56,64,128]{2,1,0:T(8,128)} %head.3), channel_id=1, source_target_pairs={{0,0},{1,1},{2,2},{3,3},{4,5},{5,4},{6,7},{7,6},{8,10},{9,11},{10,... | collective-permute-start | bytes 5505032 | tf_op jit(solution)/shard_map/ppermute | solution.py:255
  457.9 1.1 copy-start.3
  459.0 143.8 %all-to-all-start.4 = ((f32[8,16,48,128]{3,2,1,0:T(8,128)}), f32[8,16,48,128]{3,2,1,0:T(8,128)S(1)}, u32[]{:S(2)}, u32[]{:S(2)}) async-start(f32[8,16,48,128]{3,2,1,0:T(8,128)} %product.4), calls=%async_computation.4 | async-start | bytes 6291456 | tf_op jit(solution)/shard_map/all_to_all | solution.py:306
  466.2 165.0 %all-gather.11.cloned.1.call-start = ((), (), s32[]{:S(2)}) async-start(), calls=%async_computation.9 | async-start | bytes 4718592 | tf_op jit(solution)/shard_map/all_gather | solution.py:302
  466.2 136.5 %collective-permute-start.1 = (f32[56,64,128]{2,1,0:T(8,128)}, f32[56,64,128]{2,1,0:T(8,128)}, u32[]{:S(2)}, u32[]{:S(2)}) collective-permute-start(f32[56,64,128]{2,1,0:T(8,128)} %collective-permute-done), channel_id=1, source_target_pairs={{0,0},{1,5},{2,10},{3,15},{4,4},{5,1},{6,14},{7,11},{8,8},{9,13},{... | collective-permute-start | bytes 5505032 | tf_op jit(solution)/shard_map/ppermute | solution.py:255
  602.8 3.7 copy-start.1
  602.8 39.7 %collective-permute-start.2 = (f32[56,64,128]{2,1,0:T(8,128)}, f32[56,64,128]{2,1,0:T(8,128)}, u32[]{:S(2)}, u32[]{:S(2)}) collective-permute-start(f32[56,64,128]{2,1,0:T(8,128)} %collective-permute-done.1), channel_id=1, source_target_pairs={{0,0},{1,1},{2,2},{3,3},{4,5},{5,4},{6,7},{7,6},{8,10},{9,11},{10,... | collective-permute-start | bytes 5505032 | tf_op jit(solution)/shard_map/ppermute | solution.py:255
  629.2 2.1 collective-permute-start.3
  656.2 110.4 %all-to-all-start.6 = ((f32[8,16,24,128]{3,2,1,0:T(8,128)}), f32[8,16,24,128]{3,2,1,0:T(8,128)S(1)}, u32[]{:S(2)}, u32[]{:S(2)}) async-start(f32[8,16,24,128]{3,2,1,0:T(8,128)} %product.5), calls=%async_computation.6 | async-start | bytes 3145728 | tf_op jit(solution)/shard_map/all_to_all | solution.py:306
  693.1 73.5 %collective-permute-start.4 = (f32[48,64,128]{2,1,0:T(8,128)S(1)}, f32[48,64,128]{2,1,0:T(8,128)}, u32[]{:S(2)}, u32[]{:S(2)}) collective-permute-start(f32[48,64,128]{2,1,0:T(8,128)S(1)} %collective-permute-done.3), channel_id=1, source_target_pairs={{0,4},{1,1},{2,14},{3,11},{4,0},{5,5},{6,10},{7,15},{8,12},{9,9},{... | collective-permute-start | bytes 4718600 | tf_op jit(solution)/shard_map/ppermute | solution.py:255
  766.6 13.3 %copy-start.4 = (f32[8,16,24,128]{3,2,1,0:T(8,128)}, f32[8,16,24,128]{3,2,1,0:T(8,128)S(1)}, u32[]{:S(2)}) copy-start(f32[8,16,24,128]{3,2,1,0:T(8,128)S(1)} %all-to-all-done.6) | copy-start | bytes 4718596
  766.6 69.2 %collective-permute-start.5 = (f32[48,64,128]{2,1,0:T(8,128)}, f32[48,64,128]{2,1,0:T(8,128)}, u32[]{:S(2)}, u32[]{:S(2)}) collective-permute-start(f32[48,64,128]{2,1,0:T(8,128)} %collective-permute-done.4), channel_id=1, source_target_pairs={{0,1},{1,0},{2,3},{3,2},{4,4},{5,5},{6,6},{7,7},{8,11},{9,10},{10,... | collective-permute-start | bytes 4718600 | tf_op jit(solution)/shard_map/ppermute | solution.py:255
  792.4 39.0 %collective-permute-start.6 = (f32[24,64,128]{2,1,0:T(8,128)}, f32[24,64,128]{2,1,0:T(8,128)S(1)}, u32[]{:S(2)}, u32[]{:S(2)}) collective-permute-start(f32[24,64,128]{2,1,0:T(8,128)} %head.5), channel_id=1, source_target_pairs={{0,0},{1,4},{2,8},{3,12},{4,1},{5,5},{6,9},{7,13},{8,2},{9,6},{10,... | collective-permute-start | bytes 2359304 | tf_op jit(solution)/shard_map/ppermute | solution.py:255
  835.8 5.8 copy-start.2
  835.8 5.8 copy-start.5
  835.8 5.8 copy-start.14
Sparse Core Ops, SparseCore 0:
  76.2 169.8 all-gather.6
  295.8 147.0 all-gather.8
  469.7 145.6 all-gather.10

commit v3 on v2

--- a/solution.py
+++ b/solution.py
@@ -10,7 +10,7 @@
 HIGH = lax.Precision.HIGHEST
 LANES = 128
 GROUP = 8
-CHUNKS = (56, 48, 24)
+CHUNKS = (40, 56, 32)
 VMEM = 56 * 1024 * 1024
 SCALE = 8
 
@@ -121,15 +121,17 @@
             flat[pl.ds(start + n, width, stride=rows), :] = result[:, n * LANES : (n + 1) * LANES]
 
 
-def hands(pair, weights3, first, rows):
+def hands(pair, weights3, left, right):
     _, tile_cols, width = pair.shape
-    lead = first // GROUP
+    rows = left[1] + right[1]
+    turn = left[1] // GROUP
+    lead, shift = left[0] // GROUP, right[0] // GROUP - turn
     return pl.pallas_call(
         hands_kernel,
         grid=(rows // GROUP,),
         in_specs=[
-            pl.BlockSpec((GROUP, tile_cols, width), lambda g: (lead + g, 0, 0)),
-            pl.BlockSpec(weights3.shape, lambda g: (0, 0)),
+            pl.BlockSpec((GROUP, tile_cols, width), lambda g: (g + jnp.where(g < turn, lead, shift), 0, 0)),
+            pl.BlockSpec((2 * width, 3 * width), lambda g: (jnp.where(g < turn, 0, 1), 0)),
         ],
         out_specs=pl.BlockSpec((width, GROUP, tile_cols), lambda g: (0, g, 0)),
         out_shape=jax.ShapeDtypeStruct((width, rows, tile_cols), jnp.float32),
@@ -139,21 +141,17 @@
     )(pair, weights3)
 
 
-def product_kernel(left_ref, right_ref, out_ref):
+def product_kernel(low_ref, high_ref, right_ref, out_ref):
     cols = right_ref.shape[1] // 2
 
-    def lines(ref):
-        return jnp.concatenate(
-            [
-                jnp.concatenate([ref[lo * cols + c, 0] for c in range(cols)], axis=1)
-                for lo in range(2)
-            ],
-            axis=0,
-        )
-
-    left_high, left_low = parts(lines(left_ref))
+    def line(ref, lo):
+        return jnp.concatenate([ref[lo * cols + c, 0] for c in range(cols)], axis=1)
+
+    left_high, left_low = parts(
+        jnp.concatenate([line(ref, lo) for lo in range(2) for ref in (low_ref, high_ref)], axis=0)
+    )
     right_high, right_low = parts(
-        jnp.concatenate([lines(right_ref.at[half]) for half in range(2)], axis=0)
+        jnp.concatenate([line(right_ref.at[half], lo) for half in range(2) for lo in range(2)], axis=0)
     )
     result = lax.dot_general(
         jnp.concatenate([right_high, right_high, right_low], axis=1),
@@ -163,22 +161,22 @@
     )
     rows = right_ref.shape[3]
     wide = result.shape[1] // 2
-    for line in range(2):
+    for lo in range(2):
         for plane in range(cols):
-            out_ref[line * cols + plane, 0] = result[
-                plane * rows : (plane + 1) * rows, line * wide : (line + 1) * wide
+            out_ref[lo * cols + plane, 0] = result[
+                plane * rows : (plane + 1) * rows, lo * wide : (lo + 1) * wide
             ]
 
 
-def product(left, right):
+def product(low, high, right, wide):
     _, sources, owned, rows, width = right.shape
-    wide = left.shape[2]
     k_all = width * sources // 2
     return pl.pallas_call(
         product_kernel,
         grid=(owned,),
         in_specs=[
-            pl.BlockSpec((sources, 1, wide, width), lambda n: (0, n, 0, 0)),
+            pl.BlockSpec((sources, 1, wide // 2, width), lambda n: (0, n, 0, 0)),
+            pl.BlockSpec((sources, 1, wide // 2, width), lambda n: (0, n, 0, 0)),
             pl.BlockSpec((2, sources, 1, rows, width), lambda n: (0, 0, n, 0, 0)),
         ],
         out_specs=pl.BlockSpec((sources, 1, rows, wide), lambda n: (0, n, 0, 0)),
@@ -188,14 +186,14 @@
             6 * owned * 4 * rows * 2 * wide * k_all, 4 * owned * k_all * (2 * wide + 4 * rows)
         ),
         name="product",
-    )(left, right)
+    )(low, high, right)
 
 
 def head_kernel(
-    pair_ref, product_ref, gate_ref, output_ref, up_ref, down_ref, bins_ref, out_ref
+    pair_ref, product_ref, gate_ref, output_ref, up_ref, down_ref, bins_ref, *out_refs
 ):
     tile_rows, cols, width = pair_ref.shape
-    bins = out_ref.shape[1]
+    bins = out_refs[0].shape[1]
     per = 4
     flat_pair = pair_ref.reshape(tile_rows * cols, width)
     flat_product = product_ref.reshape(width * cols, tile_rows)
@@ -214,7 +212,10 @@
         pair_out = updated + times(down_ref[...], activated)
         logits = times(bins_ref[...], pair_out)
         for n in range(per):
-            out_ref[start + n] = logits[:, n * tile_rows : (n + 1) * tile_rows]
+            for part, out_ref in enumerate(out_refs):
+                out_ref[start + n] = logits[
+                    part * bins : (part + 1) * bins, n * tile_rows : (n + 1) * tile_rows
+                ]
 
 
 def head(pair, product_values, first, gate3, output3, up3, down3, bins3):
@@ -222,7 +223,7 @@
     chunk_cols = product_values.shape[1]
     steps = chunk_cols // GROUP
     lead = first // GROUP
-    bins = bins3.shape[0]
+    bins = bins3.shape[0] // 2
     whole = lambda array: pl.BlockSpec(array.shape, lambda g: (0, 0))
     macs = gate3.size + output3.size + up3.size + down3.size + bins3.size
     return pl.pallas_call(
@@ -237,29 +238,82 @@
             whole(down3),
             whole(bins3),
         ],
-        out_specs=pl.BlockSpec((GROUP, bins, tile_rows), lambda g: (g, 0, 0)),
-        out_shape=jax.ShapeDtypeStruct((chunk_cols, bins, tile_rows), jnp.float32),
+        out_specs=[pl.BlockSpec((GROUP, bins, tile_rows), lambda g: (g, 0, 0))] * 2,
+        out_shape=[jax.ShapeDtypeStruct((chunk_cols, bins, tile_rows), jnp.float32)] * 2,
         compiler_params=pltpu.CompilerParams(vmem_limit_bytes=VMEM),
         cost_estimate=estimate(
-            2 * chunk_cols * tile_rows * macs, 4 * chunk_cols * tile_rows * (2 * width + bins)
+            2 * chunk_cols * tile_rows * macs, 4 * chunk_cols * tile_rows * 2 * (width + bins)
         ),
         name="head",
     )(pair, product_values, gate3, output3, up3, down3, bins3)
 
 
-def mover(count):
+def turned_kernel(bias_ref, *refs):
+    out_ref, sources = refs[-1], refs[:-1]
+    count = len(sources) // 2
+    tile_rows, _, bins, tile_cols = out_ref.shape
+    flat = out_ref.reshape(tile_rows * 2 * bins, tile_cols)
+    for part in range(2):
+        for n in range(bins):
+            values = [
+                ref.reshape(ref.shape[0] * bins, tile_rows)[pl.ds(n, ref.shape[0], stride=bins), :]
+                for ref in sources[part * count : (part + 1) * count]
+            ]
+            result = jnp.concatenate(values, axis=0).T + bias_ref[part, n : n + 1, :]
+            flat[pl.ds(part * bins + n, tile_rows, stride=2 * bins), :] = result
+
+
+def turned(bias, own):
+    arrays = [block[part] for part in range(2) for block in own]
+    _, bins, tile_rows = arrays[0].shape
+    tile_cols = sum(block[0].shape[0] for block in own)
+    block = lambda rows: pl.BlockSpec((rows, GROUP, tile_rows), lambda g: (0, g, 0))
+    return pl.pallas_call(
+        turned_kernel,
+        grid=(bins // GROUP,),
+        in_specs=[pl.BlockSpec((2, GROUP, tile_cols), lambda g: (0, g, 0))]
+        + [block(array.shape[0]) for array in arrays],
+        out_specs=pl.BlockSpec((tile_rows, 2, GROUP, tile_cols), lambda g: (0, 0, g, 0)),
+        out_shape=jax.ShapeDtypeStruct((tile_rows, 2, bins, tile_cols), jnp.float32),
+        compiler_params=pltpu.CompilerParams(vmem_limit_bytes=VMEM),
+        cost_estimate=estimate(0, 8 * tile_rows * 2 * bins * tile_cols),
+        name="turned",
+    )(bias, *arrays)
+
+
+def joined_kernel(base_ref, low_ref, high_ref, out_ref):
+    out_ref[:, 0] = base_ref[:, 0] + low_ref[...]
+    out_ref[:, 1] = base_ref[:, 1] + high_ref[...]
+
+
+def joined(base, mirror, first):
+    rows, bins, tile_cols = mirror[0].shape
+    lead = first // GROUP
+    whole = pl.BlockSpec((GROUP, 2, bins, tile_cols), lambda g: (lead + g, 0, 0, 0))
+    block = pl.BlockSpec((GROUP, bins, tile_cols), lambda g: (g, 0, 0))
+    return pl.pallas_call(
+        joined_kernel,
+        grid=(rows // GROUP,),
+        in_specs=[whole, block, block],
+        out_specs=whole,
+        out_shape=jax.ShapeDtypeStruct(base.shape, jnp.float32),
+        input_output_aliases={0: 0},
+        compiler_params=pltpu.CompilerParams(vmem_limit_bytes=VMEM),
+        cost_estimate=estimate(0, 24 * rows * bins * tile_cols),
+        name="joined",
+    )(base, *mirror)
+
+
+def mirrored_halves(block, count):
     every = [(r, c) for r in range(count) for c in range(count)]
 
     def move(values, target):
         pairs = [(r * count + c, target(r, c)) for r, c in every]
         return lax.ppermute(values, ("half", "lo", "col"), pairs)
 
-    return move
-
-
-def swap_steps(count, turn):
-    aside = lambda r, c: r * count + (c ^ r ^ turn)
-    return [aside, lambda r, c: (c ^ r ^ turn) * count + c, aside]
+    low = move(block[0], lambda r, c: c * count + r)
+    high = move(block[1], lambda r, c: r * count + (c ^ 2))
+    return low, move(high, lambda r, c: (c ^ 2) * count + r)
 
 
 def half_shards(
@@ -280,7 +334,6 @@
     _, tile_rows, tile_cols, width = pair.shape
     tile = pair[0]
     in3 = split_weights(weights_in, gain_input)
-    left3, right3 = in3[: 2 * width], in3[2 * width :]
     gate3 = split_weights(gate_weights, gain_input)
     output3 = split_weights(weights_out, gain_product)
     up3 = split_weights(transition_in, gain_transition)
@@ -293,41 +346,45 @@
         values = values.reshape(sources, owned, *values.shape[1:])
         return lax.all_to_all(values, ("lo", "col"), split_axis=0, concat_axis=0, tiled=True)
 
+    tie = lax.optimization_barrier
     firsts = [sum(CHUNKS[:n]) for n in range(len(CHUNKS))]
-    rights = [spread(hands(tile, right3, 0, CHUNKS[0]))]
-    left = spread(hands(tile, left3, 0, tile_rows))
-    later, left = lax.optimization_barrier((tile, left))
-    for first, rows in zip(firsts[1:], CHUNKS[1:]):
-        rights.append(spread(hands(later, right3, first, rows)))
-    gathered = [lax.all_gather(right, "half") for right in rights]
-
-    def product_and_spread(right):
-        values = product(left, right)
+    lower = tile_rows // 2
+
+    def gather(values, first):
+        return lax.all_gather(values[:, :, first:], "half")
+
+    sent = [
+        hands(tile, in3, (0, 0), (firsts[0], CHUNKS[0])),
+        hands(tile, in3, (0, lower), (firsts[1], CHUNKS[1])),
+        hands(tile, in3, (lower, lower), (firsts[2], CHUNKS[2])),
+    ]
+    gathered = [gather(spread(sent[0]), 0)]
+    low = spread(sent[1])
+    gathered.append(gather(low, lower))
+    gathered[0], sent[2] = tie((gathered[0], sent[2]))
+    high = spread(sent[2])
+    gathered.append(gather(high, lower))
+
+    def blocks(right):
+        return product(low, high, right, tile_rows)
+
+    def finish(values, chunk):
         values = lax.all_to_all(values, ("lo", "col"), split_axis=0, concat_axis=0, tiled=True)
-        return values.reshape(width, values.shape[2], tile_rows)
-
-    def run_head(values, chunk):
+        values = values.reshape(width, CHUNKS[chunk], tile_rows)
         return head(tile, values, firsts[chunk], gate3, output3, up3, down3, bins3)
 
-    move = mover(row_count)
-    tie = lax.optimization_barrier
-    way = [swap_steps(row_count, turn) for turn in range(2)]
-    own = [run_head(product_and_spread(gathered[0]), 0)]
-    mirror = [move(own[0], way[0][0])]
-    right, mirror[0] = tie((gathered[1], mirror[0]))
-    mirror[0] = move(mirror[0], way[0][1])
-    values, mirror[0] = tie((product_and_spread(right), mirror[0]))
-    own.append(run_head(values, 1))
-    mirror[0] = move(mirror[0], way[0][2])
-    mirror.append(move(own[1], way[1][0]))
-    right, mirror = tie((gathered[2], mirror))
-    mirror[1] = move(mirror[1], way[1][1])
-    values, mirror = tie((product_and_spread(right), mirror))
-    own.append(run_head(values, 2))
-    mirror[1] = move(mirror[1], way[1][2])
-    mirror.append(move(own[2], lambda r, c: c * row_count + r))
-    turned = jnp.transpose(jnp.concatenate(own, axis=0), (2, 1, 0))
-    logits = turned + jnp.concatenate(mirror, axis=0) + distogram_bias[None, :, None]
+    own = [finish(blocks(gathered[0]), 0)]
+    mirror = [mirrored_halves(own[0], row_count)]
+    values, gathered[2], mirror[0] = tie((blocks(gathered[1]), gathered[2], mirror[0]))
+    own.append(finish(values, 1))
+    own.append(finish(blocks(gathered[2]), 2))
+    mirror += [mirrored_halves(block, row_count) for block in own[1:]]
+    bins = distogram_bias.shape[0] // 2
+    bias = jnp.broadcast_to(distogram_bias.reshape(2, bins, 1), (2, bins, tile_cols))
+    logits = turned(bias, own)
+    for first, block in zip(firsts, mirror):
+        logits = joined(logits, block, first)
+    logits = logits.reshape(tile_rows, 2 * bins, tile_cols)
     return jnp.swapaxes(logits, 1, 2)[None]
 
 

time: 868 us -> 729 us (0.84)
  waiting for transfers between devices: 555 us -> 443 us
  starting transfers between devices: 112 us -> 82.4 us
  Pallas kernels: 142 us -> 161 us
    ppermute x7 -> x9, waiting for transfers between devices: 276 us -> 54.5 us  [move(): return lax.ppermute(values, ('half', 'lo', 'col'), pairs)]
    all_gather x3, waiting for transfers between devices: 10.9 us -> 179 us  [gather(): return lax.all_gather(values[:, :, first:], 'half')]
    all_to_all x4 -> x3, waiting for transfers between devices: 208 us -> 140 us  [spread(): lax.all_to_all(values, ('lo', 'col'), split_axis=0, concat_axis=0, tiled=...]
    all_to_all x3, starting transfers between devices: 50.2 us -> 21 us  [finish(): lax.all_to_all(values, ('lo', 'col'), split_axis=0, concat_axis=0, tiled=...]
    pallas_call x0 -> x4, Pallas kernels: none -> 19 us  [the longest x3 13.3 us: joined(): pl.pallas_call(joined_kernel, grid=(rows // GROUP,), in_specs=[whole, blo...]
    all_to_all x4 -> x3, starting transfers between devices: 28.9 us -> 18.4 us  [spread(): lax.all_to_all(values, ('lo', 'col'), split_axis=0, concat_axis=0, tiled=...]
    ppermute x2 -> x0, local copies, waits for them, and re-layouts: 10.1 us -> none  [move(): return lax.ppermute(values, ('half', 'lo', 'col'), pairs)]
    ppermute x7 -> x9, starting transfers between devices: 33.1 us -> 43 us  [move(): return lax.ppermute(values, ('half', 'lo', 'col'), pairs)]
  transfers between devices with their start and end apart: 17 -> 18, of which waited for: 10 -> 13; matrix products, arithmetic and copies ran while one was open for 2% -> 2% of each run, Pallas kernels for 14% -> 21%
where the time goes in v3:
time: 729 us; the launch traced here: 723 us
  waiting for transfers between devices  443 us (61%)
  Pallas kernels  161 us (22%)
  starting transfers between devices  82.4 us (11%)
  local copies, waits for them, and re-layouts  18 us (2%)
  between operations  13.3 us (2%)
    all_gather x3, waiting for transfers between devices, gather(): return lax.all_gather(values[:, :, first:], 'half')  179 us
    all_to_all x3, waiting for transfers between devices, spread(): lax.all_to_all(values, ('lo', 'col'), split_axis=0, concat_axis=0, tiled=...  140 us
    all_to_all x3, waiting for transfers between devices, finish(): lax.all_to_all(values, ('lo', 'col'), split_axis=0, concat_axis=0, tiled=...  68.3 us
    pallas_call x3, Pallas kernels, head(): pl.pallas_call(head_kernel, grid=(steps,), in_specs=[pl.BlockSpec((tile_r...  61.6 us
    ppermute x9, waiting for transfers between devices, move(): return lax.ppermute(values, ('half', 'lo', 'col'), pairs)  54.5 us
    pallas_call x3, Pallas kernels, product(): pl.pallas_call(product_kernel, grid=(owned,), in_specs=[pl.BlockSpec((sou...  44.2 us
    ppermute x9, starting transfers between devices, move(): return lax.ppermute(values, ('half', 'lo', 'col'), pairs)  43 us
    pallas_call x3, Pallas kernels, hands(): pl.pallas_call(hands_kernel, grid=(rows // GROUP,), in_specs=[pl.BlockSpe...  35.8 us
  transfers between devices with their start and end apart: 18, of which 13 were waited for; matrix products, arithmetic and copies ran while one was open for 2% of the time, Pallas kernels for 21%

profile of v3, /device:TPU:12, one launch (start us, length us, event | category | flops | bytes accessed | tf_op | source)
XLA Modules:
  0.0 722.8 jit_solution(14252425987298499654)
XLA Ops:
  6.5 1.1 copy.20
  9.1 6.4 hands.4
  15.5 5.1 all-to-all-start.1
  20.6 16.2 %hands.3 = f32[128,120,128]{2,1,0:T(8,128)} custom-call(f32[128,128,128]{2,1,0:T(8,128)} %bitcast.34, bf16[512,384]{1,0:T(8,128)(2,1)} %pad_maximum_fusion.1.weights_ref), custom_call_target="tpu_custom_call" | custom-call | flops 377487360 | bytes 1966080 | tf_op jit(solution)/shard_map/hands/pallas_call | solution.py:129
  36.8 14.7 %all-to-all-done.1 = f32[8,16,40,128]{3,2,1,0:T(8,128)S(1)} async-done(((f32[8,16,40,128]{3,2,1,0:T(8,128)}), f32[8,16,40,128]{3,2,1,0:T(8,128)S(1)}, u32[]{:S(2)}, u32[]{:S(2)}) %all-to-all-start.1) | async-done | bytes 2621472 | tf_op jit(solution)/shard_map/all_to_all | solution.py:347
  51.5 1.5 copy-done
  53.0 7.2 all-to-all-start
  60.9 13.3 %hands.5 = f32[128,96,128]{2,1,0:T(8,128)} custom-call(f32[128,128,128]{2,1,0:T(8,128)} %bitcast.35, bf16[512,384]{1,0:T(8,128)(2,1)} %pad_maximum_fusion.1.weights_ref), custom_call_target="tpu_custom_call" | custom-call | flops 301989888 | bytes 1572864 | tf_op jit(solution)/shard_map/hands/pallas_call | solution.py:129
  74.1 115.3 %all-gather.7.cloned.1.call-done = f32[16,16,40,128]{3,2,1,0:T(8,128)} async-done(((f32[8,16,40,128]{3,2,1,0:T(8,128)}), f32[16,16,40,128]{3,2,1,0:T(8,128)}) %all-gather.7.cloned.1.call-update) | async-done | bytes 5242896 | tf_op jit(solution)/shard_map/all_gather | solution.py:354
  189.5 11.2 %all-to-all-done.low_ref = f32[8,16,120,128]{3,2,1,0:T(8,128)} async-done(((f32[8,16,120,128]{3,2,1,0:T(8,128)}), f32[8,16,120,128]{3,2,1,0:T(8,128)}, u32[]{:S(2)}, u32[]{:S(2)}) %all-to-all-start) | async-done | bytes 7864352 | tf_op jit(solution)/shard_map/all_to_all | solution.py:347
  200.7 6.1 all-to-all-start.2
  206.8 4.2 slice.8
  211.0 114.3 %all-to-all-done.2.high_ref = f32[8,16,96,128]{3,2,1,0:T(8,128)} async-done(((f32[8,16,96,128]{3,2,1,0:T(8,128)}), f32[8,16,96,128]{3,2,1,0:T(8,128)}, u32[]{:S(2)}, u32[]{:S(2)}) %all-to-all-start.2) | async-done | bytes 6291488 | tf_op jit(solution)/shard_map/all_to_all | solution.py:347
  325.3 14.6 %product.3 = f32[8,16,40,128]{3,2,1,0:T(8,128)} custom-call(f32[8,16,120,128]{3,2,1,0:T(8,128)} %all-to-all-done.low_ref, f32[8,16,96,128]{3,2,1,0:T(8,128)} %all-to-all-done.2.high_ref, f32[2,8,16,40,128]{4,3,2,1,0:T(8,128)} %bitcast.45), custom_call_target="tpu_custom_call" | custom-call | flops 251658240 | bytes 1703936 | tf_op jit(solution)/shard_map/product/pallas_call | solution.py:174
  339.9 5.3 all-to-all-start.3
  345.4 3.2 slice.9
  348.8 1.2 copy.23
  350.0 1.1 copy.24
  353.4 1.0 pad_maximum_fusion.up_ref
  355.2 38.6 %all-to-all-done.3 = f32[8,16,40,128]{3,2,1,0:T(8,128)S(1)} async-done(((f32[8,16,40,128]{3,2,1,0:T(8,128)}), f32[8,16,40,128]{3,2,1,0:T(8,128)S(1)}, u32[]{:S(2)}, u32[]{:S(2)}) %all-to-all-start.3) | async-done | bytes 2621472 | tf_op jit(solution)/shard_map/all_to_all | solution.py:372
  393.8 1.5 copy-done.1
  395.3 19.5 %head.3 = (f32[40,32,128]{2,1,0:T(8,128)}, f32[40,32,128]{2,1,0:T(8,128)}) custom-call(f32[128,128,128]{2,1,0:T(8,128)} %bitcast.36, f32[128,40,128]{2,1,0:T(8,128)} %bitcast.41, bf16[128,384]{1,0:T(8,128)(2,1)} %get-tuple-element.41.gate_ref, bf16[128,384]{1,0:T(8,128)(2,1)} %get-tuple-element.42.output_ref, bf16[1024,384]{1,0:T(8,128)(2,1)} %pad_maximum_fusion.up_ref, ...), custom_call_target="tpu_custom_call" | custom-call | flops 912261120 | bytes 819200 | tf_op jit(solution)/shard_map/head/pallas_call | solution.py:229
  415.3 6.5 collective-permute-start
  421.8 3.7 collective-permute-done.1
  425.6 7.5 %collective-permute-start.2 = (f32[40,32,128]{2,1,0:T(8,128)S(1)}, f32[40,32,128]{2,1,0:T(8,128)S(1)}, u32[]{:S(2)}, u32[]{:S(2)}) collective-permute-start(f32[40,32,128]{2,1,0:T(8,128)S(1)} %collective-permute-done.1), channel_id=1, source_target_pairs={{0,8},{1,12},{2,0},{3,4},{4,9},{5,13},{6,1},{7,5},{8,10},{9,14},{1... | collective-permute-start | bytes 1966088 | tf_op jit(solution)/shard_map/ppermute | solution.py:312
  433.0 15.3 %product.4 = f32[8,16,56,128]{3,2,1,0:T(8,128)} custom-call(f32[8,16,120,128]{3,2,1,0:T(8,128)} %all-to-all-done.low_ref, f32[8,16,96,128]{3,2,1,0:T(8,128)} %all-to-all-done.2.high_ref, f32[2,8,16,56,128]{4,3,2,1,0:T(8,128)} %bitcast.44), custom_call_target="tpu_custom_call" | custom-call | flops 352321536 | bytes 1966080 | tf_op jit(solution)/shard_map/product/pallas_call | solution.py:174
  448.4 64.0 %all-gather.11.cloned.1.call-done = f32[16,16,32,128]{3,2,1,0:T(8,128)} async-done(((f32[8,16,32,128]{3,2,1,0:T(8,128)}), f32[16,16,32,128]{3,2,1,0:T(8,128)}) %all-gather.11.cloned.1.call-update) | async-done | bytes 4194320 | tf_op jit(solution)/shard_map/all_gather | solution.py:354
  513.4 8.0 %all-to-all-start.4 = ((f32[8,16,56,128]{3,2,1,0:T(8,128)}), f32[8,16,56,128]{3,2,1,0:T(8,128)}, u32[]{:S(2)}, u32[]{:S(2)}) async-start(f32[8,16,56,128]{3,2,1,0:T(8,128)} %product.4), calls=%async_computation.4 | async-start | bytes 7340032 | tf_op jit(solution)/shard_map/all_to_all | solution.py:372
  521.4 14.2 %product.5 = f32[8,16,32,128]{3,2,1,0:T(8,128)} custom-call(f32[8,16,120,128]{3,2,1,0:T(8,128)} %all-to-all-done.low_ref, f32[8,16,96,128]{3,2,1,0:T(8,128)} %all-to-all-done.2.high_ref, f32[2,8,16,32,128]{4,3,2,1,0:T(8,128)} %bitcast.46), custom_call_target="tpu_custom_call" | custom-call | flops 201326592 | bytes 1572864 | tf_op jit(solution)/shard_map/product/pallas_call | solution.py:174
  535.6 29.7 %all-to-all-done.4 = f32[8,16,56,128]{3,2,1,0:T(8,128)} async-done(((f32[8,16,56,128]{3,2,1,0:T(8,128)}), f32[8,16,56,128]{3,2,1,0:T(8,128)}, u32[]{:S(2)}, u32[]{:S(2)}) %all-to-all-start.4) | async-done | bytes 3670048 | tf_op jit(solution)/shard_map/all_to_all | solution.py:372
  565.3 7.6 %all-to-all-start.5 = ((f32[8,16,32,128]{3,2,1,0:T(8,128)}), f32[8,16,32,128]{3,2,1,0:T(8,128)S(1)}, u32[]{:S(2)}, u32[]{:S(2)}) async-start(f32[8,16,32,128]{3,2,1,0:T(8,128)} %product.5), calls=%async_computation.5 | async-start | bytes 4194304 | tf_op jit(solution)/shard_map/all_to_all | solution.py:372
  572.9 26.1 %head.4 = (f32[56,32,128]{2,1,0:T(8,128)}, f32[56,32,128]{2,1,0:T(8,128)}) custom-call(f32[128,128,128]{2,1,0:T(8,128)} %bitcast.37, f32[128,56,128]{2,1,0:T(8,128)} %bitcast.14.product_ref, bf16[128,384]{1,0:T(8,128)(2,1)} %get-tuple-element.41.gate_ref, bf16[128,384]{1,0:T(8,128)(2,1)} %get-tuple-element.42.output_ref, ...), custom_call_target="tpu_custom_call" | custom-call | flops 1277165568 | bytes 1146880 | tf_op jit(solution)/shard_map/head/pallas_call | solution.py:229
  599.6 1.3 copy-done.2
  600.9 16.0 %head.5 = (f32[32,32,128]{2,1,0:T(8,128)}, f32[32,32,128]{2,1,0:T(8,128)}) custom-call(f32[128,128,128]{2,1,0:T(8,128)} %bitcast.38, f32[128,32,128]{2,1,0:T(8,128)} %bitcast.43, bf16[128,384]{1,0:T(8,128)(2,1)} %get-tuple-element.41.gate_ref, bf16[128,384]{1,0:T(8,128)(2,1)} %get-tuple-element.42.output_ref, bf16[1024,384]{1,0:T(8,128)(2,1)} %pad_maximum_fusion.up_ref, ...), custom_call_target="tpu_custom_call" | custom-call | flops 729808896 | bytes 655360 | tf_op jit(solution)/shard_map/head/pallas_call | solution.py:229
  616.8 1.5 collective-permute-start.7
  618.3 2.5 collective-permute-start.3
  620.8 1.3 collective-permute-done.4
  622.1 1.1 collective-permute-start.5
  623.2 3.6 collective-permute-start.6
  626.8 5.4 collective-permute-done.7
  632.2 19.2 %collective-permute-start.8 = (f32[32,32,128]{2,1,0:T(8,128)}, f32[32,32,128]{2,1,0:T(8,128)}, u32[]{:S(2)}, u32[]{:S(2)}) collective-permute-start(f32[32,32,128]{2,1,0:T(8,128)} %collective-permute-done.7), channel_id=1, source_target_pairs={{0,8},{1,12},{2,0},{3,4},{4,9},{5,13},{6,1},{7,5},{8,10},{9,14},{1... | collective-permute-start | bytes 1572872 | tf_op jit(solution)/shard_map/ppermute | solution.py:312
  652.2 5.8 turned.1.base_ref
  658.0 4.3 joined.3.base_ref
  662.3 23.0 %collective-permute-done.3.low_ref = f32[56,32,128]{2,1,0:T(8,128)S(1)} collective-permute-done((f32[56,32,128]{2,1,0:T(8,128)S(1)}, f32[56,32,128]{2,1,0:T(8,128)S(1)}, u32[]{:S(2)}, u32[]{:S(2)}) %collective-permute-start.3) | collective-permute-done | bytes 917536 | tf_op jit(solution)/shard_map/ppermute | solution.py:312
  685.3 16.3 %collective-permute-done.5.high_ref = f32[56,32,128]{2,1,0:T(8,128)S(1)} collective-permute-done((f32[56,32,128]{2,1,0:T(8,128)}, f32[56,32,128]{2,1,0:T(8,128)S(1)}, u32[]{:S(2)}, u32[]{:S(2)}) %collective-permute-start.5) | collective-permute-done | bytes 917536 | tf_op jit(solution)/shard_map/ppermute | solution.py:312
  702.6 5.4 joined.4.base_ref
  708.0 4.7 collective-permute-done.8.high_ref
  712.8 3.6 joined.5
  (54 shorter events, 9.5 us)
Async XLA Ops:
  15.5 36.0 %all-to-all-start.1 = ((f32[8,16,40,128]{3,2,1,0:T(8,128)}), f32[8,16,40,128]{3,2,1,0:T(8,128)S(1)}, u32[]{:S(2)}, u32[]{:S(2)}) async-start(f32[8,16,40,128]{3,2,1,0:T(8,128)} %bitcast.42), calls=%async_computation.1 | async-start | bytes 5242880 | tf_op jit(solution)/shard_map/all_to_all | solution.py:347
  51.5 1.5 copy-start
  53.0 147.7 %all-to-all-start = ((f32[8,16,120,128]{3,2,1,0:T(8,128)}), f32[8,16,120,128]{3,2,1,0:T(8,128)}, u32[]{:S(2)}, u32[]{:S(2)}) async-start(f32[8,16,120,128]{3,2,1,0:T(8,128)} %bitcast.39), calls=%async_computation | async-start | bytes 15728640 | tf_op jit(solution)/shard_map/all_to_all | solution.py:347
  60.1 129.3 %all-gather.7.cloned.1.call-start = ((), (), s32[]{:S(2)}) async-start(), calls=%async_computation.6 | async-start | bytes 7864320 | tf_op jit(solution)/shard_map/all_gather | solution.py:354
  200.7 124.6 %all-to-all-start.2 = ((f32[8,16,96,128]{3,2,1,0:T(8,128)}), f32[8,16,96,128]{3,2,1,0:T(8,128)}, u32[]{:S(2)}, u32[]{:S(2)}) async-start(f32[8,16,96,128]{3,2,1,0:T(8,128)} %bitcast.40), calls=%async_computation.2 | async-start | bytes 12582912 | tf_op jit(solution)/shard_map/all_to_all | solution.py:347
  206.8 226.2 %all-gather.9.cloned.1.call-start = ((), (), s32[]{:S(2)}) async-start(), calls=%async_computation.7 | async-start | bytes 11010048 | tf_op jit(solution)/shard_map/all_gather | solution.py:354
  339.9 53.9 %all-to-all-start.3 = ((f32[8,16,40,128]{3,2,1,0:T(8,128)}), f32[8,16,40,128]{3,2,1,0:T(8,128)S(1)}, u32[]{:S(2)}, u32[]{:S(2)}) async-start(f32[8,16,40,128]{3,2,1,0:T(8,128)} %product.3), calls=%async_computation.3 | async-start | bytes 5242880 | tf_op jit(solution)/shard_map/all_to_all | solution.py:372
  345.3 3.3 copy-start.9
  345.3 3.4 copy-start.10
  345.3 7.2 copy-start.11
  345.3 7.2 %copy-start.12 = (f32[128]{0:T(128)S(1)}, f32[128]{0:T(128)}, u32[]{:S(2)}) copy-start(f32[128]{0:T(128)} %param.16) | copy-start | bytes 1540
  345.3 8.0 %copy-start.13 = (f32[128]{0:T(128)S(1)}, f32[128]{0:T(128)}, u32[]{:S(2)}) copy-start(f32[128]{0:T(128)} %param.17) | copy-start | bytes 1540
  345.3 167.0 %all-gather.11.cloned.1.call-start = ((), (), s32[]{:S(2)}) async-start(), calls=%async_computation.8 | async-start | bytes 6291456 | tf_op jit(solution)/shard_map/all_gather | solution.py:354
  393.8 1.5 copy-start.1
  414.8 10.8 %collective-permute-start.1 = (f32[40,32,128]{2,1,0:T(8,128)}, f32[40,32,128]{2,1,0:T(8,128)S(1)}, u32[]{:S(2)}, u32[]{:S(2)}) collective-permute-start(f32[40,32,128]{2,1,0:T(8,128)} %get-tuple-element.20.refs_3_), channel_id=1, source_target_pairs={{0,2},{1,3},{2,0},{3,1},{4,6},{5,7},{6,4},{7,5},{8,10},{9,11},{10,... | collective-permute-start | bytes 1966088 | tf_op jit(solution)/shard_map/ppermute | solution.py:312
  415.3 97.1 %collective-permute-start = (f32[40,32,128]{2,1,0:T(8,128)}, f32[40,32,128]{2,1,0:T(8,128)S(1)}, u32[]{:S(2)}, u32[]{:S(2)}) collective-permute-start(f32[40,32,128]{2,1,0:T(8,128)} %get-tuple-element.19.refs_0_), channel_id=1, source_target_pairs={{0,0},{1,4},{2,8},{3,12},{4,1},{5,5},{6,9},{7,13},{8,2},{9,6},{10,... | collective-permute-start | bytes 1966088 | tf_op jit(solution)/shard_map/ppermute | solution.py:312
  425.6 86.8 %collective-permute-start.2 = (f32[40,32,128]{2,1,0:T(8,128)S(1)}, f32[40,32,128]{2,1,0:T(8,128)S(1)}, u32[]{:S(2)}, u32[]{:S(2)}) collective-permute-start(f32[40,32,128]{2,1,0:T(8,128)S(1)} %collective-permute-done.1), channel_id=1, source_target_pairs={{0,8},{1,12},{2,0},{3,4},{4,9},{5,13},{6,1},{7,5},{8,10},{9,14},{1... | collective-permute-start | bytes 1966088 | tf_op jit(solution)/shard_map/ppermute | solution.py:312
  512.4 0.9 copy-start.6
  512.4 1.1 copy-start.7
  513.4 51.8 %all-to-all-start.4 = ((f32[8,16,56,128]{3,2,1,0:T(8,128)}), f32[8,16,56,128]{3,2,1,0:T(8,128)}, u32[]{:S(2)}, u32[]{:S(2)}) async-start(f32[8,16,56,128]{3,2,1,0:T(8,128)} %product.4), calls=%async_computation.4 | async-start | bytes 7340032 | tf_op jit(solution)/shard_map/all_to_all | solution.py:372
  565.3 34.3 %all-to-all-start.5 = ((f32[8,16,32,128]{3,2,1,0:T(8,128)}), f32[8,16,32,128]{3,2,1,0:T(8,128)S(1)}, u32[]{:S(2)}, u32[]{:S(2)}) async-start(f32[8,16,32,128]{3,2,1,0:T(8,128)} %product.5), calls=%async_computation.5 | async-start | bytes 4194304 | tf_op jit(solution)/shard_map/all_to_all | solution.py:372
  599.0 23.1 %collective-permute-start.4 = (f32[56,32,128]{2,1,0:T(8,128)}, f32[56,32,128]{2,1,0:T(8,128)}, u32[]{:S(2)}, u32[]{:S(2)}) collective-permute-start(f32[56,32,128]{2,1,0:T(8,128)} %get-tuple-element.25.refs_4_), channel_id=1, source_target_pairs={{0,2},{1,3},{2,0},{3,1},{4,6},{5,7},{6,4},{7,5},{8,10},{9,11},{10,... | collective-permute-start | bytes 2752520 | tf_op jit(solution)/shard_map/ppermute | solution.py:312
  599.5 1.3 copy-start.2
  600.9 17.4 %copy-start.5 = (f32[56,32,128]{2,1,0:T(8,128)S(1)}, f32[56,32,128]{2,1,0:T(8,128)}, u32[]{:S(2)}) copy-start(f32[56,32,128]{2,1,0:T(8,128)} %get-tuple-element.22.refs_1_) | copy-start | bytes 2752516
  600.9 50.6 %copy-start.14 = (f32[64]{0:T(128)S(1)}, f32[64]{0:T(128)}, u32[]{:S(2)}) copy-start(f32[64]{0:T(128)} %param.21) | copy-start | bytes 772
  616.8 15.4 %collective-permute-start.7 = (f32[32,32,128]{2,1,0:T(8,128)}, f32[32,32,128]{2,1,0:T(8,128)}, u32[]{:S(2)}, u32[]{:S(2)}) collective-permute-start(f32[32,32,128]{2,1,0:T(8,128)} %get-tuple-element.26.refs_5_), channel_id=1, source_target_pairs={{0,2},{1,3},{2,0},{3,1},{4,6},{5,7},{6,4},{7,5},{8,10},{9,11},{10,... | collective-permute-start | bytes 1572872 | tf_op jit(solution)/shard_map/ppermute | solution.py:312
  618.3 67.0 %collective-permute-start.3 = (f32[56,32,128]{2,1,0:T(8,128)S(1)}, f32[56,32,128]{2,1,0:T(8,128)S(1)}, u32[]{:S(2)}, u32[]{:S(2)}) collective-permute-start(f32[56,32,128]{2,1,0:T(8,128)S(1)} %copy-done.5), channel_id=1, source_target_pairs={{0,0},{1,4},{2,8},{3,12},{4,1},{5,5},{6,9},{7,13},{8,2},{9,6},{10,... | collective-permute-start | bytes 2752520 | tf_op jit(solution)/shard_map/ppermute | solution.py:312
  622.1 79.5 %collective-permute-start.5 = (f32[56,32,128]{2,1,0:T(8,128)}, f32[56,32,128]{2,1,0:T(8,128)S(1)}, u32[]{:S(2)}, u32[]{:S(2)}) collective-permute-start(f32[56,32,128]{2,1,0:T(8,128)} %collective-permute-done.4), channel_id=1, source_target_pairs={{0,8},{1,12},{2,0},{3,4},{4,9},{5,13},{6,1},{7,5},{8,10},{9,14},{1... | collective-permute-start | bytes 2752520 | tf_op jit(solution)/shard_map/ppermute | solution.py:312
  623.2 84.8 %collective-permute-start.6 = (f32[32,32,128]{2,1,0:T(8,128)}, f32[32,32,128]{2,1,0:T(8,128)S(1)}, u32[]{:S(2)}, u32[]{:S(2)}) collective-permute-start(f32[32,32,128]{2,1,0:T(8,128)} %get-tuple-element.24.refs_2_), channel_id=1, source_target_pairs={{0,0},{1,4},{2,8},{3,12},{4,1},{5,5},{6,9},{7,13},{8,2},{9,6},{10,... | collective-permute-start | bytes 1572872 | tf_op jit(solution)/shard_map/ppermute | solution.py:312
  632.2 80.5 %collective-permute-start.8 = (f32[32,32,128]{2,1,0:T(8,128)}, f32[32,32,128]{2,1,0:T(8,128)}, u32[]{:S(2)}, u32[]{:S(2)}) collective-permute-start(f32[32,32,128]{2,1,0:T(8,128)} %collective-permute-done.7), channel_id=1, source_target_pairs={{0,8},{1,12},{2,0},{3,4},{4,9},{5,13},{6,1},{7,5},{8,10},{9,14},{1... | collective-permute-start | bytes 1572872 | tf_op jit(solution)/shard_map/ppermute | solution.py:312
  685.3 16.3 %copy-start.3 = (f32[56,32,128]{2,1,0:T(8,128)}, f32[56,32,128]{2,1,0:T(8,128)S(1)}, u32[]{:S(2)}) copy-start(f32[56,32,128]{2,1,0:T(8,128)S(1)} %collective-permute-done.3.low_ref) | copy-start | bytes 2752516
  701.6 1.0 copy-start.4
  708.0 4.7 copy-start.8
Sparse Core Ops, SparseCore 0:
  62.5 126.9 all-gather.6
  211.2 169.8 all-gather.8
  382.6 129.6 all-gather.10

commit v4 on v3

--- a/solution.py
+++ b/solution.py
@@ -11,6 +11,8 @@
 LANES = 128
 GROUP = 8
 CHUNKS = (40, 56, 32)
+LOWER = 40
+PARTS = 4
 VMEM = 56 * 1024 * 1024
 SCALE = 8
 
@@ -141,8 +143,9 @@
     )(pair, weights3)
 
 
-def product_kernel(low_ref, high_ref, right_ref, out_ref):
-    cols = right_ref.shape[1] // 2
+def product_kernel(half_ref, low_ref, high_ref, own_ref, other_ref, out_ref):
+    cols = own_ref.shape[0] // 2
+    half = half_ref[0]
 
     def line(ref, lo):
         return jnp.concatenate([ref[lo * cols + c, 0] for c in range(cols)], axis=1)
@@ -151,7 +154,7 @@
         jnp.concatenate([line(ref, lo) for lo in range(2) for ref in (low_ref, high_ref)], axis=0)
     )
     right_high, right_low = parts(
-        jnp.concatenate([line(right_ref.at[half], lo) for half in range(2) for lo in range(2)], axis=0)
+        jnp.concatenate([line(ref, lo) for ref in (own_ref, other_ref) for lo in range(2)], axis=0)
     )
     result = lax.dot_general(
         jnp.concatenate([right_high, right_high, right_low], axis=1),
@@ -159,34 +162,36 @@
         (((1,), (1,)), ((), ())),
         preferred_element_type=jnp.float32,
     )
-    rows = right_ref.shape[3]
+    rows = own_ref.shape[2]
     wide = result.shape[1] // 2
     for lo in range(2):
-        for plane in range(cols):
+        for piece in range(cols):
+            source, other_lo = divmod(piece, 2)
+            plane = 2 * jnp.where(half == source, 0, 1) + other_lo
             out_ref[lo * cols + plane, 0] = result[
-                plane * rows : (plane + 1) * rows, lo * wide : (lo + 1) * wide
+                piece * rows : (piece + 1) * rows, lo * wide : (lo + 1) * wide
             ]
 
 
-def product(low, high, right, wide):
-    _, sources, owned, rows, width = right.shape
+def product(half, low, high, own, other, wide):
+    sources, owned, rows, width = own.shape
     k_all = width * sources // 2
+    spec = lambda height: pl.BlockSpec((sources, 1, height, width), lambda n, half: (0, n, 0, 0))
     return pl.pallas_call(
         product_kernel,
-        grid=(owned,),
-        in_specs=[
-            pl.BlockSpec((sources, 1, wide // 2, width), lambda n: (0, n, 0, 0)),
-            pl.BlockSpec((sources, 1, wide // 2, width), lambda n: (0, n, 0, 0)),
-            pl.BlockSpec((2, sources, 1, rows, width), lambda n: (0, 0, n, 0, 0)),
-        ],
-        out_specs=pl.BlockSpec((sources, 1, rows, wide), lambda n: (0, n, 0, 0)),
+        grid_spec=pltpu.PrefetchScalarGridSpec(
+            num_scalar_prefetch=1,
+            grid=(owned,),
+            in_specs=[spec(LOWER), spec(wide - LOWER), spec(rows), spec(rows)],
+            out_specs=pl.BlockSpec((sources, 1, rows, wide), lambda n, half: (0, n, 0, 0)),
+        ),
         out_shape=jax.ShapeDtypeStruct((sources, owned, rows, wide), jnp.float32),
         compiler_params=pltpu.CompilerParams(vmem_limit_bytes=VMEM),
         cost_estimate=estimate(
             6 * owned * 4 * rows * 2 * wide * k_all, 4 * owned * k_all * (2 * wide + 4 * rows)
         ),
         name="product",
-    )(low, high, right)
+    )(half, low, high, own, other)
 
 
 def head_kernel(
@@ -223,7 +228,7 @@
     chunk_cols = product_values.shape[1]
     steps = chunk_cols // GROUP
     lead = first // GROUP
-    bins = bins3.shape[0] // 2
+    bins = bins3.shape[0] // PARTS
     whole = lambda array: pl.BlockSpec(array.shape, lambda g: (0, 0))
     macs = gate3.size + output3.size + up3.size + down3.size + bins3.size
     return pl.pallas_call(
@@ -238,11 +243,11 @@
             whole(down3),
             whole(bins3),
         ],
-        out_specs=[pl.BlockSpec((GROUP, bins, tile_rows), lambda g: (g, 0, 0))] * 2,
-        out_shape=[jax.ShapeDtypeStruct((chunk_cols, bins, tile_rows), jnp.float32)] * 2,
+        out_specs=[pl.BlockSpec((GROUP, bins, tile_rows), lambda g: (g, 0, 0))] * PARTS,
+        out_shape=[jax.ShapeDtypeStruct((chunk_cols, bins, tile_rows), jnp.float32)] * PARTS,
         compiler_params=pltpu.CompilerParams(vmem_limit_bytes=VMEM),
         cost_estimate=estimate(
-            2 * chunk_cols * tile_rows * macs, 4 * chunk_cols * tile_rows * 2 * (width + bins)
+            2 * chunk_cols * tile_rows * macs, 4 * chunk_cols * tile_rows * (2 * width + PARTS * bins)
         ),
         name="head",
     )(pair, product_values, gate3, output3, up3, down3, bins3)
@@ -250,70 +255,74 @@
 
 def turned_kernel(bias_ref, *refs):
     out_ref, sources = refs[-1], refs[:-1]
-    count = len(sources) // 2
+    count = len(sources) // PARTS
     tile_rows, _, bins, tile_cols = out_ref.shape
-    flat = out_ref.reshape(tile_rows * 2 * bins, tile_cols)
-    for part in range(2):
+    flat = out_ref.reshape(tile_rows * PARTS * bins, tile_cols)
+    for part in range(PARTS):
         for n in range(bins):
             values = [
                 ref.reshape(ref.shape[0] * bins, tile_rows)[pl.ds(n, ref.shape[0], stride=bins), :]
                 for ref in sources[part * count : (part + 1) * count]
             ]
             result = jnp.concatenate(values, axis=0).T + bias_ref[part, n : n + 1, :]
-            flat[pl.ds(part * bins + n, tile_rows, stride=2 * bins), :] = result
+            flat[pl.ds(part * bins + n, tile_rows, stride=PARTS * bins), :] = result
 
 
 def turned(bias, own):
-    arrays = [block[part] for part in range(2) for block in own]
+    arrays = [block[part] for part in range(PARTS) for block in own]
     _, bins, tile_rows = arrays[0].shape
     tile_cols = sum(block[0].shape[0] for block in own)
     block = lambda rows: pl.BlockSpec((rows, GROUP, tile_rows), lambda g: (0, g, 0))
     return pl.pallas_call(
         turned_kernel,
         grid=(bins // GROUP,),
-        in_specs=[pl.BlockSpec((2, GROUP, tile_cols), lambda g: (0, g, 0))]
+        in_specs=[pl.BlockSpec((PARTS, GROUP, tile_cols), lambda g: (0, g, 0))]
         + [block(array.shape[0]) for array in arrays],
-        out_specs=pl.BlockSpec((tile_rows, 2, GROUP, tile_cols), lambda g: (0, 0, g, 0)),
-        out_shape=jax.ShapeDtypeStruct((tile_rows, 2, bins, tile_cols), jnp.float32),
+        out_specs=pl.BlockSpec((tile_rows, PARTS, GROUP, tile_cols), lambda g: (0, 0, g, 0)),
+        out_shape=jax.ShapeDtypeStruct((tile_rows, PARTS, bins, tile_cols), jnp.float32),
         compiler_params=pltpu.CompilerParams(vmem_limit_bytes=VMEM),
-        cost_estimate=estimate(0, 8 * tile_rows * 2 * bins * tile_cols),
+        cost_estimate=estimate(0, 8 * tile_rows * PARTS * bins * tile_cols),
         name="turned",
     )(bias, *arrays)
 
 
-def joined_kernel(base_ref, low_ref, high_ref, out_ref):
-    out_ref[:, 0] = base_ref[:, 0] + low_ref[...]
-    out_ref[:, 1] = base_ref[:, 1] + high_ref[...]
+def joined_kernel(base_ref, *refs):
+    out_ref = refs[-1]
+    for part, ref in enumerate(refs[:-1]):
+        out_ref[:, part] = base_ref[:, part] + ref[...]
 
 
 def joined(base, mirror, first):
     rows, bins, tile_cols = mirror[0].shape
     lead = first // GROUP
-    whole = pl.BlockSpec((GROUP, 2, bins, tile_cols), lambda g: (lead + g, 0, 0, 0))
+    whole = pl.BlockSpec((GROUP, PARTS, bins, tile_cols), lambda g: (lead + g, 0, 0, 0))
     block = pl.BlockSpec((GROUP, bins, tile_cols), lambda g: (g, 0, 0))
     return pl.pallas_call(
         joined_kernel,
         grid=(rows // GROUP,),
-        in_specs=[whole, block, block],
+        in_specs=[whole] + [block] * PARTS,
         out_specs=whole,
         out_shape=jax.ShapeDtypeStruct(base.shape, jnp.float32),
         input_output_aliases={0: 0},
         compiler_params=pltpu.CompilerParams(vmem_limit_bytes=VMEM),
-        cost_estimate=estimate(0, 24 * rows * bins * tile_cols),
+        cost_estimate=estimate(0, 12 * PARTS * rows * bins * tile_cols),
         name="joined",
     )(base, *mirror)
 
 
-def mirrored_halves(block, count):
+def mirrored_parts(block, count):
     every = [(r, c) for r in range(count) for c in range(count)]
 
     def move(values, target):
         pairs = [(r * count + c, target(r, c)) for r, c in every]
         return lax.ppermute(values, ("half", "lo", "col"), pairs)
 
-    low = move(block[0], lambda r, c: c * count + r)
-    high = move(block[1], lambda r, c: r * count + (c ^ 2))
-    return low, move(high, lambda r, c: (c ^ 2) * count + r)
+    result = []
+    for part, values in enumerate(block):
+        if part:
+            values = move(values, lambda r, c: r * count + (c ^ part))
+        result.append(move(values, lambda r, c: (c ^ part) * count + r))
+    return result
 
 
 def half_shards(
@@ -347,44 +356,45 @@
         return lax.all_to_all(values, ("lo", "col"), split_axis=0, concat_axis=0, tiled=True)
 
     tie = lax.optimization_barrier
+    half = lax.axis_index("half").astype(jnp.int32).reshape(1)
     firsts = [sum(CHUNKS[:n]) for n in range(len(CHUNKS))]
-    lower = tile_rows // 2
-
-    def gather(values, first):
-        return lax.all_gather(values[:, :, first:], "half")
-
-    sent = [
-        hands(tile, in3, (0, 0), (firsts[0], CHUNKS[0])),
-        hands(tile, in3, (0, lower), (firsts[1], CHUNKS[1])),
-        hands(tile, in3, (lower, lower), (firsts[2], CHUNKS[2])),
-    ]
-    gathered = [gather(spread(sent[0]), 0)]
-    low = spread(sent[1])
-    gathered.append(gather(low, lower))
-    gathered[0], sent[2] = tie((gathered[0], sent[2]))
-    high = spread(sent[2])
-    gathered.append(gather(high, lower))
-
-    def blocks(right):
-        return product(low, high, right, tile_rows)
+    upper = tile_rows - LOWER
+
+    def exchange(values):
+        return lax.ppermute(values, "half", [(0, 1), (1, 0)])
 
     def finish(values, chunk):
         values = lax.all_to_all(values, ("lo", "col"), split_axis=0, concat_axis=0, tiled=True)
         values = values.reshape(width, CHUNKS[chunk], tile_rows)
         return head(tile, values, firsts[chunk], gate3, output3, up3, down3, bins3)
 
-    own = [finish(blocks(gathered[0]), 0)]
-    mirror = [mirrored_halves(own[0], row_count)]
-    values, gathered[2], mirror[0] = tie((blocks(gathered[1]), gathered[2], mirror[0]))
+    right = spread(hands(tile, in3, (0, 0), (firsts[0], CHUNKS[0])))
+    rights, others = [right], [exchange(right)]
+    low = spread(hands(tile, in3, (0, LOWER), (firsts[1], CHUNKS[1])))
+    rights.append(low[:, :, LOWER:])
+    others.append(exchange(rights[1]))
+    sent = hands(tile, in3, (LOWER, upper), (firsts[2], CHUNKS[2]))
+    sent, others[0] = tie((sent, others[0]))
+    high = spread(sent)
+    rights.append(high[:, :, upper:])
+    others.append(exchange(rights[2]))
+
+    def blocks(chunk):
+        return product(half, low, high, rights[chunk], others[chunk], tile_rows)
+
+    values, others[1] = tie((blocks(0), others[1]))
+    own = [finish(values, 0)]
+    mirror = [mirrored_parts(own[0], row_count)]
+    values, others[2], mirror[0] = tie((blocks(1), others[2], mirror[0]))
     own.append(finish(values, 1))
-    own.append(finish(blocks(gathered[2]), 2))
-    mirror += [mirrored_halves(block, row_count) for block in own[1:]]
-    bins = distogram_bias.shape[0] // 2
-    bias = jnp.broadcast_to(distogram_bias.reshape(2, bins, 1), (2, bins, tile_cols))
+    own.append(finish(blocks(2), 2))
+    mirror += [mirrored_parts(block, row_count) for block in own[1:]]
+    bins = distogram_bias.shape[0] // PARTS
+    bias = jnp.broadcast_to(distogram_bias.reshape(PARTS, bins, 1), (PARTS, bins, tile_cols))
     logits = turned(bias, own)
     for first, block in zip(firsts, mirror):
         logits = joined(logits, block, first)
-    logits = logits.reshape(tile_rows, 2 * bins, tile_cols)
+    logits = logits.reshape(tile_rows, PARTS * bins, tile_cols)
     return jnp.swapaxes(logits, 1, 2)[None]
 
 

time: 729 us -> 689 us (0.945)
  waiting for transfers between devices: 443 us -> 387 us
  starting transfers between devices: 82.4 us -> 107 us
  between operations: 13.3 us -> 0.28 us
    all_gather x3 -> x0, waiting for transfers between devices: 179 us -> none  [gather(): return lax.all_gather(values[:, :, first:], 'half')]
    ppermute x0 -> x3, waiting for transfers between devices: none -> 107 us  [exchange(): return lax.ppermute(values, 'half', [(0, 1), (1, 0)])]
    all_to_all x3, waiting for transfers between devices: 140 us -> 175 us  [spread(): lax.all_to_all(values, ('lo', 'col'), split_axis=0, concat_axis=0, tiled=...]
    ppermute x9 -> x21, starting transfers between devices: 43 us -> 59.9 us  [move(): return lax.ppermute(values, ('half', 'lo', 'col'), pairs)]
    ppermute x9 -> x21, waiting for transfers between devices: 54.5 us -> 42.2 us  [move(): return lax.ppermute(values, ('half', 'lo', 'col'), pairs)]
    all_to_all x3, starting transfers between devices: 18.4 us -> 26.9 us  [spread(): lax.all_to_all(values, ('lo', 'col'), split_axis=0, concat_axis=0, tiled=...]
  transfers between devices with their start and end apart: 18 -> 30, of which waited for: 13 -> 11; matrix products, arithmetic and copies ran while one was open for 2% -> 2% of each run, Pallas kernels for 21% -> 22%
where the time goes in v4:
time: 689 us; the launch traced here: 680 us
  waiting for transfers between devices  387 us (56%)
  Pallas kernels  161 us (23%)
  starting transfers between devices  107 us (16%)
  local copies, waits for them, and re-layouts  17 us (2%)
  other arithmetic  7.32 us (1%)
    all_to_all x3, waiting for transfers between devices, spread(): lax.all_to_all(values, ('lo', 'col'), split_axis=0, concat_axis=0, tiled=...  175 us
    ppermute x3, waiting for transfers between devices, exchange(): return lax.ppermute(values, 'half', [(0, 1), (1, 0)])  107 us
    all_to_all x3, waiting for transfers between devices, finish(): lax.all_to_all(values, ('lo', 'col'), split_axis=0, concat_axis=0, tiled=...  63.3 us
    pallas_call x3, Pallas kernels, head(): pl.pallas_call(head_kernel, grid=(steps,), in_specs=[pl.BlockSpec((tile_r...  61.4 us
    ppermute x21, starting transfers between devices, move(): return lax.ppermute(values, ('half', 'lo', 'col'), pairs)  59.9 us
    pallas_call x3, Pallas kernels, product(): pl.pallas_call(product_kernel, grid_spec=pltpu.PrefetchScalarGridSpec(num...  44.2 us
    ppermute x21, waiting for transfers between devices, move(): return lax.ppermute(values, ('half', 'lo', 'col'), pairs)  42.2 us
    pallas_call x3, Pallas kernels, hands(): pl.pallas_call(hands_kernel, grid=(rows // GROUP,), in_specs=[pl.BlockSpe...  35.7 us
  transfers between devices with their start and end apart: 30, of which 11 were waited for; matrix products, arithmetic and copies ran while one was open for 2% of the time, Pallas kernels for 22%

profile of v4, /device:TPU:12, one launch (start us, length us, event | category | flops | bytes accessed | tf_op | source)
XLA Modules:
  0.0 679.8 jit_solution(13907453650879374045)
XLA Ops:
  2.6 6.4 hands.5
  8.9 5.1 all-to-all-start.1
  14.1 13.1 %hands.3 = f32[128,96,128]{2,1,0:T(8,128)} custom-call(f32[128,128,128]{2,1,0:T(8,128)} %bitcast.32, bf16[512,384]{1,0:T(8,128)(2,1)} %pad_maximum_fusion.1.weights_ref), custom_call_target="tpu_custom_call" | custom-call | flops 301989888 | bytes 1572864 | tf_op jit(solution)/shard_map/hands/pallas_call | solution.py:131
  27.2 17.8 %all-to-all-done.1.own_ref = f32[8,16,40,128]{3,2,1,0:T(8,128)S(1)} async-done(((f32[8,16,40,128]{3,2,1,0:T(8,128)}), f32[8,16,40,128]{3,2,1,0:T(8,128)S(1)}, u32[]{:S(2)}, u32[]{:S(2)}) %all-to-all-start.1) | async-done | bytes 2621472 | tf_op jit(solution)/shard_map/all_to_all | solution.py:356
  45.0 7.2 %all-to-all-start = ((f32[8,16,96,128]{3,2,1,0:T(8,128)}), f32[8,16,96,128]{3,2,1,0:T(8,128)}, u32[]{:S(2)}, u32[]{:S(2)}) async-start(f32[8,16,96,128]{3,2,1,0:T(8,128)} %bitcast.38), calls=%async_computation | async-start | bytes 12582912 | tf_op jit(solution)/shard_map/all_to_all | solution.py:356
  52.2 2.5 collective-permute-start
  54.7 16.2 %hands.4 = f32[128,120,128]{2,1,0:T(8,128)} custom-call(f32[128,128,128]{2,1,0:T(8,128)} %bitcast.33, bf16[512,384]{1,0:T(8,128)(2,1)} %pad_maximum_fusion.1.weights_ref), custom_call_target="tpu_custom_call" | custom-call | flops 377487360 | bytes 1966080 | tf_op jit(solution)/shard_map/hands/pallas_call | solution.py:131
  70.9 107.0 %collective-permute-done.other_ref = f32[8,16,40,128]{3,2,1,0:T(8,128)} collective-permute-done((f32[8,16,40,128]{3,2,1,0:T(8,128)S(1)}, f32[8,16,40,128]{3,2,1,0:T(8,128)}, u32[]{:S(2)}, u32[]{:S(2)}) %collective-permute-start) | collective-permute-done | bytes 2621472 | tf_op jit(solution)/shard_map/ppermute | solution.py:364
  177.8 14.6 %all-to-all-start.2 = ((f32[8,16,120,128]{3,2,1,0:T(8,128)}), f32[8,16,120,128]{3,2,1,0:T(8,128)}, u32[]{:S(2)}, u32[]{:S(2)}) async-start(f32[8,16,120,128]{3,2,1,0:T(8,128)} %bitcast.37), calls=%async_computation.2 | async-start | bytes 15728640 | tf_op jit(solution)/shard_map/all_to_all | solution.py:356
  192.4 4.2 slice.8.own_ref
  196.6 156.8 %all-to-all-done.2.high_ref = f32[8,16,120,128]{3,2,1,0:T(8,128)} async-done(((f32[8,16,120,128]{3,2,1,0:T(8,128)}), f32[8,16,120,128]{3,2,1,0:T(8,128)}, u32[]{:S(2)}, u32[]{:S(2)}) %all-to-all-start.2) | async-done | bytes 7864352 | tf_op jit(solution)/shard_map/all_to_all | solution.py:356
  353.4 14.7 %product.3 = f32[8,16,40,128]{3,2,1,0:T(8,128)} custom-call(s32[1]{0:T(128)} %bitcast.1.half_ref, f32[8,16,96,128]{3,2,1,0:T(8,128)} %all-to-all-done.low_ref, f32[8,16,120,128]{3,2,1,0:T(8,128)} %all-to-all-done.2.high_ref, f32[8,16,40,128]{3,2,1,0:T(8,128)} %copy-done, f32[8,16,40,128]{3,2,1,0:T(8,128)} %collective-permute-done.other_ref), custom_call_target="tpu_custom_call" | custom-call | flops 251658240 | bytes 1703936 | tf_op jit(solution)/shard_map/product/pallas_call | solution.py:180
  368.1 6.6 all-to-all-start.3
  374.8 3.1 slice.9.own_ref
  382.0 1.3 pad_maximum_fusion.5.bins_ref
  387.2 37.6 %all-to-all-done.3 = f32[8,16,40,128]{3,2,1,0:T(8,128)S(1)} async-done(((f32[8,16,40,128]{3,2,1,0:T(8,128)}), f32[8,16,40,128]{3,2,1,0:T(8,128)S(1)}, u32[]{:S(2)}, u32[]{:S(2)}) %all-to-all-start.3) | async-done | bytes 2621472 | tf_op jit(solution)/shard_map/all_to_all | solution.py:367
  424.8 1.6 copy-done.1
  426.3 19.3 %head.3 = (f32[40,16,128]{2,1,0:T(8,128)}, f32[40,16,128]{2,1,0:T(8,128)}, f32[40,16,128]{2,1,0:T(8,128)}, f32[40,16,128]{2,1,0:T(8,128)}) custom-call(f32[128,128,128]{2,1,0:T(8,128)} %bitcast.34, f32[128,40,128]{2,1,0:T(8,128)} %bitcast.39, bf16[128,384]{1,0:T(8,128)(2,1)} %get-tuple-element.61.gate_ref, bf16[128,384]{1,0:T(8,128)(2,1)} %get-tuple-element.62.output_ref, ...), custom_call_target="tpu_custom_call" | custom-call | flops 912261120 | bytes 819200 | tf_op jit(solution)/shard_map/head/pallas_call | solution.py:234
  445.6 1.4 collective-permute-start.4
  447.5 1.6 collective-permute-start.8
  449.1 2.4 collective-permute-start.3
  451.5 3.5 collective-permute-done.4
  455.0 2.8 collective-permute-start.5
  457.8 15.2 %collective-permute-start.7 = (f32[40,16,128]{2,1,0:T(8,128)S(1)}, f32[40,16,128]{2,1,0:T(8,128)}, u32[]{:S(2)}, u32[]{:S(2)}) collective-permute-start(f32[40,16,128]{2,1,0:T(8,128)S(1)} %collective-permute-done.6), channel_id=1, source_target_pairs={{0,8},{1,12},{2,0},{3,4},{4,9},{5,13},{6,1},{7,5},{8,10},{9,14},{1... | collective-permute-start | bytes 983048 | tf_op jit(solution)/shard_map/ppermute | solution.py:318
  473.3 15.3 %product.4 = f32[8,16,56,128]{3,2,1,0:T(8,128)} custom-call(s32[1]{0:T(128)} %bitcast.1.half_ref, f32[8,16,96,128]{3,2,1,0:T(8,128)} %all-to-all-done.low_ref, f32[8,16,120,128]{3,2,1,0:T(8,128)} %all-to-all-done.2.high_ref, f32[8,16,56,128]{3,2,1,0:T(8,128)} %slice.8.own_ref, f32[8,16,56,128]{3,2,1,0:T(8,128)} %collective-permute-done.1.other_ref), custom_call_target="tpu_custom_call" | custom-call | flops 352321536 | bytes 1966080 | tf_op jit(solution)/shard_map/product/pallas_call | solution.py:180
  488.6 5.1 collective-permute-done.3.refs_0_
  493.7 2.5 collective-permute-done.5.refs_1_
  496.2 4.5 all-to-all-start.4
  500.7 14.2 %product.5 = f32[8,16,32,128]{3,2,1,0:T(8,128)} custom-call(s32[1]{0:T(128)} %bitcast.1.half_ref, f32[8,16,96,128]{3,2,1,0:T(8,128)} %all-to-all-done.low_ref, f32[8,16,120,128]{3,2,1,0:T(8,128)} %all-to-all-done.2.high_ref, f32[8,16,32,128]{3,2,1,0:T(8,128)} %slice.9.own_ref, f32[8,16,32,128]{3,2,1,0:T(8,128)} %collective-permute-done.2.other_ref), custom_call_target="tpu_custom_call" | custom-call | flops 201326592 | bytes 1572864 | tf_op jit(solution)/shard_map/product/pallas_call | solution.py:180
  514.8 25.7 %all-to-all-done.4 = f32[8,16,56,128]{3,2,1,0:T(8,128)} async-done(((f32[8,16,56,128]{3,2,1,0:T(8,128)}), f32[8,16,56,128]{3,2,1,0:T(8,128)}, u32[]{:S(2)}, u32[]{:S(2)}) %all-to-all-start.4) | async-done | bytes 3670048 | tf_op jit(solution)/shard_map/all_to_all | solution.py:367
  540.6 6.1 all-to-all-start.5
  546.7 26.1 %head.4 = (f32[56,16,128]{2,1,0:T(8,128)}, f32[56,16,128]{2,1,0:T(8,128)}, f32[56,16,128]{2,1,0:T(8,128)}, f32[56,16,128]{2,1,0:T(8,128)}) custom-call(f32[128,128,128]{2,1,0:T(8,128)} %bitcast.35, f32[128,56,128]{2,1,0:T(8,128)} %bitcast.12.product_ref, bf16[128,384]{1,0:T(8,128)(2,1)} %get-tuple-element.61.gate_ref, ...), custom_call_target="tpu_custom_call" | custom-call | flops 1277165568 | bytes 1146880 | tf_op jit(solution)/shard_map/head/pallas_call | solution.py:234
  572.8 1.5 collective-permute-start.11
  574.9 1.3 copy-done.2
  576.2 16.0 %head.5 = (f32[32,16,128]{2,1,0:T(8,128)}, f32[32,16,128]{2,1,0:T(8,128)}, f32[32,16,128]{2,1,0:T(8,128)}, f32[32,16,128]{2,1,0:T(8,128)}) custom-call(f32[128,128,128]{2,1,0:T(8,128)} %bitcast.36, f32[128,32,128]{2,1,0:T(8,128)} %bitcast.41, bf16[128,384]{1,0:T(8,128)(2,1)} %get-tuple-element.61.gate_ref, bf16[128,384]{1,0:T(8,128)(2,1)} %get-tuple-element.62.output_ref, ...), custom_call_target="tpu_custom_call" | custom-call | flops 729808896 | bytes 655360 | tf_op jit(solution)/shard_map/head/pallas_call | solution.py:234
  592.8 2.4 collective-permute-start.15
  595.7 6.1 collective-permute-done.18
  601.8 3.8 collective-permute-start.10
  605.6 2.0 collective-permute-start.12
  607.6 8.8 %collective-permute-start.14 = (f32[56,16,128]{2,1,0:T(8,128)}, f32[56,16,128]{2,1,0:T(8,128)S(1)}, u32[]{:S(2)}, u32[]{:S(2)}) collective-permute-start(f32[56,16,128]{2,1,0:T(8,128)} %collective-permute-done.13), channel_id=1, source_target_pairs={{0,8},{1,12},{2,0},{3,4},{4,9},{5,13},{6,1},{7,5},{8,10},{9,14},{1... | collective-permute-start | bytes 1376264 | tf_op jit(solution)/shard_map/ppermute | solution.py:318
  616.5 12.9 %collective-permute-start.22 = (f32[32,16,128]{2,1,0:T(8,128)}, f32[32,16,128]{2,1,0:T(8,128)}, u32[]{:S(2)}, u32[]{:S(2)}) collective-permute-start(f32[32,16,128]{2,1,0:T(8,128)} %get-tuple-element.44.refs_11_), channel_id=1, source_target_pairs={{0,3},{1,2},{2,1},{3,0},{4,7},{5,6},{6,5},{7,4},{8,11},{9,10},{10,... | collective-permute-start | bytes 786440 | tf_op jit(solution)/shard_map/ppermute | solution.py:318
  629.4 16.7 %collective-permute-done.22 = f32[32,16,128]{2,1,0:T(8,128)} collective-permute-done((f32[32,16,128]{2,1,0:T(8,128)}, f32[32,16,128]{2,1,0:T(8,128)}, u32[]{:S(2)}, u32[]{:S(2)}) %collective-permute-start.22) | collective-permute-done | bytes 262176 | tf_op jit(solution)/shard_map/ppermute | solution.py:318
  646.2 1.9 collective-permute-start.17
  648.6 8.3 %collective-permute-done.12.refs_1_ = f32[56,16,128]{2,1,0:T(8,128)S(1)} collective-permute-done((f32[56,16,128]{2,1,0:T(8,128)}, f32[56,16,128]{2,1,0:T(8,128)S(1)}, u32[]{:S(2)}, u32[]{:S(2)}) %collective-permute-start.12) | collective-permute-done | bytes 458784 | tf_op jit(solution)/shard_map/ppermute | solution.py:318
  657.9 6.3 turned.1.base_ref
  664.2 4.2 joined.3.base_ref
  669.3 5.4 joined.4.base_ref
  676.3 3.5 joined.5
  (83 shorter events, 17.0 us)
Async XLA Ops:
  8.9 36.0 %all-to-all-start.1 = ((f32[8,16,40,128]{3,2,1,0:T(8,128)}), f32[8,16,40,128]{3,2,1,0:T(8,128)S(1)}, u32[]{:S(2)}, u32[]{:S(2)}) async-start(f32[8,16,40,128]{3,2,1,0:T(8,128)} %bitcast.40), calls=%async_computation.1 | async-start | bytes 5242880 | tf_op jit(solution)/shard_map/all_to_all | solution.py:356
  45.0 7.2 %copy-start = (f32[8,16,40,128]{3,2,1,0:T(8,128)}, f32[8,16,40,128]{3,2,1,0:T(8,128)S(1)}, u32[]{:S(2)}) copy-start(f32[8,16,40,128]{3,2,1,0:T(8,128)S(1)} %all-to-all-done.1.own_ref) | copy-start | bytes 7864324
  45.0 132.9 %all-to-all-start = ((f32[8,16,96,128]{3,2,1,0:T(8,128)}), f32[8,16,96,128]{3,2,1,0:T(8,128)}, u32[]{:S(2)}, u32[]{:S(2)}) async-start(f32[8,16,96,128]{3,2,1,0:T(8,128)} %bitcast.38), calls=%async_computation | async-start | bytes 12582912 | tf_op jit(solution)/shard_map/all_to_all | solution.py:356
  52.2 125.7 %collective-permute-start = (f32[8,16,40,128]{3,2,1,0:T(8,128)S(1)}, f32[8,16,40,128]{3,2,1,0:T(8,128)}, u32[]{:S(2)}, u32[]{:S(2)}) collective-permute-start(f32[8,16,40,128]{3,2,1,0:T(8,128)S(1)} %all-to-all-done.1.own_ref), channel_id=1, source_target_pairs={{0,8},{8,0},{1,9},{9,1},{2,10},{10,2},{3,11},{11,3},{4,12},{12,4},... | collective-permute-start | bytes 7864328 | tf_op jit(solution)/shard_map/ppermute | solution.py:364
  177.8 175.6 %all-to-all-start.2 = ((f32[8,16,120,128]{3,2,1,0:T(8,128)}), f32[8,16,120,128]{3,2,1,0:T(8,128)}, u32[]{:S(2)}, u32[]{:S(2)}) async-start(f32[8,16,120,128]{3,2,1,0:T(8,128)} %bitcast.37), calls=%async_computation.2 | async-start | bytes 15728640 | tf_op jit(solution)/shard_map/all_to_all | solution.py:356
  196.6 171.5 %collective-permute-start.1 = (f32[8,16,56,128]{3,2,1,0:T(8,128)}, f32[8,16,56,128]{3,2,1,0:T(8,128)}, u32[]{:S(2)}, u32[]{:S(2)}) collective-permute-start(f32[8,16,56,128]{3,2,1,0:T(8,128)} %slice.8.own_ref), channel_id=1, source_target_pairs={{0,8},{8,0},{1,9},{9,1},{2,10},{10,2},{3,11},{11,3},{4,12},{12,4},... | collective-permute-start | bytes 11010056 | tf_op jit(solution)/shard_map/ppermute | solution.py:364
  368.1 6.6 copy-start.14
  368.1 6.7 copy-start.17
  368.1 56.7 %all-to-all-start.3 = ((f32[8,16,40,128]{3,2,1,0:T(8,128)}), f32[8,16,40,128]{3,2,1,0:T(8,128)S(1)}, u32[]{:S(2)}, u32[]{:S(2)}) async-start(f32[8,16,40,128]{3,2,1,0:T(8,128)} %product.3), calls=%async_computation.3 | async-start | bytes 5242880 | tf_op jit(solution)/shard_map/all_to_all | solution.py:367
  374.7 4.3 copy-start.16
  374.7 4.9 copy-start.15
  377.9 110.7 %collective-permute-start.2 = (f32[8,16,32,128]{3,2,1,0:T(8,128)}, f32[8,16,32,128]{3,2,1,0:T(8,128)}, u32[]{:S(2)}, u32[]{:S(2)}) collective-permute-start(f32[8,16,32,128]{3,2,1,0:T(8,128)} %slice.9.own_ref), channel_id=1, source_target_pairs={{0,8},{8,0},{1,9},{9,1},{2,10},{10,2},{3,11},{11,3},{4,12},{12,4},... | collective-permute-start | bytes 6291464 | tf_op jit(solution)/shard_map/ppermute | solution.py:364
  424.8 1.6 copy-start.1
  445.6 9.4 %collective-permute-start.4 = (f32[40,16,128]{2,1,0:T(8,128)}, f32[40,16,128]{2,1,0:T(8,128)S(1)}, u32[]{:S(2)}, u32[]{:S(2)}) collective-permute-start(f32[40,16,128]{2,1,0:T(8,128)} %get-tuple-element.32.refs_3_), channel_id=1, source_target_pairs={{0,1},{1,0},{2,3},{3,2},{4,5},{5,4},{6,7},{7,6},{8,9},{9,8},{10,11... | collective-permute-start | bytes 983048 | tf_op jit(solution)/shard_map/ppermute | solution.py:318
  447.0 10.8 %collective-permute-start.6 = (f32[40,16,128]{2,1,0:T(8,128)}, f32[40,16,128]{2,1,0:T(8,128)S(1)}, u32[]{:S(2)}, u32[]{:S(2)}) collective-permute-start(f32[40,16,128]{2,1,0:T(8,128)} %get-tuple-element.33.refs_6_), channel_id=1, source_target_pairs={{0,2},{1,3},{2,0},{3,1},{4,6},{5,7},{6,4},{7,5},{8,10},{9,11},{10,... | collective-permute-start | bytes 983048 | tf_op jit(solution)/shard_map/ppermute | solution.py:318
  447.5 25.4 %collective-permute-start.8 = (f32[40,16,128]{2,1,0:T(8,128)}, f32[40,16,128]{2,1,0:T(8,128)S(1)}, u32[]{:S(2)}, u32[]{:S(2)}) collective-permute-start(f32[40,16,128]{2,1,0:T(8,128)} %get-tuple-element.34.refs_9_), channel_id=1, source_target_pairs={{0,3},{1,2},{2,1},{3,0},{4,7},{5,6},{6,5},{7,4},{8,11},{9,10},{10,... | collective-permute-start | bytes 983048 | tf_op jit(solution)/shard_map/ppermute | solution.py:318
  449.1 44.6 %collective-permute-start.3 = (f32[40,16,128]{2,1,0:T(8,128)}, f32[40,16,128]{2,1,0:T(8,128)S(1)}, u32[]{:S(2)}, u32[]{:S(2)}) collective-permute-start(f32[40,16,128]{2,1,0:T(8,128)} %get-tuple-element.30.refs_0_), channel_id=1, source_target_pairs={{0,0},{1,4},{2,8},{3,12},{4,1},{5,5},{6,9},{7,13},{8,2},{9,6},{10,... | collective-permute-start | bytes 983048 | tf_op jit(solution)/shard_map/ppermute | solution.py:318
  455.0 41.2 %collective-permute-start.5 = (f32[40,16,128]{2,1,0:T(8,128)S(1)}, f32[40,16,128]{2,1,0:T(8,128)}, u32[]{:S(2)}, u32[]{:S(2)}) collective-permute-start(f32[40,16,128]{2,1,0:T(8,128)S(1)} %collective-permute-done.4), channel_id=1, source_target_pairs={{0,4},{1,0},{2,12},{3,8},{4,5},{5,1},{6,13},{7,9},{8,6},{9,2},{10,... | collective-permute-start | bytes 983048 | tf_op jit(solution)/shard_map/ppermute | solution.py:318
  457.8 38.4 %collective-permute-start.7 = (f32[40,16,128]{2,1,0:T(8,128)S(1)}, f32[40,16,128]{2,1,0:T(8,128)}, u32[]{:S(2)}, u32[]{:S(2)}) collective-permute-start(f32[40,16,128]{2,1,0:T(8,128)S(1)} %collective-permute-done.6), channel_id=1, source_target_pairs={{0,8},{1,12},{2,0},{3,4},{4,9},{5,13},{6,1},{7,5},{8,10},{9,14},{1... | collective-permute-start | bytes 983048 | tf_op jit(solution)/shard_map/ppermute | solution.py:318
  473.0 23.2 %collective-permute-start.9 = (f32[40,16,128]{2,1,0:T(8,128)S(1)}, f32[40,16,128]{2,1,0:T(8,128)}, u32[]{:S(2)}, u32[]{:S(2)}) collective-permute-start(f32[40,16,128]{2,1,0:T(8,128)S(1)} %collective-permute-done.8), channel_id=1, source_target_pairs={{0,12},{1,8},{2,4},{3,0},{4,13},{5,9},{6,5},{7,1},{8,14},{9,10},{1... | collective-permute-start | bytes 983048 | tf_op jit(solution)/shard_map/ppermute | solution.py:318
  493.7 2.5 copy-start.9
  496.2 44.4 %all-to-all-start.4 = ((f32[8,16,56,128]{3,2,1,0:T(8,128)}), f32[8,16,56,128]{3,2,1,0:T(8,128)}, u32[]{:S(2)}, u32[]{:S(2)}) async-start(f32[8,16,56,128]{3,2,1,0:T(8,128)} %product.4), calls=%async_computation.4 | async-start | bytes 7340032 | tf_op jit(solution)/shard_map/all_to_all | solution.py:367
  540.6 34.3 %all-to-all-start.5 = ((f32[8,16,32,128]{3,2,1,0:T(8,128)}), f32[8,16,32,128]{3,2,1,0:T(8,128)S(1)}, u32[]{:S(2)}, u32[]{:S(2)}) async-start(f32[8,16,32,128]{3,2,1,0:T(8,128)} %product.5), calls=%async_computation.5 | async-start | bytes 4194304 | tf_op jit(solution)/shard_map/all_to_all | solution.py:367
  572.8 32.7 %collective-permute-start.11 = (f32[56,16,128]{2,1,0:T(8,128)}, f32[56,16,128]{2,1,0:T(8,128)}, u32[]{:S(2)}, u32[]{:S(2)}) collective-permute-start(f32[56,16,128]{2,1,0:T(8,128)} %get-tuple-element.39.refs_4_), channel_id=1, source_target_pairs={{0,1},{1,0},{2,3},{3,2},{4,5},{5,4},{6,7},{7,6},{8,9},{9,8},{10,11... | collective-permute-start | bytes 1376264 | tf_op jit(solution)/shard_map/ppermute | solution.py:318
  574.3 33.3 %collective-permute-start.13 = (f32[56,16,128]{2,1,0:T(8,128)}, f32[56,16,128]{2,1,0:T(8,128)}, u32[]{:S(2)}, u32[]{:S(2)}) collective-permute-start(f32[56,16,128]{2,1,0:T(8,128)} %get-tuple-element.41.refs_7_), channel_id=1, source_target_pairs={{0,2},{1,3},{2,0},{3,1},{4,6},{5,7},{6,4},{7,5},{8,10},{9,11},{10,... | collective-permute-start | bytes 1376264 | tf_op jit(solution)/shard_map/ppermute | solution.py:318
  574.9 1.3 copy-start.2
  576.2 16.6 %copy-start.4 = (f32[56,16,128]{2,1,0:T(8,128)S(1)}, f32[56,16,128]{2,1,0:T(8,128)}, u32[]{:S(2)}) copy-start(f32[56,16,128]{2,1,0:T(8,128)} %get-tuple-element.43.refs_10_) | copy-start | bytes 1376260
  576.2 25.6 %copy-start.3 = (f32[56,16,128]{2,1,0:T(8,128)S(1)}, f32[56,16,128]{2,1,0:T(8,128)}, u32[]{:S(2)}) copy-start(f32[56,16,128]{2,1,0:T(8,128)} %get-tuple-element.36.refs_1_) | copy-start | bytes 1376260
  576.2 80.8 %copy-start.18 = (f32[64]{0:T(128)S(1)}, f32[64]{0:T(128)}, u32[]{:S(2)}) copy-start(f32[64]{0:T(128)} %param.21) | copy-start | bytes 772
  592.2 9.6 %collective-permute-start.18 = (f32[32,16,128]{2,1,0:T(8,128)}, f32[32,16,128]{2,1,0:T(8,128)}, u32[]{:S(2)}, u32[]{:S(2)}) collective-permute-start(f32[32,16,128]{2,1,0:T(8,128)} %get-tuple-element.40.refs_5_), channel_id=1, source_target_pairs={{0,1},{1,0},{2,3},{3,2},{4,5},{5,4},{6,7},{7,6},{8,9},{9,8},{10,11... | collective-permute-start | bytes 786440 | tf_op jit(solution)/shard_map/ppermute | solution.py:318
  592.8 36.6 %collective-permute-start.15 = (f32[56,16,128]{2,1,0:T(8,128)S(1)}, f32[56,16,128]{2,1,0:T(8,128)S(1)}, u32[]{:S(2)}, u32[]{:S(2)}) collective-permute-start(f32[56,16,128]{2,1,0:T(8,128)S(1)} %copy-done.4), channel_id=1, source_target_pairs={{0,3},{1,2},{2,1},{3,0},{4,7},{5,6},{6,5},{7,4},{8,11},{9,10},{10,... | collective-permute-start | bytes 1376264 | tf_op jit(solution)/shard_map/ppermute | solution.py:318
  595.2 21.3 %collective-permute-start.20 = (f32[32,16,128]{2,1,0:T(8,128)}, f32[32,16,128]{2,1,0:T(8,128)}, u32[]{:S(2)}, u32[]{:S(2)}) collective-permute-start(f32[32,16,128]{2,1,0:T(8,128)} %get-tuple-element.42.refs_8_), channel_id=1, source_target_pairs={{0,2},{1,3},{2,0},{3,1},{4,6},{5,7},{6,4},{7,5},{8,10},{9,11},{10,... | collective-permute-start | bytes 786440 | tf_op jit(solution)/shard_map/ppermute | solution.py:318
  601.8 46.3 %collective-permute-start.10 = (f32[56,16,128]{2,1,0:T(8,128)S(1)}, f32[56,16,128]{2,1,0:T(8,128)S(1)}, u32[]{:S(2)}, u32[]{:S(2)}) collective-permute-start(f32[56,16,128]{2,1,0:T(8,128)S(1)} %copy-done.3), channel_id=1, source_target_pairs={{0,0},{1,4},{2,8},{3,12},{4,1},{5,5},{6,9},{7,13},{8,2},{9,6},{10,... | collective-permute-start | bytes 1376264 | tf_op jit(solution)/shard_map/ppermute | solution.py:318
  605.6 51.4 %collective-permute-start.12 = (f32[56,16,128]{2,1,0:T(8,128)}, f32[56,16,128]{2,1,0:T(8,128)S(1)}, u32[]{:S(2)}, u32[]{:S(2)}) collective-permute-start(f32[56,16,128]{2,1,0:T(8,128)} %collective-permute-done.11), channel_id=1, source_target_pairs={{0,4},{1,0},{2,12},{3,8},{4,5},{5,1},{6,13},{7,9},{8,6},{9,2},{10,... | collective-permute-start | bytes 1376264 | tf_op jit(solution)/shard_map/ppermute | solution.py:318
  607.6 49.3 %collective-permute-start.14 = (f32[56,16,128]{2,1,0:T(8,128)}, f32[56,16,128]{2,1,0:T(8,128)S(1)}, u32[]{:S(2)}, u32[]{:S(2)}) collective-permute-start(f32[56,16,128]{2,1,0:T(8,128)} %collective-permute-done.13), channel_id=1, source_target_pairs={{0,8},{1,12},{2,0},{3,4},{4,9},{5,13},{6,1},{7,5},{8,10},{9,14},{1... | collective-permute-start | bytes 1376264 | tf_op jit(solution)/shard_map/ppermute | solution.py:318
  616.5 29.7 %collective-permute-start.22 = (f32[32,16,128]{2,1,0:T(8,128)}, f32[32,16,128]{2,1,0:T(8,128)}, u32[]{:S(2)}, u32[]{:S(2)}) collective-permute-start(f32[32,16,128]{2,1,0:T(8,128)} %get-tuple-element.44.refs_11_), channel_id=1, source_target_pairs={{0,3},{1,2},{2,1},{3,0},{4,7},{5,6},{6,5},{7,4},{8,11},{9,10},{10,... | collective-permute-start | bytes 786440 | tf_op jit(solution)/shard_map/ppermute | solution.py:318
  629.4 39.1 %collective-permute-start.16 = (f32[56,16,128]{2,1,0:T(8,128)S(1)}, f32[56,16,128]{2,1,0:T(8,128)S(1)}, u32[]{:S(2)}, u32[]{:S(2)}) collective-permute-start(f32[56,16,128]{2,1,0:T(8,128)S(1)} %collective-permute-done.15), channel_id=1, source_target_pairs={{0,12},{1,8},{2,4},{3,0},{4,13},{5,9},{6,5},{7,1},{8,14},{9,10},{1... | collective-permute-start | bytes 1376264 | tf_op jit(solution)/shard_map/ppermute | solution.py:318
  646.2 28.5 %collective-permute-start.17 = (f32[32,16,128]{2,1,0:T(8,128)}, f32[32,16,128]{2,1,0:T(8,128)S(1)}, u32[]{:S(2)}, u32[]{:S(2)}) collective-permute-start(f32[32,16,128]{2,1,0:T(8,128)} %get-tuple-element.38.refs_2_), channel_id=1, source_target_pairs={{0,0},{1,4},{2,8},{3,12},{4,1},{5,5},{6,9},{7,13},{8,2},{9,6},{10,... | collective-permute-start | bytes 786440 | tf_op jit(solution)/shard_map/ppermute | solution.py:318
  648.1 16.1 %copy-start.5 = (f32[56,16,128]{2,1,0:T(8,128)}, f32[56,16,128]{2,1,0:T(8,128)S(1)}, u32[]{:S(2)}) copy-start(f32[56,16,128]{2,1,0:T(8,128)S(1)} %collective-permute-done.10.refs_0_) | copy-start | bytes 1376260
  648.1 26.6 %collective-permute-start.19 = (f32[32,16,128]{2,1,0:T(8,128)}, f32[32,16,128]{2,1,0:T(8,128)S(1)}, u32[]{:S(2)}, u32[]{:S(2)}) collective-permute-start(f32[32,16,128]{2,1,0:T(8,128)} %collective-permute-done.18), channel_id=1, source_target_pairs={{0,4},{1,0},{2,12},{3,8},{4,5},{5,1},{6,13},{7,9},{8,6},{9,2},{10,... | collective-permute-start | bytes 786440 | tf_op jit(solution)/shard_map/ppermute | solution.py:318
  656.9 7.3 %copy-start.6 = (f32[56,16,128]{2,1,0:T(8,128)}, f32[56,16,128]{2,1,0:T(8,128)S(1)}, u32[]{:S(2)}) copy-start(f32[56,16,128]{2,1,0:T(8,128)S(1)} %collective-permute-done.12.refs_1_) | copy-start | bytes 1376260
  656.9 17.7 %collective-permute-start.21 = (f32[32,16,128]{2,1,0:T(8,128)}, f32[32,16,128]{2,1,0:T(8,128)S(1)}, u32[]{:S(2)}, u32[]{:S(2)}) collective-permute-start(f32[32,16,128]{2,1,0:T(8,128)} %collective-permute-done.20), channel_id=1, source_target_pairs={{0,8},{1,12},{2,0},{3,4},{4,9},{5,13},{6,1},{7,5},{8,10},{9,14},{1... | collective-permute-start | bytes 786440 | tf_op jit(solution)/shard_map/ppermute | solution.py:318
  657.0 7.3 %copy-start.7 = (f32[56,16,128]{2,1,0:T(8,128)}, f32[56,16,128]{2,1,0:T(8,128)S(1)}, u32[]{:S(2)}) copy-start(f32[56,16,128]{2,1,0:T(8,128)S(1)} %collective-permute-done.14.refs_2_) | copy-start | bytes 1376260
  657.0 17.7 %collective-permute-start.23 = (f32[32,16,128]{2,1,0:T(8,128)}, f32[32,16,128]{2,1,0:T(8,128)S(1)}, u32[]{:S(2)}, u32[]{:S(2)}) collective-permute-start(f32[32,16,128]{2,1,0:T(8,128)} %collective-permute-done.22), channel_id=1, source_target_pairs={{0,12},{1,8},{2,4},{3,0},{4,13},{5,9},{6,5},{7,1},{8,14},{9,10},{1... | collective-permute-start | bytes 786440 | tf_op jit(solution)/shard_map/ppermute | solution.py:318
  668.5 0.8 copy-start.8
  674.7 0.7 copy-start.10
  674.7 0.8 copy-start.11
  674.7 0.9 copy-start.12
  (1 other events, 0.7 us)

commit v5 on v4

--- a/solution.py
+++ b/solution.py
@@ -10,9 +10,9 @@
 HIGH = lax.Precision.HIGHEST
 LANES = 128
 GROUP = 8
-CHUNKS = (40, 56, 32)
-LOWER = 40
-PARTS = 4
+CHUNKS = (40, 40, 48)
+LOWER = 48
+PARTS = (4, 2)
 VMEM = 56 * 1024 * 1024
 SCALE = 8
 
@@ -143,7 +143,8 @@
     )(pair, weights3)
 
 
-def product_kernel(half_ref, low_ref, high_ref, own_ref, other_ref, out_ref):
+def product_kernel(half_ref, low_ref, high_ref, own_ref, other_ref, *refs):
+    out_ref = refs[-1]
     cols = own_ref.shape[0] // 2
     half = half_ref[0]
 
@@ -173,25 +174,29 @@
             ]
 
 
-def product(half, low, high, own, other, wide):
+def product(half, low, high, own, other, wide, blocks=1, into=None):
     sources, owned, rows, width = own.shape
     k_all = width * sources // 2
     spec = lambda height: pl.BlockSpec((sources, 1, height, width), lambda n, half: (0, n, 0, 0))
+    place = 0 if into is None else blocks - 1
+    kept = [] if into is None else [into]
     return pl.pallas_call(
         product_kernel,
         grid_spec=pltpu.PrefetchScalarGridSpec(
             num_scalar_prefetch=1,
             grid=(owned,),
-            in_specs=[spec(LOWER), spec(wide - LOWER), spec(rows), spec(rows)],
-            out_specs=pl.BlockSpec((sources, 1, rows, wide), lambda n, half: (0, n, 0, 0)),
+            in_specs=[spec(LOWER), spec(wide - LOWER), spec(rows), spec(rows)]
+            + [pl.BlockSpec(memory_space=pl.ANY)] * len(kept),
+            out_specs=pl.BlockSpec((sources, 1, rows, wide), lambda n, half: (0, n, place, 0)),
         ),
-        out_shape=jax.ShapeDtypeStruct((sources, owned, rows, wide), jnp.float32),
+        out_shape=jax.ShapeDtypeStruct((sources, owned, blocks * rows, wide), jnp.float32),
+        input_output_aliases={5: 0} if kept else {},
         compiler_params=pltpu.CompilerParams(vmem_limit_bytes=VMEM),
         cost_estimate=estimate(
             6 * owned * 4 * rows * 2 * wide * k_all, 4 * owned * k_all * (2 * wide + 4 * rows)
         ),
         name="product",
-    )(half, low, high, own, other)
+    )(half, low, high, own, other, *kept)
 
 
 def head_kernel(
@@ -223,12 +228,12 @@
                 ]
 
 
-def head(pair, product_values, first, gate3, output3, up3, down3, bins3):
+def head(pair, product_values, first, count, gate3, output3, up3, down3, bins3):
     tile_rows, tile_cols, width = pair.shape
     chunk_cols = product_values.shape[1]
     steps = chunk_cols // GROUP
     lead = first // GROUP
-    bins = bins3.shape[0] // PARTS
+    bins = bins3.shape[0] // count
     whole = lambda array: pl.BlockSpec(array.shape, lambda g: (0, 0))
     macs = gate3.size + output3.size + up3.size + down3.size + bins3.size
     return pl.pallas_call(
@@ -243,86 +248,83 @@
             whole(down3),
             whole(bins3),
         ],
-        out_specs=[pl.BlockSpec((GROUP, bins, tile_rows), lambda g: (g, 0, 0))] * PARTS,
-        out_shape=[jax.ShapeDtypeStruct((chunk_cols, bins, tile_rows), jnp.float32)] * PARTS,
+        out_specs=[pl.BlockSpec((GROUP, bins, tile_rows), lambda g: (g, 0, 0))] * count,
+        out_shape=[jax.ShapeDtypeStruct((chunk_cols, bins, tile_rows), jnp.float32)] * count,
         compiler_params=pltpu.CompilerParams(vmem_limit_bytes=VMEM),
         cost_estimate=estimate(
-            2 * chunk_cols * tile_rows * macs, 4 * chunk_cols * tile_rows * (2 * width + PARTS * bins)
+            2 * chunk_cols * tile_rows * macs, 4 * chunk_cols * tile_rows * (2 * width + count * bins)
         ),
         name="head",
     )(pair, product_values, gate3, output3, up3, down3, bins3)
 
 
-def turned_kernel(bias_ref, *refs):
-    out_ref, sources = refs[-1], refs[:-1]
-    count = len(sources) // PARTS
-    tile_rows, _, bins, tile_cols = out_ref.shape
-    flat = out_ref.reshape(tile_rows * PARTS * bins, tile_cols)
-    for part in range(PARTS):
+def symmetric_kernel(bias_ref, *refs):
+    out_ref, blocks = refs[-1], refs[:-1]
+    tile_rows, quarters, bins, tile_cols = out_ref.shape
+    count = len(blocks) // (2 * quarters)
+    flat = out_ref.reshape(tile_rows * quarters * bins, tile_cols)
+    for quarter in range(quarters):
         for n in range(bins):
-            values = [
-                ref.reshape(ref.shape[0] * bins, tile_rows)[pl.ds(n, ref.shape[0], stride=bins), :]
-                for ref in sources[part * count : (part + 1) * count]
-            ]
-            result = jnp.concatenate(values, axis=0).T + bias_ref[part, n : n + 1, :]
-            flat[pl.ds(part * bins + n, tile_rows, stride=PARTS * bins), :] = result
-
-
-def turned(bias, own):
-    arrays = [block[part] for part in range(PARTS) for block in own]
-    _, bins, tile_rows = arrays[0].shape
-    tile_cols = sum(block[0].shape[0] for block in own)
-    block = lambda rows: pl.BlockSpec((rows, GROUP, tile_rows), lambda g: (0, g, 0))
+
+            def joined(start):
+                chosen = blocks[(start + quarter) * count : (start + quarter + 1) * count]
+                values = [
+                    ref.reshape(ref.shape[0] * bins, ref.shape[2])[
+                        pl.ds(n, ref.shape[0], stride=bins), :
+                    ]
+                    for ref in chosen
+                ]
+                return jnp.concatenate(values, axis=0)
+
+            result = joined(0).T + joined(quarters) + bias_ref[quarter, n : n + 1, :]
+            flat[pl.ds(quarter * bins + n, tile_rows, stride=quarters * bins), :] = result
+
+
+def symmetric(bias, own, mirror):
+    quarters, bins, tile_cols = bias.shape
+    tile_rows = own[0][0].shape[2]
+    arrays, specs = [], []
+    for quarter in range(quarters):
+        for block in own:
+            part, rest = divmod(quarter * bins, block[0].shape[1])
+            arrays.append((part, rest // GROUP, block[0].shape))
+    chosen = [own[n % len(own)][part] for n, (part, _, _) in enumerate(arrays)]
+    chosen += [mirror[n % len(own)][part] for n, (part, _, _) in enumerate(arrays)]
+    specs = [
+        pl.BlockSpec((shape[0], GROUP, shape[2]), lambda g, lead=lead: (0, lead + g, 0))
+        for _, lead, shape in arrays
+    ] * 2
     return pl.pallas_call(
-        turned_kernel,
+        symmetric_kernel,
         grid=(bins // GROUP,),
-        in_specs=[pl.BlockSpec((PARTS, GROUP, tile_cols), lambda g: (0, g, 0))]
-        + [block(array.shape[0]) for array in arrays],
-        out_specs=pl.BlockSpec((tile_rows, PARTS, GROUP, tile_cols), lambda g: (0, 0, g, 0)),
-        out_shape=jax.ShapeDtypeStruct((tile_rows, PARTS, bins, tile_cols), jnp.float32),
+        in_specs=[pl.BlockSpec((quarters, GROUP, tile_cols), lambda g: (0, g, 0))] + specs,
+        out_specs=pl.BlockSpec((tile_rows, quarters, GROUP, tile_cols), lambda g: (0, 0, g, 0)),
+        out_shape=jax.ShapeDtypeStruct((tile_rows, quarters, bins, tile_cols), jnp.float32),
         compiler_params=pltpu.CompilerParams(vmem_limit_bytes=VMEM),
-        cost_estimate=estimate(0, 8 * tile_rows * PARTS * bins * tile_cols),
-        name="turned",
-    )(bias, *arrays)
-
-
-def joined_kernel(base_ref, *refs):
-    out_ref = refs[-1]
-    for part, ref in enumerate(refs[:-1]):
-        out_ref[:, part] = base_ref[:, part] + ref[...]
-
-
-def joined(base, mirror, first):
-    rows, bins, tile_cols = mirror[0].shape
-    lead = first // GROUP
-    whole = pl.BlockSpec((GROUP, PARTS, bins, tile_cols), lambda g: (lead + g, 0, 0, 0))
-    block = pl.BlockSpec((GROUP, bins, tile_cols), lambda g: (g, 0, 0))
-    return pl.pallas_call(
-        joined_kernel,
-        grid=(rows // GROUP,),
-        in_specs=[whole] + [block] * PARTS,
-        out_specs=whole,
-        out_shape=jax.ShapeDtypeStruct(base.shape, jnp.float32),
-        input_output_aliases={0: 0},
-        compiler_params=pltpu.CompilerParams(vmem_limit_bytes=VMEM),
-        cost_estimate=estimate(0, 12 * PARTS * rows * bins * tile_cols),
-        name="joined",
-    )(base, *mirror)
-
-
-def mirrored_parts(block, count):
+        cost_estimate=estimate(0, 12 * tile_rows * quarters * bins * tile_cols),
+        name="symmetric",
+    )(bias, *chosen)
+
+
+def move(values, count, target):
     every = [(r, c) for r in range(count) for c in range(count)]
-
-    def move(values, target):
-        pairs = [(r * count + c, target(r, c)) for r, c in every]
-        return lax.ppermute(values, ("half", "lo", "col"), pairs)
-
-    result = []
-    for part, values in enumerate(block):
-        if part:
-            values = move(values, lambda r, c: r * count + (c ^ part))
-        result.append(move(values, lambda r, c: (c ^ part) * count + r))
-    return result
+    pairs = [(r * count + c, target(r, c)) for r, c in every]
+    return lax.ppermute(values, ("half", "lo", "col"), pairs)
+
+
+def turn_of(block, part):
+    return part if len(block) == 4 else 2 * part
+
+
+def aside(block, count):
+    return [block[0]] + [
+        move(block[n], count, lambda r, c: r * count + (c ^ turn_of(block, n)))
+        for n in range(1, len(block))
+    ]
+
+
+def across(block, count, part):
+    return move(block[part], count, lambda r, c: (c ^ turn_of(block, part)) * count + r)
 
 
 def half_shards(
@@ -363,38 +365,39 @@
     def exchange(values):
         return lax.ppermute(values, "half", [(0, 1), (1, 0)])
 
-    def finish(values, chunk):
+    def blocks(chunk, count=1, into=None):
+        return product(half, low, high, rights[chunk], others[chunk], tile_rows, count, into)
+
+    def delivered(values):
         values = lax.all_to_all(values, ("lo", "col"), split_axis=0, concat_axis=0, tiled=True)
-        values = values.reshape(width, CHUNKS[chunk], tile_rows)
-        return head(tile, values, firsts[chunk], gate3, output3, up3, down3, bins3)
+        return values.reshape(width, values.shape[2], tile_rows)
+
+    def run_head(values, first, count):
+        return head(tile, values, first, count, gate3, output3, up3, down3, bins3)
+
+    def mirrored_parts(block):
+        shifted = aside(block, row_count)
+        return [across(shifted, row_count, part) for part in range(len(block))]
 
     right = spread(hands(tile, in3, (0, 0), (firsts[0], CHUNKS[0])))
     rights, others = [right], [exchange(right)]
     low = spread(hands(tile, in3, (0, LOWER), (firsts[1], CHUNKS[1])))
     rights.append(low[:, :, LOWER:])
+    sent = hands(tile, in3, (LOWER, upper), (firsts[2], CHUNKS[2]))
+    sent, others[0], rights[1] = tie((sent, others[0], rights[1]))
     others.append(exchange(rights[1]))
-    sent = hands(tile, in3, (LOWER, upper), (firsts[2], CHUNKS[2]))
-    sent, others[0] = tie((sent, others[0]))
     high = spread(sent)
     rights.append(high[:, :, upper:])
+    values, rights[2] = tie((blocks(1, 2, blocks(0, 2)), rights[2]))
     others.append(exchange(rights[2]))
-
-    def blocks(chunk):
-        return product(half, low, high, rights[chunk], others[chunk], tile_rows)
-
-    values, others[1] = tie((blocks(0), others[1]))
-    own = [finish(values, 0)]
-    mirror = [mirrored_parts(own[0], row_count)]
-    values, others[2], mirror[0] = tie((blocks(1), others[2], mirror[0]))
-    own.append(finish(values, 1))
-    own.append(finish(blocks(2), 2))
-    mirror += [mirrored_parts(block, row_count) for block in own[1:]]
-    bins = distogram_bias.shape[0] // PARTS
-    bias = jnp.broadcast_to(distogram_bias.reshape(PARTS, bins, 1), (PARTS, bins, tile_cols))
-    logits = turned(bias, own)
-    for first, block in zip(firsts, mirror):
-        logits = joined(logits, block, first)
-    logits = logits.reshape(tile_rows, PARTS * bins, tile_cols)
+    own = [run_head(delivered(values), 0, PARTS[0])]
+    values, own[0] = tie((delivered(blocks(2)), own[0]))
+    own.append(run_head(values, firsts[2], PARTS[1]))
+    mirror = [mirrored_parts(block) for block in own]
+    quarters = 4
+    bins = distogram_bias.shape[0] // quarters
+    bias = jnp.broadcast_to(distogram_bias.reshape(quarters, bins, 1), (quarters, bins, tile_cols))
+    logits = symmetric(bias, own, mirror).reshape(tile_rows, quarters * bins, tile_cols)
     return jnp.swapaxes(logits, 1, 2)[None]
 
 

time: 689 us -> 765 us (1.11)
  waiting for transfers between devices: 387 us -> 524 us
  starting transfers between devices: 107 us -> 69.8 us
  Pallas kernels: 161 us -> 147 us
    ppermute x21 -> x10, waiting for transfers between devices: 42.2 us -> 131 us  [move(): return lax.ppermute(values, ('half', 'lo', 'col'), pairs)]
    all_to_all x3, waiting for transfers between devices: 175 us -> 260 us  [spread(): lax.all_to_all(values, ('lo', 'col'), split_axis=0, concat_axis=0, tiled=...]
    all_to_all x3 -> x2, waiting for transfers between devices: 63.3 us -> 0.01 us  [delivered(): lax.all_to_all(values, ('lo', 'col'), split_axis=0, concat_axis=0, tiled=...]
    ppermute x21 -> x10, starting transfers between devices: 59.9 us -> 26.2 us  [move(): return lax.ppermute(values, ('half', 'lo', 'col'), pairs)]
    ppermute x3, waiting for transfers between devices: 107 us -> 133 us  [exchange(): return lax.ppermute(values, 'half', [(0, 1), (1, 0)])]
    pallas_call x4 -> x1, Pallas kernels: 19.5 us -> 6.97 us  [symmetric(): pl.pallas_call(symmetric_kernel, grid=(bins // GROUP,), in_specs=[pl.Bloc...]
    all_to_all x3 -> x2, starting transfers between devices: 17.1 us -> 14.7 us  [delivered(): lax.all_to_all(values, ('lo', 'col'), split_axis=0, concat_axis=0, tiled=...]
    pallas_call x3 -> x2, Pallas kernels: 61.4 us -> 59.1 us  [head(): pl.pallas_call(head_kernel, grid=(steps,), in_specs=[pl.BlockSpec((tile_r...]
  transfers between devices with their start and end apart: 30 -> 18, of which waited for: 11 -> 8; matrix products, arithmetic and copies ran while one was open for 2% -> 2% of each run, Pallas kernels for 22% -> 13%
where the time goes in v5:
time: 765 us; the launch traced here: 762 us
  waiting for transfers between devices  524 us (68%)
  Pallas kernels  147 us (19%)
  starting transfers between devices  69.8 us (9%)
  local copies, waits for them, and re-layouts  14.5 us (2%)
    all_to_all x3, waiting for transfers between devices, spread(): lax.all_to_all(values, ('lo', 'col'), split_axis=0, concat_axis=0, tiled=...  260 us
    ppermute x3, waiting for transfers between devices, exchange(): return lax.ppermute(values, 'half', [(0, 1), (1, 0)])  133 us
    ppermute x10, waiting for transfers between devices, move(): return lax.ppermute(values, ('half', 'lo', 'col'), pairs)  131 us
    pallas_call x2, Pallas kernels, head(): pl.pallas_call(head_kernel, grid=(steps,), in_specs=[pl.BlockSpec((tile_r...  59.1 us
    pallas_call x3, Pallas kernels, product(): pl.pallas_call(product_kernel, grid_spec=pltpu.PrefetchScalarGridSpec(num...  45 us
    pallas_call x3, Pallas kernels, hands(): pl.pallas_call(hands_kernel, grid=(rows // GROUP,), in_specs=[pl.BlockSpe...  35.5 us
    ppermute x10, starting transfers between devices, move(): return lax.ppermute(values, ('half', 'lo', 'col'), pairs)  26.2 us
    all_to_all x3, starting transfers between devices, spread(): lax.all_to_all(values, ('lo', 'col'), split_axis=0, concat_axis=0, tiled=...  25.8 us
  transfers between devices with their start and end apart: 18, of which 8 were waited for; matrix products, arithmetic and copies ran while one was open for 2% of the time, Pallas kernels for 13%

profile of v5, /device:TPU:12, one launch (start us, length us, event | category | flops | bytes accessed | tf_op | source)
XLA Modules:
  0.0 761.9 jit_solution(17584486505624867096)
XLA Ops:
  0.0 1.1 copy.13
  1.1 0.7 reduce-precision_convert_fusion.2
  1.8 0.8 pad_maximum_fusion.1.weights_ref
  2.6 6.4 hands.5
  9.0 5.1 all-to-all-start.1
  14.1 12.2 %hands.3 = f32[128,88,128]{2,1,0:T(8,128)} custom-call(f32[128,128,128]{2,1,0:T(8,128)} %bitcast.31, bf16[512,384]{1,0:T(8,128)(2,1)} %pad_maximum_fusion.1.weights_ref), custom_call_target="tpu_custom_call" | custom-call | flops 276824064 | bytes 1441792 | tf_op jit(solution)/shard_map/hands/pallas_call | solution.py:131
  26.3 18.7 %all-to-all-done.1.own_ref = f32[8,16,40,128]{3,2,1,0:T(8,128)S(1)} async-done(((f32[8,16,40,128]{3,2,1,0:T(8,128)}), f32[8,16,40,128]{3,2,1,0:T(8,128)S(1)}, u32[]{:S(2)}, u32[]{:S(2)}) %all-to-all-start.1) | async-done | bytes 2621472 | tf_op jit(solution)/shard_map/all_to_all | solution.py:358
  45.0 7.2 all-to-all-start
  52.2 2.5 collective-permute-start
  54.7 17.0 %hands.4 = f32[128,128,128]{2,1,0:T(8,128)} custom-call(f32[128,128,128]{2,1,0:T(8,128)} %bitcast.32, bf16[512,384]{1,0:T(8,128)(2,1)} %pad_maximum_fusion.1.weights_ref), custom_call_target="tpu_custom_call" | custom-call | flops 402653184 | bytes 2097152 | tf_op jit(solution)/shard_map/hands/pallas_call | solution.py:131
  71.7 97.5 %all-to-all-done.low_ref = f32[8,16,88,128]{3,2,1,0:T(8,128)} async-done(((f32[8,16,88,128]{3,2,1,0:T(8,128)}), f32[8,16,88,128]{3,2,1,0:T(8,128)}, u32[]{:S(2)}, u32[]{:S(2)}) %all-to-all-start) | async-done | bytes 5767200 | tf_op jit(solution)/shard_map/all_to_all | solution.py:358
  169.1 3.4 slice.8.own_ref
  172.6 13.4 %all-to-all-start.2 = ((f32[8,16,128,128]{3,2,1,0:T(8,128)}), f32[8,16,128,128]{3,2,1,0:T(8,128)}, u32[]{:S(2)}, u32[]{:S(2)}) async-start(f32[8,16,128,128]{3,2,1,0:T(8,128)} %bitcast.35), calls=%async_computation.2 | async-start | bytes 16777216 | tf_op jit(solution)/shard_map/all_to_all | solution.py:358
  186.0 144.0 %all-to-all-done.2.high_ref = f32[8,16,128,128]{3,2,1,0:T(8,128)} async-done(((f32[8,16,128,128]{3,2,1,0:T(8,128)}), f32[8,16,128,128]{3,2,1,0:T(8,128)}, u32[]{:S(2)}, u32[]{:S(2)}) %all-to-all-start.2) | async-done | bytes 8388640 | tf_op jit(solution)/shard_map/all_to_all | solution.py:358
  330.1 2.2 slice.9.own_ref
  332.3 15.4 %product.3.refs_0_ = f32[8,16,80,128]{3,2,1,0:T(8,128)} custom-call(s32[1]{0:T(128)} %bitcast.half_ref, f32[8,16,88,128]{3,2,1,0:T(8,128)} %all-to-all-done.low_ref, f32[8,16,128,128]{3,2,1,0:T(8,128)} %all-to-all-done.2.high_ref, f32[8,16,40,128]{3,2,1,0:T(8,128)} %copy-done.2, f32[8,16,40,128]{3,2,1,0:T(8,128)} %collective-permute-done.other_ref), custom_call_target="tpu_custom_call" | custom-call | flops 251658240 | bytes 1703936 | tf_op jit(solution)/shard_map/product/pallas_call | solution.py:183
  347.7 14.6 %product.4 = f32[8,16,80,128]{3,2,1,0:T(8,128)} custom-call(s32[1]{0:T(128)} %bitcast.half_ref, f32[8,16,88,128]{3,2,1,0:T(8,128)} %all-to-all-done.low_ref, f32[8,16,128,128]{3,2,1,0:T(8,128)} %all-to-all-done.2.high_ref, f32[8,16,40,128]{3,2,1,0:T(8,128)} %slice.8.own_ref, ...), custom_call_target="tpu_custom_call", output_to_operand_aliasing={{}: (5, {})} | custom-call | flops 251658240 | bytes 1703936 | tf_op jit(solution)/shard_map/product/pallas_call | solution.py:183
  362.3 7.0 all-to-all-start.4
  369.3 0.6 collective-permute-start.2
  370.0 133.4 %collective-permute-done.2.other_ref = f32[8,16,48,128]{3,2,1,0:T(8,128)S(1)} collective-permute-done((f32[8,16,48,128]{3,2,1,0:T(8,128)S(1)}, f32[8,16,48,128]{3,2,1,0:T(8,128)S(1)}, u32[]{:S(2)}, u32[]{:S(2)}) %collective-permute-start.2) | collective-permute-done | bytes 3145760 | tf_op jit(solution)/shard_map/ppermute | solution.py:366
  503.4 1.7 copy-done.3
  505.1 15.0 %product.5 = f32[8,16,48,128]{3,2,1,0:T(8,128)} custom-call(s32[1]{0:T(128)} %bitcast.half_ref, f32[8,16,88,128]{3,2,1,0:T(8,128)} %all-to-all-done.low_ref, f32[8,16,128,128]{3,2,1,0:T(8,128)} %all-to-all-done.2.high_ref, f32[8,16,48,128]{3,2,1,0:T(8,128)} %copy-done, f32[8,16,48,128]{3,2,1,0:T(8,128)} %copy-done.3), custom_call_target="tpu_custom_call" | custom-call | flops 301989888 | bytes 1835008 | tf_op jit(solution)/shard_map/product/pallas_call | solution.py:183
  520.1 7.7 %all-to-all-start.3 = ((f32[8,16,48,128]{3,2,1,0:T(8,128)}), f32[8,16,48,128]{3,2,1,0:T(8,128)S(1)}, u32[]{:S(2)}, u32[]{:S(2)}) async-start(f32[8,16,48,128]{3,2,1,0:T(8,128)} %product.5), calls=%async_computation.3 | async-start | bytes 6291456 | tf_op jit(solution)/shard_map/all_to_all | solution.py:372
  528.0 2.0 copy.16
  530.0 1.1 copy.17
  531.1 0.8 reduce-precision_convert_fusion.5
  531.9 0.6 pad_maximum_fusion.5.bins_ref
  532.6 0.7 pad_maximum_fusion.3
  533.3 1.1 reduce-precision_convert_fusion
  534.4 1.0 pad_maximum_fusion.up_ref
  535.4 0.8 pad_maximum_fusion.2.down_ref
  536.2 36.2 %head.2 = (f32[80,16,128]{2,1,0:T(8,128)}, f32[80,16,128]{2,1,0:T(8,128)}, f32[80,16,128]{2,1,0:T(8,128)}, f32[80,16,128]{2,1,0:T(8,128)}) custom-call(f32[128,128,128]{2,1,0:T(8,128)} %bitcast.33, f32[128,80,128]{2,1,0:T(8,128)} %bitcast.7.product_ref, bf16[128,384]{1,0:T(8,128)(2,1)} %get-tuple-element.49.gate_ref, ...), custom_call_target="tpu_custom_call" | custom-call | flops 1824522240 | bytes 1638400 | tf_op jit(solution)/shard_map/head/pallas_call | solution.py:239
  572.4 1.7 copy-done.1
  574.1 22.8 %head.3 = (f32[48,32,128]{2,1,0:T(8,128)}, f32[48,32,128]{2,1,0:T(8,128)}) custom-call(f32[128,128,128]{2,1,0:T(8,128)} %bitcast.34, f32[128,48,128]{2,1,0:T(8,128)} %bitcast.37, bf16[128,384]{1,0:T(8,128)(2,1)} %get-tuple-element.49.gate_ref, bf16[128,384]{1,0:T(8,128)(2,1)} %get-tuple-element.50.output_ref, bf16[1024,384]{1,0:T(8,128)(2,1)} %pad_maximum_fusion.up_ref, ...), custom_call_target="tpu_custom_call" | custom-call | flops 1094713344 | bytes 983040 | tf_op jit(solution)/shard_map/head/pallas_call | solution.py:239
  596.9 0.6 collective-permute-start.9
  597.5 2.4 collective-permute-start.11
  599.9 0.6 collective-permute-start.5
  600.4 0.6 collective-permute-start.7
  601.0 3.7 collective-permute-start.3
  604.7 64.8 %collective-permute-done.11 = f32[80,16,128]{2,1,0:T(8,128)} collective-permute-done((f32[80,16,128]{2,1,0:T(8,128)S(1)}, f32[80,16,128]{2,1,0:T(8,128)}, u32[]{:S(2)}, u32[]{:S(2)}) %collective-permute-start.11) | collective-permute-done | bytes 655392 | tf_op jit(solution)/shard_map/ppermute | solution.py:312
  669.5 3.7 collective-permute-start.4
  673.4 13.2 %collective-permute-start.12 = (f32[80,16,128]{2,1,0:T(8,128)}, f32[80,16,128]{2,1,0:T(8,128)S(1)}, u32[]{:S(2)}, u32[]{:S(2)}) collective-permute-start(f32[80,16,128]{2,1,0:T(8,128)} %collective-permute-done.11), channel_id=1, source_target_pairs={{0,12},{1,8},{2,4},{3,0},{4,13},{5,9},{6,5},{7,1},{8,14},{9,10},{1... | collective-permute-start | bytes 1966088 | tf_op jit(solution)/shard_map/ppermute | solution.py:312
  686.5 1.4 collective-permute-start.6
  688.1 7.1 collective-permute-done.4.refs_9_.refs_11_
  695.2 43.0 %collective-permute-done.12.refs_14_ = f32[80,16,128]{2,1,0:T(8,128)S(1)} collective-permute-done((f32[80,16,128]{2,1,0:T(8,128)}, f32[80,16,128]{2,1,0:T(8,128)S(1)}, u32[]{:S(2)}, u32[]{:S(2)}) %collective-permute-start.12) | collective-permute-done | bytes 655392 | tf_op jit(solution)/shard_map/ppermute | solution.py:312
  738.3 15.8 %collective-permute-done.8.refs_12_ = f32[80,16,128]{2,1,0:T(8,128)} collective-permute-done((f32[80,16,128]{2,1,0:T(8,128)}, f32[80,16,128]{2,1,0:T(8,128)}, u32[]{:S(2)}, u32[]{:S(2)}) %collective-permute-start.8) | collective-permute-done | bytes 655392 | tf_op jit(solution)/shard_map/ppermute | solution.py:312
  754.0 0.8 broadcast_in_dim.7.bias_ref
  754.9 7.0 symmetric.1
  (55 shorter events, 0.6 us)
Async XLA Ops:
  9.0 36.0 %all-to-all-start.1 = ((f32[8,16,40,128]{3,2,1,0:T(8,128)}), f32[8,16,40,128]{3,2,1,0:T(8,128)S(1)}, u32[]{:S(2)}, u32[]{:S(2)}) async-start(f32[8,16,40,128]{3,2,1,0:T(8,128)} %bitcast.38), calls=%async_computation.1 | async-start | bytes 5242880 | tf_op jit(solution)/shard_map/all_to_all | solution.py:358
  45.0 7.2 copy-start.2
  45.0 124.2 %all-to-all-start = ((f32[8,16,88,128]{3,2,1,0:T(8,128)}), f32[8,16,88,128]{3,2,1,0:T(8,128)}, u32[]{:S(2)}, u32[]{:S(2)}) async-start(f32[8,16,88,128]{3,2,1,0:T(8,128)} %bitcast.36), calls=%async_computation | async-start | bytes 11534336 | tf_op jit(solution)/shard_map/all_to_all | solution.py:358
  52.2 120.4 %collective-permute-start = (f32[8,16,40,128]{3,2,1,0:T(8,128)S(1)}, f32[8,16,40,128]{3,2,1,0:T(8,128)}, u32[]{:S(2)}, u32[]{:S(2)}) collective-permute-start(f32[8,16,40,128]{3,2,1,0:T(8,128)S(1)} %all-to-all-done.1.own_ref), channel_id=1, source_target_pairs={{0,8},{8,0},{1,9},{9,1},{2,10},{10,2},{3,11},{11,3},{4,12},{12,4},... | collective-permute-start | bytes 7864328 | tf_op jit(solution)/shard_map/ppermute | solution.py:366
  172.6 157.5 %all-to-all-start.2 = ((f32[8,16,128,128]{3,2,1,0:T(8,128)}), f32[8,16,128,128]{3,2,1,0:T(8,128)}, u32[]{:S(2)}, u32[]{:S(2)}) async-start(f32[8,16,128,128]{3,2,1,0:T(8,128)} %bitcast.35), calls=%async_computation.2 | async-start | bytes 16777216 | tf_op jit(solution)/shard_map/all_to_all | solution.py:358
  186.0 161.7 %collective-permute-start.1 = (f32[8,16,40,128]{3,2,1,0:T(8,128)}, f32[8,16,40,128]{3,2,1,0:T(8,128)}, u32[]{:S(2)}, u32[]{:S(2)}) collective-permute-start(f32[8,16,40,128]{3,2,1,0:T(8,128)} %slice.8.own_ref), channel_id=1, source_target_pairs={{0,8},{8,0},{1,9},{9,1},{2,10},{10,2},{3,11},{11,3},{4,12},{12,4},... | collective-permute-start | bytes 7864328 | tf_op jit(solution)/shard_map/ppermute | solution.py:366
  332.3 37.0 %copy-start = (f32[8,16,48,128]{3,2,1,0:T(8,128)}, f32[8,16,48,128]{3,2,1,0:T(8,128)S(1)}, u32[]{:S(2)}) copy-start(f32[8,16,48,128]{3,2,1,0:T(8,128)S(1)} %slice.9.own_ref) | copy-start | bytes 9437188
  362.3 157.8 %all-to-all-start.4 = ((f32[8,16,80,128]{3,2,1,0:T(8,128)}), f32[8,16,80,128]{3,2,1,0:T(8,128)}, u32[]{:S(2)}, u32[]{:S(2)}) async-start(f32[8,16,80,128]{3,2,1,0:T(8,128)} %product.4), calls=%async_computation.4 | async-start | bytes 10485760 | tf_op jit(solution)/shard_map/all_to_all | solution.py:372
  369.3 134.0 %collective-permute-start.2 = (f32[8,16,48,128]{3,2,1,0:T(8,128)S(1)}, f32[8,16,48,128]{3,2,1,0:T(8,128)S(1)}, u32[]{:S(2)}, u32[]{:S(2)}) collective-permute-start(f32[8,16,48,128]{3,2,1,0:T(8,128)S(1)} %slice.9.own_ref), channel_id=1, source_target_pairs={{0,8},{8,0},{1,9},{9,1},{2,10},{10,2},{3,11},{11,3},{4,12},{12,4},... | collective-permute-start | bytes 9437192 | tf_op jit(solution)/shard_map/ppermute | solution.py:366
  503.4 1.7 copy-start.3
  520.1 7.7 %copy-start.13 = (f32[128,128]{1,0:T(8,128)S(1)}, f32[128,128]{1,0:T(8,128)}, u32[]{:S(2)}) copy-start(f32[128,128]{1,0:T(8,128)} %param.15) | copy-start | bytes 196612
  520.1 7.8 %copy-start.14 = (f32[128,128]{1,0:T(8,128)S(1)}, f32[128,128]{1,0:T(8,128)}, u32[]{:S(2)}) copy-start(f32[128,128]{1,0:T(8,128)} %param.14) | copy-start | bytes 196612
  520.1 12.5 %copy-start.15 = (f32[128]{0:T(128)S(1)}, f32[128]{0:T(128)}, u32[]{:S(2)}) copy-start(f32[128]{0:T(128)} %param.12) | copy-start | bytes 1540
  520.1 12.5 %copy-start.16 = (f32[128]{0:T(128)S(1)}, f32[128]{0:T(128)}, u32[]{:S(2)}) copy-start(f32[128]{0:T(128)} %param.16) | copy-start | bytes 1540
  520.1 13.2 %copy-start.17 = (f32[128]{0:T(128)S(1)}, f32[128]{0:T(128)}, u32[]{:S(2)}) copy-start(f32[128]{0:T(128)} %param.17) | copy-start | bytes 1540
  520.1 52.3 %all-to-all-start.3 = ((f32[8,16,48,128]{3,2,1,0:T(8,128)}), f32[8,16,48,128]{3,2,1,0:T(8,128)S(1)}, u32[]{:S(2)}, u32[]{:S(2)}) async-start(f32[8,16,48,128]{3,2,1,0:T(8,128)} %product.5), calls=%async_computation.3 | async-start | bytes 6291456 | tf_op jit(solution)/shard_map/all_to_all | solution.py:372
  572.4 1.7 copy-start.1
  574.1 23.4 %copy-start.9 = (f32[80,16,128]{2,1,0:T(8,128)S(1)}, f32[80,16,128]{2,1,0:T(8,128)}, u32[]{:S(2)}) copy-start(f32[80,16,128]{2,1,0:T(8,128)} %get-tuple-element.36.refs_6_) | copy-start | bytes 1966084
  574.1 25.8 %copy-start.7 = (f32[80,16,128]{2,1,0:T(8,128)S(1)}, f32[80,16,128]{2,1,0:T(8,128)}, u32[]{:S(2)}) copy-start(f32[80,16,128]{2,1,0:T(8,128)} %get-tuple-element.33.refs_2_) | copy-start | bytes 1966084
  574.1 26.3 %copy-start.8 = (f32[80,16,128]{2,1,0:T(8,128)S(1)}, f32[80,16,128]{2,1,0:T(8,128)}, u32[]{:S(2)}) copy-start(f32[80,16,128]{2,1,0:T(8,128)} %get-tuple-element.34.refs_4_) | copy-start | bytes 1966084
  574.1 26.9 %copy-start.6 = (f32[80,16,128]{2,1,0:T(8,128)S(1)}, f32[80,16,128]{2,1,0:T(8,128)}, u32[]{:S(2)}) copy-start(f32[80,16,128]{2,1,0:T(8,128)} %get-tuple-element.30.refs_0_) | copy-start | bytes 1966084
  574.1 113.9 %copy-start.18 = (f32[64]{0:T(128)S(1)}, f32[64]{0:T(128)}, u32[]{:S(2)}) copy-start(f32[64]{0:T(128)} %param.21) | copy-start | bytes 772
  596.9 76.3 %collective-permute-start.9 = (f32[48,32,128]{2,1,0:T(8,128)}, f32[48,32,128]{2,1,0:T(8,128)}, u32[]{:S(2)}, u32[]{:S(2)}) collective-permute-start(f32[48,32,128]{2,1,0:T(8,128)} %get-tuple-element.35.refs_5_.refs_7_), channel_id=1, source_target_pairs={{0,2},{1,3},{2,0},{3,1},{4,6},{5,7},{6,4},{7,5},{8,10},{9,11},{10,... | collective-permute-start | bytes 2359304 | tf_op jit(solution)/shard_map/ppermute | solution.py:312
  597.5 72.0 %collective-permute-start.11 = (f32[80,16,128]{2,1,0:T(8,128)S(1)}, f32[80,16,128]{2,1,0:T(8,128)}, u32[]{:S(2)}, u32[]{:S(2)}) collective-permute-start(f32[80,16,128]{2,1,0:T(8,128)S(1)} %copy-done.9), channel_id=1, source_target_pairs={{0,3},{1,2},{2,1},{3,0},{4,7},{5,6},{6,5},{7,4},{8,11},{9,10},{10,... | collective-permute-start | bytes 1966088 | tf_op jit(solution)/shard_map/ppermute | solution.py:312
  599.9 73.5 %collective-permute-start.5 = (f32[80,16,128]{2,1,0:T(8,128)S(1)}, f32[80,16,128]{2,1,0:T(8,128)}, u32[]{:S(2)}, u32[]{:S(2)}) collective-permute-start(f32[80,16,128]{2,1,0:T(8,128)S(1)} %copy-done.7), channel_id=1, source_target_pairs={{0,1},{1,0},{2,3},{3,2},{4,5},{5,4},{6,7},{7,6},{8,9},{9,8},{10,11... | collective-permute-start | bytes 1966088 | tf_op jit(solution)/shard_map/ppermute | solution.py:312
  600.4 86.1 %collective-permute-start.7 = (f32[80,16,128]{2,1,0:T(8,128)S(1)}, f32[80,16,128]{2,1,0:T(8,128)}, u32[]{:S(2)}, u32[]{:S(2)}) collective-permute-start(f32[80,16,128]{2,1,0:T(8,128)S(1)} %copy-done.8), channel_id=1, source_target_pairs={{0,2},{1,3},{2,0},{3,1},{4,6},{5,7},{6,4},{7,5},{8,10},{9,11},{10,... | collective-permute-start | bytes 1966088 | tf_op jit(solution)/shard_map/ppermute | solution.py:312
  601.0 87.0 %collective-permute-start.3 = (f32[80,16,128]{2,1,0:T(8,128)S(1)}, f32[80,16,128]{2,1,0:T(8,128)S(1)}, u32[]{:S(2)}, u32[]{:S(2)}) collective-permute-start(f32[80,16,128]{2,1,0:T(8,128)S(1)} %copy-done.6), channel_id=1, source_target_pairs={{0,0},{1,4},{2,8},{3,12},{4,1},{5,5},{6,9},{7,13},{8,2},{9,6},{10,... | collective-permute-start | bytes 1966088 | tf_op jit(solution)/shard_map/ppermute | solution.py:312
  669.5 25.7 %collective-permute-start.4 = (f32[48,32,128]{2,1,0:T(8,128)}, f32[48,32,128]{2,1,0:T(8,128)S(1)}, u32[]{:S(2)}, u32[]{:S(2)}) collective-permute-start(f32[48,32,128]{2,1,0:T(8,128)} %get-tuple-element.32.refs_1_.refs_3_), channel_id=1, source_target_pairs={{0,0},{1,4},{2,8},{3,12},{4,1},{5,5},{6,9},{7,13},{8,2},{9,6},{10,... | collective-permute-start | bytes 2359304 | tf_op jit(solution)/shard_map/ppermute | solution.py:312
  673.3 80.7 %collective-permute-start.10 = (f32[48,32,128]{2,1,0:T(8,128)}, f32[48,32,128]{2,1,0:T(8,128)S(1)}, u32[]{:S(2)}, u32[]{:S(2)}) collective-permute-start(f32[48,32,128]{2,1,0:T(8,128)} %collective-permute-done.9), channel_id=1, source_target_pairs={{0,8},{1,12},{2,0},{3,4},{4,9},{5,13},{6,1},{7,5},{8,10},{9,14},{1... | collective-permute-start | bytes 2359304 | tf_op jit(solution)/shard_map/ppermute | solution.py:312
  673.4 64.9 %collective-permute-start.12 = (f32[80,16,128]{2,1,0:T(8,128)}, f32[80,16,128]{2,1,0:T(8,128)S(1)}, u32[]{:S(2)}, u32[]{:S(2)}) collective-permute-start(f32[80,16,128]{2,1,0:T(8,128)} %collective-permute-done.11), channel_id=1, source_target_pairs={{0,12},{1,8},{2,4},{3,0},{4,13},{5,9},{6,5},{7,1},{8,14},{9,10},{1... | collective-permute-start | bytes 1966088 | tf_op jit(solution)/shard_map/ppermute | solution.py:312
  686.5 51.7 %collective-permute-start.6 = (f32[80,16,128]{2,1,0:T(8,128)}, f32[80,16,128]{2,1,0:T(8,128)S(1)}, u32[]{:S(2)}, u32[]{:S(2)}) collective-permute-start(f32[80,16,128]{2,1,0:T(8,128)} %collective-permute-done.5), channel_id=1, source_target_pairs={{0,4},{1,0},{2,12},{3,8},{4,5},{5,1},{6,13},{7,9},{8,6},{9,2},{10,... | collective-permute-start | bytes 1966088 | tf_op jit(solution)/shard_map/ppermute | solution.py:312
  688.0 66.8 %copy-start.10 = (f32[80,16,128]{2,1,0:T(8,128)}, f32[80,16,128]{2,1,0:T(8,128)S(1)}, u32[]{:S(2)}) copy-start(f32[80,16,128]{2,1,0:T(8,128)S(1)} %collective-permute-done.3.refs_8_) | copy-start | bytes 1966084
  688.0 66.1 %collective-permute-start.8 = (f32[80,16,128]{2,1,0:T(8,128)}, f32[80,16,128]{2,1,0:T(8,128)}, u32[]{:S(2)}, u32[]{:S(2)}) collective-permute-start(f32[80,16,128]{2,1,0:T(8,128)} %collective-permute-done.7), channel_id=1, source_target_pairs={{0,8},{1,12},{2,0},{3,4},{4,9},{5,13},{6,1},{7,5},{8,10},{9,14},{1... | collective-permute-start | bytes 1966088 | tf_op jit(solution)/shard_map/ppermute | solution.py:312
  695.2 59.6 %copy-start.4 = (f32[48,32,128]{2,1,0:T(8,128)}, f32[48,32,128]{2,1,0:T(8,128)S(1)}, u32[]{:S(2)}) copy-start(f32[48,32,128]{2,1,0:T(8,128)S(1)} %collective-permute-done.4.refs_9_.refs_11_) | copy-start | bytes 2359300
  738.3 16.6 %copy-start.11 = (f32[80,16,128]{2,1,0:T(8,128)}, f32[80,16,128]{2,1,0:T(8,128)S(1)}, u32[]{:S(2)}) copy-start(f32[80,16,128]{2,1,0:T(8,128)S(1)} %collective-permute-done.12.refs_14_) | copy-start | bytes 1966084
  738.3 16.6 %copy-start.12 = (f32[80,16,128]{2,1,0:T(8,128)}, f32[80,16,128]{2,1,0:T(8,128)S(1)}, u32[]{:S(2)}) copy-start(f32[80,16,128]{2,1,0:T(8,128)S(1)} %collective-permute-done.6.refs_10_) | copy-start | bytes 1966084
  754.0 0.9 copy-start.5

commit v6 on v5

--- a/solution.py
+++ b/solution.py
@@ -10,9 +10,9 @@
 HIGH = lax.Precision.HIGHEST
 LANES = 128
 GROUP = 8
-CHUNKS = (40, 40, 48)
-LOWER = 48
-PARTS = (4, 2)
+CHUNKS = (40, 56, 32)
+LOWER = 40
+PARTS = (4, 4, 2)
 VMEM = 56 * 1024 * 1024
 SCALE = 8
 
@@ -143,8 +143,7 @@
     )(pair, weights3)
 
 
-def product_kernel(half_ref, low_ref, high_ref, own_ref, other_ref, *refs):
-    out_ref = refs[-1]
+def product_kernel(half_ref, low_ref, high_ref, own_ref, other_ref, out_ref):
     cols = own_ref.shape[0] // 2
     half = half_ref[0]
 
@@ -174,29 +173,25 @@
             ]
 
 
-def product(half, low, high, own, other, wide, blocks=1, into=None):
+def product(half, low, high, own, other, wide):
     sources, owned, rows, width = own.shape
     k_all = width * sources // 2
     spec = lambda height: pl.BlockSpec((sources, 1, height, width), lambda n, half: (0, n, 0, 0))
-    place = 0 if into is None else blocks - 1
-    kept = [] if into is None else [into]
     return pl.pallas_call(
         product_kernel,
         grid_spec=pltpu.PrefetchScalarGridSpec(
             num_scalar_prefetch=1,
             grid=(owned,),
-            in_specs=[spec(LOWER), spec(wide - LOWER), spec(rows), spec(rows)]
-            + [pl.BlockSpec(memory_space=pl.ANY)] * len(kept),
-            out_specs=pl.BlockSpec((sources, 1, rows, wide), lambda n, half: (0, n, place, 0)),
+            in_specs=[spec(LOWER), spec(wide - LOWER), spec(rows), spec(rows)],
+            out_specs=pl.BlockSpec((sources, 1, rows, wide), lambda n, half: (0, n, 0, 0)),
         ),
-        out_shape=jax.ShapeDtypeStruct((sources, owned, blocks * rows, wide), jnp.float32),
-        input_output_aliases={5: 0} if kept else {},
+        out_shape=jax.ShapeDtypeStruct((sources, owned, rows, wide), jnp.float32),
         compiler_params=pltpu.CompilerParams(vmem_limit_bytes=VMEM),
         cost_estimate=estimate(
             6 * owned * 4 * rows * 2 * wide * k_all, 4 * owned * k_all * (2 * wide + 4 * rows)
         ),
         name="product",
-    )(half, low, high, own, other, *kept)
+    )(half, low, high, own, other)
 
 
 def head_kernel(
@@ -365,15 +360,17 @@
     def exchange(values):
         return lax.ppermute(values, "half", [(0, 1), (1, 0)])
 
-    def blocks(chunk, count=1, into=None):
-        return product(half, low, high, rights[chunk], others[chunk], tile_rows, count, into)
+    def blocks(chunk):
+        return product(half, low, high, rights[chunk], others[chunk], tile_rows)
 
     def delivered(values):
         values = lax.all_to_all(values, ("lo", "col"), split_axis=0, concat_axis=0, tiled=True)
         return values.reshape(width, values.shape[2], tile_rows)
 
-    def run_head(values, first, count):
-        return head(tile, values, first, count, gate3, output3, up3, down3, bins3)
+    def run_head(values, chunk):
+        return head(
+            tile, values, firsts[chunk], PARTS[chunk], gate3, output3, up3, down3, bins3
+        )
 
     def mirrored_parts(block):
         shifted = aside(block, row_count)
@@ -388,12 +385,15 @@
     others.append(exchange(rights[1]))
     high = spread(sent)
     rights.append(high[:, :, upper:])
-    values, rights[2] = tie((blocks(1, 2, blocks(0, 2)), rights[2]))
+    values, others[1], rights[2] = tie((blocks(0), others[1], rights[2]))
     others.append(exchange(rights[2]))
-    own = [run_head(delivered(values), 0, PARTS[0])]
-    values, own[0] = tie((delivered(blocks(2)), own[0]))
-    own.append(run_head(values, firsts[2], PARTS[1]))
-    mirror = [mirrored_parts(block) for block in own]
+    values, after = tie((delivered(values), blocks(1)))
+    own = [run_head(values, 0)]
+    mirror = [mirrored_parts(own[0])]
+    after, others[2], mirror[0] = tie((after, others[2], mirror[0]))
+    own.append(run_head(delivered(after), 1))
+    own.append(run_head(delivered(blocks(2)), 2))
+    mirror += [mirrored_parts(block) for block in own[1:]]
     quarters = 4
     bins = distogram_bias.shape[0] // quarters
     bias = jnp.broadcast_to(distogram_bias.reshape(quarters, bins, 1), (quarters, bins, tile_cols))

time: 765 us -> 725 us (0.948); the launches traced: 762 us -> 711 us
  waiting for transfers between devices: 524 us -> 424 us
  blocking collectives: 0 us -> 26.2 us
  starting transfers between devices: 69.8 us -> 91.4 us
    ppermute x3, waiting for transfers between devices: 133 us -> 1.27 us  [exchange(): return lax.ppermute(values, 'half', [(0, 1), (1, 0)])]
    all_to_all x2, waiting for transfers between devices: 0.01 us -> 68.8 us  [delivered(): lax.all_to_all(values, ('lo', 'col'), split_axis=0, concat_axis=0, tiled=...]
    ppermute x10 -> x17, waiting for transfers between devices: 131 us -> 71.2 us  [move(): return lax.ppermute(values, ('half', 'lo', 'col'), pairs)]
    all_to_all x0 -> x1, blocking collectives: none -> 26.2 us  [delivered(): lax.all_to_all(values, ('lo', 'col'), split_axis=0, concat_axis=0, tiled=...]
    ppermute x10 -> x17, starting transfers between devices: 26.2 us -> 49.4 us  [move(): return lax.ppermute(values, ('half', 'lo', 'col'), pairs)]
    all_to_all x3, waiting for transfers between devices: 260 us -> 283 us  [spread(): lax.all_to_all(values, ('lo', 'col'), split_axis=0, concat_axis=0, tiled=...]
    pallas_call x2 -> x3, Pallas kernels: 59.1 us -> 61.3 us  [head(): pl.pallas_call(head_kernel, grid=(steps,), in_specs=[pl.BlockSpec((tile_r...]
  transfers between devices with their start and end apart: 18 -> 25, of which waited for: 8 -> 14; matrix products, arithmetic and copies ran while one was open for 2% -> 2% of each run, Pallas kernels for 13% -> 17%
where the time goes in v6:
time: 725 us; the launch traced here: 711 us
  waiting for transfers between devices  424 us (58%)
  Pallas kernels  148 us (20%)
  starting transfers between devices  91.4 us (13%)
  blocking collectives  26.2 us (4%)
  local copies, waits for them, and re-layouts  13.3 us (2%)
  other arithmetic  7.4 us (1%)
    all_to_all x3, waiting for transfers between devices, spread(): lax.all_to_all(values, ('lo', 'col'), split_axis=0, concat_axis=0, tiled=...  283 us
    ppermute x17, waiting for transfers between devices, move(): return lax.ppermute(values, ('half', 'lo', 'col'), pairs)  71.2 us
    all_to_all x2, waiting for transfers between devices, delivered(): lax.all_to_all(values, ('lo', 'col'), split_axis=0, concat_axis=0, tiled=...  68.8 us
    pallas_call x3, Pallas kernels, head(): pl.pallas_call(head_kernel, grid=(steps,), in_specs=[pl.BlockSpec((tile_r...  61.3 us
    ppermute x17, starting transfers between devices, move(): return lax.ppermute(values, ('half', 'lo', 'col'), pairs)  49.4 us
    pallas_call x3, Pallas kernels, product(): pl.pallas_call(product_kernel, grid_spec=pltpu.PrefetchScalarGridSpec(num...  44.1 us
    pallas_call x3, Pallas kernels, hands(): pl.pallas_call(hands_kernel, grid=(rows // GROUP,), in_specs=[pl.BlockSpe...  35.6 us
    all_to_all x1, blocking collectives, delivered(): lax.all_to_all(values, ('lo', 'col'), split_axis=0, concat_axis=0, tiled=...  26.2 us
  transfers between devices with their start and end apart: 25, of which 14 were waited for; matrix products, arithmetic and copies ran while one was open for 2% of the time, Pallas kernels for 17%

profile of v6, /device:TPU:12, one launch (start us, length us, event | category | flops | bytes accessed | tf_op | source)
XLA Modules:
  0.0 710.5 jit_solution(1481587520294681614)
XLA Ops:
  0.0 1.1 copy.12
  2.6 6.4 hands.5
  9.0 5.1 all-to-all-start.1
  14.1 13.0 %hands.3 = f32[128,96,128]{2,1,0:T(8,128)} custom-call(f32[128,128,128]{2,1,0:T(8,128)} %bitcast.32, bf16[512,384]{1,0:T(8,128)(2,1)} %pad_maximum_fusion.1.weights_ref), custom_call_target="tpu_custom_call" | custom-call | flops 301989888 | bytes 1572864 | tf_op jit(solution)/shard_map/hands/pallas_call | solution.py:131
  27.1 17.8 %all-to-all-done.1.own_ref = f32[8,16,40,128]{3,2,1,0:T(8,128)S(1)} async-done(((f32[8,16,40,128]{3,2,1,0:T(8,128)}), f32[8,16,40,128]{3,2,1,0:T(8,128)S(1)}, u32[]{:S(2)}, u32[]{:S(2)}) %all-to-all-start.1) | async-done | bytes 2621472 | tf_op jit(solution)/shard_map/all_to_all | solution.py:353
  45.0 7.2 %all-to-all-start = ((f32[8,16,96,128]{3,2,1,0:T(8,128)}), f32[8,16,96,128]{3,2,1,0:T(8,128)}, u32[]{:S(2)}, u32[]{:S(2)}) async-start(f32[8,16,96,128]{3,2,1,0:T(8,128)} %bitcast.38), calls=%async_computation | async-start | bytes 12582912 | tf_op jit(solution)/shard_map/all_to_all | solution.py:353
  52.1 2.6 collective-permute-start
  54.7 16.2 %hands.4 = f32[128,120,128]{2,1,0:T(8,128)} custom-call(f32[128,128,128]{2,1,0:T(8,128)} %bitcast.33, bf16[512,384]{1,0:T(8,128)(2,1)} %pad_maximum_fusion.1.weights_ref), custom_call_target="tpu_custom_call" | custom-call | flops 377487360 | bytes 1966080 | tf_op jit(solution)/shard_map/hands/pallas_call | solution.py:131
  70.9 103.8 %all-to-all-done.low_ref = f32[8,16,96,128]{3,2,1,0:T(8,128)} async-done(((f32[8,16,96,128]{3,2,1,0:T(8,128)}), f32[8,16,96,128]{3,2,1,0:T(8,128)}, u32[]{:S(2)}, u32[]{:S(2)}) %all-to-all-start) | async-done | bytes 6291488 | tf_op jit(solution)/shard_map/all_to_all | solution.py:353
  174.7 4.2 slice.8.own_ref
  178.9 13.5 %all-to-all-start.2 = ((f32[8,16,120,128]{3,2,1,0:T(8,128)}), f32[8,16,120,128]{3,2,1,0:T(8,128)}, u32[]{:S(2)}, u32[]{:S(2)}) async-start(f32[8,16,120,128]{3,2,1,0:T(8,128)} %bitcast.37), calls=%async_computation.2 | async-start | bytes 15728640 | tf_op jit(solution)/shard_map/all_to_all | solution.py:353
  192.4 160.9 %all-to-all-done.2.high_ref = f32[8,16,120,128]{3,2,1,0:T(8,128)} async-done(((f32[8,16,120,128]{3,2,1,0:T(8,128)}), f32[8,16,120,128]{3,2,1,0:T(8,128)}, u32[]{:S(2)}, u32[]{:S(2)}) %all-to-all-start.2) | async-done | bytes 7864352 | tf_op jit(solution)/shard_map/all_to_all | solution.py:353
  353.3 3.1 slice.9.own_ref
  356.4 14.6 %product.3 = f32[8,16,40,128]{3,2,1,0:T(8,128)} custom-call(s32[1]{0:T(128)} %bitcast.1.half_ref, f32[8,16,96,128]{3,2,1,0:T(8,128)} %all-to-all-done.low_ref, f32[8,16,120,128]{3,2,1,0:T(8,128)} %all-to-all-done.2.high_ref, f32[8,16,40,128]{3,2,1,0:T(8,128)} %copy-done, f32[8,16,40,128]{3,2,1,0:T(8,128)} %collective-permute-done.other_ref), custom_call_target="tpu_custom_call" | custom-call | flops 251658240 | bytes 1703936 | tf_op jit(solution)/shard_map/product/pallas_call | solution.py:180
  371.0 6.5 all-to-all-start.3
  377.7 1.1 collective-permute-start.2
  379.5 1.2 copy.15
  380.8 1.1 copy.16
  381.8 1.3 pad_maximum_fusion.5.bins_ref
  385.3 1.0 pad_maximum_fusion.up_ref
  387.1 15.3 %product.4 = f32[8,16,56,128]{3,2,1,0:T(8,128)} custom-call(s32[1]{0:T(128)} %bitcast.1.half_ref, f32[8,16,96,128]{3,2,1,0:T(8,128)} %all-to-all-done.low_ref, f32[8,16,120,128]{3,2,1,0:T(8,128)} %all-to-all-done.2.high_ref, f32[8,16,56,128]{3,2,1,0:T(8,128)} %slice.8.own_ref, f32[8,16,56,128]{3,2,1,0:T(8,128)} %collective-permute-done.1.other_ref), custom_call_target="tpu_custom_call" | custom-call | flops 352321536 | bytes 1966080 | tf_op jit(solution)/shard_map/product/pallas_call | solution.py:180
  402.4 29.2 %all-to-all-done.3 = f32[8,16,40,128]{3,2,1,0:T(8,128)S(1)} async-done(((f32[8,16,40,128]{3,2,1,0:T(8,128)}), f32[8,16,40,128]{3,2,1,0:T(8,128)S(1)}, u32[]{:S(2)}, u32[]{:S(2)}) %all-to-all-start.3) | async-done | bytes 2621472 | tf_op jit(solution)/shard_map/all_to_all | solution.py:367
  431.7 1.5 copy-done.1
  433.1 19.2 %head.3 = (f32[40,16,128]{2,1,0:T(8,128)}, f32[40,16,128]{2,1,0:T(8,128)}, f32[40,16,128]{2,1,0:T(8,128)}, f32[40,16,128]{2,1,0:T(8,128)}) custom-call(f32[128,128,128]{2,1,0:T(8,128)} %bitcast.34, f32[128,40,128]{2,1,0:T(8,128)} %bitcast.39, bf16[128,384]{1,0:T(8,128)(2,1)} %get-tuple-element.65.gate_ref, bf16[128,384]{1,0:T(8,128)(2,1)} %get-tuple-element.66.output_ref, ...), custom_call_target="tpu_custom_call" | custom-call | flops 912261120 | bytes 819200 | tf_op jit(solution)/shard_map/head/pallas_call | solution.py:234
  452.4 2.8 collective-permute-start.4
  456.7 5.1 collective-permute-start.3
  461.9 2.1 collective-permute-done.4
  464.0 5.1 collective-permute-start.5
  469.2 13.6 %collective-permute-start.7 = (f32[40,16,128]{2,1,0:T(8,128)S(1)}, f32[40,16,128]{2,1,0:T(8,128)}, u32[]{:S(2)}, u32[]{:S(2)}) collective-permute-start(f32[40,16,128]{2,1,0:T(8,128)S(1)} %collective-permute-done.6), channel_id=1, source_target_pairs={{0,8},{1,12},{2,0},{3,4},{4,9},{5,13},{6,1},{7,5},{8,10},{9,14},{1... | collective-permute-start | bytes 983048 | tf_op jit(solution)/shard_map/ppermute | solution.py:307
  482.9 1.3 collective-permute-done.2.other_ref
  484.2 10.6 %collective-permute-done.3.refs_12_ = f32[40,16,128]{2,1,0:T(8,128)S(1)} collective-permute-done((f32[40,16,128]{2,1,0:T(8,128)}, f32[40,16,128]{2,1,0:T(8,128)S(1)}, u32[]{:S(2)}, u32[]{:S(2)}) %collective-permute-start.3) | collective-permute-done | bytes 327712 | tf_op jit(solution)/shard_map/ppermute | solution.py:307
  494.8 3.7 collective-permute-done.5.refs_15_
  499.4 14.1 %product.5 = f32[8,16,32,128]{3,2,1,0:T(8,128)} custom-call(s32[1]{0:T(128)} %bitcast.1.half_ref, f32[8,16,96,128]{3,2,1,0:T(8,128)} %all-to-all-done.low_ref, f32[8,16,120,128]{3,2,1,0:T(8,128)} %all-to-all-done.2.high_ref, f32[8,16,32,128]{3,2,1,0:T(8,128)} %slice.9.own_ref, f32[8,16,32,128]{3,2,1,0:T(8,128)} %collective-permute-done.2.other_ref), custom_call_target="tpu_custom_call" | custom-call | flops 201326592 | bytes 1572864 | tf_op jit(solution)/shard_map/product/pallas_call | solution.py:180
  513.5 26.2 %all_to_all.30 = f32[8,16,32,128]{3,2,1,0:T(8,128)} all-to-all(f32[8,16,32,128]{3,2,1,0:T(8,128)} %product.5), channel_id=1, replica_groups=mesh['crop'=2,'half'=2,'lo'=2,'col'=4] {'lo','col'}, dimensions={0} | all-to-all | bytes 4194304 | tf_op jit(solution)/shard_map/all_to_all | solution.py:367
  539.7 6.0 all-to-all-start.4
  545.8 15.9 %head.5 = (f32[32,32,128]{2,1,0:T(8,128)}, f32[32,32,128]{2,1,0:T(8,128)}) custom-call(f32[128,128,128]{2,1,0:T(8,128)} %bitcast.35, f32[128,32,128]{2,1,0:T(8,128)} %bitcast.41, bf16[128,384]{1,0:T(8,128)(2,1)} %get-tuple-element.65.gate_ref, bf16[128,384]{1,0:T(8,128)(2,1)} %get-tuple-element.66.output_ref, bf16[1024,384]{1,0:T(8,128)(2,1)} %pad_maximum_fusion.up_ref, ...), custom_call_target="tpu_custom_call" | custom-call | flops 729808896 | bytes 655360 | tf_op jit(solution)/shard_map/head/pallas_call | solution.py:234
  562.2 4.3 collective-permute-start.11
  566.5 39.5 %all-to-all-done.4 = f32[8,16,56,128]{3,2,1,0:T(8,128)} async-done(((f32[8,16,56,128]{3,2,1,0:T(8,128)}), f32[8,16,56,128]{3,2,1,0:T(8,128)}, u32[]{:S(2)}, u32[]{:S(2)}) %all-to-all-start.4) | async-done | bytes 3670048 | tf_op jit(solution)/shard_map/all_to_all | solution.py:367
  606.1 26.1 %head.4 = (f32[56,16,128]{2,1,0:T(8,128)}, f32[56,16,128]{2,1,0:T(8,128)}, f32[56,16,128]{2,1,0:T(8,128)}, f32[56,16,128]{2,1,0:T(8,128)}) custom-call(f32[128,128,128]{2,1,0:T(8,128)} %bitcast.36, f32[128,56,128]{2,1,0:T(8,128)} %bitcast.12.product_ref, bf16[128,384]{1,0:T(8,128)(2,1)} %get-tuple-element.65.gate_ref, ...), custom_call_target="tpu_custom_call" | custom-call | flops 1277165568 | bytes 1146880 | tf_op jit(solution)/shard_map/head/pallas_call | solution.py:234
  632.2 7.3 %collective-permute-start.14 = (f32[56,16,128]{2,1,0:T(8,128)}, f32[56,16,128]{2,1,0:T(8,128)}, u32[]{:S(2)}, u32[]{:S(2)}) collective-permute-start(f32[56,16,128]{2,1,0:T(8,128)} %get-tuple-element.46.refs_7_), channel_id=1, source_target_pairs={{0,2},{1,3},{2,0},{3,1},{4,6},{5,7},{6,4},{7,5},{8,10},{9,11},{10,... | collective-permute-start | bytes 1376264 | tf_op jit(solution)/shard_map/ppermute | solution.py:307
  639.5 1.4 collective-permute-start.18
  640.9 3.5 collective-permute-start.17
  644.4 3.9 collective-permute-start.10
  648.3 26.8 %collective-permute-done.12 = f32[56,16,128]{2,1,0:T(8,128)} collective-permute-done((f32[56,16,128]{2,1,0:T(8,128)}, f32[56,16,128]{2,1,0:T(8,128)}, u32[]{:S(2)}, u32[]{:S(2)}) %collective-permute-start.12) | collective-permute-done | bytes 458784 | tf_op jit(solution)/shard_map/ppermute | solution.py:307
  675.3 12.4 %collective-permute-done.17.refs_20_.refs_23_ = f32[32,32,128]{2,1,0:T(8,128)S(1)} collective-permute-done((f32[32,32,128]{2,1,0:T(8,128)S(1)}, f32[32,32,128]{2,1,0:T(8,128)S(1)}, u32[]{:S(2)}, u32[]{:S(2)}) %collective-permute-start.17) | collective-permute-done | bytes 524320 | tf_op jit(solution)/shard_map/ppermute | solution.py:307
  687.7 1.7 collective-permute-done.13.refs_16_
  689.4 13.0 %collective-permute-done.15.refs_19_ = f32[56,16,128]{2,1,0:T(8,128)S(1)} collective-permute-done((f32[56,16,128]{2,1,0:T(8,128)}, f32[56,16,128]{2,1,0:T(8,128)S(1)}, u32[]{:S(2)}, u32[]{:S(2)}) %collective-permute-start.15) | collective-permute-done | bytes 458784 | tf_op jit(solution)/shard_map/ppermute | solution.py:307
  703.3 7.1 symmetric.1
  (63 shorter events, 9.5 us)
Async XLA Ops:
  9.0 36.0 %all-to-all-start.1 = ((f32[8,16,40,128]{3,2,1,0:T(8,128)}), f32[8,16,40,128]{3,2,1,0:T(8,128)S(1)}, u32[]{:S(2)}, u32[]{:S(2)}) async-start(f32[8,16,40,128]{3,2,1,0:T(8,128)} %bitcast.40), calls=%async_computation.1 | async-start | bytes 5242880 | tf_op jit(solution)/shard_map/all_to_all | solution.py:353
  45.0 7.2 %copy-start = (f32[8,16,40,128]{3,2,1,0:T(8,128)}, f32[8,16,40,128]{3,2,1,0:T(8,128)S(1)}, u32[]{:S(2)}) copy-start(f32[8,16,40,128]{3,2,1,0:T(8,128)S(1)} %all-to-all-done.1.own_ref) | copy-start | bytes 7864324
  45.0 129.8 %all-to-all-start = ((f32[8,16,96,128]{3,2,1,0:T(8,128)}), f32[8,16,96,128]{3,2,1,0:T(8,128)}, u32[]{:S(2)}, u32[]{:S(2)}) async-start(f32[8,16,96,128]{3,2,1,0:T(8,128)} %bitcast.38), calls=%async_computation | async-start | bytes 12582912 | tf_op jit(solution)/shard_map/all_to_all | solution.py:353
  52.1 126.8 %collective-permute-start = (f32[8,16,40,128]{3,2,1,0:T(8,128)S(1)}, f32[8,16,40,128]{3,2,1,0:T(8,128)}, u32[]{:S(2)}, u32[]{:S(2)}) collective-permute-start(f32[8,16,40,128]{3,2,1,0:T(8,128)S(1)} %all-to-all-done.1.own_ref), channel_id=1, source_target_pairs={{0,8},{8,0},{1,9},{9,1},{2,10},{10,2},{3,11},{11,3},{4,12},{12,4},... | collective-permute-start | bytes 7864328 | tf_op jit(solution)/shard_map/ppermute | solution.py:361
  178.9 174.4 %all-to-all-start.2 = ((f32[8,16,120,128]{3,2,1,0:T(8,128)}), f32[8,16,120,128]{3,2,1,0:T(8,128)}, u32[]{:S(2)}, u32[]{:S(2)}) async-start(f32[8,16,120,128]{3,2,1,0:T(8,128)} %bitcast.37), calls=%async_computation.2 | async-start | bytes 15728640 | tf_op jit(solution)/shard_map/all_to_all | solution.py:353
  192.4 178.6 %collective-permute-start.1 = (f32[8,16,56,128]{3,2,1,0:T(8,128)}, f32[8,16,56,128]{3,2,1,0:T(8,128)}, u32[]{:S(2)}, u32[]{:S(2)}) collective-permute-start(f32[8,16,56,128]{3,2,1,0:T(8,128)} %slice.8.own_ref), channel_id=1, source_target_pairs={{0,8},{8,0},{1,9},{9,1},{2,10},{10,2},{3,11},{11,3},{4,12},{12,4},... | collective-permute-start | bytes 11010056 | tf_op jit(solution)/shard_map/ppermute | solution.py:361
  371.0 6.6 copy-start.10
  371.0 6.7 copy-start.13
  371.0 7.8 %copy-start.12 = (f32[128,64]{0,1:T(8,128)S(1)}, f32[128,64]{0,1:T(8,128)}, u32[]{:S(2)}) copy-start(f32[128,64]{0,1:T(8,128)} %param.20) | copy-start | bytes 98308
  371.0 8.4 %copy-start.11 = (f32[128,128]{1,0:T(8,128)S(1)}, f32[128,128]{1,0:T(8,128)}, u32[]{:S(2)}) copy-start(f32[128,128]{1,0:T(8,128)} %param.15) | copy-start | bytes 196612
  371.0 60.6 %all-to-all-start.3 = ((f32[8,16,40,128]{3,2,1,0:T(8,128)}), f32[8,16,40,128]{3,2,1,0:T(8,128)S(1)}, u32[]{:S(2)}, u32[]{:S(2)}) async-start(f32[8,16,40,128]{3,2,1,0:T(8,128)} %product.3), calls=%async_computation.3 | async-start | bytes 5242880 | tf_op jit(solution)/shard_map/all_to_all | solution.py:367
  377.7 106.5 %collective-permute-start.2 = (f32[8,16,32,128]{3,2,1,0:T(8,128)}, f32[8,16,32,128]{3,2,1,0:T(8,128)}, u32[]{:S(2)}, u32[]{:S(2)}) collective-permute-start(f32[8,16,32,128]{3,2,1,0:T(8,128)} %slice.9.own_ref), channel_id=1, source_target_pairs={{0,8},{8,0},{1,9},{9,1},{2,10},{10,2},{3,11},{11,3},{4,12},{12,4},... | collective-permute-start | bytes 6291464 | tf_op jit(solution)/shard_map/ppermute | solution.py:361
  431.7 1.5 copy-start.1
  452.4 11.7 %collective-permute-start.4 = (f32[40,16,128]{2,1,0:T(8,128)}, f32[40,16,128]{2,1,0:T(8,128)S(1)}, u32[]{:S(2)}, u32[]{:S(2)}) collective-permute-start(f32[40,16,128]{2,1,0:T(8,128)} %get-tuple-element.38.refs_3_), channel_id=1, source_target_pairs={{0,1},{1,0},{2,3},{3,2},{4,5},{5,4},{6,7},{7,6},{8,9},{9,8},{10,11... | collective-permute-start | bytes 983048 | tf_op jit(solution)/shard_map/ppermute | solution.py:307
  455.2 14.0 %collective-permute-start.6 = (f32[40,16,128]{2,1,0:T(8,128)}, f32[40,16,128]{2,1,0:T(8,128)S(1)}, u32[]{:S(2)}, u32[]{:S(2)}) collective-permute-start(f32[40,16,128]{2,1,0:T(8,128)} %get-tuple-element.39.refs_6_), channel_id=1, source_target_pairs={{0,2},{1,3},{2,0},{3,1},{4,6},{5,7},{6,4},{7,5},{8,10},{9,11},{10,... | collective-permute-start | bytes 983048 | tf_op jit(solution)/shard_map/ppermute | solution.py:307
  455.8 27.1 %collective-permute-start.8 = (f32[40,16,128]{2,1,0:T(8,128)}, f32[40,16,128]{2,1,0:T(8,128)S(1)}, u32[]{:S(2)}, u32[]{:S(2)}) collective-permute-start(f32[40,16,128]{2,1,0:T(8,128)} %get-tuple-element.40.refs_9_), channel_id=1, source_target_pairs={{0,3},{1,2},{2,1},{3,0},{4,7},{5,6},{6,5},{7,4},{8,11},{9,10},{10,... | collective-permute-start | bytes 983048 | tf_op jit(solution)/shard_map/ppermute | solution.py:307
  456.7 38.0 %collective-permute-start.3 = (f32[40,16,128]{2,1,0:T(8,128)}, f32[40,16,128]{2,1,0:T(8,128)S(1)}, u32[]{:S(2)}, u32[]{:S(2)}) collective-permute-start(f32[40,16,128]{2,1,0:T(8,128)} %get-tuple-element.35.refs_0_), channel_id=1, source_target_pairs={{0,0},{1,4},{2,8},{3,12},{4,1},{5,5},{6,9},{7,13},{8,2},{9,6},{10,... | collective-permute-start | bytes 983048 | tf_op jit(solution)/shard_map/ppermute | solution.py:307
  464.0 34.4 %collective-permute-start.5 = (f32[40,16,128]{2,1,0:T(8,128)S(1)}, f32[40,16,128]{2,1,0:T(8,128)S(1)}, u32[]{:S(2)}, u32[]{:S(2)}) collective-permute-start(f32[40,16,128]{2,1,0:T(8,128)S(1)} %collective-permute-done.4), channel_id=1, source_target_pairs={{0,4},{1,0},{2,12},{3,8},{4,5},{5,1},{6,13},{7,9},{8,6},{9,2},{10,... | collective-permute-start | bytes 983048 | tf_op jit(solution)/shard_map/ppermute | solution.py:307
  469.2 29.3 %collective-permute-start.7 = (f32[40,16,128]{2,1,0:T(8,128)S(1)}, f32[40,16,128]{2,1,0:T(8,128)}, u32[]{:S(2)}, u32[]{:S(2)}) collective-permute-start(f32[40,16,128]{2,1,0:T(8,128)S(1)} %collective-permute-done.6), channel_id=1, source_target_pairs={{0,8},{1,12},{2,0},{3,4},{4,9},{5,13},{6,1},{7,5},{8,10},{9,14},{1... | collective-permute-start | bytes 983048 | tf_op jit(solution)/shard_map/ppermute | solution.py:307
  482.8 16.5 %collective-permute-start.9 = (f32[40,16,128]{2,1,0:T(8,128)S(1)}, f32[40,16,128]{2,1,0:T(8,128)}, u32[]{:S(2)}, u32[]{:S(2)}) collective-permute-start(f32[40,16,128]{2,1,0:T(8,128)S(1)} %collective-permute-done.8), channel_id=1, source_target_pairs={{0,12},{1,8},{2,4},{3,0},{4,13},{5,9},{6,5},{7,1},{8,14},{9,10},{1... | collective-permute-start | bytes 983048 | tf_op jit(solution)/shard_map/ppermute | solution.py:307
  494.7 18.8 %copy-start.8 = (f32[40,16,128]{2,1,0:T(8,128)}, f32[40,16,128]{2,1,0:T(8,128)S(1)}, u32[]{:S(2)}) copy-start(f32[40,16,128]{2,1,0:T(8,128)S(1)} %collective-permute-done.3.refs_12_) | copy-start | bytes 983044
  498.4 15.1 %copy-start.9 = (f32[40,16,128]{2,1,0:T(8,128)}, f32[40,16,128]{2,1,0:T(8,128)S(1)}, u32[]{:S(2)}) copy-start(f32[40,16,128]{2,1,0:T(8,128)S(1)} %collective-permute-done.5.refs_15_) | copy-start | bytes 983044
  539.7 66.3 %all-to-all-start.4 = ((f32[8,16,56,128]{3,2,1,0:T(8,128)}), f32[8,16,56,128]{3,2,1,0:T(8,128)}, u32[]{:S(2)}, u32[]{:S(2)}) async-start(f32[8,16,56,128]{3,2,1,0:T(8,128)} %product.4), calls=%async_computation.4 | async-start | bytes 7340032 | tf_op jit(solution)/shard_map/all_to_all | solution.py:367
  561.7 79.2 %collective-permute-start.16 = (f32[32,32,128]{2,1,0:T(8,128)}, f32[32,32,128]{2,1,0:T(8,128)S(1)}, u32[]{:S(2)}, u32[]{:S(2)}) collective-permute-start(f32[32,32,128]{2,1,0:T(8,128)} %get-tuple-element.47.refs_8_.refs_11_), channel_id=1, source_target_pairs={{0,2},{1,3},{2,0},{3,1},{4,6},{5,7},{6,4},{7,5},{8,10},{9,11},{10,... | collective-permute-start | bytes 1572872 | tf_op jit(solution)/shard_map/ppermute | solution.py:307
  562.2 82.2 %collective-permute-start.11 = (f32[32,32,128]{2,1,0:T(8,128)}, f32[32,32,128]{2,1,0:T(8,128)S(1)}, u32[]{:S(2)}, u32[]{:S(2)}) collective-permute-start(f32[32,32,128]{2,1,0:T(8,128)} %get-tuple-element.44.refs_2_.refs_5_), channel_id=1, source_target_pairs={{0,0},{1,4},{2,8},{3,12},{4,1},{5,5},{6,9},{7,13},{8,2},{9,6},{10,... | collective-permute-start | bytes 1572872 | tf_op jit(solution)/shard_map/ppermute | solution.py:307
  606.1 69.1 %copy-start.14 = (f32[64]{0:T(128)S(1)}, f32[64]{0:T(128)}, u32[]{:S(2)}) copy-start(f32[64]{0:T(128)} %param.21) | copy-start | bytes 772
  632.2 42.9 %collective-permute-start.12 = (f32[56,16,128]{2,1,0:T(8,128)}, f32[56,16,128]{2,1,0:T(8,128)}, u32[]{:S(2)}, u32[]{:S(2)}) collective-permute-start(f32[56,16,128]{2,1,0:T(8,128)} %get-tuple-element.45.refs_4_), channel_id=1, source_target_pairs={{0,1},{1,0},{2,3},{3,2},{4,5},{5,4},{6,7},{7,6},{8,9},{9,8},{10,11... | collective-permute-start | bytes 1376264 | tf_op jit(solution)/shard_map/ppermute | solution.py:307
  632.2 42.8 %collective-permute-start.14 = (f32[56,16,128]{2,1,0:T(8,128)}, f32[56,16,128]{2,1,0:T(8,128)}, u32[]{:S(2)}, u32[]{:S(2)}) collective-permute-start(f32[56,16,128]{2,1,0:T(8,128)} %get-tuple-element.46.refs_7_), channel_id=1, source_target_pairs={{0,2},{1,3},{2,0},{3,1},{4,6},{5,7},{6,4},{7,5},{8,10},{9,11},{10,... | collective-permute-start | bytes 1376264 | tf_op jit(solution)/shard_map/ppermute | solution.py:307
  639.5 35.6 %collective-permute-start.18 = (f32[56,16,128]{2,1,0:T(8,128)}, f32[56,16,128]{2,1,0:T(8,128)}, u32[]{:S(2)}, u32[]{:S(2)}) collective-permute-start(f32[56,16,128]{2,1,0:T(8,128)} %get-tuple-element.48.refs_10_), channel_id=1, source_target_pairs={{0,3},{1,2},{2,1},{3,0},{4,7},{5,6},{6,5},{7,4},{8,11},{9,10},{10,... | collective-permute-start | bytes 1376264 | tf_op jit(solution)/shard_map/ppermute | solution.py:307
  640.9 46.7 %collective-permute-start.17 = (f32[32,32,128]{2,1,0:T(8,128)S(1)}, f32[32,32,128]{2,1,0:T(8,128)S(1)}, u32[]{:S(2)}, u32[]{:S(2)}) collective-permute-start(f32[32,32,128]{2,1,0:T(8,128)S(1)} %collective-permute-done.16), channel_id=1, source_target_pairs={{0,8},{1,12},{2,0},{3,4},{4,9},{5,13},{6,1},{7,5},{8,10},{9,14},{1... | collective-permute-start | bytes 1572872 | tf_op jit(solution)/shard_map/ppermute | solution.py:307
  644.4 58.8 %copy-start.2 = (f32[32,32,128]{2,1,0:T(8,128)}, f32[32,32,128]{2,1,0:T(8,128)S(1)}, u32[]{:S(2)}) copy-start(f32[32,32,128]{2,1,0:T(8,128)S(1)} %collective-permute-done.11.refs_14_.refs_17_) | copy-start | bytes 1572868
  644.4 43.3 %collective-permute-start.10 = (f32[56,16,128]{2,1,0:T(8,128)}, f32[56,16,128]{2,1,0:T(8,128)S(1)}, u32[]{:S(2)}, u32[]{:S(2)}) collective-permute-start(f32[56,16,128]{2,1,0:T(8,128)} %get-tuple-element.42.refs_1_), channel_id=1, source_target_pairs={{0,0},{1,4},{2,8},{3,12},{4,1},{5,5},{6,9},{7,13},{8,2},{9,6},{10,... | collective-permute-start | bytes 1376264 | tf_op jit(solution)/shard_map/ppermute | solution.py:307
  675.1 14.3 %collective-permute-start.13 = (f32[56,16,128]{2,1,0:T(8,128)}, f32[56,16,128]{2,1,0:T(8,128)S(1)}, u32[]{:S(2)}, u32[]{:S(2)}) collective-permute-start(f32[56,16,128]{2,1,0:T(8,128)} %collective-permute-done.12), channel_id=1, source_target_pairs={{0,4},{1,0},{2,12},{3,8},{4,5},{5,1},{6,13},{7,9},{8,6},{9,2},{10,... | collective-permute-start | bytes 1376264 | tf_op jit(solution)/shard_map/ppermute | solution.py:307
  675.1 27.3 %collective-permute-start.15 = (f32[56,16,128]{2,1,0:T(8,128)}, f32[56,16,128]{2,1,0:T(8,128)S(1)}, u32[]{:S(2)}, u32[]{:S(2)}) collective-permute-start(f32[56,16,128]{2,1,0:T(8,128)} %collective-permute-done.14), channel_id=1, source_target_pairs={{0,8},{1,12},{2,0},{3,4},{4,9},{5,13},{6,1},{7,5},{8,10},{9,14},{1... | collective-permute-start | bytes 1376264 | tf_op jit(solution)/shard_map/ppermute | solution.py:307
  675.1 27.3 %collective-permute-start.19 = (f32[56,16,128]{2,1,0:T(8,128)}, f32[56,16,128]{2,1,0:T(8,128)S(1)}, u32[]{:S(2)}, u32[]{:S(2)}) collective-permute-start(f32[56,16,128]{2,1,0:T(8,128)} %collective-permute-done.18), channel_id=1, source_target_pairs={{0,12},{1,8},{2,4},{3,0},{4,13},{5,9},{6,5},{7,1},{8,14},{9,10},{1... | collective-permute-start | bytes 1376264 | tf_op jit(solution)/shard_map/ppermute | solution.py:307
  687.7 15.5 %copy-start.3 = (f32[32,32,128]{2,1,0:T(8,128)}, f32[32,32,128]{2,1,0:T(8,128)S(1)}, u32[]{:S(2)}) copy-start(f32[32,32,128]{2,1,0:T(8,128)S(1)} %collective-permute-done.17.refs_20_.refs_23_) | copy-start | bytes 1572868
  687.7 15.5 %copy-start.4 = (f32[56,16,128]{2,1,0:T(8,128)}, f32[56,16,128]{2,1,0:T(8,128)S(1)}, u32[]{:S(2)}) copy-start(f32[56,16,128]{2,1,0:T(8,128)S(1)} %collective-permute-done.10.refs_13_) | copy-start | bytes 1376260
  689.4 13.8 %copy-start.5 = (f32[56,16,128]{2,1,0:T(8,128)}, f32[56,16,128]{2,1,0:T(8,128)S(1)}, u32[]{:S(2)}) copy-start(f32[56,16,128]{2,1,0:T(8,128)S(1)} %collective-permute-done.13.refs_16_) | copy-start | bytes 1376260
  702.4 0.8 copy-start.6
  702.4 0.9 copy-start.7

commit v7 on v6

--- a/solution.py
+++ b/solution.py
@@ -391,8 +391,10 @@
     own = [run_head(values, 0)]
     mirror = [mirrored_parts(own[0])]
     after, others[2], mirror[0] = tie((after, others[2], mirror[0]))
-    own.append(run_head(delivered(after), 1))
-    own.append(run_head(delivered(blocks(2)), 2))
+    values, after = tie((delivered(after), blocks(2)))
+    own.append(run_head(values, 1))
+    values, own[1] = tie((delivered(after), own[1]))
+    own.append(run_head(values, 2))
     mirror += [mirrored_parts(block) for block in own[1:]]
     quarters = 4
     bins = distogram_bias.shape[0] // quarters

time: 725 us -> 711 us (0.981); the launches traced: 711 us -> 706 us
  starting transfers between devices: 91.4 us -> 118 us
  blocking collectives: 26.2 us -> 0 us
    all_to_all x1 -> x0, blocking collectives: 26.2 us -> none  [delivered(): lax.all_to_all(values, ('lo', 'col'), split_axis=0, concat_axis=0, tiled=...]
    ppermute x17, starting transfers between devices: 49.4 us -> 69.6 us  [move(): return lax.ppermute(values, ('half', 'lo', 'col'), pairs)]
    all_to_all x2 -> x3, waiting for transfers between devices: 68.8 us -> 55.3 us  [delivered(): lax.all_to_all(values, ('lo', 'col'), split_axis=0, concat_axis=0, tiled=...]
    all_to_all x2 -> x3, starting transfers between devices: 12.6 us -> 19.3 us  [delivered(): lax.all_to_all(values, ('lo', 'col'), split_axis=0, concat_axis=0, tiled=...]
  transfers between devices with their start and end apart: 25 -> 26, of which waited for: 14 -> 16; matrix products, arithmetic and copies ran while one was open for 2% -> 2% of each run, Pallas kernels for 17% -> 17%
where the time goes in v7:
time: 711 us; the launch traced here: 706 us
  waiting for transfers between devices  417 us (59%)
  Pallas kernels  148 us (21%)
  starting transfers between devices  118 us (17%)
  local copies, waits for them, and re-layouts  14.9 us (2%)
  other arithmetic  7.41 us (1%)
    all_to_all x3, waiting for transfers between devices, spread(): lax.all_to_all(values, ('lo', 'col'), split_axis=0, concat_axis=0, tiled=...  283 us
    ppermute x17, waiting for transfers between devices, move(): return lax.ppermute(values, ('half', 'lo', 'col'), pairs)  77.1 us
    ppermute x17, starting transfers between devices, move(): return lax.ppermute(values, ('half', 'lo', 'col'), pairs)  69.6 us
    pallas_call x3, Pallas kernels, head(): pl.pallas_call(head_kernel, grid=(steps,), in_specs=[pl.BlockSpec((tile_r...  61.4 us
    all_to_all x3, waiting for transfers between devices, delivered(): lax.all_to_all(values, ('lo', 'col'), split_axis=0, concat_axis=0, tiled=...  55.3 us
    pallas_call x3, Pallas kernels, product(): pl.pallas_call(product_kernel, grid_spec=pltpu.PrefetchScalarGridSpec(num...  44 us
    pallas_call x3, Pallas kernels, hands(): pl.pallas_call(hands_kernel, grid=(rows // GROUP,), in_specs=[pl.BlockSpe...  35.6 us
    all_to_all x3, starting transfers between devices, spread(): lax.all_to_all(values, ('lo', 'col'), split_axis=0, concat_axis=0, tiled=...  25.8 us
  transfers between devices with their start and end apart: 26, of which 16 were waited for; matrix products, arithmetic and copies ran while one was open for 2% of the time, Pallas kernels for 17%

profile of v7, /device:TPU:12, one launch (start us, length us, event | category | flops | bytes accessed | tf_op | source)
XLA Modules:
  0.0 705.6 jit_solution(13209041950720530899)
XLA Ops:
  2.6 6.4 hands.5
  9.0 5.1 all-to-all-start.1
  14.1 13.1 %hands.3 = f32[128,96,128]{2,1,0:T(8,128)} custom-call(f32[128,128,128]{2,1,0:T(8,128)} %bitcast.32, bf16[512,384]{1,0:T(8,128)(2,1)} %pad_maximum_fusion.1.weights_ref), custom_call_target="tpu_custom_call" | custom-call | flops 301989888 | bytes 1572864 | tf_op jit(solution)/shard_map/hands/pallas_call | solution.py:131
  27.2 17.7 %all-to-all-done.1.own_ref = f32[8,16,40,128]{3,2,1,0:T(8,128)S(1)} async-done(((f32[8,16,40,128]{3,2,1,0:T(8,128)}), f32[8,16,40,128]{3,2,1,0:T(8,128)S(1)}, u32[]{:S(2)}, u32[]{:S(2)}) %all-to-all-start.1) | async-done | bytes 2621472 | tf_op jit(solution)/shard_map/all_to_all | solution.py:353
  44.9 7.2 %all-to-all-start = ((f32[8,16,96,128]{3,2,1,0:T(8,128)}), f32[8,16,96,128]{3,2,1,0:T(8,128)}, u32[]{:S(2)}, u32[]{:S(2)}) async-start(f32[8,16,96,128]{3,2,1,0:T(8,128)} %bitcast.38), calls=%async_computation | async-start | bytes 12582912 | tf_op jit(solution)/shard_map/all_to_all | solution.py:353
  52.1 2.6 collective-permute-start
  54.7 16.2 %hands.4 = f32[128,120,128]{2,1,0:T(8,128)} custom-call(f32[128,128,128]{2,1,0:T(8,128)} %bitcast.33, bf16[512,384]{1,0:T(8,128)(2,1)} %pad_maximum_fusion.1.weights_ref), custom_call_target="tpu_custom_call" | custom-call | flops 377487360 | bytes 1966080 | tf_op jit(solution)/shard_map/hands/pallas_call | solution.py:131
  70.9 103.9 %all-to-all-done.low_ref = f32[8,16,96,128]{3,2,1,0:T(8,128)} async-done(((f32[8,16,96,128]{3,2,1,0:T(8,128)}), f32[8,16,96,128]{3,2,1,0:T(8,128)}, u32[]{:S(2)}, u32[]{:S(2)}) %all-to-all-start) | async-done | bytes 6291488 | tf_op jit(solution)/shard_map/all_to_all | solution.py:353
  174.7 4.2 slice.8.own_ref
  178.9 13.5 %all-to-all-start.2 = ((f32[8,16,120,128]{3,2,1,0:T(8,128)}), f32[8,16,120,128]{3,2,1,0:T(8,128)}, u32[]{:S(2)}, u32[]{:S(2)}) async-start(f32[8,16,120,128]{3,2,1,0:T(8,128)} %bitcast.37), calls=%async_computation.2 | async-start | bytes 15728640 | tf_op jit(solution)/shard_map/all_to_all | solution.py:353
  192.4 161.0 %all-to-all-done.2.high_ref = f32[8,16,120,128]{3,2,1,0:T(8,128)} async-done(((f32[8,16,120,128]{3,2,1,0:T(8,128)}), f32[8,16,120,128]{3,2,1,0:T(8,128)}, u32[]{:S(2)}, u32[]{:S(2)}) %all-to-all-start.2) | async-done | bytes 7864352 | tf_op jit(solution)/shard_map/all_to_all | solution.py:353
  353.3 3.1 slice.9.own_ref
  356.4 14.6 %product.3 = f32[8,16,40,128]{3,2,1,0:T(8,128)} custom-call(s32[1]{0:T(128)} %bitcast.1.half_ref, f32[8,16,96,128]{3,2,1,0:T(8,128)} %all-to-all-done.low_ref, f32[8,16,120,128]{3,2,1,0:T(8,128)} %all-to-all-done.2.high_ref, f32[8,16,40,128]{3,2,1,0:T(8,128)} %copy-done, f32[8,16,40,128]{3,2,1,0:T(8,128)} %collective-permute-done.other_ref), custom_call_target="tpu_custom_call" | custom-call | flops 251658240 | bytes 1703936 | tf_op jit(solution)/shard_map/product/pallas_call | solution.py:180
  371.1 6.6 all-to-all-start.3
  379.5 1.2 copy.15
  381.9 1.3 pad_maximum_fusion.5.bins_ref
  387.1 15.3 %product.4 = f32[8,16,56,128]{3,2,1,0:T(8,128)} custom-call(s32[1]{0:T(128)} %bitcast.1.half_ref, f32[8,16,96,128]{3,2,1,0:T(8,128)} %all-to-all-done.low_ref, f32[8,16,120,128]{3,2,1,0:T(8,128)} %all-to-all-done.2.high_ref, f32[8,16,56,128]{3,2,1,0:T(8,128)} %slice.8.own_ref, f32[8,16,56,128]{3,2,1,0:T(8,128)} %collective-permute-done.1.other_ref), custom_call_target="tpu_custom_call" | custom-call | flops 352321536 | bytes 1966080 | tf_op jit(solution)/shard_map/product/pallas_call | solution.py:180
  402.4 29.1 %all-to-all-done.3 = f32[8,16,40,128]{3,2,1,0:T(8,128)S(1)} async-done(((f32[8,16,40,128]{3,2,1,0:T(8,128)}), f32[8,16,40,128]{3,2,1,0:T(8,128)S(1)}, u32[]{:S(2)}, u32[]{:S(2)}) %all-to-all-start.3) | async-done | bytes 2621472 | tf_op jit(solution)/shard_map/all_to_all | solution.py:367
  431.6 1.5 copy-done.1
  433.1 19.2 %head.3 = (f32[40,16,128]{2,1,0:T(8,128)}, f32[40,16,128]{2,1,0:T(8,128)}, f32[40,16,128]{2,1,0:T(8,128)}, f32[40,16,128]{2,1,0:T(8,128)}) custom-call(f32[128,128,128]{2,1,0:T(8,128)} %bitcast.34, f32[128,40,128]{2,1,0:T(8,128)} %bitcast.39, bf16[128,384]{1,0:T(8,128)(2,1)} %get-tuple-element.79.gate_ref, bf16[128,384]{1,0:T(8,128)(2,1)} %get-tuple-element.80.output_ref, ...), custom_call_target="tpu_custom_call" | custom-call | flops 912261120 | bytes 819200 | tf_op jit(solution)/shard_map/head/pallas_call | solution.py:234
  452.3 2.7 collective-permute-start.4
  456.5 5.5 collective-permute-start.3
  462.0 1.8 collective-permute-done.4
  463.8 5.4 collective-permute-start.5
  469.3 13.4 %collective-permute-start.7 = (f32[40,16,128]{2,1,0:T(8,128)S(1)}, f32[40,16,128]{2,1,0:T(8,128)}, u32[]{:S(2)}, u32[]{:S(2)}) collective-permute-start(f32[40,16,128]{2,1,0:T(8,128)S(1)} %collective-permute-done.6), channel_id=1, source_target_pairs={{0,8},{1,12},{2,0},{3,4},{4,9},{5,13},{6,1},{7,5},{8,10},{9,14},{1... | collective-permute-start | bytes 983048 | tf_op jit(solution)/shard_map/ppermute | solution.py:307
  482.7 1.5 collective-permute-done.2.other_ref
  484.2 10.8 %collective-permute-done.3.refs_12_ = f32[40,16,128]{2,1,0:T(8,128)} collective-permute-done((f32[40,16,128]{2,1,0:T(8,128)}, f32[40,16,128]{2,1,0:T(8,128)}, u32[]{:S(2)}, u32[]{:S(2)}) %collective-permute-start.3) | collective-permute-done | bytes 327712 | tf_op jit(solution)/shard_map/ppermute | solution.py:307
  495.0 3.7 collective-permute-done.5.refs_15_
  499.1 6.6 all-to-all-start.4
  505.7 14.1 %product.5 = f32[8,16,32,128]{3,2,1,0:T(8,128)} custom-call(s32[1]{0:T(128)} %bitcast.1.half_ref, f32[8,16,96,128]{3,2,1,0:T(8,128)} %all-to-all-done.low_ref, f32[8,16,120,128]{3,2,1,0:T(8,128)} %all-to-all-done.2.high_ref, f32[8,16,32,128]{3,2,1,0:T(8,128)} %slice.9.own_ref, f32[8,16,32,128]{3,2,1,0:T(8,128)} %collective-permute-done.2.other_ref), custom_call_target="tpu_custom_call" | custom-call | flops 201326592 | bytes 1572864 | tf_op jit(solution)/shard_map/product/pallas_call | solution.py:180
  519.8 26.2 %all-to-all-done.4 = f32[8,16,56,128]{3,2,1,0:T(8,128)} async-done(((f32[8,16,56,128]{3,2,1,0:T(8,128)}), f32[8,16,56,128]{3,2,1,0:T(8,128)}, u32[]{:S(2)}, u32[]{:S(2)}) %all-to-all-start.4) | async-done | bytes 3670048 | tf_op jit(solution)/shard_map/all_to_all | solution.py:367
  546.0 6.1 all-to-all-start.5
  552.1 26.1 %head.4 = (f32[56,16,128]{2,1,0:T(8,128)}, f32[56,16,128]{2,1,0:T(8,128)}, f32[56,16,128]{2,1,0:T(8,128)}, f32[56,16,128]{2,1,0:T(8,128)}) custom-call(f32[128,128,128]{2,1,0:T(8,128)} %bitcast.35, f32[128,56,128]{2,1,0:T(8,128)} %bitcast.12.product_ref, bf16[128,384]{1,0:T(8,128)(2,1)} %get-tuple-element.79.gate_ref, ...), custom_call_target="tpu_custom_call" | custom-call | flops 1277165568 | bytes 1146880 | tf_op jit(solution)/shard_map/head/pallas_call | solution.py:234
  578.3 1.3 copy-done.2
  579.6 16.0 %head.5 = (f32[32,32,128]{2,1,0:T(8,128)}, f32[32,32,128]{2,1,0:T(8,128)}) custom-call(f32[128,128,128]{2,1,0:T(8,128)} %bitcast.36, f32[128,32,128]{2,1,0:T(8,128)} %bitcast.41, bf16[128,384]{1,0:T(8,128)(2,1)} %get-tuple-element.79.gate_ref, bf16[128,384]{1,0:T(8,128)(2,1)} %get-tuple-element.80.output_ref, bf16[1024,384]{1,0:T(8,128)(2,1)} %pad_maximum_fusion.up_ref, ...), custom_call_target="tpu_custom_call" | custom-call | flops 729808896 | bytes 655360 | tf_op jit(solution)/shard_map/head/pallas_call | solution.py:234
  596.2 1.5 collective-permute-start.12
  597.7 1.5 collective-permute-start.14
  599.7 3.0 collective-permute-start.10
  602.7 7.0 collective-permute-done.12
  609.8 3.0 collective-permute-start.11
  612.8 5.9 collective-permute-done.16
  618.7 23.4 %collective-permute-start.17 = (f32[32,32,128]{2,1,0:T(8,128)}, f32[32,32,128]{2,1,0:T(8,128)S(1)}, u32[]{:S(2)}, u32[]{:S(2)}) collective-permute-start(f32[32,32,128]{2,1,0:T(8,128)} %collective-permute-done.16), channel_id=1, source_target_pairs={{0,8},{1,12},{2,0},{3,4},{4,9},{5,13},{6,1},{7,5},{8,10},{9,14},{1... | collective-permute-start | bytes 1572872 | tf_op jit(solution)/shard_map/ppermute | solution.py:307
  642.2 7.5 %collective-permute-start.13 = (f32[56,16,128]{2,1,0:T(8,128)}, f32[56,16,128]{2,1,0:T(8,128)S(1)}, u32[]{:S(2)}, u32[]{:S(2)}) collective-permute-start(f32[56,16,128]{2,1,0:T(8,128)} %collective-permute-done.12), channel_id=1, source_target_pairs={{0,4},{1,0},{2,12},{3,8},{4,5},{5,1},{6,13},{7,9},{8,6},{9,2},{10,... | collective-permute-start | bytes 1376264 | tf_op jit(solution)/shard_map/ppermute | solution.py:307
  649.7 12.5 %collective-permute-done.18 = f32[56,16,128]{2,1,0:T(8,128)} collective-permute-done((f32[56,16,128]{2,1,0:T(8,128)S(1)}, f32[56,16,128]{2,1,0:T(8,128)}, u32[]{:S(2)}, u32[]{:S(2)}) %collective-permute-start.18) | collective-permute-done | bytes 458784 | tf_op jit(solution)/shard_map/ppermute | solution.py:307
  662.4 2.1 collective-permute-done.11.refs_14_.refs_17_
  664.5 5.2 collective-permute-done.13.refs_16_
  669.7 27.6 %collective-permute-done.15.refs_19_ = f32[56,16,128]{2,1,0:T(8,128)S(1)} collective-permute-done((f32[56,16,128]{2,1,0:T(8,128)}, f32[56,16,128]{2,1,0:T(8,128)S(1)}, u32[]{:S(2)}, u32[]{:S(2)}) %collective-permute-start.15) | collective-permute-done | bytes 458784 | tf_op jit(solution)/shard_map/ppermute | solution.py:307
  698.4 7.1 %symmetric.1 = f32[128,4,16,128]{3,2,1,0:T(8,128)} custom-call(f32[4,16,128]{2,1,0:T(8,128)} %broadcast_in_dim.7.bias_ref, f32[40,16,128]{2,1,0:T(8,128)} %get-tuple-element.42.refs_0_, f32[56,16,128]{2,1,0:T(8,128)} %get-tuple-element.56.refs_1_, f32[32,32,128]{2,1,0:T(8,128)} %get-tuple-element.58.refs_2_.refs_5_, ...), custom_call_target="tpu_custom_call" | custom-call | bytes 1572864 | tf_op jit(solution)/shard_map/symmetric/pallas_call | solution.py:292
  (70 shorter events, 13.8 us)
Async XLA Ops:
  9.0 36.0 %all-to-all-start.1 = ((f32[8,16,40,128]{3,2,1,0:T(8,128)}), f32[8,16,40,128]{3,2,1,0:T(8,128)S(1)}, u32[]{:S(2)}, u32[]{:S(2)}) async-start(f32[8,16,40,128]{3,2,1,0:T(8,128)} %bitcast.40), calls=%async_computation.1 | async-start | bytes 5242880 | tf_op jit(solution)/shard_map/all_to_all | solution.py:353
  44.9 7.2 %copy-start = (f32[8,16,40,128]{3,2,1,0:T(8,128)}, f32[8,16,40,128]{3,2,1,0:T(8,128)S(1)}, u32[]{:S(2)}) copy-start(f32[8,16,40,128]{3,2,1,0:T(8,128)S(1)} %all-to-all-done.1.own_ref) | copy-start | bytes 7864324
  44.9 129.8 %all-to-all-start = ((f32[8,16,96,128]{3,2,1,0:T(8,128)}), f32[8,16,96,128]{3,2,1,0:T(8,128)}, u32[]{:S(2)}, u32[]{:S(2)}) async-start(f32[8,16,96,128]{3,2,1,0:T(8,128)} %bitcast.38), calls=%async_computation | async-start | bytes 12582912 | tf_op jit(solution)/shard_map/all_to_all | solution.py:353
  52.1 126.8 %collective-permute-start = (f32[8,16,40,128]{3,2,1,0:T(8,128)S(1)}, f32[8,16,40,128]{3,2,1,0:T(8,128)}, u32[]{:S(2)}, u32[]{:S(2)}) collective-permute-start(f32[8,16,40,128]{3,2,1,0:T(8,128)S(1)} %all-to-all-done.1.own_ref), channel_id=1, source_target_pairs={{0,8},{8,0},{1,9},{9,1},{2,10},{10,2},{3,11},{11,3},{4,12},{12,4},... | collective-permute-start | bytes 7864328 | tf_op jit(solution)/shard_map/ppermute | solution.py:361
  178.9 174.5 %all-to-all-start.2 = ((f32[8,16,120,128]{3,2,1,0:T(8,128)}), f32[8,16,120,128]{3,2,1,0:T(8,128)}, u32[]{:S(2)}, u32[]{:S(2)}) async-start(f32[8,16,120,128]{3,2,1,0:T(8,128)} %bitcast.37), calls=%async_computation.2 | async-start | bytes 15728640 | tf_op jit(solution)/shard_map/all_to_all | solution.py:353
  192.4 178.7 %collective-permute-start.1 = (f32[8,16,56,128]{3,2,1,0:T(8,128)}, f32[8,16,56,128]{3,2,1,0:T(8,128)}, u32[]{:S(2)}, u32[]{:S(2)}) collective-permute-start(f32[8,16,56,128]{3,2,1,0:T(8,128)} %slice.8.own_ref), channel_id=1, source_target_pairs={{0,8},{8,0},{1,9},{9,1},{2,10},{10,2},{3,11},{11,3},{4,12},{12,4},... | collective-permute-start | bytes 11010056 | tf_op jit(solution)/shard_map/ppermute | solution.py:361
  371.1 6.6 copy-start.13
  371.1 6.7 copy-start.16
  371.1 7.7 %copy-start.15 = (f32[128,64]{0,1:T(8,128)S(1)}, f32[128,64]{0,1:T(8,128)}, u32[]{:S(2)}) copy-start(f32[128,64]{0,1:T(8,128)} %param.20) | copy-start | bytes 98308
  371.1 8.4 %copy-start.14 = (f32[128,128]{1,0:T(8,128)S(1)}, f32[128,128]{1,0:T(8,128)}, u32[]{:S(2)}) copy-start(f32[128,128]{1,0:T(8,128)} %param.15) | copy-start | bytes 196612
  371.1 60.5 %all-to-all-start.3 = ((f32[8,16,40,128]{3,2,1,0:T(8,128)}), f32[8,16,40,128]{3,2,1,0:T(8,128)S(1)}, u32[]{:S(2)}, u32[]{:S(2)}) async-start(f32[8,16,40,128]{3,2,1,0:T(8,128)} %product.3), calls=%async_computation.3 | async-start | bytes 5242880 | tf_op jit(solution)/shard_map/all_to_all | solution.py:367
  377.8 106.4 %collective-permute-start.2 = (f32[8,16,32,128]{3,2,1,0:T(8,128)}, f32[8,16,32,128]{3,2,1,0:T(8,128)}, u32[]{:S(2)}, u32[]{:S(2)}) collective-permute-start(f32[8,16,32,128]{3,2,1,0:T(8,128)} %slice.9.own_ref), channel_id=1, source_target_pairs={{0,8},{8,0},{1,9},{9,1},{2,10},{10,2},{3,11},{11,3},{4,12},{12,4},... | collective-permute-start | bytes 6291464 | tf_op jit(solution)/shard_map/ppermute | solution.py:361
  431.6 1.5 copy-start.1
  452.3 11.5 %collective-permute-start.4 = (f32[40,16,128]{2,1,0:T(8,128)}, f32[40,16,128]{2,1,0:T(8,128)S(1)}, u32[]{:S(2)}, u32[]{:S(2)}) collective-permute-start(f32[40,16,128]{2,1,0:T(8,128)} %get-tuple-element.45.refs_3_), channel_id=1, source_target_pairs={{0,1},{1,0},{2,3},{3,2},{4,5},{5,4},{6,7},{7,6},{8,9},{9,8},{10,11... | collective-permute-start | bytes 983048 | tf_op jit(solution)/shard_map/ppermute | solution.py:307
  455.0 14.3 %collective-permute-start.6 = (f32[40,16,128]{2,1,0:T(8,128)}, f32[40,16,128]{2,1,0:T(8,128)S(1)}, u32[]{:S(2)}, u32[]{:S(2)}) collective-permute-start(f32[40,16,128]{2,1,0:T(8,128)} %get-tuple-element.46.refs_6_), channel_id=1, source_target_pairs={{0,2},{1,3},{2,0},{3,1},{4,6},{5,7},{6,4},{7,5},{8,10},{9,11},{10,... | collective-permute-start | bytes 983048 | tf_op jit(solution)/shard_map/ppermute | solution.py:307
  455.5 27.1 %collective-permute-start.8 = (f32[40,16,128]{2,1,0:T(8,128)}, f32[40,16,128]{2,1,0:T(8,128)S(1)}, u32[]{:S(2)}, u32[]{:S(2)}) collective-permute-start(f32[40,16,128]{2,1,0:T(8,128)} %get-tuple-element.47.refs_9_), channel_id=1, source_target_pairs={{0,3},{1,2},{2,1},{3,0},{4,7},{5,6},{6,5},{7,4},{8,11},{9,10},{10,... | collective-permute-start | bytes 983048 | tf_op jit(solution)/shard_map/ppermute | solution.py:307
  456.5 38.5 %collective-permute-start.3 = (f32[40,16,128]{2,1,0:T(8,128)}, f32[40,16,128]{2,1,0:T(8,128)}, u32[]{:S(2)}, u32[]{:S(2)}) collective-permute-start(f32[40,16,128]{2,1,0:T(8,128)} %get-tuple-element.42.refs_0_), channel_id=1, source_target_pairs={{0,0},{1,4},{2,8},{3,12},{4,1},{5,5},{6,9},{7,13},{8,2},{9,6},{10,... | collective-permute-start | bytes 983048 | tf_op jit(solution)/shard_map/ppermute | solution.py:307
  463.8 34.9 %collective-permute-start.5 = (f32[40,16,128]{2,1,0:T(8,128)S(1)}, f32[40,16,128]{2,1,0:T(8,128)}, u32[]{:S(2)}, u32[]{:S(2)}) collective-permute-start(f32[40,16,128]{2,1,0:T(8,128)S(1)} %collective-permute-done.4), channel_id=1, source_target_pairs={{0,4},{1,0},{2,12},{3,8},{4,5},{5,1},{6,13},{7,9},{8,6},{9,2},{10,... | collective-permute-start | bytes 983048 | tf_op jit(solution)/shard_map/ppermute | solution.py:307
  469.3 29.5 %collective-permute-start.7 = (f32[40,16,128]{2,1,0:T(8,128)S(1)}, f32[40,16,128]{2,1,0:T(8,128)}, u32[]{:S(2)}, u32[]{:S(2)}) collective-permute-start(f32[40,16,128]{2,1,0:T(8,128)S(1)} %collective-permute-done.6), channel_id=1, source_target_pairs={{0,8},{1,12},{2,0},{3,4},{4,9},{5,13},{6,1},{7,5},{8,10},{9,14},{1... | collective-permute-start | bytes 983048 | tf_op jit(solution)/shard_map/ppermute | solution.py:307
  482.6 16.5 %collective-permute-start.9 = (f32[40,16,128]{2,1,0:T(8,128)S(1)}, f32[40,16,128]{2,1,0:T(8,128)}, u32[]{:S(2)}, u32[]{:S(2)}) collective-permute-start(f32[40,16,128]{2,1,0:T(8,128)S(1)} %collective-permute-done.8), channel_id=1, source_target_pairs={{0,12},{1,8},{2,4},{3,0},{4,13},{5,9},{6,5},{7,1},{8,14},{9,10},{1... | collective-permute-start | bytes 983048 | tf_op jit(solution)/shard_map/ppermute | solution.py:307
  499.1 46.9 %all-to-all-start.4 = ((f32[8,16,56,128]{3,2,1,0:T(8,128)}), f32[8,16,56,128]{3,2,1,0:T(8,128)}, u32[]{:S(2)}, u32[]{:S(2)}) async-start(f32[8,16,56,128]{3,2,1,0:T(8,128)} %product.4), calls=%async_computation.4 | async-start | bytes 7340032 | tf_op jit(solution)/shard_map/all_to_all | solution.py:367
  546.0 32.3 %all-to-all-start.5 = ((f32[8,16,32,128]{3,2,1,0:T(8,128)}), f32[8,16,32,128]{3,2,1,0:T(8,128)S(1)}, u32[]{:S(2)}, u32[]{:S(2)}) async-start(f32[8,16,32,128]{3,2,1,0:T(8,128)} %product.5), calls=%async_computation.5 | async-start | bytes 4194304 | tf_op jit(solution)/shard_map/all_to_all | solution.py:367
  578.3 1.3 copy-start.2
  579.6 16.6 %copy-start.6 = (f32[56,16,128]{2,1,0:T(8,128)S(1)}, f32[56,16,128]{2,1,0:T(8,128)}, u32[]{:S(2)}) copy-start(f32[56,16,128]{2,1,0:T(8,128)} %get-tuple-element.59.refs_4_) | copy-start | bytes 1376260
  579.6 18.1 %copy-start.7 = (f32[56,16,128]{2,1,0:T(8,128)S(1)}, f32[56,16,128]{2,1,0:T(8,128)}, u32[]{:S(2)}) copy-start(f32[56,16,128]{2,1,0:T(8,128)} %get-tuple-element.60.refs_7_) | copy-start | bytes 1376260
  579.6 19.5 %copy-start.8 = (f32[56,16,128]{2,1,0:T(8,128)S(1)}, f32[56,16,128]{2,1,0:T(8,128)}, u32[]{:S(2)}) copy-start(f32[56,16,128]{2,1,0:T(8,128)} %get-tuple-element.62.refs_10_) | copy-start | bytes 1376260
  579.6 20.1 %copy-start.5 = (f32[56,16,128]{2,1,0:T(8,128)S(1)}, f32[56,16,128]{2,1,0:T(8,128)}, u32[]{:S(2)}) copy-start(f32[56,16,128]{2,1,0:T(8,128)} %get-tuple-element.56.refs_1_) | copy-start | bytes 1376260
  579.6 82.7 %copy-start.17 = (f32[64]{0:T(128)S(1)}, f32[64]{0:T(128)}, u32[]{:S(2)}) copy-start(f32[64]{0:T(128)} %param.21) | copy-start | bytes 772
  595.6 23.1 %collective-permute-start.16 = (f32[32,32,128]{2,1,0:T(8,128)}, f32[32,32,128]{2,1,0:T(8,128)}, u32[]{:S(2)}, u32[]{:S(2)}) collective-permute-start(f32[32,32,128]{2,1,0:T(8,128)} %get-tuple-element.61.refs_8_.refs_11_), channel_id=1, source_target_pairs={{0,2},{1,3},{2,0},{3,1},{4,6},{5,7},{6,4},{7,5},{8,10},{9,11},{10,... | collective-permute-start | bytes 1572872 | tf_op jit(solution)/shard_map/ppermute | solution.py:307
  596.2 13.6 %collective-permute-start.12 = (f32[56,16,128]{2,1,0:T(8,128)S(1)}, f32[56,16,128]{2,1,0:T(8,128)}, u32[]{:S(2)}, u32[]{:S(2)}) collective-permute-start(f32[56,16,128]{2,1,0:T(8,128)S(1)} %copy-done.6), channel_id=1, source_target_pairs={{0,1},{1,0},{2,3},{3,2},{4,5},{5,4},{6,7},{7,6},{8,9},{9,8},{10,11... | collective-permute-start | bytes 1376264 | tf_op jit(solution)/shard_map/ppermute | solution.py:307
  597.7 44.5 %collective-permute-start.14 = (f32[56,16,128]{2,1,0:T(8,128)S(1)}, f32[56,16,128]{2,1,0:T(8,128)}, u32[]{:S(2)}, u32[]{:S(2)}) collective-permute-start(f32[56,16,128]{2,1,0:T(8,128)S(1)} %copy-done.7), channel_id=1, source_target_pairs={{0,2},{1,3},{2,0},{3,1},{4,6},{5,7},{6,4},{7,5},{8,10},{9,11},{10,... | collective-permute-start | bytes 1376264 | tf_op jit(solution)/shard_map/ppermute | solution.py:307
  599.1 63.1 %collective-permute-start.18 = (f32[56,16,128]{2,1,0:T(8,128)S(1)}, f32[56,16,128]{2,1,0:T(8,128)}, u32[]{:S(2)}, u32[]{:S(2)}) collective-permute-start(f32[56,16,128]{2,1,0:T(8,128)S(1)} %copy-done.8), channel_id=1, source_target_pairs={{0,3},{1,2},{2,1},{3,0},{4,7},{5,6},{6,5},{7,4},{8,11},{9,10},{10,... | collective-permute-start | bytes 1376264 | tf_op jit(solution)/shard_map/ppermute | solution.py:307
  599.7 62.5 %collective-permute-start.10 = (f32[56,16,128]{2,1,0:T(8,128)S(1)}, f32[56,16,128]{2,1,0:T(8,128)S(1)}, u32[]{:S(2)}, u32[]{:S(2)}) collective-permute-start(f32[56,16,128]{2,1,0:T(8,128)S(1)} %copy-done.5), channel_id=1, source_target_pairs={{0,0},{1,4},{2,8},{3,12},{4,1},{5,5},{6,9},{7,13},{8,2},{9,6},{10,... | collective-permute-start | bytes 1376264 | tf_op jit(solution)/shard_map/ppermute | solution.py:307
  609.8 54.7 %collective-permute-start.11 = (f32[32,32,128]{2,1,0:T(8,128)}, f32[32,32,128]{2,1,0:T(8,128)S(1)}, u32[]{:S(2)}, u32[]{:S(2)}) collective-permute-start(f32[32,32,128]{2,1,0:T(8,128)} %get-tuple-element.58.refs_2_.refs_5_), channel_id=1, source_target_pairs={{0,0},{1,4},{2,8},{3,12},{4,1},{5,5},{6,9},{7,13},{8,2},{9,6},{10,... | collective-permute-start | bytes 1572872 | tf_op jit(solution)/shard_map/ppermute | solution.py:307
  618.7 78.5 %collective-permute-start.17 = (f32[32,32,128]{2,1,0:T(8,128)}, f32[32,32,128]{2,1,0:T(8,128)S(1)}, u32[]{:S(2)}, u32[]{:S(2)}) collective-permute-start(f32[32,32,128]{2,1,0:T(8,128)} %collective-permute-done.16), channel_id=1, source_target_pairs={{0,8},{1,12},{2,0},{3,4},{4,9},{5,13},{6,1},{7,5},{8,10},{9,14},{1... | collective-permute-start | bytes 1572872 | tf_op jit(solution)/shard_map/ppermute | solution.py:307
  642.2 27.5 %collective-permute-start.13 = (f32[56,16,128]{2,1,0:T(8,128)}, f32[56,16,128]{2,1,0:T(8,128)S(1)}, u32[]{:S(2)}, u32[]{:S(2)}) collective-permute-start(f32[56,16,128]{2,1,0:T(8,128)} %collective-permute-done.12), channel_id=1, source_target_pairs={{0,4},{1,0},{2,12},{3,8},{4,5},{5,1},{6,13},{7,9},{8,6},{9,2},{10,... | collective-permute-start | bytes 1376264 | tf_op jit(solution)/shard_map/ppermute | solution.py:307
  662.2 35.1 %collective-permute-start.15 = (f32[56,16,128]{2,1,0:T(8,128)}, f32[56,16,128]{2,1,0:T(8,128)S(1)}, u32[]{:S(2)}, u32[]{:S(2)}) collective-permute-start(f32[56,16,128]{2,1,0:T(8,128)} %collective-permute-done.14), channel_id=1, source_target_pairs={{0,8},{1,12},{2,0},{3,4},{4,9},{5,13},{6,1},{7,5},{8,10},{9,14},{1... | collective-permute-start | bytes 1376264 | tf_op jit(solution)/shard_map/ppermute | solution.py:307
  662.2 35.9 %copy-start.9 = (f32[56,16,128]{2,1,0:T(8,128)}, f32[56,16,128]{2,1,0:T(8,128)S(1)}, u32[]{:S(2)}) copy-start(f32[56,16,128]{2,1,0:T(8,128)S(1)} %collective-permute-done.10.refs_13_) | copy-start | bytes 1376260
  662.2 35.0 %collective-permute-start.19 = (f32[56,16,128]{2,1,0:T(8,128)}, f32[56,16,128]{2,1,0:T(8,128)S(1)}, u32[]{:S(2)}, u32[]{:S(2)}) collective-permute-start(f32[56,16,128]{2,1,0:T(8,128)} %collective-permute-done.18), channel_id=1, source_target_pairs={{0,12},{1,8},{2,4},{3,0},{4,13},{5,9},{6,5},{7,1},{8,14},{9,10},{1... | collective-permute-start | bytes 1376264 | tf_op jit(solution)/shard_map/ppermute | solution.py:307
  664.5 33.6 %copy-start.3 = (f32[32,32,128]{2,1,0:T(8,128)}, f32[32,32,128]{2,1,0:T(8,128)S(1)}, u32[]{:S(2)}) copy-start(f32[32,32,128]{2,1,0:T(8,128)S(1)} %collective-permute-done.11.refs_14_.refs_17_) | copy-start | bytes 1572868
  669.7 28.4 %copy-start.10 = (f32[56,16,128]{2,1,0:T(8,128)}, f32[56,16,128]{2,1,0:T(8,128)S(1)}, u32[]{:S(2)}) copy-start(f32[56,16,128]{2,1,0:T(8,128)S(1)} %collective-permute-done.13.refs_16_) | copy-start | bytes 1376260
  697.2 0.9 copy-start.11
  697.3 0.9 copy-start.12
  697.3 1.1 copy-start.4

commit v8 on v7

--- a/solution.py
+++ b/solution.py
@@ -12,7 +12,7 @@
 GROUP = 8
 CHUNKS = (40, 56, 32)
 LOWER = 40
-PARTS = (4, 4, 2)
+PARTS = (4, 4, 4)
 VMEM = 56 * 1024 * 1024
 SCALE = 8
 

time: 711 us -> 721 us (1.014)
  waiting for transfers between devices: 417 us -> 432 us
    ppermute x17 -> x21, waiting for transfers between devices: 77.1 us -> 92.3 us  [move(): return lax.ppermute(values, ('half', 'lo', 'col'), pairs)]
    ppermute x17 -> x21, starting transfers between devices: 69.6 us -> 62.8 us  [move(): return lax.ppermute(values, ('half', 'lo', 'col'), pairs)]
  transfers between devices with their start and end apart: 26 -> 30, of which waited for: 16 -> 15; matrix products, arithmetic and copies ran while one was open for 2% -> 2% of each run, Pallas kernels for 17% -> 17%
where the time goes in v8:
time: 721 us; the launch traced here: 714 us
  waiting for transfers between devices  432 us (60%)
  Pallas kernels  148 us (21%)
  starting transfers between devices  111 us (15%)
  local copies, waits for them, and re-layouts  15 us (2%)
  other arithmetic  7.34 us (1%)
    all_to_all x3, waiting for transfers between devices, spread(): lax.all_to_all(values, ('lo', 'col'), split_axis=0, concat_axis=0, tiled=...  283 us
    ppermute x21, waiting for transfers between devices, move(): return lax.ppermute(values, ('half', 'lo', 'col'), pairs)  92.3 us
    ppermute x21, starting transfers between devices, move(): return lax.ppermute(values, ('half', 'lo', 'col'), pairs)  62.8 us
    pallas_call x3, Pallas kernels, head(): pl.pallas_call(head_kernel, grid=(steps,), in_specs=[pl.BlockSpec((tile_r...  61.4 us
    all_to_all x3, waiting for transfers between devices, delivered(): lax.all_to_all(values, ('lo', 'col'), split_axis=0, concat_axis=0, tiled=...  55.4 us
    pallas_call x3, Pallas kernels, product(): pl.pallas_call(product_kernel, grid_spec=pltpu.PrefetchScalarGridSpec(num...  44.1 us
    pallas_call x3, Pallas kernels, hands(): pl.pallas_call(hands_kernel, grid=(rows // GROUP,), in_specs=[pl.BlockSpe...  35.7 us
    all_to_all x3, starting transfers between devices, spread(): lax.all_to_all(values, ('lo', 'col'), split_axis=0, concat_axis=0, tiled=...  25.8 us
  transfers between devices with their start and end apart: 30, of which 15 were waited for; matrix products, arithmetic and copies ran while one was open for 2% of the time, Pallas kernels for 17%

profile of v8, /device:TPU:12, one launch (start us, length us, event | category | flops | bytes accessed | tf_op | source)
XLA Modules:
  0.0 714.1 jit_solution(5577845987960471595)
XLA Ops:
  2.6 6.4 hands.5
  8.9 5.1 all-to-all-start.1
  14.1 13.1 %hands.3 = f32[128,96,128]{2,1,0:T(8,128)} custom-call(f32[128,128,128]{2,1,0:T(8,128)} %bitcast.32, bf16[512,384]{1,0:T(8,128)(2,1)} %pad_maximum_fusion.1.weights_ref), custom_call_target="tpu_custom_call" | custom-call | flops 301989888 | bytes 1572864 | tf_op jit(solution)/shard_map/hands/pallas_call | solution.py:131
  27.2 17.7 %all-to-all-done.1.own_ref = f32[8,16,40,128]{3,2,1,0:T(8,128)S(1)} async-done(((f32[8,16,40,128]{3,2,1,0:T(8,128)}), f32[8,16,40,128]{3,2,1,0:T(8,128)S(1)}, u32[]{:S(2)}, u32[]{:S(2)}) %all-to-all-start.1) | async-done | bytes 2621472 | tf_op jit(solution)/shard_map/all_to_all | solution.py:353
  44.9 7.2 %all-to-all-start = ((f32[8,16,96,128]{3,2,1,0:T(8,128)}), f32[8,16,96,128]{3,2,1,0:T(8,128)}, u32[]{:S(2)}, u32[]{:S(2)}) async-start(f32[8,16,96,128]{3,2,1,0:T(8,128)} %bitcast.38), calls=%async_computation | async-start | bytes 12582912 | tf_op jit(solution)/shard_map/all_to_all | solution.py:353
  52.1 2.6 collective-permute-start
  54.7 16.2 %hands.4 = f32[128,120,128]{2,1,0:T(8,128)} custom-call(f32[128,128,128]{2,1,0:T(8,128)} %bitcast.33, bf16[512,384]{1,0:T(8,128)(2,1)} %pad_maximum_fusion.1.weights_ref), custom_call_target="tpu_custom_call" | custom-call | flops 377487360 | bytes 1966080 | tf_op jit(solution)/shard_map/hands/pallas_call | solution.py:131
  70.9 103.8 %all-to-all-done.low_ref = f32[8,16,96,128]{3,2,1,0:T(8,128)} async-done(((f32[8,16,96,128]{3,2,1,0:T(8,128)}), f32[8,16,96,128]{3,2,1,0:T(8,128)}, u32[]{:S(2)}, u32[]{:S(2)}) %all-to-all-start) | async-done | bytes 6291488 | tf_op jit(solution)/shard_map/all_to_all | solution.py:353
  174.7 4.2 slice.8.own_ref
  178.9 13.5 %all-to-all-start.2 = ((f32[8,16,120,128]{3,2,1,0:T(8,128)}), f32[8,16,120,128]{3,2,1,0:T(8,128)}, u32[]{:S(2)}, u32[]{:S(2)}) async-start(f32[8,16,120,128]{3,2,1,0:T(8,128)} %bitcast.37), calls=%async_computation.2 | async-start | bytes 15728640 | tf_op jit(solution)/shard_map/all_to_all | solution.py:353
  192.4 161.0 %all-to-all-done.2.high_ref = f32[8,16,120,128]{3,2,1,0:T(8,128)} async-done(((f32[8,16,120,128]{3,2,1,0:T(8,128)}), f32[8,16,120,128]{3,2,1,0:T(8,128)}, u32[]{:S(2)}, u32[]{:S(2)}) %all-to-all-start.2) | async-done | bytes 7864352 | tf_op jit(solution)/shard_map/all_to_all | solution.py:353
  353.3 3.1 slice.9.own_ref
  356.4 14.6 %product.3 = f32[8,16,40,128]{3,2,1,0:T(8,128)} custom-call(s32[1]{0:T(128)} %bitcast.1.half_ref, f32[8,16,96,128]{3,2,1,0:T(8,128)} %all-to-all-done.low_ref, f32[8,16,120,128]{3,2,1,0:T(8,128)} %all-to-all-done.2.high_ref, f32[8,16,40,128]{3,2,1,0:T(8,128)} %copy-done, f32[8,16,40,128]{3,2,1,0:T(8,128)} %collective-permute-done.other_ref), custom_call_target="tpu_custom_call" | custom-call | flops 251658240 | bytes 1703936 | tf_op jit(solution)/shard_map/product/pallas_call | solution.py:180
  371.1 6.6 all-to-all-start.3
  381.9 1.3 pad_maximum_fusion.5.bins_ref
  387.1 15.3 %product.4 = f32[8,16,56,128]{3,2,1,0:T(8,128)} custom-call(s32[1]{0:T(128)} %bitcast.1.half_ref, f32[8,16,96,128]{3,2,1,0:T(8,128)} %all-to-all-done.low_ref, f32[8,16,120,128]{3,2,1,0:T(8,128)} %all-to-all-done.2.high_ref, f32[8,16,56,128]{3,2,1,0:T(8,128)} %slice.8.own_ref, f32[8,16,56,128]{3,2,1,0:T(8,128)} %collective-permute-done.1.other_ref), custom_call_target="tpu_custom_call" | custom-call | flops 352321536 | bytes 1966080 | tf_op jit(solution)/shard_map/product/pallas_call | solution.py:180
  402.4 29.2 %all-to-all-done.3 = f32[8,16,40,128]{3,2,1,0:T(8,128)S(1)} async-done(((f32[8,16,40,128]{3,2,1,0:T(8,128)}), f32[8,16,40,128]{3,2,1,0:T(8,128)S(1)}, u32[]{:S(2)}, u32[]{:S(2)}) %all-to-all-start.3) | async-done | bytes 2621472 | tf_op jit(solution)/shard_map/all_to_all | solution.py:367
  431.6 1.5 copy-done.1
  433.1 19.2 %head.3 = (f32[40,16,128]{2,1,0:T(8,128)}, f32[40,16,128]{2,1,0:T(8,128)}, f32[40,16,128]{2,1,0:T(8,128)}, f32[40,16,128]{2,1,0:T(8,128)}) custom-call(f32[128,128,128]{2,1,0:T(8,128)} %bitcast.34, f32[128,40,128]{2,1,0:T(8,128)} %bitcast.39, bf16[128,384]{1,0:T(8,128)(2,1)} %get-tuple-element.83.gate_ref, bf16[128,384]{1,0:T(8,128)(2,1)} %get-tuple-element.84.output_ref, ...), custom_call_target="tpu_custom_call" | custom-call | flops 912261120 | bytes 819200 | tf_op jit(solution)/shard_map/head/pallas_call | solution.py:234
  452.3 2.7 collective-permute-start.4
  456.5 5.5 collective-permute-start.3
  462.0 1.8 collective-permute-done.4
  463.8 5.5 collective-permute-start.5
  469.3 13.4 %collective-permute-start.7 = (f32[40,16,128]{2,1,0:T(8,128)S(1)}, f32[40,16,128]{2,1,0:T(8,128)}, u32[]{:S(2)}, u32[]{:S(2)}) collective-permute-start(f32[40,16,128]{2,1,0:T(8,128)S(1)} %collective-permute-done.6), channel_id=1, source_target_pairs={{0,8},{1,12},{2,0},{3,4},{4,9},{5,13},{6,1},{7,5},{8,10},{9,14},{1... | collective-permute-start | bytes 983048 | tf_op jit(solution)/shard_map/ppermute | solution.py:307
  482.7 1.5 collective-permute-done.2.other_ref
  484.2 10.8 %collective-permute-done.3.refs_12_ = f32[40,16,128]{2,1,0:T(8,128)} collective-permute-done((f32[40,16,128]{2,1,0:T(8,128)}, f32[40,16,128]{2,1,0:T(8,128)}, u32[]{:S(2)}, u32[]{:S(2)}) %collective-permute-start.3) | collective-permute-done | bytes 327712 | tf_op jit(solution)/shard_map/ppermute | solution.py:307
  495.0 3.7 collective-permute-done.5.refs_15_
  499.2 6.5 all-to-all-start.4
  505.7 14.1 %product.5 = f32[8,16,32,128]{3,2,1,0:T(8,128)} custom-call(s32[1]{0:T(128)} %bitcast.1.half_ref, f32[8,16,96,128]{3,2,1,0:T(8,128)} %all-to-all-done.low_ref, f32[8,16,120,128]{3,2,1,0:T(8,128)} %all-to-all-done.2.high_ref, f32[8,16,32,128]{3,2,1,0:T(8,128)} %slice.9.own_ref, f32[8,16,32,128]{3,2,1,0:T(8,128)} %collective-permute-done.2.other_ref), custom_call_target="tpu_custom_call" | custom-call | flops 201326592 | bytes 1572864 | tf_op jit(solution)/shard_map/product/pallas_call | solution.py:180
  519.9 26.2 %all-to-all-done.4 = f32[8,16,56,128]{3,2,1,0:T(8,128)} async-done(((f32[8,16,56,128]{3,2,1,0:T(8,128)}), f32[8,16,56,128]{3,2,1,0:T(8,128)}, u32[]{:S(2)}, u32[]{:S(2)}) %all-to-all-start.4) | async-done | bytes 3670048 | tf_op jit(solution)/shard_map/all_to_all | solution.py:367
  546.1 6.1 all-to-all-start.5
  552.2 26.1 %head.4 = (f32[56,16,128]{2,1,0:T(8,128)}, f32[56,16,128]{2,1,0:T(8,128)}, f32[56,16,128]{2,1,0:T(8,128)}, f32[56,16,128]{2,1,0:T(8,128)}) custom-call(f32[128,128,128]{2,1,0:T(8,128)} %bitcast.35, f32[128,56,128]{2,1,0:T(8,128)} %bitcast.12.product_ref, bf16[128,384]{1,0:T(8,128)(2,1)} %get-tuple-element.83.gate_ref, ...), custom_call_target="tpu_custom_call" | custom-call | flops 1277165568 | bytes 1146880 | tf_op jit(solution)/shard_map/head/pallas_call | solution.py:234
  578.3 1.3 copy-done.2
  579.6 16.1 %head.5 = (f32[32,16,128]{2,1,0:T(8,128)}, f32[32,16,128]{2,1,0:T(8,128)}, f32[32,16,128]{2,1,0:T(8,128)}, f32[32,16,128]{2,1,0:T(8,128)}) custom-call(f32[128,128,128]{2,1,0:T(8,128)} %bitcast.36, f32[128,32,128]{2,1,0:T(8,128)} %bitcast.41, bf16[128,384]{1,0:T(8,128)(2,1)} %get-tuple-element.83.gate_ref, bf16[128,384]{1,0:T(8,128)(2,1)} %get-tuple-element.84.output_ref, ...), custom_call_target="tpu_custom_call" | custom-call | flops 729808896 | bytes 655360 | tf_op jit(solution)/shard_map/head/pallas_call | solution.py:234
  595.7 1.5 collective-permute-start.14
  597.8 1.4 collective-permute-start.22
  599.2 1.5 collective-permute-start.12
  601.3 3.9 collective-permute-done.14
  605.2 1.5 collective-permute-start.20
  606.7 5.0 collective-permute-done.18
  611.6 1.9 collective-permute-start.11
  613.6 23.4 %collective-permute-done.22 = f32[32,16,128]{2,1,0:T(8,128)} collective-permute-done((f32[32,16,128]{2,1,0:T(8,128)}, f32[32,16,128]{2,1,0:T(8,128)}, u32[]{:S(2)}, u32[]{:S(2)}) %collective-permute-start.22) | collective-permute-done | bytes 262176 | tf_op jit(solution)/shard_map/ppermute | solution.py:307
  637.0 3.0 collective-permute-start.10
  640.0 20.9 %collective-permute-start.15 = (f32[32,16,128]{2,1,0:T(8,128)S(1)}, f32[32,16,128]{2,1,0:T(8,128)S(1)}, u32[]{:S(2)}, u32[]{:S(2)}) collective-permute-start(f32[32,16,128]{2,1,0:T(8,128)S(1)} %collective-permute-done.14), channel_id=1, source_target_pairs={{0,4},{1,0},{2,12},{3,8},{4,5},{5,1},{6,13},{7,9},{8,6},{9,2},{10,... | collective-permute-start | bytes 786440 | tf_op jit(solution)/shard_map/ppermute | solution.py:307
  661.0 7.9 %collective-permute-done.20 = f32[56,16,128]{2,1,0:T(8,128)} collective-permute-done((f32[56,16,128]{2,1,0:T(8,128)S(1)}, f32[56,16,128]{2,1,0:T(8,128)}, u32[]{:S(2)}, u32[]{:S(2)}) %collective-permute-start.20) | collective-permute-done | bytes 458784 | tf_op jit(solution)/shard_map/ppermute | solution.py:307
  668.9 1.3 collective-permute-start.23
  670.4 35.3 %collective-permute-done.19.refs_20_ = f32[32,16,128]{2,1,0:T(8,128)S(1)} collective-permute-done((f32[32,16,128]{2,1,0:T(8,128)}, f32[32,16,128]{2,1,0:T(8,128)S(1)}, u32[]{:S(2)}, u32[]{:S(2)}) %collective-permute-start.19) | collective-permute-done | bytes 262176 | tf_op jit(solution)/shard_map/ppermute | solution.py:307
  706.9 7.0 symmetric.1
  (82 shorter events, 15.2 us)
Async XLA Ops:
  8.9 36.0 %all-to-all-start.1 = ((f32[8,16,40,128]{3,2,1,0:T(8,128)}), f32[8,16,40,128]{3,2,1,0:T(8,128)S(1)}, u32[]{:S(2)}, u32[]{:S(2)}) async-start(f32[8,16,40,128]{3,2,1,0:T(8,128)} %bitcast.40), calls=%async_computation.1 | async-start | bytes 5242880 | tf_op jit(solution)/shard_map/all_to_all | solution.py:353
  44.9 7.2 %copy-start = (f32[8,16,40,128]{3,2,1,0:T(8,128)}, f32[8,16,40,128]{3,2,1,0:T(8,128)S(1)}, u32[]{:S(2)}) copy-start(f32[8,16,40,128]{3,2,1,0:T(8,128)S(1)} %all-to-all-done.1.own_ref) | copy-start | bytes 7864324
  44.9 129.8 %all-to-all-start = ((f32[8,16,96,128]{3,2,1,0:T(8,128)}), f32[8,16,96,128]{3,2,1,0:T(8,128)}, u32[]{:S(2)}, u32[]{:S(2)}) async-start(f32[8,16,96,128]{3,2,1,0:T(8,128)} %bitcast.38), calls=%async_computation | async-start | bytes 12582912 | tf_op jit(solution)/shard_map/all_to_all | solution.py:353
  52.1 126.8 %collective-permute-start = (f32[8,16,40,128]{3,2,1,0:T(8,128)S(1)}, f32[8,16,40,128]{3,2,1,0:T(8,128)}, u32[]{:S(2)}, u32[]{:S(2)}) collective-permute-start(f32[8,16,40,128]{3,2,1,0:T(8,128)S(1)} %all-to-all-done.1.own_ref), channel_id=1, source_target_pairs={{0,8},{8,0},{1,9},{9,1},{2,10},{10,2},{3,11},{11,3},{4,12},{12,4},... | collective-permute-start | bytes 7864328 | tf_op jit(solution)/shard_map/ppermute | solution.py:361
  178.9 174.5 %all-to-all-start.2 = ((f32[8,16,120,128]{3,2,1,0:T(8,128)}), f32[8,16,120,128]{3,2,1,0:T(8,128)}, u32[]{:S(2)}, u32[]{:S(2)}) async-start(f32[8,16,120,128]{3,2,1,0:T(8,128)} %bitcast.37), calls=%async_computation.2 | async-start | bytes 15728640 | tf_op jit(solution)/shard_map/all_to_all | solution.py:353
  192.4 178.7 %collective-permute-start.1 = (f32[8,16,56,128]{3,2,1,0:T(8,128)}, f32[8,16,56,128]{3,2,1,0:T(8,128)}, u32[]{:S(2)}, u32[]{:S(2)}) collective-permute-start(f32[8,16,56,128]{3,2,1,0:T(8,128)} %slice.8.own_ref), channel_id=1, source_target_pairs={{0,8},{8,0},{1,9},{9,1},{2,10},{10,2},{3,11},{11,3},{4,12},{12,4},... | collective-permute-start | bytes 11010056 | tf_op jit(solution)/shard_map/ppermute | solution.py:361
  371.1 6.6 copy-start.15
  371.1 6.7 copy-start.18
  371.1 7.7 %copy-start.17 = (f32[128,64]{0,1:T(8,128)S(1)}, f32[128,64]{0,1:T(8,128)}, u32[]{:S(2)}) copy-start(f32[128,64]{0,1:T(8,128)} %param.20) | copy-start | bytes 98308
  371.1 8.3 %copy-start.16 = (f32[128,128]{1,0:T(8,128)S(1)}, f32[128,128]{1,0:T(8,128)}, u32[]{:S(2)}) copy-start(f32[128,128]{1,0:T(8,128)} %param.15) | copy-start | bytes 196612
  371.1 60.5 %all-to-all-start.3 = ((f32[8,16,40,128]{3,2,1,0:T(8,128)}), f32[8,16,40,128]{3,2,1,0:T(8,128)S(1)}, u32[]{:S(2)}, u32[]{:S(2)}) async-start(f32[8,16,40,128]{3,2,1,0:T(8,128)} %product.3), calls=%async_computation.3 | async-start | bytes 5242880 | tf_op jit(solution)/shard_map/all_to_all | solution.py:367
  377.8 106.4 %collective-permute-start.2 = (f32[8,16,32,128]{3,2,1,0:T(8,128)}, f32[8,16,32,128]{3,2,1,0:T(8,128)}, u32[]{:S(2)}, u32[]{:S(2)}) collective-permute-start(f32[8,16,32,128]{3,2,1,0:T(8,128)} %slice.9.own_ref), channel_id=1, source_target_pairs={{0,8},{8,0},{1,9},{9,1},{2,10},{10,2},{3,11},{11,3},{4,12},{12,4},... | collective-permute-start | bytes 6291464 | tf_op jit(solution)/shard_map/ppermute | solution.py:361
  431.6 1.5 copy-start.1
  452.3 11.5 %collective-permute-start.4 = (f32[40,16,128]{2,1,0:T(8,128)}, f32[40,16,128]{2,1,0:T(8,128)S(1)}, u32[]{:S(2)}, u32[]{:S(2)}) collective-permute-start(f32[40,16,128]{2,1,0:T(8,128)} %get-tuple-element.47.refs_3_), channel_id=1, source_target_pairs={{0,1},{1,0},{2,3},{3,2},{4,5},{5,4},{6,7},{7,6},{8,9},{9,8},{10,11... | collective-permute-start | bytes 983048 | tf_op jit(solution)/shard_map/ppermute | solution.py:307
  455.0 14.3 %collective-permute-start.6 = (f32[40,16,128]{2,1,0:T(8,128)}, f32[40,16,128]{2,1,0:T(8,128)S(1)}, u32[]{:S(2)}, u32[]{:S(2)}) collective-permute-start(f32[40,16,128]{2,1,0:T(8,128)} %get-tuple-element.48.refs_6_), channel_id=1, source_target_pairs={{0,2},{1,3},{2,0},{3,1},{4,6},{5,7},{6,4},{7,5},{8,10},{9,11},{10,... | collective-permute-start | bytes 983048 | tf_op jit(solution)/shard_map/ppermute | solution.py:307
  455.5 27.1 %collective-permute-start.8 = (f32[40,16,128]{2,1,0:T(8,128)}, f32[40,16,128]{2,1,0:T(8,128)S(1)}, u32[]{:S(2)}, u32[]{:S(2)}) collective-permute-start(f32[40,16,128]{2,1,0:T(8,128)} %get-tuple-element.49.refs_9_), channel_id=1, source_target_pairs={{0,3},{1,2},{2,1},{3,0},{4,7},{5,6},{6,5},{7,4},{8,11},{9,10},{10,... | collective-permute-start | bytes 983048 | tf_op jit(solution)/shard_map/ppermute | solution.py:307
  456.5 38.5 %collective-permute-start.3 = (f32[40,16,128]{2,1,0:T(8,128)}, f32[40,16,128]{2,1,0:T(8,128)}, u32[]{:S(2)}, u32[]{:S(2)}) collective-permute-start(f32[40,16,128]{2,1,0:T(8,128)} %get-tuple-element.44.refs_0_), channel_id=1, source_target_pairs={{0,0},{1,4},{2,8},{3,12},{4,1},{5,5},{6,9},{7,13},{8,2},{9,6},{10,... | collective-permute-start | bytes 983048 | tf_op jit(solution)/shard_map/ppermute | solution.py:307
  463.8 34.9 %collective-permute-start.5 = (f32[40,16,128]{2,1,0:T(8,128)S(1)}, f32[40,16,128]{2,1,0:T(8,128)}, u32[]{:S(2)}, u32[]{:S(2)}) collective-permute-start(f32[40,16,128]{2,1,0:T(8,128)S(1)} %collective-permute-done.4), channel_id=1, source_target_pairs={{0,4},{1,0},{2,12},{3,8},{4,5},{5,1},{6,13},{7,9},{8,6},{9,2},{10,... | collective-permute-start | bytes 983048 | tf_op jit(solution)/shard_map/ppermute | solution.py:307
  469.3 29.4 %collective-permute-start.7 = (f32[40,16,128]{2,1,0:T(8,128)S(1)}, f32[40,16,128]{2,1,0:T(8,128)}, u32[]{:S(2)}, u32[]{:S(2)}) collective-permute-start(f32[40,16,128]{2,1,0:T(8,128)S(1)} %collective-permute-done.6), channel_id=1, source_target_pairs={{0,8},{1,12},{2,0},{3,4},{4,9},{5,13},{6,1},{7,5},{8,10},{9,14},{1... | collective-permute-start | bytes 983048 | tf_op jit(solution)/shard_map/ppermute | solution.py:307
  482.7 16.6 %collective-permute-start.9 = (f32[40,16,128]{2,1,0:T(8,128)S(1)}, f32[40,16,128]{2,1,0:T(8,128)}, u32[]{:S(2)}, u32[]{:S(2)}) collective-permute-start(f32[40,16,128]{2,1,0:T(8,128)S(1)} %collective-permute-done.8), channel_id=1, source_target_pairs={{0,12},{1,8},{2,4},{3,0},{4,13},{5,9},{6,5},{7,1},{8,14},{9,10},{1... | collective-permute-start | bytes 983048 | tf_op jit(solution)/shard_map/ppermute | solution.py:307
  499.2 46.8 %all-to-all-start.4 = ((f32[8,16,56,128]{3,2,1,0:T(8,128)}), f32[8,16,56,128]{3,2,1,0:T(8,128)}, u32[]{:S(2)}, u32[]{:S(2)}) async-start(f32[8,16,56,128]{3,2,1,0:T(8,128)} %product.4), calls=%async_computation.4 | async-start | bytes 7340032 | tf_op jit(solution)/shard_map/all_to_all | solution.py:367
  546.1 32.2 %all-to-all-start.5 = ((f32[8,16,32,128]{3,2,1,0:T(8,128)}), f32[8,16,32,128]{3,2,1,0:T(8,128)S(1)}, u32[]{:S(2)}, u32[]{:S(2)}) async-start(f32[8,16,32,128]{3,2,1,0:T(8,128)} %product.5), calls=%async_computation.5 | async-start | bytes 4194304 | tf_op jit(solution)/shard_map/all_to_all | solution.py:367
  578.3 1.3 copy-start.2
  579.6 19.6 %copy-start.4 = (f32[56,16,128]{2,1,0:T(8,128)S(1)}, f32[56,16,128]{2,1,0:T(8,128)}, u32[]{:S(2)}) copy-start(f32[56,16,128]{2,1,0:T(8,128)} %get-tuple-element.61.refs_4_) | copy-start | bytes 1376260
  579.6 21.1 %copy-start.5 = (f32[56,16,128]{2,1,0:T(8,128)S(1)}, f32[56,16,128]{2,1,0:T(8,128)}, u32[]{:S(2)}) copy-start(f32[56,16,128]{2,1,0:T(8,128)} %get-tuple-element.63.refs_7_) | copy-start | bytes 1376260
  579.6 25.6 %copy-start.6 = (f32[56,16,128]{2,1,0:T(8,128)S(1)}, f32[56,16,128]{2,1,0:T(8,128)}, u32[]{:S(2)}) copy-start(f32[56,16,128]{2,1,0:T(8,128)} %get-tuple-element.65.refs_10_) | copy-start | bytes 1376260
  579.6 57.3 %copy-start.3 = (f32[56,16,128]{2,1,0:T(8,128)S(1)}, f32[56,16,128]{2,1,0:T(8,128)}, u32[]{:S(2)}) copy-start(f32[56,16,128]{2,1,0:T(8,128)} %get-tuple-element.58.refs_1_) | copy-start | bytes 1376260
  579.6 90.6 %copy-start.19 = (f32[64]{0:T(128)S(1)}, f32[64]{0:T(128)}, u32[]{:S(2)}) copy-start(f32[64]{0:T(128)} %param.21) | copy-start | bytes 772
  595.7 9.5 %collective-permute-start.14 = (f32[32,16,128]{2,1,0:T(8,128)}, f32[32,16,128]{2,1,0:T(8,128)S(1)}, u32[]{:S(2)}, u32[]{:S(2)}) collective-permute-start(f32[32,16,128]{2,1,0:T(8,128)} %get-tuple-element.62.refs_5_), channel_id=1, source_target_pairs={{0,1},{1,0},{2,3},{3,2},{4,5},{5,4},{6,7},{7,6},{8,9},{9,8},{10,11... | collective-permute-start | bytes 786440 | tf_op jit(solution)/shard_map/ppermute | solution.py:307
  597.2 14.4 %collective-permute-start.18 = (f32[32,16,128]{2,1,0:T(8,128)}, f32[32,16,128]{2,1,0:T(8,128)}, u32[]{:S(2)}, u32[]{:S(2)}) collective-permute-start(f32[32,16,128]{2,1,0:T(8,128)} %get-tuple-element.64.refs_8_), channel_id=1, source_target_pairs={{0,2},{1,3},{2,0},{3,1},{4,6},{5,7},{6,4},{7,5},{8,10},{9,11},{10,... | collective-permute-start | bytes 786440 | tf_op jit(solution)/shard_map/ppermute | solution.py:307
  597.8 39.2 %collective-permute-start.22 = (f32[32,16,128]{2,1,0:T(8,128)}, f32[32,16,128]{2,1,0:T(8,128)}, u32[]{:S(2)}, u32[]{:S(2)}) collective-permute-start(f32[32,16,128]{2,1,0:T(8,128)} %get-tuple-element.66.refs_11_), channel_id=1, source_target_pairs={{0,3},{1,2},{2,1},{3,0},{4,7},{5,6},{6,5},{7,4},{8,11},{9,10},{10,... | collective-permute-start | bytes 786440 | tf_op jit(solution)/shard_map/ppermute | solution.py:307
  599.2 61.7 %collective-permute-start.12 = (f32[56,16,128]{2,1,0:T(8,128)S(1)}, f32[56,16,128]{2,1,0:T(8,128)}, u32[]{:S(2)}, u32[]{:S(2)}) collective-permute-start(f32[56,16,128]{2,1,0:T(8,128)S(1)} %copy-done.4), channel_id=1, source_target_pairs={{0,1},{1,0},{2,3},{3,2},{4,5},{5,4},{6,7},{7,6},{8,9},{9,8},{10,11... | collective-permute-start | bytes 1376264 | tf_op jit(solution)/shard_map/ppermute | solution.py:307
  600.7 60.2 %collective-permute-start.16 = (f32[56,16,128]{2,1,0:T(8,128)S(1)}, f32[56,16,128]{2,1,0:T(8,128)}, u32[]{:S(2)}, u32[]{:S(2)}) collective-permute-start(f32[56,16,128]{2,1,0:T(8,128)S(1)} %copy-done.5), channel_id=1, source_target_pairs={{0,2},{1,3},{2,0},{3,1},{4,6},{5,7},{6,4},{7,5},{8,10},{9,11},{10,... | collective-permute-start | bytes 1376264 | tf_op jit(solution)/shard_map/ppermute | solution.py:307
  605.2 63.6 %collective-permute-start.20 = (f32[56,16,128]{2,1,0:T(8,128)S(1)}, f32[56,16,128]{2,1,0:T(8,128)}, u32[]{:S(2)}, u32[]{:S(2)}) collective-permute-start(f32[56,16,128]{2,1,0:T(8,128)S(1)} %copy-done.6), channel_id=1, source_target_pairs={{0,3},{1,2},{2,1},{3,0},{4,7},{5,6},{6,5},{7,4},{8,11},{9,10},{10,... | collective-permute-start | bytes 1376264 | tf_op jit(solution)/shard_map/ppermute | solution.py:307
  611.6 28.3 %collective-permute-start.11 = (f32[32,16,128]{2,1,0:T(8,128)}, f32[32,16,128]{2,1,0:T(8,128)S(1)}, u32[]{:S(2)}, u32[]{:S(2)}) collective-permute-start(f32[32,16,128]{2,1,0:T(8,128)} %get-tuple-element.60.refs_2_), channel_id=1, source_target_pairs={{0,0},{1,4},{2,8},{3,12},{4,1},{5,5},{6,9},{7,13},{8,2},{9,6},{10,... | collective-permute-start | bytes 786440 | tf_op jit(solution)/shard_map/ppermute | solution.py:307
  637.0 31.9 %collective-permute-start.10 = (f32[56,16,128]{2,1,0:T(8,128)S(1)}, f32[56,16,128]{2,1,0:T(8,128)S(1)}, u32[]{:S(2)}, u32[]{:S(2)}) collective-permute-start(f32[56,16,128]{2,1,0:T(8,128)S(1)} %copy-done.3), channel_id=1, source_target_pairs={{0,0},{1,4},{2,8},{3,12},{4,1},{5,5},{6,9},{7,13},{8,2},{9,6},{10,... | collective-permute-start | bytes 1376264 | tf_op jit(solution)/shard_map/ppermute | solution.py:307
  640.0 66.6 %copy-start.11 = (f32[32,16,128]{2,1,0:T(8,128)}, f32[32,16,128]{2,1,0:T(8,128)S(1)}, u32[]{:S(2)}) copy-start(f32[32,16,128]{2,1,0:T(8,128)S(1)} %collective-permute-done.11.refs_14_) | copy-start | bytes 786436
  640.0 28.9 %collective-permute-start.15 = (f32[32,16,128]{2,1,0:T(8,128)S(1)}, f32[32,16,128]{2,1,0:T(8,128)S(1)}, u32[]{:S(2)}, u32[]{:S(2)}) collective-permute-start(f32[32,16,128]{2,1,0:T(8,128)S(1)} %collective-permute-done.14), channel_id=1, source_target_pairs={{0,4},{1,0},{2,12},{3,8},{4,5},{5,1},{6,13},{7,9},{8,6},{9,2},{10,... | collective-permute-start | bytes 786440 | tf_op jit(solution)/shard_map/ppermute | solution.py:307
  660.9 44.7 %collective-permute-start.13 = (f32[56,16,128]{2,1,0:T(8,128)}, f32[56,16,128]{2,1,0:T(8,128)S(1)}, u32[]{:S(2)}, u32[]{:S(2)}) collective-permute-start(f32[56,16,128]{2,1,0:T(8,128)} %collective-permute-done.12), channel_id=1, source_target_pairs={{0,4},{1,0},{2,12},{3,8},{4,5},{5,1},{6,13},{7,9},{8,6},{9,2},{10,... | collective-permute-start | bytes 1376264 | tf_op jit(solution)/shard_map/ppermute | solution.py:307
  661.0 44.7 %collective-permute-start.17 = (f32[56,16,128]{2,1,0:T(8,128)}, f32[56,16,128]{2,1,0:T(8,128)S(1)}, u32[]{:S(2)}, u32[]{:S(2)}) collective-permute-start(f32[56,16,128]{2,1,0:T(8,128)} %collective-permute-done.16), channel_id=1, source_target_pairs={{0,8},{1,12},{2,0},{3,4},{4,9},{5,13},{6,1},{7,5},{8,10},{9,14},{1... | collective-permute-start | bytes 1376264 | tf_op jit(solution)/shard_map/ppermute | solution.py:307
  668.8 36.8 %collective-permute-start.21 = (f32[56,16,128]{2,1,0:T(8,128)}, f32[56,16,128]{2,1,0:T(8,128)S(1)}, u32[]{:S(2)}, u32[]{:S(2)}) collective-permute-start(f32[56,16,128]{2,1,0:T(8,128)} %collective-permute-done.20), channel_id=1, source_target_pairs={{0,12},{1,8},{2,4},{3,0},{4,13},{5,9},{6,5},{7,1},{8,14},{9,10},{1... | collective-permute-start | bytes 1376264 | tf_op jit(solution)/shard_map/ppermute | solution.py:307
  668.9 37.7 %copy-start.7 = (f32[56,16,128]{2,1,0:T(8,128)}, f32[56,16,128]{2,1,0:T(8,128)S(1)}, u32[]{:S(2)}) copy-start(f32[56,16,128]{2,1,0:T(8,128)S(1)} %collective-permute-done.10.refs_13_) | copy-start | bytes 1376260
  668.9 36.8 %collective-permute-start.19 = (f32[32,16,128]{2,1,0:T(8,128)}, f32[32,16,128]{2,1,0:T(8,128)S(1)}, u32[]{:S(2)}, u32[]{:S(2)}) collective-permute-start(f32[32,16,128]{2,1,0:T(8,128)} %collective-permute-done.18), channel_id=1, source_target_pairs={{0,8},{1,12},{2,0},{3,4},{4,9},{5,13},{6,1},{7,5},{8,10},{9,14},{1... | collective-permute-start | bytes 786440 | tf_op jit(solution)/shard_map/ppermute | solution.py:307
  668.9 37.6 %copy-start.12 = (f32[32,16,128]{2,1,0:T(8,128)}, f32[32,16,128]{2,1,0:T(8,128)S(1)}, u32[]{:S(2)}) copy-start(f32[32,16,128]{2,1,0:T(8,128)S(1)} %collective-permute-done.15.refs_17_) | copy-start | bytes 786436
  668.9 36.7 %collective-permute-start.23 = (f32[32,16,128]{2,1,0:T(8,128)}, f32[32,16,128]{2,1,0:T(8,128)S(1)}, u32[]{:S(2)}, u32[]{:S(2)}) collective-permute-start(f32[32,16,128]{2,1,0:T(8,128)} %collective-permute-done.22), channel_id=1, source_target_pairs={{0,12},{1,8},{2,4},{3,0},{4,13},{5,9},{6,5},{7,1},{8,14},{9,10},{1... | collective-permute-start | bytes 786440 | tf_op jit(solution)/shard_map/ppermute | solution.py:307
  705.6 1.0 copy-start.8
  705.7 1.1 copy-start.9
  705.7 1.2 copy-start.10
  (2 other events, 1.9 us)

commit v9 on v8

--- a/solution.py
+++ b/solution.py
@@ -393,9 +393,13 @@
     after, others[2], mirror[0] = tie((after, others[2], mirror[0]))
     values, after = tie((delivered(after), blocks(2)))
     own.append(run_head(values, 1))
+    shifted = aside(own[1], row_count)
+    straight = across(shifted, row_count, 0)
     values, own[1] = tie((delivered(after), own[1]))
-    own.append(run_head(values, 2))
-    mirror += [mirrored_parts(block) for block in own[1:]]
+    late, shifted, straight = tie((run_head(values, 2), shifted, straight))
+    own.append(late)
+    mirror.append([straight] + [across(shifted, row_count, part) for part in range(1, PARTS[1])])
+    mirror.append(mirrored_parts(late))
     quarters = 4
     bins = distogram_bias.shape[0] // quarters
     bias = jnp.broadcast_to(distogram_bias.reshape(quarters, bins, 1), (quarters, bins, tile_cols))

time: 721 us -> 705 us (0.978)
  waiting for transfers between devices: 432 us -> 413 us
    ppermute x21, waiting for transfers between devices: 92.3 us -> 73 us  [move(): return lax.ppermute(values, ('half', 'lo', 'col'), pairs)]
  transfers between devices with their start and end apart: 30 -> 30, of which waited for: 15 -> 15; matrix products, arithmetic and copies ran while one was open for 2% -> 2% of each run, Pallas kernels for 17% -> 19%
where the time goes in v9:
time: 705 us; the launch traced here: 696 us
  waiting for transfers between devices  413 us (59%)
  Pallas kernels  148 us (21%)
  starting transfers between devices  113 us (16%)
  local copies, waits for them, and re-layouts  14.6 us (2%)
  other arithmetic  7.37 us (1%)
    all_to_all x3, waiting for transfers between devices, spread(): lax.all_to_all(values, ('lo', 'col'), split_axis=0, concat_axis=0, tiled=...  283 us
    ppermute x21, waiting for transfers between devices, move(): return lax.ppermute(values, ('half', 'lo', 'col'), pairs)  73 us
    ppermute x21, starting transfers between devices, move(): return lax.ppermute(values, ('half', 'lo', 'col'), pairs)  64.5 us
    pallas_call x3, Pallas kernels, head(): pl.pallas_call(head_kernel, grid=(steps,), in_specs=[pl.BlockSpec((tile_r...  61.3 us
    all_to_all x3, waiting for transfers between devices, delivered(): lax.all_to_all(values, ('lo', 'col'), split_axis=0, concat_axis=0, tiled=...  56.1 us
    pallas_call x3, Pallas kernels, product(): pl.pallas_call(product_kernel, grid_spec=pltpu.PrefetchScalarGridSpec(num...  44.2 us
    pallas_call x3, Pallas kernels, hands(): pl.pallas_call(hands_kernel, grid=(rows // GROUP,), in_specs=[pl.BlockSpe...  35.7 us
    all_to_all x3, starting transfers between devices, spread(): lax.all_to_all(values, ('lo', 'col'), split_axis=0, concat_axis=0, tiled=...  25.8 us
  transfers between devices with their start and end apart: 30, of which 15 were waited for; matrix products, arithmetic and copies ran while one was open for 2% of the time, Pallas kernels for 19%

profile of v9, /device:TPU:12, one launch (start us, length us, event | category | flops | bytes accessed | tf_op | source)
XLA Modules:
  0.0 696.3 jit_solution(16889824860740154602)
XLA Ops:
  2.6 6.4 hands.5
  8.9 5.1 all-to-all-start.1
  14.1 13.1 %hands.3 = f32[128,96,128]{2,1,0:T(8,128)} custom-call(f32[128,128,128]{2,1,0:T(8,128)} %bitcast.32, bf16[512,384]{1,0:T(8,128)(2,1)} %pad_maximum_fusion.1.weights_ref), custom_call_target="tpu_custom_call" | custom-call | flops 301989888 | bytes 1572864 | tf_op jit(solution)/shard_map/hands/pallas_call | solution.py:131
  27.2 17.8 %all-to-all-done.1.own_ref = f32[8,16,40,128]{3,2,1,0:T(8,128)S(1)} async-done(((f32[8,16,40,128]{3,2,1,0:T(8,128)}), f32[8,16,40,128]{3,2,1,0:T(8,128)S(1)}, u32[]{:S(2)}, u32[]{:S(2)}) %all-to-all-start.1) | async-done | bytes 2621472 | tf_op jit(solution)/shard_map/all_to_all | solution.py:353
  45.0 7.2 %all-to-all-start = ((f32[8,16,96,128]{3,2,1,0:T(8,128)}), f32[8,16,96,128]{3,2,1,0:T(8,128)}, u32[]{:S(2)}, u32[]{:S(2)}) async-start(f32[8,16,96,128]{3,2,1,0:T(8,128)} %bitcast.38), calls=%async_computation | async-start | bytes 12582912 | tf_op jit(solution)/shard_map/all_to_all | solution.py:353
  52.2 2.5 collective-permute-start
  54.7 16.2 %hands.4 = f32[128,120,128]{2,1,0:T(8,128)} custom-call(f32[128,128,128]{2,1,0:T(8,128)} %bitcast.33, bf16[512,384]{1,0:T(8,128)(2,1)} %pad_maximum_fusion.1.weights_ref), custom_call_target="tpu_custom_call" | custom-call | flops 377487360 | bytes 1966080 | tf_op jit(solution)/shard_map/hands/pallas_call | solution.py:131
  70.9 103.9 %all-to-all-done.low_ref = f32[8,16,96,128]{3,2,1,0:T(8,128)} async-done(((f32[8,16,96,128]{3,2,1,0:T(8,128)}), f32[8,16,96,128]{3,2,1,0:T(8,128)}, u32[]{:S(2)}, u32[]{:S(2)}) %all-to-all-start) | async-done | bytes 6291488 | tf_op jit(solution)/shard_map/all_to_all | solution.py:353
  174.7 4.2 slice.8.own_ref
  178.9 13.5 %all-to-all-start.2 = ((f32[8,16,120,128]{3,2,1,0:T(8,128)}), f32[8,16,120,128]{3,2,1,0:T(8,128)}, u32[]{:S(2)}, u32[]{:S(2)}) async-start(f32[8,16,120,128]{3,2,1,0:T(8,128)} %bitcast.37), calls=%async_computation.2 | async-start | bytes 15728640 | tf_op jit(solution)/shard_map/all_to_all | solution.py:353
  192.4 161.0 %all-to-all-done.2.high_ref = f32[8,16,120,128]{3,2,1,0:T(8,128)} async-done(((f32[8,16,120,128]{3,2,1,0:T(8,128)}), f32[8,16,120,128]{3,2,1,0:T(8,128)}, u32[]{:S(2)}, u32[]{:S(2)}) %all-to-all-start.2) | async-done | bytes 7864352 | tf_op jit(solution)/shard_map/all_to_all | solution.py:353
  353.4 3.1 slice.9.own_ref
  356.5 14.6 %product.3 = f32[8,16,40,128]{3,2,1,0:T(8,128)} custom-call(s32[1]{0:T(128)} %bitcast.1.half_ref, f32[8,16,96,128]{3,2,1,0:T(8,128)} %all-to-all-done.low_ref, f32[8,16,120,128]{3,2,1,0:T(8,128)} %all-to-all-done.2.high_ref, f32[8,16,40,128]{3,2,1,0:T(8,128)} %copy-done, f32[8,16,40,128]{3,2,1,0:T(8,128)} %collective-permute-done.other_ref), custom_call_target="tpu_custom_call" | custom-call | flops 251658240 | bytes 1703936 | tf_op jit(solution)/shard_map/product/pallas_call | solution.py:180
  371.1 6.6 all-to-all-start.3
  379.7 1.2 copy.15
  382.0 1.3 pad_maximum_fusion.5.bins_ref
  387.3 15.4 %product.4 = f32[8,16,56,128]{3,2,1,0:T(8,128)} custom-call(s32[1]{0:T(128)} %bitcast.1.half_ref, f32[8,16,96,128]{3,2,1,0:T(8,128)} %all-to-all-done.low_ref, f32[8,16,120,128]{3,2,1,0:T(8,128)} %all-to-all-done.2.high_ref, f32[8,16,56,128]{3,2,1,0:T(8,128)} %slice.8.own_ref, f32[8,16,56,128]{3,2,1,0:T(8,128)} %collective-permute-done.1.other_ref), custom_call_target="tpu_custom_call" | custom-call | flops 352321536 | bytes 1966080 | tf_op jit(solution)/shard_map/product/pallas_call | solution.py:180
  402.7 29.2 %all-to-all-done.3 = f32[8,16,40,128]{3,2,1,0:T(8,128)S(1)} async-done(((f32[8,16,40,128]{3,2,1,0:T(8,128)}), f32[8,16,40,128]{3,2,1,0:T(8,128)S(1)}, u32[]{:S(2)}, u32[]{:S(2)}) %all-to-all-start.3) | async-done | bytes 2621472 | tf_op jit(solution)/shard_map/all_to_all | solution.py:367
  431.9 1.5 copy-done.1
  433.3 19.2 %head.3 = (f32[40,16,128]{2,1,0:T(8,128)}, f32[40,16,128]{2,1,0:T(8,128)}, f32[40,16,128]{2,1,0:T(8,128)}, f32[40,16,128]{2,1,0:T(8,128)}) custom-call(f32[128,128,128]{2,1,0:T(8,128)} %bitcast.34, f32[128,40,128]{2,1,0:T(8,128)} %bitcast.39, bf16[128,384]{1,0:T(8,128)(2,1)} %get-tuple-element.99.gate_ref, bf16[128,384]{1,0:T(8,128)(2,1)} %get-tuple-element.100.output_ref, ...), custom_call_target="tpu_custom_call" | custom-call | flops 912261120 | bytes 819200 | tf_op jit(solution)/shard_map/head/pallas_call | solution.py:234
  452.6 2.9 collective-permute-start.4
  457.0 5.0 collective-permute-start.3
  462.1 2.2 collective-permute-done.4
  464.3 5.0 collective-permute-start.5
  469.4 13.8 %collective-permute-start.7 = (f32[40,16,128]{2,1,0:T(8,128)S(1)}, f32[40,16,128]{2,1,0:T(8,128)S(1)}, u32[]{:S(2)}, u32[]{:S(2)}) collective-permute-start(f32[40,16,128]{2,1,0:T(8,128)S(1)} %collective-permute-done.6), channel_id=1, source_target_pairs={{0,8},{1,12},{2,0},{3,4},{4,9},{5,13},{6,1},{7,5},{8,10},{9,14},{1... | collective-permute-start | bytes 983048 | tf_op jit(solution)/shard_map/ppermute | solution.py:307
  484.4 10.5 %collective-permute-done.3.refs_12_ = f32[40,16,128]{2,1,0:T(8,128)S(1)} collective-permute-done((f32[40,16,128]{2,1,0:T(8,128)}, f32[40,16,128]{2,1,0:T(8,128)S(1)}, u32[]{:S(2)}, u32[]{:S(2)}) %collective-permute-start.3) | collective-permute-done | bytes 327712 | tf_op jit(solution)/shard_map/ppermute | solution.py:307
  494.9 3.7 collective-permute-done.5.refs_15_
  499.7 6.3 all-to-all-start.4
  505.9 14.1 %product.5 = f32[8,16,32,128]{3,2,1,0:T(8,128)} custom-call(s32[1]{0:T(128)} %bitcast.1.half_ref, f32[8,16,96,128]{3,2,1,0:T(8,128)} %all-to-all-done.low_ref, f32[8,16,120,128]{3,2,1,0:T(8,128)} %all-to-all-done.2.high_ref, f32[8,16,32,128]{3,2,1,0:T(8,128)} %slice.9.own_ref, f32[8,16,32,128]{3,2,1,0:T(8,128)} %collective-permute-done.2.other_ref), custom_call_target="tpu_custom_call" | custom-call | flops 201326592 | bytes 1572864 | tf_op jit(solution)/shard_map/product/pallas_call | solution.py:180
  520.1 26.9 %all-to-all-done.4 = f32[8,16,56,128]{3,2,1,0:T(8,128)} async-done(((f32[8,16,56,128]{3,2,1,0:T(8,128)}), f32[8,16,56,128]{3,2,1,0:T(8,128)}, u32[]{:S(2)}, u32[]{:S(2)}) %all-to-all-start.4) | async-done | bytes 3670048 | tf_op jit(solution)/shard_map/all_to_all | solution.py:367
  546.9 6.1 all-to-all-start.5
  553.0 26.1 %head.4 = (f32[56,16,128]{2,1,0:T(8,128)}, f32[56,16,128]{2,1,0:T(8,128)}, f32[56,16,128]{2,1,0:T(8,128)}, f32[56,16,128]{2,1,0:T(8,128)}) custom-call(f32[128,128,128]{2,1,0:T(8,128)} %bitcast.35, f32[128,56,128]{2,1,0:T(8,128)} %bitcast.12.product_ref, bf16[128,384]{1,0:T(8,128)(2,1)} %get-tuple-element.99.gate_ref, ...), custom_call_target="tpu_custom_call" | custom-call | flops 1277165568 | bytes 1146880 | tf_op jit(solution)/shard_map/head/pallas_call | solution.py:234
  579.2 1.5 collective-permute-start.10
  581.2 1.4 collective-permute-start.12
  582.7 2.1 collective-permute-start.13
  584.8 1.3 copy-done.2
  586.1 15.9 %head.5 = (f32[32,16,128]{2,1,0:T(8,128)}, f32[32,16,128]{2,1,0:T(8,128)}, f32[32,16,128]{2,1,0:T(8,128)}, f32[32,16,128]{2,1,0:T(8,128)}) custom-call(f32[128,128,128]{2,1,0:T(8,128)} %bitcast.36, f32[128,32,128]{2,1,0:T(8,128)} %bitcast.41, bf16[128,384]{1,0:T(8,128)(2,1)} %get-tuple-element.99.gate_ref, bf16[128,384]{1,0:T(8,128)(2,1)} %get-tuple-element.100.output_ref, ...), custom_call_target="tpu_custom_call" | custom-call | flops 729808896 | bytes 655360 | tf_op jit(solution)/shard_map/head/pallas_call | solution.py:234
  602.1 19.5 %collective-permute-done.12 = f32[56,16,128]{2,1,0:T(8,128)} collective-permute-done((f32[56,16,128]{2,1,0:T(8,128)}, f32[56,16,128]{2,1,0:T(8,128)}, u32[]{:S(2)}, u32[]{:S(2)}) %collective-permute-start.12) | collective-permute-done | bytes 458784 | tf_op jit(solution)/shard_map/ppermute | solution.py:307
  621.7 2.2 collective-permute-start.15
  625.1 3.6 collective-permute-start.14
  628.8 1.7 collective-permute-done.16
  630.4 8.7 %collective-permute-start.18 = (f32[56,16,128]{2,1,0:T(8,128)S(1)}, f32[56,16,128]{2,1,0:T(8,128)S(1)}, u32[]{:S(2)}, u32[]{:S(2)}) collective-permute-start(f32[56,16,128]{2,1,0:T(8,128)S(1)} %collective-permute-done.11), channel_id=1, source_target_pairs={{0,8},{1,12},{2,0},{3,4},{4,9},{5,13},{6,1},{7,5},{8,10},{9,14},{1... | collective-permute-start | bytes 1376264 | tf_op jit(solution)/shard_map/ppermute | solution.py:307
  639.2 1.9 collective-permute-start.21
  641.1 12.7 %collective-permute-start.17 = (f32[32,16,128]{2,1,0:T(8,128)}, f32[32,16,128]{2,1,0:T(8,128)S(1)}, u32[]{:S(2)}, u32[]{:S(2)}) collective-permute-start(f32[32,16,128]{2,1,0:T(8,128)} %collective-permute-done.16), channel_id=1, source_target_pairs={{0,4},{1,0},{2,12},{3,8},{4,5},{5,1},{6,13},{7,9},{8,6},{9,2},{10,... | collective-permute-start | bytes 786440 | tf_op jit(solution)/shard_map/ppermute | solution.py:307
  653.8 10.9 %collective-permute-done.14.refs_14_ = f32[32,16,128]{2,1,0:T(8,128)S(1)} collective-permute-done((f32[32,16,128]{2,1,0:T(8,128)}, f32[32,16,128]{2,1,0:T(8,128)S(1)}, u32[]{:S(2)}, u32[]{:S(2)}) %collective-permute-start.14) | collective-permute-done | bytes 262176 | tf_op jit(solution)/shard_map/ppermute | solution.py:307
  664.8 17.8 %collective-permute-done.21.refs_22_ = f32[56,16,128]{2,1,0:T(8,128)S(1)} collective-permute-done((f32[56,16,128]{2,1,0:T(8,128)}, f32[56,16,128]{2,1,0:T(8,128)S(1)}, u32[]{:S(2)}, u32[]{:S(2)}) %collective-permute-start.21) | collective-permute-done | bytes 458784 | tf_op jit(solution)/shard_map/ppermute | solution.py:307
  682.6 5.6 collective-permute-done.20.refs_20_
  689.1 7.1 %symmetric.1 = f32[128,4,16,128]{3,2,1,0:T(8,128)} custom-call(f32[4,16,128]{2,1,0:T(8,128)} %broadcast_in_dim.7.bias_ref, f32[40,16,128]{2,1,0:T(8,128)} %get-tuple-element.52.refs_0_, f32[56,16,128]{2,1,0:T(8,128)} %get-tuple-element.66.refs_1_, f32[32,16,128]{2,1,0:T(8,128)} %get-tuple-element.72.refs_2_, f32[40,16,128]{2,1,0:T(8,128)} %get-tuple-element.55.refs_3_, ...), custom_call_target="tpu_custom_call" | custom-call | bytes 1572864 | tf_op jit(solution)/shard_map/symmetric/pallas_call | solution.py:292
  (80 shorter events, 16.2 us)
Async XLA Ops:
  8.9 36.0 %all-to-all-start.1 = ((f32[8,16,40,128]{3,2,1,0:T(8,128)}), f32[8,16,40,128]{3,2,1,0:T(8,128)S(1)}, u32[]{:S(2)}, u32[]{:S(2)}) async-start(f32[8,16,40,128]{3,2,1,0:T(8,128)} %bitcast.40), calls=%async_computation.1 | async-start | bytes 5242880 | tf_op jit(solution)/shard_map/all_to_all | solution.py:353
  45.0 7.2 %copy-start = (f32[8,16,40,128]{3,2,1,0:T(8,128)}, f32[8,16,40,128]{3,2,1,0:T(8,128)S(1)}, u32[]{:S(2)}) copy-start(f32[8,16,40,128]{3,2,1,0:T(8,128)S(1)} %all-to-all-done.1.own_ref) | copy-start | bytes 7864324
  45.0 129.8 %all-to-all-start = ((f32[8,16,96,128]{3,2,1,0:T(8,128)}), f32[8,16,96,128]{3,2,1,0:T(8,128)}, u32[]{:S(2)}, u32[]{:S(2)}) async-start(f32[8,16,96,128]{3,2,1,0:T(8,128)} %bitcast.38), calls=%async_computation | async-start | bytes 12582912 | tf_op jit(solution)/shard_map/all_to_all | solution.py:353
  52.2 126.7 %collective-permute-start = (f32[8,16,40,128]{3,2,1,0:T(8,128)S(1)}, f32[8,16,40,128]{3,2,1,0:T(8,128)}, u32[]{:S(2)}, u32[]{:S(2)}) collective-permute-start(f32[8,16,40,128]{3,2,1,0:T(8,128)S(1)} %all-to-all-done.1.own_ref), channel_id=1, source_target_pairs={{0,8},{8,0},{1,9},{9,1},{2,10},{10,2},{3,11},{11,3},{4,12},{12,4},... | collective-permute-start | bytes 7864328 | tf_op jit(solution)/shard_map/ppermute | solution.py:361
  178.9 174.4 %all-to-all-start.2 = ((f32[8,16,120,128]{3,2,1,0:T(8,128)}), f32[8,16,120,128]{3,2,1,0:T(8,128)}, u32[]{:S(2)}, u32[]{:S(2)}) async-start(f32[8,16,120,128]{3,2,1,0:T(8,128)} %bitcast.37), calls=%async_computation.2 | async-start | bytes 15728640 | tf_op jit(solution)/shard_map/all_to_all | solution.py:353
  192.4 178.7 %collective-permute-start.1 = (f32[8,16,56,128]{3,2,1,0:T(8,128)}, f32[8,16,56,128]{3,2,1,0:T(8,128)}, u32[]{:S(2)}, u32[]{:S(2)}) collective-permute-start(f32[8,16,56,128]{3,2,1,0:T(8,128)} %slice.8.own_ref), channel_id=1, source_target_pairs={{0,8},{8,0},{1,9},{9,1},{2,10},{10,2},{3,11},{11,3},{4,12},{12,4},... | collective-permute-start | bytes 11010056 | tf_op jit(solution)/shard_map/ppermute | solution.py:361
  371.1 6.6 copy-start.14
  371.1 6.7 copy-start.17
  371.1 7.9 %copy-start.16 = (f32[128,64]{0,1:T(8,128)S(1)}, f32[128,64]{0,1:T(8,128)}, u32[]{:S(2)}) copy-start(f32[128,64]{0,1:T(8,128)} %param.20) | copy-start | bytes 98308
  371.1 8.5 %copy-start.15 = (f32[128,128]{1,0:T(8,128)S(1)}, f32[128,128]{1,0:T(8,128)}, u32[]{:S(2)}) copy-start(f32[128,128]{1,0:T(8,128)} %param.15) | copy-start | bytes 196612
  371.1 60.7 %all-to-all-start.3 = ((f32[8,16,40,128]{3,2,1,0:T(8,128)}), f32[8,16,40,128]{3,2,1,0:T(8,128)S(1)}, u32[]{:S(2)}, u32[]{:S(2)}) async-start(f32[8,16,40,128]{3,2,1,0:T(8,128)} %product.3), calls=%async_computation.3 | async-start | bytes 5242880 | tf_op jit(solution)/shard_map/all_to_all | solution.py:367
  377.8 106.6 %collective-permute-start.2 = (f32[8,16,32,128]{3,2,1,0:T(8,128)}, f32[8,16,32,128]{3,2,1,0:T(8,128)}, u32[]{:S(2)}, u32[]{:S(2)}) collective-permute-start(f32[8,16,32,128]{3,2,1,0:T(8,128)} %slice.9.own_ref), channel_id=1, source_target_pairs={{0,8},{8,0},{1,9},{9,1},{2,10},{10,2},{3,11},{11,3},{4,12},{12,4},... | collective-permute-start | bytes 6291464 | tf_op jit(solution)/shard_map/ppermute | solution.py:361
  431.8 1.5 copy-start.1
  452.6 11.7 %collective-permute-start.4 = (f32[40,16,128]{2,1,0:T(8,128)}, f32[40,16,128]{2,1,0:T(8,128)S(1)}, u32[]{:S(2)}, u32[]{:S(2)}) collective-permute-start(f32[40,16,128]{2,1,0:T(8,128)} %get-tuple-element.55.refs_3_), channel_id=1, source_target_pairs={{0,1},{1,0},{2,3},{3,2},{4,5},{5,4},{6,7},{7,6},{8,9},{9,8},{10,11... | collective-permute-start | bytes 983048 | tf_op jit(solution)/shard_map/ppermute | solution.py:307
  455.5 13.9 %collective-permute-start.6 = (f32[40,16,128]{2,1,0:T(8,128)}, f32[40,16,128]{2,1,0:T(8,128)S(1)}, u32[]{:S(2)}, u32[]{:S(2)}) collective-permute-start(f32[40,16,128]{2,1,0:T(8,128)} %get-tuple-element.56.refs_6_), channel_id=1, source_target_pairs={{0,2},{1,3},{2,0},{3,1},{4,6},{5,7},{6,4},{7,5},{8,10},{9,11},{10,... | collective-permute-start | bytes 983048 | tf_op jit(solution)/shard_map/ppermute | solution.py:307
  456.0 27.1 %collective-permute-start.8 = (f32[40,16,128]{2,1,0:T(8,128)}, f32[40,16,128]{2,1,0:T(8,128)S(1)}, u32[]{:S(2)}, u32[]{:S(2)}) collective-permute-start(f32[40,16,128]{2,1,0:T(8,128)} %get-tuple-element.57.refs_9_), channel_id=1, source_target_pairs={{0,3},{1,2},{2,1},{3,0},{4,7},{5,6},{6,5},{7,4},{8,11},{9,10},{10,... | collective-permute-start | bytes 983048 | tf_op jit(solution)/shard_map/ppermute | solution.py:307
  457.0 37.9 %collective-permute-start.3 = (f32[40,16,128]{2,1,0:T(8,128)}, f32[40,16,128]{2,1,0:T(8,128)S(1)}, u32[]{:S(2)}, u32[]{:S(2)}) collective-permute-start(f32[40,16,128]{2,1,0:T(8,128)} %get-tuple-element.52.refs_0_), channel_id=1, source_target_pairs={{0,0},{1,4},{2,8},{3,12},{4,1},{5,5},{6,9},{7,13},{8,2},{9,6},{10,... | collective-permute-start | bytes 983048 | tf_op jit(solution)/shard_map/ppermute | solution.py:307
  464.3 34.3 %collective-permute-start.5 = (f32[40,16,128]{2,1,0:T(8,128)S(1)}, f32[40,16,128]{2,1,0:T(8,128)S(1)}, u32[]{:S(2)}, u32[]{:S(2)}) collective-permute-start(f32[40,16,128]{2,1,0:T(8,128)S(1)} %collective-permute-done.4), channel_id=1, source_target_pairs={{0,4},{1,0},{2,12},{3,8},{4,5},{5,1},{6,13},{7,9},{8,6},{9,2},{10,... | collective-permute-start | bytes 983048 | tf_op jit(solution)/shard_map/ppermute | solution.py:307
  469.4 29.2 %collective-permute-start.7 = (f32[40,16,128]{2,1,0:T(8,128)S(1)}, f32[40,16,128]{2,1,0:T(8,128)S(1)}, u32[]{:S(2)}, u32[]{:S(2)}) collective-permute-start(f32[40,16,128]{2,1,0:T(8,128)S(1)} %collective-permute-done.6), channel_id=1, source_target_pairs={{0,8},{1,12},{2,0},{3,4},{4,9},{5,13},{6,1},{7,5},{8,10},{9,14},{1... | collective-permute-start | bytes 983048 | tf_op jit(solution)/shard_map/ppermute | solution.py:307
  483.2 16.5 %collective-permute-start.9 = (f32[40,16,128]{2,1,0:T(8,128)S(1)}, f32[40,16,128]{2,1,0:T(8,128)}, u32[]{:S(2)}, u32[]{:S(2)}) collective-permute-start(f32[40,16,128]{2,1,0:T(8,128)S(1)} %collective-permute-done.8), channel_id=1, source_target_pairs={{0,12},{1,8},{2,4},{3,0},{4,13},{5,9},{6,5},{7,1},{8,14},{9,10},{1... | collective-permute-start | bytes 983048 | tf_op jit(solution)/shard_map/ppermute | solution.py:307
  494.9 4.7 copy-start.7
  498.6 1.0 copy-start.8
  498.6 1.0 copy-start.9
  499.7 47.3 %all-to-all-start.4 = ((f32[8,16,56,128]{3,2,1,0:T(8,128)}), f32[8,16,56,128]{3,2,1,0:T(8,128)}, u32[]{:S(2)}, u32[]{:S(2)}) async-start(f32[8,16,56,128]{3,2,1,0:T(8,128)} %product.4), calls=%async_computation.4 | async-start | bytes 7340032 | tf_op jit(solution)/shard_map/all_to_all | solution.py:367
  546.9 37.9 %all-to-all-start.5 = ((f32[8,16,32,128]{3,2,1,0:T(8,128)}), f32[8,16,32,128]{3,2,1,0:T(8,128)S(1)}, u32[]{:S(2)}, u32[]{:S(2)}) async-start(f32[8,16,32,128]{3,2,1,0:T(8,128)} %product.5), calls=%async_computation.5 | async-start | bytes 4194304 | tf_op jit(solution)/shard_map/all_to_all | solution.py:367
  579.2 22.9 %collective-permute-start.10 = (f32[56,16,128]{2,1,0:T(8,128)}, f32[56,16,128]{2,1,0:T(8,128)}, u32[]{:S(2)}, u32[]{:S(2)}) collective-permute-start(f32[56,16,128]{2,1,0:T(8,128)} %get-tuple-element.73.refs_4_), channel_id=1, source_target_pairs={{0,1},{1,0},{2,3},{3,2},{4,5},{5,4},{6,7},{7,6},{8,9},{9,8},{10,11... | collective-permute-start | bytes 1376264 | tf_op jit(solution)/shard_map/ppermute | solution.py:307
  580.7 21.4 %collective-permute-start.11 = (f32[56,16,128]{2,1,0:T(8,128)}, f32[56,16,128]{2,1,0:T(8,128)S(1)}, u32[]{:S(2)}, u32[]{:S(2)}) collective-permute-start(f32[56,16,128]{2,1,0:T(8,128)} %get-tuple-element.75.refs_7_), channel_id=1, source_target_pairs={{0,2},{1,3},{2,0},{3,1},{4,6},{5,7},{6,4},{7,5},{8,10},{9,11},{10,... | collective-permute-start | bytes 1376264 | tf_op jit(solution)/shard_map/ppermute | solution.py:307
  581.2 40.4 %collective-permute-start.12 = (f32[56,16,128]{2,1,0:T(8,128)}, f32[56,16,128]{2,1,0:T(8,128)}, u32[]{:S(2)}, u32[]{:S(2)}) collective-permute-start(f32[56,16,128]{2,1,0:T(8,128)} %get-tuple-element.77.refs_10_), channel_id=1, source_target_pairs={{0,3},{1,2},{2,1},{3,0},{4,7},{5,6},{6,5},{7,4},{8,11},{9,10},{10,... | collective-permute-start | bytes 1376264 | tf_op jit(solution)/shard_map/ppermute | solution.py:307
  582.7 38.9 %collective-permute-start.13 = (f32[56,16,128]{2,1,0:T(8,128)}, f32[56,16,128]{2,1,0:T(8,128)S(1)}, u32[]{:S(2)}, u32[]{:S(2)}) collective-permute-start(f32[56,16,128]{2,1,0:T(8,128)} %get-tuple-element.66.refs_1_), channel_id=1, source_target_pairs={{0,0},{1,4},{2,8},{3,12},{4,1},{5,5},{6,9},{7,13},{8,2},{9,6},{10,... | collective-permute-start | bytes 1376264 | tf_op jit(solution)/shard_map/ppermute | solution.py:307
  584.8 1.3 copy-start.2
  586.1 78.6 %copy-start.18 = (f32[64]{0:T(128)S(1)}, f32[64]{0:T(128)}, u32[]{:S(2)}) copy-start(f32[64]{0:T(128)} %param.21) | copy-start | bytes 772
  621.6 67.4 %copy-start.3 = (f32[56,16,128]{2,1,0:T(8,128)}, f32[56,16,128]{2,1,0:T(8,128)S(1)}, u32[]{:S(2)}) copy-start(f32[56,16,128]{2,1,0:T(8,128)S(1)} %collective-permute-done.13.refs_13_) | copy-start | bytes 1376260
  621.6 8.8 %collective-permute-start.16 = (f32[32,16,128]{2,1,0:T(8,128)}, f32[32,16,128]{2,1,0:T(8,128)}, u32[]{:S(2)}, u32[]{:S(2)}) collective-permute-start(f32[32,16,128]{2,1,0:T(8,128)} %get-tuple-element.74.refs_5_), channel_id=1, source_target_pairs={{0,1},{1,0},{2,3},{3,2},{4,5},{5,4},{6,7},{7,6},{8,9},{9,8},{10,11... | collective-permute-start | bytes 786440 | tf_op jit(solution)/shard_map/ppermute | solution.py:307
  621.6 17.6 %collective-permute-start.19 = (f32[32,16,128]{2,1,0:T(8,128)}, f32[32,16,128]{2,1,0:T(8,128)}, u32[]{:S(2)}, u32[]{:S(2)}) collective-permute-start(f32[32,16,128]{2,1,0:T(8,128)} %get-tuple-element.76.refs_8_), channel_id=1, source_target_pairs={{0,2},{1,3},{2,0},{3,1},{4,6},{5,7},{6,4},{7,5},{8,10},{9,11},{10,... | collective-permute-start | bytes 786440 | tf_op jit(solution)/shard_map/ppermute | solution.py:307
  621.7 43.0 %collective-permute-start.15 = (f32[56,16,128]{2,1,0:T(8,128)}, f32[56,16,128]{2,1,0:T(8,128)S(1)}, u32[]{:S(2)}, u32[]{:S(2)}) collective-permute-start(f32[56,16,128]{2,1,0:T(8,128)} %collective-permute-done.10), channel_id=1, source_target_pairs={{0,4},{1,0},{2,12},{3,8},{4,5},{5,1},{6,13},{7,9},{8,6},{9,2},{10,... | collective-permute-start | bytes 1376264 | tf_op jit(solution)/shard_map/ppermute | solution.py:307
  624.0 17.1 %collective-permute-start.22 = (f32[32,16,128]{2,1,0:T(8,128)}, f32[32,16,128]{2,1,0:T(8,128)}, u32[]{:S(2)}, u32[]{:S(2)}) collective-permute-start(f32[32,16,128]{2,1,0:T(8,128)} %get-tuple-element.78.refs_11_), channel_id=1, source_target_pairs={{0,3},{1,2},{2,1},{3,0},{4,7},{5,6},{6,5},{7,4},{8,11},{9,10},{10,... | collective-permute-start | bytes 786440 | tf_op jit(solution)/shard_map/ppermute | solution.py:307
  625.1 39.5 %collective-permute-start.14 = (f32[32,16,128]{2,1,0:T(8,128)}, f32[32,16,128]{2,1,0:T(8,128)S(1)}, u32[]{:S(2)}, u32[]{:S(2)}) collective-permute-start(f32[32,16,128]{2,1,0:T(8,128)} %get-tuple-element.72.refs_2_), channel_id=1, source_target_pairs={{0,0},{1,4},{2,8},{3,12},{4,1},{5,5},{6,9},{7,13},{8,2},{9,6},{10,... | collective-permute-start | bytes 786440 | tf_op jit(solution)/shard_map/ppermute | solution.py:307
  630.4 34.4 %collective-permute-start.18 = (f32[56,16,128]{2,1,0:T(8,128)S(1)}, f32[56,16,128]{2,1,0:T(8,128)S(1)}, u32[]{:S(2)}, u32[]{:S(2)}) collective-permute-start(f32[56,16,128]{2,1,0:T(8,128)S(1)} %collective-permute-done.11), channel_id=1, source_target_pairs={{0,8},{1,12},{2,0},{3,4},{4,9},{5,13},{6,1},{7,5},{8,10},{9,14},{1... | collective-permute-start | bytes 1376264 | tf_op jit(solution)/shard_map/ppermute | solution.py:307
  639.2 43.4 %collective-permute-start.21 = (f32[56,16,128]{2,1,0:T(8,128)}, f32[56,16,128]{2,1,0:T(8,128)S(1)}, u32[]{:S(2)}, u32[]{:S(2)}) collective-permute-start(f32[56,16,128]{2,1,0:T(8,128)} %collective-permute-done.12), channel_id=1, source_target_pairs={{0,12},{1,8},{2,4},{3,0},{4,13},{5,9},{6,5},{7,1},{8,14},{9,10},{1... | collective-permute-start | bytes 1376264 | tf_op jit(solution)/shard_map/ppermute | solution.py:307
  641.1 41.5 %collective-permute-start.17 = (f32[32,16,128]{2,1,0:T(8,128)}, f32[32,16,128]{2,1,0:T(8,128)S(1)}, u32[]{:S(2)}, u32[]{:S(2)}) collective-permute-start(f32[32,16,128]{2,1,0:T(8,128)} %collective-permute-done.16), channel_id=1, source_target_pairs={{0,4},{1,0},{2,12},{3,8},{4,5},{5,1},{6,13},{7,9},{8,6},{9,2},{10,... | collective-permute-start | bytes 786440 | tf_op jit(solution)/shard_map/ppermute | solution.py:307
  664.7 24.4 %copy-start.10 = (f32[32,16,128]{2,1,0:T(8,128)}, f32[32,16,128]{2,1,0:T(8,128)S(1)}, u32[]{:S(2)}) copy-start(f32[32,16,128]{2,1,0:T(8,128)S(1)} %collective-permute-done.14.refs_14_) | copy-start | bytes 786436
  664.7 23.5 %collective-permute-start.20 = (f32[32,16,128]{2,1,0:T(8,128)}, f32[32,16,128]{2,1,0:T(8,128)S(1)}, u32[]{:S(2)}, u32[]{:S(2)}) collective-permute-start(f32[32,16,128]{2,1,0:T(8,128)} %collective-permute-done.19), channel_id=1, source_target_pairs={{0,8},{1,12},{2,0},{3,4},{4,9},{5,13},{6,1},{7,5},{8,10},{9,14},{1... | collective-permute-start | bytes 786440 | tf_op jit(solution)/shard_map/ppermute | solution.py:307
  664.7 24.4 %copy-start.4 = (f32[56,16,128]{2,1,0:T(8,128)}, f32[56,16,128]{2,1,0:T(8,128)S(1)}, u32[]{:S(2)}) copy-start(f32[56,16,128]{2,1,0:T(8,128)S(1)} %collective-permute-done.15.refs_16_) | copy-start | bytes 1376260
  664.7 23.6 %collective-permute-start.23 = (f32[32,16,128]{2,1,0:T(8,128)}, f32[32,16,128]{2,1,0:T(8,128)S(1)}, u32[]{:S(2)}, u32[]{:S(2)}) collective-permute-start(f32[32,16,128]{2,1,0:T(8,128)} %collective-permute-done.22), channel_id=1, source_target_pairs={{0,12},{1,8},{2,4},{3,0},{4,13},{5,9},{6,5},{7,1},{8,14},{9,10},{1... | collective-permute-start | bytes 786440 | tf_op jit(solution)/shard_map/ppermute | solution.py:307
  664.8 24.2 %copy-start.5 = (f32[56,16,128]{2,1,0:T(8,128)}, f32[56,16,128]{2,1,0:T(8,128)S(1)}, u32[]{:S(2)}) copy-start(f32[56,16,128]{2,1,0:T(8,128)S(1)} %collective-permute-done.18.refs_19_) | copy-start | bytes 1376260
  682.6 6.4 copy-start.6
  682.6 6.4 copy-start.11
  688.2 0.9 copy-start.12
  (1 other events, 0.9 us)

commit v10 on v4

--- a/solution.py
+++ b/solution.py
@@ -10,6 +10,7 @@
 HIGH = lax.Precision.HIGHEST
 LANES = 128
 GROUP = 8
+STEP = 2
 CHUNKS = (40, 56, 32)
 LOWER = 40
 PARTS = 4
@@ -146,44 +147,52 @@
 def product_kernel(half_ref, low_ref, high_ref, own_ref, other_ref, out_ref):
     cols = own_ref.shape[0] // 2
     half = half_ref[0]
-
-    def line(ref, lo):
-        return jnp.concatenate([ref[lo * cols + c, 0] for c in range(cols)], axis=1)
-
-    left_high, left_low = parts(
-        jnp.concatenate([line(ref, lo) for lo in range(2) for ref in (low_ref, high_ref)], axis=0)
-    )
-    right_high, right_low = parts(
-        jnp.concatenate([line(ref, lo) for ref in (own_ref, other_ref) for lo in range(2)], axis=0)
-    )
-    result = lax.dot_general(
-        jnp.concatenate([right_high, right_high, right_low], axis=1),
-        jnp.concatenate([left_high, left_low, left_high], axis=1),
-        (((1,), (1,)), ((), ())),
-        preferred_element_type=jnp.float32,
-    )
     rows = own_ref.shape[2]
-    wide = result.shape[1] // 2
-    for lo in range(2):
-        for piece in range(cols):
-            source, other_lo = divmod(piece, 2)
-            plane = 2 * jnp.where(half == source, 0, 1) + other_lo
-            out_ref[lo * cols + plane, 0] = result[
-                piece * rows : (piece + 1) * rows, lo * wide : (lo + 1) * wide
-            ]
+    for n in range(own_ref.shape[1]):
+
+        def line(ref, lo):
+            return jnp.concatenate([ref[lo * cols + c, n] for c in range(cols)], axis=1)
+
+        left_high, left_low = parts(
+            jnp.concatenate(
+                [line(ref, lo) for lo in range(2) for ref in (low_ref, high_ref)], axis=0
+            )
+        )
+        right_high, right_low = parts(
+            jnp.concatenate(
+                [line(ref, lo) for ref in (own_ref, other_ref) for lo in range(2)], axis=0
+            )
+        )
+        result = lax.dot_general(
+            jnp.concatenate([right_high, right_high, right_low], axis=1),
+            jnp.concatenate([left_high, left_low, left_high], axis=1),
+            (((1,), (1,)), ((), ())),
+            preferred_element_type=jnp.float32,
+        )
+        wide = result.shape[1] // 2
+        for lo in range(2):
+            for piece in range(cols):
+                source, other_lo = divmod(piece, 2)
+                plane = 2 * jnp.where(half == source, 0, 1) + other_lo
+                out_ref[lo * cols + plane, n] = result[
+                    piece * rows : (piece + 1) * rows, lo * wide : (lo + 1) * wide
+                ]
 
 
 def product(half, low, high, own, other, wide):
     sources, owned, rows, width = own.shape
     k_all = width * sources // 2
-    spec = lambda height: pl.BlockSpec((sources, 1, height, width), lambda n, half: (0, n, 0, 0))
+    spec_out = pl.BlockSpec((sources, STEP, rows, wide), lambda n, half: (0, n, 0, 0))
+    spec = lambda height: pl.BlockSpec(
+        (sources, STEP, height, width), lambda n, half: (0, n, 0, 0)
+    )
     return pl.pallas_call(
         product_kernel,
         grid_spec=pltpu.PrefetchScalarGridSpec(
             num_scalar_prefetch=1,
-            grid=(owned,),
+            grid=(owned // STEP,),
             in_specs=[spec(LOWER), spec(wide - LOWER), spec(rows), spec(rows)],
-            out_specs=pl.BlockSpec((sources, 1, rows, wide), lambda n, half: (0, n, 0, 0)),
+            out_specs=spec_out,
         ),
         out_shape=jax.ShapeDtypeStruct((sources, owned, rows, wide), jnp.float32),
         compiler_params=pltpu.CompilerParams(vmem_limit_bytes=VMEM),
@@ -310,19 +319,22 @@
     )(base, *mirror)
 
 
-def mirrored_parts(block, count):
+def move(values, count, target):
     every = [(r, c) for r in range(count) for c in range(count)]
-
-    def move(values, target):
-        pairs = [(r * count + c, target(r, c)) for r, c in every]
-        return lax.ppermute(values, ("half", "lo", "col"), pairs)
-
-    result = []
-    for part, values in enumerate(block):
-        if part:
-            values = move(values, lambda r, c: r * count + (c ^ part))
-        result.append(move(values, lambda r, c: (c ^ part) * count + r))
-    return result
+    pairs = [(r * count + c, target(r, c)) for r, c in every]
+    return lax.ppermute(values, ("half", "lo", "col"), pairs)
+
+
+def aside(block, count):
+    return [block[0]] + [
+        move(block[n], count, lambda r, c: r * count + (c ^ n)) for n in range(1, len(block))
+    ]
+
+
+def across(shifted, count):
+    return [
+        move(values, count, lambda r, c: (c ^ n) * count + r) for n, values in enumerate(shifted)
+    ]
 
 
 def half_shards(
@@ -384,11 +396,13 @@
 
     values, others[1] = tie((blocks(0), others[1]))
     own = [finish(values, 0)]
-    mirror = [mirrored_parts(own[0], row_count)]
-    values, others[2], mirror[0] = tie((blocks(1), others[2], mirror[0]))
+    shifted = aside(own[0], row_count)
+    values, others[2], shifted = tie((blocks(1), others[2], shifted))
+    mirror = [across(shifted, row_count)]
     own.append(finish(values, 1))
-    own.append(finish(blocks(2), 2))
-    mirror += [mirrored_parts(block, row_count) for block in own[1:]]
+    values, mirror[0] = tie((blocks(2), mirror[0]))
+    own.append(finish(values, 2))
+    mirror += [across(aside(block, row_count), row_count) for block in own[1:]]
     bins = distogram_bias.shape[0] // PARTS
     bias = jnp.broadcast_to(distogram_bias.reshape(PARTS, bins, 1), (PARTS, bins, tile_cols))
     logits = turned(bias, own)

time: 689 us -> 677 us (0.983)
  Pallas kernels: 161 us -> 148 us
  starting transfers between devices: 107 us -> 116 us
    all_to_all x3, waiting for transfers between devices: 63.3 us -> 36.8 us  [finish(): lax.all_to_all(values, ('lo', 'col'), split_axis=0, concat_axis=0, tiled=...]
    all_to_all x3, starting transfers between devices: 17.1 us -> 35.9 us  [finish(): lax.all_to_all(values, ('lo', 'col'), split_axis=0, concat_axis=0, tiled=...]
    ppermute x21, waiting for transfers between devices: 42.2 us -> 57 us  [move(): return lax.ppermute(values, ('half', 'lo', 'col'), pairs)]
    pallas_call x3, Pallas kernels: 44.2 us -> 31.7 us  [product(): pl.pallas_call(product_kernel, grid_spec=pltpu.PrefetchScalarGridSpec(num...]
    ppermute x21, starting transfers between devices: 59.9 us -> 48.5 us  [move(): return lax.ppermute(values, ('half', 'lo', 'col'), pairs)]
    ppermute x3, waiting for transfers between devices: 107 us -> 118 us  [exchange(): return lax.ppermute(values, 'half', [(0, 1), (1, 0)])]
  transfers between devices with their start and end apart: 30 -> 30, of which waited for: 11 -> 12; matrix products, arithmetic and copies ran while one was open for 2% -> 2% of each run, Pallas kernels for 22% -> 21%
where the time goes in v10:
time: 677 us; the launch traced here: 673 us
  waiting for transfers between devices  386 us (57%)
  Pallas kernels  148 us (22%)
  starting transfers between devices  116 us (17%)
  local copies, waits for them, and re-layouts  18.2 us (3%)
    all_to_all x3, waiting for transfers between devices, spread(): lax.all_to_all(values, ('lo', 'col'), split_axis=0, concat_axis=0, tiled=...  175 us
    ppermute x3, waiting for transfers between devices, exchange(): return lax.ppermute(values, 'half', [(0, 1), (1, 0)])  118 us
    pallas_call x3, Pallas kernels, head(): pl.pallas_call(head_kernel, grid=(steps,), in_specs=[pl.BlockSpec((tile_r...  61.4 us
    ppermute x21, waiting for transfers between devices, move(): return lax.ppermute(values, ('half', 'lo', 'col'), pairs)  57 us
    ppermute x21, starting transfers between devices, move(): return lax.ppermute(values, ('half', 'lo', 'col'), pairs)  48.5 us
    all_to_all x3, waiting for transfers between devices, finish(): lax.all_to_all(values, ('lo', 'col'), split_axis=0, concat_axis=0, tiled=...  36.8 us
    all_to_all x3, starting transfers between devices, finish(): lax.all_to_all(values, ('lo', 'col'), split_axis=0, concat_axis=0, tiled=...  35.9 us
    pallas_call x3, Pallas kernels, hands(): pl.pallas_call(hands_kernel, grid=(rows // GROUP,), in_specs=[pl.BlockSpe...  35.6 us
  transfers between devices with their start and end apart: 30, of which 12 were waited for; matrix products, arithmetic and copies ran while one was open for 2% of the time, Pallas kernels for 21%

profile of v10, /device:TPU:12, one launch (start us, length us, event | category | flops | bytes accessed | tf_op | source)
XLA Modules:
  0.0 673.2 jit_solution(1917318780480528135)
XLA Ops:
  2.6 6.4 hands.5
  8.9 5.1 all-to-all-start.1
  14.1 13.1 %hands.3 = f32[128,96,128]{2,1,0:T(8,128)} custom-call(f32[128,128,128]{2,1,0:T(8,128)} %bitcast.32, bf16[512,384]{1,0:T(8,128)(2,1)} %pad_maximum_fusion.1.weights_ref), custom_call_target="tpu_custom_call" | custom-call | flops 301989888 | bytes 1572864 | tf_op jit(solution)/shard_map/hands/pallas_call | solution.py:132
  27.1 17.8 %all-to-all-done.1.own_ref = f32[8,16,40,128]{3,2,1,0:T(8,128)S(1)} async-done(((f32[8,16,40,128]{3,2,1,0:T(8,128)}), f32[8,16,40,128]{3,2,1,0:T(8,128)S(1)}, u32[]{:S(2)}, u32[]{:S(2)}) %all-to-all-start.1) | async-done | bytes 2621472 | tf_op jit(solution)/shard_map/all_to_all | solution.py:368
  45.0 7.2 %all-to-all-start = ((f32[8,16,96,128]{3,2,1,0:T(8,128)}), f32[8,16,96,128]{3,2,1,0:T(8,128)}, u32[]{:S(2)}, u32[]{:S(2)}) async-start(f32[8,16,96,128]{3,2,1,0:T(8,128)} %bitcast.38), calls=%async_computation | async-start | bytes 12582912 | tf_op jit(solution)/shard_map/all_to_all | solution.py:368
  52.2 2.5 collective-permute-start
  54.7 16.2 %hands.4 = f32[128,120,128]{2,1,0:T(8,128)} custom-call(f32[128,128,128]{2,1,0:T(8,128)} %bitcast.33, bf16[512,384]{1,0:T(8,128)(2,1)} %pad_maximum_fusion.1.weights_ref), custom_call_target="tpu_custom_call" | custom-call | flops 377487360 | bytes 1966080 | tf_op jit(solution)/shard_map/hands/pallas_call | solution.py:132
  70.9 107.0 %collective-permute-done.other_ref = f32[8,16,40,128]{3,2,1,0:T(8,128)} collective-permute-done((f32[8,16,40,128]{3,2,1,0:T(8,128)S(1)}, f32[8,16,40,128]{3,2,1,0:T(8,128)}, u32[]{:S(2)}, u32[]{:S(2)}) %collective-permute-start) | collective-permute-done | bytes 2621472 | tf_op jit(solution)/shard_map/ppermute | solution.py:376
  177.8 14.5 %all-to-all-start.2 = ((f32[8,16,120,128]{3,2,1,0:T(8,128)}), f32[8,16,120,128]{3,2,1,0:T(8,128)}, u32[]{:S(2)}, u32[]{:S(2)}) async-start(f32[8,16,120,128]{3,2,1,0:T(8,128)} %bitcast.37), calls=%async_computation.2 | async-start | bytes 15728640 | tf_op jit(solution)/shard_map/all_to_all | solution.py:368
  192.3 4.2 slice.8.own_ref
  196.5 156.8 %all-to-all-done.2.high_ref = f32[8,16,120,128]{3,2,1,0:T(8,128)} async-done(((f32[8,16,120,128]{3,2,1,0:T(8,128)}), f32[8,16,120,128]{3,2,1,0:T(8,128)}, u32[]{:S(2)}, u32[]{:S(2)}) %all-to-all-start.2) | async-done | bytes 7864352 | tf_op jit(solution)/shard_map/all_to_all | solution.py:368
  353.3 10.5 %product.3 = f32[8,16,40,128]{3,2,1,0:T(8,128)} custom-call(s32[1]{0:T(128)} %bitcast.1.half_ref, f32[8,16,96,128]{3,2,1,0:T(8,128)} %all-to-all-done.low_ref, f32[8,16,120,128]{3,2,1,0:T(8,128)} %all-to-all-done.2.high_ref, f32[8,16,40,128]{3,2,1,0:T(8,128)} %copy-done, f32[8,16,40,128]{3,2,1,0:T(8,128)} %collective-permute-done.other_ref), custom_call_target="tpu_custom_call" | custom-call | flops 251658240 | bytes 1703936 | tf_op jit(solution)/shard_map/product/pallas_call | solution.py:189
  363.8 6.8 %all-to-all-start.3 = ((f32[8,16,40,128]{3,2,1,0:T(8,128)}), f32[8,16,40,128]{3,2,1,0:T(8,128)S(1)}, u32[]{:S(2)}, u32[]{:S(2)}) async-start(f32[8,16,40,128]{3,2,1,0:T(8,128)} %product.3), calls=%async_computation.3 | async-start | bytes 5242880 | tf_op jit(solution)/shard_map/all_to_all | solution.py:379
  373.2 3.1 slice.9.own_ref
  376.3 1.7 collective-permute-start.2
  381.4 36.8 %all-to-all-done.3 = f32[8,16,40,128]{3,2,1,0:T(8,128)S(1)} async-done(((f32[8,16,40,128]{3,2,1,0:T(8,128)}), f32[8,16,40,128]{3,2,1,0:T(8,128)S(1)}, u32[]{:S(2)}, u32[]{:S(2)}) %all-to-all-start.3) | async-done | bytes 2621472 | tf_op jit(solution)/shard_map/all_to_all | solution.py:379
  418.2 1.5 copy-done.1
  419.7 19.2 %head.3 = (f32[40,16,128]{2,1,0:T(8,128)}, f32[40,16,128]{2,1,0:T(8,128)}, f32[40,16,128]{2,1,0:T(8,128)}, f32[40,16,128]{2,1,0:T(8,128)}) custom-call(f32[128,128,128]{2,1,0:T(8,128)} %bitcast.34, f32[128,40,128]{2,1,0:T(8,128)} %bitcast.39, bf16[128,384]{1,0:T(8,128)(2,1)} %get-tuple-element.71.gate_ref, bf16[128,384]{1,0:T(8,128)(2,1)} %get-tuple-element.72.output_ref, ...), custom_call_target="tpu_custom_call" | custom-call | flops 912261120 | bytes 819200 | tf_op jit(solution)/shard_map/head/pallas_call | solution.py:243
  439.0 1.6 collective-permute-start.3
  441.1 1.4 collective-permute-start.5
  442.5 11.1 %product.4 = f32[8,16,56,128]{3,2,1,0:T(8,128)} custom-call(s32[1]{0:T(128)} %bitcast.1.half_ref, f32[8,16,96,128]{3,2,1,0:T(8,128)} %all-to-all-done.low_ref, f32[8,16,120,128]{3,2,1,0:T(8,128)} %all-to-all-done.2.high_ref, f32[8,16,56,128]{3,2,1,0:T(8,128)} %slice.8.own_ref, f32[8,16,56,128]{3,2,1,0:T(8,128)} %collective-permute-done.1.other_ref), custom_call_target="tpu_custom_call" | custom-call | flops 352321536 | bytes 1966080 | tf_op jit(solution)/shard_map/product/pallas_call | solution.py:189
  453.6 10.9 %collective-permute-done.2.other_ref = f32[8,16,32,128]{3,2,1,0:T(8,128)} collective-permute-done((f32[8,16,32,128]{3,2,1,0:T(8,128)}, f32[8,16,32,128]{3,2,1,0:T(8,128)}, u32[]{:S(2)}, u32[]{:S(2)}) %collective-permute-start.2) | collective-permute-done | bytes 2097184 | tf_op jit(solution)/shard_map/ppermute | solution.py:376
  464.5 6.8 %all-to-all-start.4 = ((f32[8,16,56,128]{3,2,1,0:T(8,128)}), f32[8,16,56,128]{3,2,1,0:T(8,128)}, u32[]{:S(2)}, u32[]{:S(2)}) async-start(f32[8,16,56,128]{3,2,1,0:T(8,128)} %product.4), calls=%async_computation.4 | async-start | bytes 7340032 | tf_op jit(solution)/shard_map/all_to_all | solution.py:379
  471.3 3.7 collective-permute-start.6
  475.1 3.0 collective-permute-start.7
  478.0 3.3 collective-permute-start.9
  481.3 10.1 %product.5 = f32[8,16,32,128]{3,2,1,0:T(8,128)} custom-call(s32[1]{0:T(128)} %bitcast.1.half_ref, f32[8,16,96,128]{3,2,1,0:T(8,128)} %all-to-all-done.low_ref, f32[8,16,120,128]{3,2,1,0:T(8,128)} %all-to-all-done.2.high_ref, f32[8,16,32,128]{3,2,1,0:T(8,128)} %slice.9.own_ref, f32[8,16,32,128]{3,2,1,0:T(8,128)} %collective-permute-done.2.other_ref), custom_call_target="tpu_custom_call" | custom-call | flops 201326592 | bytes 1572864 | tf_op jit(solution)/shard_map/product/pallas_call | solution.py:189
  491.4 1.8 collective-permute-done.6.refs_0_
  493.9 5.2 collective-permute-done.7.refs_1_
  499.8 24.0 %collective-permute-done.8.refs_2_ = f32[40,16,128]{2,1,0:T(8,128)S(1)} collective-permute-done((f32[40,16,128]{2,1,0:T(8,128)S(1)}, f32[40,16,128]{2,1,0:T(8,128)S(1)}, u32[]{:S(2)}, u32[]{:S(2)}) %collective-permute-start.8) | collective-permute-done | bytes 327712 | tf_op jit(solution)/shard_map/ppermute | solution.py:325
  524.6 22.3 %all-to-all-start.5 = ((f32[8,16,32,128]{3,2,1,0:T(8,128)}), f32[8,16,32,128]{3,2,1,0:T(8,128)S(1)}, u32[]{:S(2)}, u32[]{:S(2)}) async-start(f32[8,16,32,128]{3,2,1,0:T(8,128)} %product.5), calls=%async_computation.5 | async-start | bytes 4194304 | tf_op jit(solution)/shard_map/all_to_all | solution.py:379
  546.9 26.1 %head.4 = (f32[56,16,128]{2,1,0:T(8,128)}, f32[56,16,128]{2,1,0:T(8,128)}, f32[56,16,128]{2,1,0:T(8,128)}, f32[56,16,128]{2,1,0:T(8,128)}) custom-call(f32[128,128,128]{2,1,0:T(8,128)} %bitcast.35, f32[128,56,128]{2,1,0:T(8,128)} %bitcast.12.product_ref, bf16[128,384]{1,0:T(8,128)(2,1)} %get-tuple-element.71.gate_ref, ...), custom_call_target="tpu_custom_call" | custom-call | flops 1277165568 | bytes 1146880 | tf_op jit(solution)/shard_map/head/pallas_call | solution.py:243
  573.0 1.5 collective-permute-start.11
  576.4 16.0 %head.5 = (f32[32,16,128]{2,1,0:T(8,128)}, f32[32,16,128]{2,1,0:T(8,128)}, f32[32,16,128]{2,1,0:T(8,128)}, f32[32,16,128]{2,1,0:T(8,128)}) custom-call(f32[128,128,128]{2,1,0:T(8,128)} %bitcast.36, f32[128,32,128]{2,1,0:T(8,128)} %bitcast.41, bf16[128,384]{1,0:T(8,128)(2,1)} %get-tuple-element.71.gate_ref, bf16[128,384]{1,0:T(8,128)(2,1)} %get-tuple-element.72.output_ref, ...), custom_call_target="tpu_custom_call" | custom-call | flops 729808896 | bytes 655360 | tf_op jit(solution)/shard_map/head/pallas_call | solution.py:243
  593.0 2.4 collective-permute-start.15
  595.9 3.4 collective-permute-done.18
  599.3 1.9 collective-permute-start.10
  601.3 3.9 collective-permute-start.12
  605.1 13.0 %collective-permute-start.14 = (f32[56,16,128]{2,1,0:T(8,128)}, f32[56,16,128]{2,1,0:T(8,128)S(1)}, u32[]{:S(2)}, u32[]{:S(2)}) collective-permute-start(f32[56,16,128]{2,1,0:T(8,128)} %collective-permute-done.13), channel_id=1, source_target_pairs={{0,8},{1,12},{2,0},{3,4},{4,9},{5,13},{6,1},{7,5},{8,10},{9,14},{1... | collective-permute-start | bytes 1376264 | tf_op jit(solution)/shard_map/ppermute | solution.py:325
  618.1 7.6 %collective-permute-start.22 = (f32[32,16,128]{2,1,0:T(8,128)}, f32[32,16,128]{2,1,0:T(8,128)}, u32[]{:S(2)}, u32[]{:S(2)}) collective-permute-start(f32[32,16,128]{2,1,0:T(8,128)} %get-tuple-element.54.refs_11_), channel_id=1, source_target_pairs={{0,3},{1,2},{2,1},{3,0},{4,7},{5,6},{6,5},{7,4},{8,11},{9,10},{10,... | collective-permute-start | bytes 786440 | tf_op jit(solution)/shard_map/ppermute | solution.py:325
  625.8 16.8 %collective-permute-done.22 = f32[32,16,128]{2,1,0:T(8,128)} collective-permute-done((f32[32,16,128]{2,1,0:T(8,128)}, f32[32,16,128]{2,1,0:T(8,128)}, u32[]{:S(2)}, u32[]{:S(2)}) %collective-permute-start.22) | collective-permute-done | bytes 262176 | tf_op jit(solution)/shard_map/ppermute | solution.py:325
  642.6 1.9 collective-permute-start.17
  645.2 3.7 collective-permute-done.12.refs_1_
  650.1 6.3 turned.1.base_ref
  656.5 4.2 joined.3.base_ref
  661.5 5.4 joined.4.base_ref
  666.9 2.1 collective-permute-done.23.refs_3_
  669.7 3.5 joined.5
  (93 shorter events, 17.6 us)
Async XLA Ops:
  8.9 36.0 %all-to-all-start.1 = ((f32[8,16,40,128]{3,2,1,0:T(8,128)}), f32[8,16,40,128]{3,2,1,0:T(8,128)S(1)}, u32[]{:S(2)}, u32[]{:S(2)}) async-start(f32[8,16,40,128]{3,2,1,0:T(8,128)} %bitcast.40), calls=%async_computation.1 | async-start | bytes 5242880 | tf_op jit(solution)/shard_map/all_to_all | solution.py:368
  45.0 7.2 %copy-start = (f32[8,16,40,128]{3,2,1,0:T(8,128)}, f32[8,16,40,128]{3,2,1,0:T(8,128)S(1)}, u32[]{:S(2)}) copy-start(f32[8,16,40,128]{3,2,1,0:T(8,128)S(1)} %all-to-all-done.1.own_ref) | copy-start | bytes 7864324
  45.0 132.9 %all-to-all-start = ((f32[8,16,96,128]{3,2,1,0:T(8,128)}), f32[8,16,96,128]{3,2,1,0:T(8,128)}, u32[]{:S(2)}, u32[]{:S(2)}) async-start(f32[8,16,96,128]{3,2,1,0:T(8,128)} %bitcast.38), calls=%async_computation | async-start | bytes 12582912 | tf_op jit(solution)/shard_map/all_to_all | solution.py:368
  52.2 125.7 %collective-permute-start = (f32[8,16,40,128]{3,2,1,0:T(8,128)S(1)}, f32[8,16,40,128]{3,2,1,0:T(8,128)}, u32[]{:S(2)}, u32[]{:S(2)}) collective-permute-start(f32[8,16,40,128]{3,2,1,0:T(8,128)S(1)} %all-to-all-done.1.own_ref), channel_id=1, source_target_pairs={{0,8},{8,0},{1,9},{9,1},{2,10},{10,2},{3,11},{11,3},{4,12},{12,4},... | collective-permute-start | bytes 7864328 | tf_op jit(solution)/shard_map/ppermute | solution.py:376
  177.8 175.5 %all-to-all-start.2 = ((f32[8,16,120,128]{3,2,1,0:T(8,128)}), f32[8,16,120,128]{3,2,1,0:T(8,128)}, u32[]{:S(2)}, u32[]{:S(2)}) async-start(f32[8,16,120,128]{3,2,1,0:T(8,128)} %bitcast.37), calls=%async_computation.2 | async-start | bytes 15728640 | tf_op jit(solution)/shard_map/all_to_all | solution.py:368
  196.5 167.3 %collective-permute-start.1 = (f32[8,16,56,128]{3,2,1,0:T(8,128)}, f32[8,16,56,128]{3,2,1,0:T(8,128)}, u32[]{:S(2)}, u32[]{:S(2)}) collective-permute-start(f32[8,16,56,128]{3,2,1,0:T(8,128)} %slice.8.own_ref), channel_id=1, source_target_pairs={{0,8},{8,0},{1,9},{9,1},{2,10},{10,2},{3,11},{11,3},{4,12},{12,4},... | collective-permute-start | bytes 11010056 | tf_op jit(solution)/shard_map/ppermute | solution.py:376
  363.8 6.8 %copy-start.17 = (f32[128,128]{1,0:T(8,128)S(1)}, f32[128,128]{1,0:T(8,128)}, u32[]{:S(2)}) copy-start(f32[128,128]{1,0:T(8,128)} %param.15) | copy-start | bytes 196612
  363.8 6.9 %copy-start.18 = (f32[128,128]{1,0:T(8,128)S(1)}, f32[128,128]{1,0:T(8,128)}, u32[]{:S(2)}) copy-start(f32[128,128]{1,0:T(8,128)} %param.14) | copy-start | bytes 196612
  363.8 54.4 %all-to-all-start.3 = ((f32[8,16,40,128]{3,2,1,0:T(8,128)}), f32[8,16,40,128]{3,2,1,0:T(8,128)S(1)}, u32[]{:S(2)}, u32[]{:S(2)}) async-start(f32[8,16,40,128]{3,2,1,0:T(8,128)} %product.3), calls=%async_computation.3 | async-start | bytes 5242880 | tf_op jit(solution)/shard_map/all_to_all | solution.py:379
  372.1 6.6 copy-start.20
  372.1 6.6 copy-start.21
  372.1 7.4 %copy-start.22 = (f32[128]{0:T(128)S(1)}, f32[128]{0:T(128)}, u32[]{:S(2)}) copy-start(f32[128]{0:T(128)} %param.17) | copy-start | bytes 1540
  373.2 4.9 copy-start.19
  376.3 88.2 %collective-permute-start.2 = (f32[8,16,32,128]{3,2,1,0:T(8,128)}, f32[8,16,32,128]{3,2,1,0:T(8,128)}, u32[]{:S(2)}, u32[]{:S(2)}) collective-permute-start(f32[8,16,32,128]{3,2,1,0:T(8,128)} %slice.9.own_ref), channel_id=1, source_target_pairs={{0,8},{8,0},{1,9},{9,1},{2,10},{10,2},{3,11},{11,3},{4,12},{12,4},... | collective-permute-start | bytes 6291464 | tf_op jit(solution)/shard_map/ppermute | solution.py:376
  418.2 1.5 copy-start.1
  439.0 25.5 %collective-permute-start.3 = (f32[40,16,128]{2,1,0:T(8,128)}, f32[40,16,128]{2,1,0:T(8,128)S(1)}, u32[]{:S(2)}, u32[]{:S(2)}) collective-permute-start(f32[40,16,128]{2,1,0:T(8,128)} %get-tuple-element.37.refs_3_), channel_id=1, source_target_pairs={{0,1},{1,0},{2,3},{3,2},{4,5},{5,4},{6,7},{7,6},{8,9},{9,8},{10,11... | collective-permute-start | bytes 983048 | tf_op jit(solution)/shard_map/ppermute | solution.py:325
  440.6 24.0 %collective-permute-start.4 = (f32[40,16,128]{2,1,0:T(8,128)}, f32[40,16,128]{2,1,0:T(8,128)S(1)}, u32[]{:S(2)}, u32[]{:S(2)}) collective-permute-start(f32[40,16,128]{2,1,0:T(8,128)} %get-tuple-element.38.refs_6_), channel_id=1, source_target_pairs={{0,2},{1,3},{2,0},{3,1},{4,6},{5,7},{6,4},{7,5},{8,10},{9,11},{10,... | collective-permute-start | bytes 983048 | tf_op jit(solution)/shard_map/ppermute | solution.py:325
  441.1 23.4 %collective-permute-start.5 = (f32[40,16,128]{2,1,0:T(8,128)}, f32[40,16,128]{2,1,0:T(8,128)S(1)}, u32[]{:S(2)}, u32[]{:S(2)}) collective-permute-start(f32[40,16,128]{2,1,0:T(8,128)} %get-tuple-element.39.refs_9_), channel_id=1, source_target_pairs={{0,3},{1,2},{2,1},{3,0},{4,7},{5,6},{6,5},{7,4},{8,11},{9,10},{10,... | collective-permute-start | bytes 983048 | tf_op jit(solution)/shard_map/ppermute | solution.py:325
  464.5 6.8 %copy-start.9 = (f32[40,16,128]{2,1,0:T(8,128)S(1)}, f32[40,16,128]{2,1,0:T(8,128)}, u32[]{:S(2)}) copy-start(f32[40,16,128]{2,1,0:T(8,128)} %get-tuple-element.43.refs_0_) | copy-start | bytes 983044
  464.5 60.0 %all-to-all-start.4 = ((f32[8,16,56,128]{3,2,1,0:T(8,128)}), f32[8,16,56,128]{3,2,1,0:T(8,128)}, u32[]{:S(2)}, u32[]{:S(2)}) async-start(f32[8,16,56,128]{3,2,1,0:T(8,128)} %product.4), calls=%async_computation.4 | async-start | bytes 7340032 | tf_op jit(solution)/shard_map/all_to_all | solution.py:379
  471.3 21.9 %collective-permute-start.6 = (f32[40,16,128]{2,1,0:T(8,128)S(1)}, f32[40,16,128]{2,1,0:T(8,128)S(1)}, u32[]{:S(2)}, u32[]{:S(2)}) collective-permute-start(f32[40,16,128]{2,1,0:T(8,128)S(1)} %copy-done.9), channel_id=1, source_target_pairs={{0,0},{1,4},{2,8},{3,12},{4,1},{5,5},{6,9},{7,13},{8,2},{9,6},{10,... | collective-permute-start | bytes 983048 | tf_op jit(solution)/shard_map/ppermute | solution.py:325
  475.1 24.0 %collective-permute-start.7 = (f32[40,16,128]{2,1,0:T(8,128)S(1)}, f32[40,16,128]{2,1,0:T(8,128)S(1)}, u32[]{:S(2)}, u32[]{:S(2)}) collective-permute-start(f32[40,16,128]{2,1,0:T(8,128)S(1)} %collective-permute-done.3), channel_id=1, source_target_pairs={{0,4},{1,0},{2,12},{3,8},{4,5},{5,1},{6,13},{7,9},{8,6},{9,2},{10,... | collective-permute-start | bytes 983048 | tf_op jit(solution)/shard_map/ppermute | solution.py:325
  478.0 45.8 %collective-permute-start.8 = (f32[40,16,128]{2,1,0:T(8,128)S(1)}, f32[40,16,128]{2,1,0:T(8,128)S(1)}, u32[]{:S(2)}, u32[]{:S(2)}) collective-permute-start(f32[40,16,128]{2,1,0:T(8,128)S(1)} %collective-permute-done.4), channel_id=1, source_target_pairs={{0,8},{1,12},{2,0},{3,4},{4,9},{5,13},{6,1},{7,5},{8,10},{9,14},{1... | collective-permute-start | bytes 983048 | tf_op jit(solution)/shard_map/ppermute | solution.py:325
  478.0 46.5 %collective-permute-start.9 = (f32[40,16,128]{2,1,0:T(8,128)S(1)}, f32[40,16,128]{2,1,0:T(8,128)}, u32[]{:S(2)}, u32[]{:S(2)}) collective-permute-start(f32[40,16,128]{2,1,0:T(8,128)S(1)} %collective-permute-done.5), channel_id=1, source_target_pairs={{0,12},{1,8},{2,4},{3,0},{4,13},{5,9},{6,5},{7,1},{8,14},{9,10},{1... | collective-permute-start | bytes 983048 | tf_op jit(solution)/shard_map/ppermute | solution.py:325
  524.6 50.5 %all-to-all-start.5 = ((f32[8,16,32,128]{3,2,1,0:T(8,128)}), f32[8,16,32,128]{3,2,1,0:T(8,128)S(1)}, u32[]{:S(2)}, u32[]{:S(2)}) async-start(f32[8,16,32,128]{3,2,1,0:T(8,128)} %product.5), calls=%async_computation.5 | async-start | bytes 4194304 | tf_op jit(solution)/shard_map/all_to_all | solution.py:379
  573.0 28.2 %collective-permute-start.11 = (f32[56,16,128]{2,1,0:T(8,128)}, f32[56,16,128]{2,1,0:T(8,128)}, u32[]{:S(2)}, u32[]{:S(2)}) collective-permute-start(f32[56,16,128]{2,1,0:T(8,128)} %get-tuple-element.49.refs_4_), channel_id=1, source_target_pairs={{0,1},{1,0},{2,3},{3,2},{4,5},{5,4},{6,7},{7,6},{8,9},{9,8},{10,11... | collective-permute-start | bytes 1376264 | tf_op jit(solution)/shard_map/ppermute | solution.py:325
  574.5 30.6 %collective-permute-start.13 = (f32[56,16,128]{2,1,0:T(8,128)}, f32[56,16,128]{2,1,0:T(8,128)}, u32[]{:S(2)}, u32[]{:S(2)}) collective-permute-start(f32[56,16,128]{2,1,0:T(8,128)} %get-tuple-element.51.refs_7_), channel_id=1, source_target_pairs={{0,2},{1,3},{2,0},{3,1},{4,6},{5,7},{6,4},{7,5},{8,10},{9,11},{10,... | collective-permute-start | bytes 1376264 | tf_op jit(solution)/shard_map/ppermute | solution.py:325
  576.4 16.6 %copy-start.4 = (f32[56,16,128]{2,1,0:T(8,128)S(1)}, f32[56,16,128]{2,1,0:T(8,128)}, u32[]{:S(2)}) copy-start(f32[56,16,128]{2,1,0:T(8,128)} %get-tuple-element.53.refs_10_) | copy-start | bytes 1376260
  576.4 22.9 %copy-start.3 = (f32[56,16,128]{2,1,0:T(8,128)S(1)}, f32[56,16,128]{2,1,0:T(8,128)}, u32[]{:S(2)}) copy-start(f32[56,16,128]{2,1,0:T(8,128)} %get-tuple-element.41.refs_1_) | copy-start | bytes 1376260
  576.4 72.9 %copy-start.23 = (f32[64]{0:T(128)S(1)}, f32[64]{0:T(128)}, u32[]{:S(2)}) copy-start(f32[64]{0:T(128)} %param.21) | copy-start | bytes 772
  592.4 6.9 %collective-permute-start.18 = (f32[32,16,128]{2,1,0:T(8,128)}, f32[32,16,128]{2,1,0:T(8,128)}, u32[]{:S(2)}, u32[]{:S(2)}) collective-permute-start(f32[32,16,128]{2,1,0:T(8,128)} %get-tuple-element.50.refs_5_), channel_id=1, source_target_pairs={{0,1},{1,0},{2,3},{3,2},{4,5},{5,4},{6,7},{7,6},{8,9},{9,8},{10,11... | collective-permute-start | bytes 786440 | tf_op jit(solution)/shard_map/ppermute | solution.py:325
  593.0 32.8 %collective-permute-start.15 = (f32[56,16,128]{2,1,0:T(8,128)S(1)}, f32[56,16,128]{2,1,0:T(8,128)S(1)}, u32[]{:S(2)}, u32[]{:S(2)}) collective-permute-start(f32[56,16,128]{2,1,0:T(8,128)S(1)} %copy-done.4), channel_id=1, source_target_pairs={{0,3},{1,2},{2,1},{3,0},{4,7},{5,6},{6,5},{7,4},{8,11},{9,10},{10,... | collective-permute-start | bytes 1376264 | tf_op jit(solution)/shard_map/ppermute | solution.py:325
  595.4 22.8 %collective-permute-start.20 = (f32[32,16,128]{2,1,0:T(8,128)}, f32[32,16,128]{2,1,0:T(8,128)}, u32[]{:S(2)}, u32[]{:S(2)}) collective-permute-start(f32[32,16,128]{2,1,0:T(8,128)} %get-tuple-element.52.refs_8_), channel_id=1, source_target_pairs={{0,2},{1,3},{2,0},{3,1},{4,6},{5,7},{6,4},{7,5},{8,10},{9,11},{10,... | collective-permute-start | bytes 786440 | tf_op jit(solution)/shard_map/ppermute | solution.py:325
  599.3 45.2 %collective-permute-start.10 = (f32[56,16,128]{2,1,0:T(8,128)S(1)}, f32[56,16,128]{2,1,0:T(8,128)S(1)}, u32[]{:S(2)}, u32[]{:S(2)}) collective-permute-start(f32[56,16,128]{2,1,0:T(8,128)S(1)} %copy-done.3), channel_id=1, source_target_pairs={{0,0},{1,4},{2,8},{3,12},{4,1},{5,5},{6,9},{7,13},{8,2},{9,6},{10,... | collective-permute-start | bytes 1376264 | tf_op jit(solution)/shard_map/ppermute | solution.py:325
  601.3 47.7 %collective-permute-start.12 = (f32[56,16,128]{2,1,0:T(8,128)}, f32[56,16,128]{2,1,0:T(8,128)S(1)}, u32[]{:S(2)}, u32[]{:S(2)}) collective-permute-start(f32[56,16,128]{2,1,0:T(8,128)} %collective-permute-done.11), channel_id=1, source_target_pairs={{0,4},{1,0},{2,12},{3,8},{4,5},{5,1},{6,13},{7,9},{8,6},{9,2},{10,... | collective-permute-start | bytes 1376264 | tf_op jit(solution)/shard_map/ppermute | solution.py:325
  605.1 43.8 %collective-permute-start.14 = (f32[56,16,128]{2,1,0:T(8,128)}, f32[56,16,128]{2,1,0:T(8,128)S(1)}, u32[]{:S(2)}, u32[]{:S(2)}) collective-permute-start(f32[56,16,128]{2,1,0:T(8,128)} %collective-permute-done.13), channel_id=1, source_target_pairs={{0,8},{1,12},{2,0},{3,4},{4,9},{5,13},{6,1},{7,5},{8,10},{9,14},{1... | collective-permute-start | bytes 1376264 | tf_op jit(solution)/shard_map/ppermute | solution.py:325
  618.1 24.5 %collective-permute-start.22 = (f32[32,16,128]{2,1,0:T(8,128)}, f32[32,16,128]{2,1,0:T(8,128)}, u32[]{:S(2)}, u32[]{:S(2)}) collective-permute-start(f32[32,16,128]{2,1,0:T(8,128)} %get-tuple-element.54.refs_11_), channel_id=1, source_target_pairs={{0,3},{1,2},{2,1},{3,0},{4,7},{5,6},{6,5},{7,4},{8,11},{9,10},{10,... | collective-permute-start | bytes 786440 | tf_op jit(solution)/shard_map/ppermute | solution.py:325
  625.8 34.9 %collective-permute-start.16 = (f32[56,16,128]{2,1,0:T(8,128)S(1)}, f32[56,16,128]{2,1,0:T(8,128)S(1)}, u32[]{:S(2)}, u32[]{:S(2)}) collective-permute-start(f32[56,16,128]{2,1,0:T(8,128)S(1)} %collective-permute-done.15), channel_id=1, source_target_pairs={{0,12},{1,8},{2,4},{3,0},{4,13},{5,9},{6,5},{7,1},{8,14},{9,10},{1... | collective-permute-start | bytes 1376264 | tf_op jit(solution)/shard_map/ppermute | solution.py:325
  642.6 24.3 %collective-permute-start.17 = (f32[32,16,128]{2,1,0:T(8,128)}, f32[32,16,128]{2,1,0:T(8,128)S(1)}, u32[]{:S(2)}, u32[]{:S(2)}) collective-permute-start(f32[32,16,128]{2,1,0:T(8,128)} %get-tuple-element.48.refs_2_), channel_id=1, source_target_pairs={{0,0},{1,4},{2,8},{3,12},{4,1},{5,5},{6,9},{7,13},{8,2},{9,6},{10,... | collective-permute-start | bytes 786440 | tf_op jit(solution)/shard_map/ppermute | solution.py:325
  644.5 11.9 %copy-start.5 = (f32[56,16,128]{2,1,0:T(8,128)}, f32[56,16,128]{2,1,0:T(8,128)S(1)}, u32[]{:S(2)}) copy-start(f32[56,16,128]{2,1,0:T(8,128)S(1)} %collective-permute-done.10.refs_0_) | copy-start | bytes 1376260
  644.5 22.4 %collective-permute-start.19 = (f32[32,16,128]{2,1,0:T(8,128)}, f32[32,16,128]{2,1,0:T(8,128)S(1)}, u32[]{:S(2)}, u32[]{:S(2)}) collective-permute-start(f32[32,16,128]{2,1,0:T(8,128)} %collective-permute-done.18), channel_id=1, source_target_pairs={{0,4},{1,0},{2,12},{3,8},{4,5},{5,1},{6,13},{7,9},{8,6},{9,2},{10,... | collective-permute-start | bytes 786440 | tf_op jit(solution)/shard_map/ppermute | solution.py:325
  649.0 7.5 %copy-start.6 = (f32[56,16,128]{2,1,0:T(8,128)}, f32[56,16,128]{2,1,0:T(8,128)S(1)}, u32[]{:S(2)}) copy-start(f32[56,16,128]{2,1,0:T(8,128)S(1)} %collective-permute-done.12.refs_1_) | copy-start | bytes 1376260
  649.0 17.9 %collective-permute-start.21 = (f32[32,16,128]{2,1,0:T(8,128)}, f32[32,16,128]{2,1,0:T(8,128)S(1)}, u32[]{:S(2)}, u32[]{:S(2)}) collective-permute-start(f32[32,16,128]{2,1,0:T(8,128)} %collective-permute-done.20), channel_id=1, source_target_pairs={{0,8},{1,12},{2,0},{3,4},{4,9},{5,13},{6,1},{7,5},{8,10},{9,14},{1... | collective-permute-start | bytes 786440 | tf_op jit(solution)/shard_map/ppermute | solution.py:325
  649.0 7.5 %copy-start.7 = (f32[56,16,128]{2,1,0:T(8,128)}, f32[56,16,128]{2,1,0:T(8,128)S(1)}, u32[]{:S(2)}) copy-start(f32[56,16,128]{2,1,0:T(8,128)S(1)} %collective-permute-done.14.refs_2_) | copy-start | bytes 1376260
  649.0 20.0 %collective-permute-start.23 = (f32[32,16,128]{2,1,0:T(8,128)}, f32[32,16,128]{2,1,0:T(8,128)S(1)}, u32[]{:S(2)}, u32[]{:S(2)}) collective-permute-start(f32[32,16,128]{2,1,0:T(8,128)} %collective-permute-done.22), channel_id=1, source_target_pairs={{0,12},{1,8},{2,4},{3,0},{4,13},{5,9},{6,5},{7,1},{8,14},{9,10},{1... | collective-permute-start | bytes 786440 | tf_op jit(solution)/shard_map/ppermute | solution.py:325
  666.9 2.1 copy-start.13
  666.9 2.1 copy-start.14
  666.9 2.1 copy-start.15
  (6 other events, 5.0 us)

commit v11 on v10

--- a/solution.py
+++ b/solution.py
@@ -375,9 +375,11 @@
     def exchange(values):
         return lax.ppermute(values, "half", [(0, 1), (1, 0)])
 
-    def finish(values, chunk):
+    def delivered(values):
         values = lax.all_to_all(values, ("lo", "col"), split_axis=0, concat_axis=0, tiled=True)
-        values = values.reshape(width, CHUNKS[chunk], tile_rows)
+        return values.reshape(width, values.shape[2], tile_rows)
+
+    def run_head(values, chunk):
         return head(tile, values, firsts[chunk], gate3, output3, up3, down3, bins3)
 
     right = spread(hands(tile, in3, (0, 0), (firsts[0], CHUNKS[0])))
@@ -395,18 +397,22 @@
         return product(half, low, high, rights[chunk], others[chunk], tile_rows)
 
     values, others[1] = tie((blocks(0), others[1]))
-    own = [finish(values, 0)]
+    own = [run_head(delivered(values), 0)]
     shifted = aside(own[0], row_count)
     values, others[2], shifted = tie((blocks(1), others[2], shifted))
     mirror = [across(shifted, row_count)]
-    own.append(finish(values, 1))
-    values, mirror[0] = tie((blocks(2), mirror[0]))
-    own.append(finish(values, 2))
-    mirror += [across(aside(block, row_count), row_count) for block in own[1:]]
+    values, after = tie((delivered(values), blocks(2)))
+    own.append(run_head(values, 1))
+    values, mirror[0] = tie((delivered(after), mirror[0]))
+    own.append(run_head(values, 2))
+    mirror.append(across(aside(own[1], row_count), row_count))
+    shifted = aside(own[2], row_count)
     bins = distogram_bias.shape[0] // PARTS
     bias = jnp.broadcast_to(distogram_bias.reshape(PARTS, bins, 1), (PARTS, bins, tile_cols))
-    logits = turned(bias, own)
-    for first, block in zip(firsts, mirror):
+    logits = joined(turned(bias, own), mirror[0], firsts[0])
+    logits, shifted[1:] = tie((logits, shifted[1:]))
+    mirror.append(across(shifted, row_count))
+    for first, block in zip(firsts[1:], mirror[1:]):
         logits = joined(logits, block, first)
     logits = logits.reshape(tile_rows, PARTS * bins, tile_cols)
     return jnp.swapaxes(logits, 1, 2)[None]

time: 677 us -> 677 us (level)
  starting transfers between devices: 116 us -> 129 us
  waiting for transfers between devices: 386 us -> 376 us
    ppermute x21, waiting for transfers between devices: 57 us -> 16.8 us  [move(): return lax.ppermute(values, ('half', 'lo', 'col'), pairs)]
    ppermute x21, starting transfers between devices: 48.5 us -> 78.3 us  [move(): return lax.ppermute(values, ('half', 'lo', 'col'), pairs)]
    all_to_all x3, waiting for transfers between devices: 36.8 us -> 66.4 us  [delivered(): lax.all_to_all(values, ('lo', 'col'), split_axis=0, concat_axis=0, tiled=...]
    all_to_all x3, starting transfers between devices: 35.9 us -> 19.3 us  [delivered(): lax.all_to_all(values, ('lo', 'col'), split_axis=0, concat_axis=0, tiled=...]
  transfers between devices with their start and end apart: 30 -> 30, of which waited for: 12 -> 10; matrix products, arithmetic and copies ran while one was open for 2% -> 2% of each run, Pallas kernels for 21% -> 20%
where the time goes in v11:
time: 677 us; the launch traced here: 675 us
  waiting for transfers between devices  376 us (56%)
  Pallas kernels  148 us (22%)
  starting transfers between devices  129 us (19%)
  local copies, waits for them, and re-layouts  16.7 us (2%)
    all_to_all x3, waiting for transfers between devices, spread(): lax.all_to_all(values, ('lo', 'col'), split_axis=0, concat_axis=0, tiled=...  175 us
    ppermute x3, waiting for transfers between devices, exchange(): return lax.ppermute(values, 'half', [(0, 1), (1, 0)])  118 us
    ppermute x21, starting transfers between devices, move(): return lax.ppermute(values, ('half', 'lo', 'col'), pairs)  78.3 us
    all_to_all x3, waiting for transfers between devices, delivered(): lax.all_to_all(values, ('lo', 'col'), split_axis=0, concat_axis=0, tiled=...  66.4 us
    pallas_call x3, Pallas kernels, head(): pl.pallas_call(head_kernel, grid=(steps,), in_specs=[pl.BlockSpec((tile_r...  61.4 us
    pallas_call x3, Pallas kernels, hands(): pl.pallas_call(hands_kernel, grid=(rows // GROUP,), in_specs=[pl.BlockSpe...  35.6 us
    pallas_call x3, Pallas kernels, product(): pl.pallas_call(product_kernel, grid_spec=pltpu.PrefetchScalarGridSpec(num...  31.6 us
    all_to_all x3, starting transfers between devices, spread(): lax.all_to_all(values, ('lo', 'col'), split_axis=0, concat_axis=0, tiled=...  26.8 us
  transfers between devices with their start and end apart: 30, of which 10 were waited for; matrix products, arithmetic and copies ran while one was open for 2% of the time, Pallas kernels for 20%

profile of v11, /device:TPU:12, one launch (start us, length us, event | category | flops | bytes accessed | tf_op | source)
XLA Modules:
  0.0 674.7 jit_solution(13254087193734838750)
XLA Ops:
  2.6 6.4 hands.5
  9.0 5.1 all-to-all-start.1
  14.1 13.1 %hands.3 = f32[128,96,128]{2,1,0:T(8,128)} custom-call(f32[128,128,128]{2,1,0:T(8,128)} %bitcast.32, bf16[512,384]{1,0:T(8,128)(2,1)} %pad_maximum_fusion.1.weights_ref), custom_call_target="tpu_custom_call" | custom-call | flops 301989888 | bytes 1572864 | tf_op jit(solution)/shard_map/hands/pallas_call | solution.py:132
  27.2 17.8 %all-to-all-done.1.own_ref = f32[8,16,40,128]{3,2,1,0:T(8,128)S(1)} async-done(((f32[8,16,40,128]{3,2,1,0:T(8,128)}), f32[8,16,40,128]{3,2,1,0:T(8,128)S(1)}, u32[]{:S(2)}, u32[]{:S(2)}) %all-to-all-start.1) | async-done | bytes 2621472 | tf_op jit(solution)/shard_map/all_to_all | solution.py:368
  45.0 7.2 %all-to-all-start = ((f32[8,16,96,128]{3,2,1,0:T(8,128)}), f32[8,16,96,128]{3,2,1,0:T(8,128)}, u32[]{:S(2)}, u32[]{:S(2)}) async-start(f32[8,16,96,128]{3,2,1,0:T(8,128)} %bitcast.38), calls=%async_computation | async-start | bytes 12582912 | tf_op jit(solution)/shard_map/all_to_all | solution.py:368
  52.1 2.6 collective-permute-start
  54.7 16.1 %hands.4 = f32[128,120,128]{2,1,0:T(8,128)} custom-call(f32[128,128,128]{2,1,0:T(8,128)} %bitcast.33, bf16[512,384]{1,0:T(8,128)(2,1)} %pad_maximum_fusion.1.weights_ref), custom_call_target="tpu_custom_call" | custom-call | flops 377487360 | bytes 1966080 | tf_op jit(solution)/shard_map/hands/pallas_call | solution.py:132
  70.9 107.0 %collective-permute-done.other_ref = f32[8,16,40,128]{3,2,1,0:T(8,128)} collective-permute-done((f32[8,16,40,128]{3,2,1,0:T(8,128)S(1)}, f32[8,16,40,128]{3,2,1,0:T(8,128)}, u32[]{:S(2)}, u32[]{:S(2)}) %collective-permute-start) | collective-permute-done | bytes 2621472 | tf_op jit(solution)/shard_map/ppermute | solution.py:376
  177.9 14.5 %all-to-all-start.2 = ((f32[8,16,120,128]{3,2,1,0:T(8,128)}), f32[8,16,120,128]{3,2,1,0:T(8,128)}, u32[]{:S(2)}, u32[]{:S(2)}) async-start(f32[8,16,120,128]{3,2,1,0:T(8,128)} %bitcast.37), calls=%async_computation.2 | async-start | bytes 15728640 | tf_op jit(solution)/shard_map/all_to_all | solution.py:368
  192.4 4.2 slice.8.own_ref
  196.6 156.8 %all-to-all-done.2.high_ref = f32[8,16,120,128]{3,2,1,0:T(8,128)} async-done(((f32[8,16,120,128]{3,2,1,0:T(8,128)}), f32[8,16,120,128]{3,2,1,0:T(8,128)}, u32[]{:S(2)}, u32[]{:S(2)}) %all-to-all-start.2) | async-done | bytes 7864352 | tf_op jit(solution)/shard_map/all_to_all | solution.py:368
  353.4 10.4 %product.3 = f32[8,16,40,128]{3,2,1,0:T(8,128)} custom-call(s32[1]{0:T(128)} %bitcast.1.half_ref, f32[8,16,96,128]{3,2,1,0:T(8,128)} %all-to-all-done.low_ref, f32[8,16,120,128]{3,2,1,0:T(8,128)} %all-to-all-done.2.high_ref, f32[8,16,40,128]{3,2,1,0:T(8,128)} %copy-done, f32[8,16,40,128]{3,2,1,0:T(8,128)} %collective-permute-done.other_ref), custom_call_target="tpu_custom_call" | custom-call | flops 251658240 | bytes 1703936 | tf_op jit(solution)/shard_map/product/pallas_call | solution.py:189
  363.8 6.7 all-to-all-start.3
  373.1 3.1 slice.9.own_ref
  376.3 1.9 collective-permute-start.2
  381.4 36.8 %all-to-all-done.3 = f32[8,16,40,128]{3,2,1,0:T(8,128)S(1)} async-done(((f32[8,16,40,128]{3,2,1,0:T(8,128)}), f32[8,16,40,128]{3,2,1,0:T(8,128)S(1)}, u32[]{:S(2)}, u32[]{:S(2)}) %all-to-all-start.3) | async-done | bytes 2621472 | tf_op jit(solution)/shard_map/all_to_all | solution.py:379
  418.2 1.5 copy-done.1
  419.7 19.2 %head.3 = (f32[40,16,128]{2,1,0:T(8,128)}, f32[40,16,128]{2,1,0:T(8,128)}, f32[40,16,128]{2,1,0:T(8,128)}, f32[40,16,128]{2,1,0:T(8,128)}) custom-call(f32[128,128,128]{2,1,0:T(8,128)} %bitcast.34, f32[128,40,128]{2,1,0:T(8,128)} %bitcast.39, bf16[128,384]{1,0:T(8,128)(2,1)} %get-tuple-element.83.gate_ref, bf16[128,384]{1,0:T(8,128)(2,1)} %get-tuple-element.84.output_ref, ...), custom_call_target="tpu_custom_call" | custom-call | flops 912261120 | bytes 819200 | tf_op jit(solution)/shard_map/head/pallas_call | solution.py:243
  438.9 1.6 collective-permute-start.3
  442.4 11.1 %product.4 = f32[8,16,56,128]{3,2,1,0:T(8,128)} custom-call(s32[1]{0:T(128)} %bitcast.1.half_ref, f32[8,16,96,128]{3,2,1,0:T(8,128)} %all-to-all-done.low_ref, f32[8,16,120,128]{3,2,1,0:T(8,128)} %all-to-all-done.2.high_ref, f32[8,16,56,128]{3,2,1,0:T(8,128)} %slice.8.own_ref, f32[8,16,56,128]{3,2,1,0:T(8,128)} %collective-permute-done.1.other_ref), custom_call_target="tpu_custom_call" | custom-call | flops 352321536 | bytes 1966080 | tf_op jit(solution)/shard_map/product/pallas_call | solution.py:189
  453.5 11.1 %collective-permute-done.2.other_ref = f32[8,16,32,128]{3,2,1,0:T(8,128)} collective-permute-done((f32[8,16,32,128]{3,2,1,0:T(8,128)}, f32[8,16,32,128]{3,2,1,0:T(8,128)}, u32[]{:S(2)}, u32[]{:S(2)}) %collective-permute-start.2) | collective-permute-done | bytes 2097184 | tf_op jit(solution)/shard_map/ppermute | solution.py:376
  464.6 6.5 all-to-all-start.4
  471.1 10.1 %product.5 = f32[8,16,32,128]{3,2,1,0:T(8,128)} custom-call(s32[1]{0:T(128)} %bitcast.1.half_ref, f32[8,16,96,128]{3,2,1,0:T(8,128)} %all-to-all-done.low_ref, f32[8,16,120,128]{3,2,1,0:T(8,128)} %all-to-all-done.2.high_ref, f32[8,16,32,128]{3,2,1,0:T(8,128)} %slice.9.own_ref, f32[8,16,32,128]{3,2,1,0:T(8,128)} %collective-permute-done.2.other_ref), custom_call_target="tpu_custom_call" | custom-call | flops 201326592 | bytes 1572864 | tf_op jit(solution)/shard_map/product/pallas_call | solution.py:189
  481.2 29.6 %all-to-all-done.4 = f32[8,16,56,128]{3,2,1,0:T(8,128)} async-done(((f32[8,16,56,128]{3,2,1,0:T(8,128)}), f32[8,16,56,128]{3,2,1,0:T(8,128)}, u32[]{:S(2)}, u32[]{:S(2)}) %all-to-all-start.4) | async-done | bytes 3670048 | tf_op jit(solution)/shard_map/all_to_all | solution.py:379
  510.8 6.1 all-to-all-start.5
  516.9 3.3 collective-permute-start.6
  520.2 3.4 collective-permute-start.7
  523.6 2.8 collective-permute-start.9
  526.4 26.1 %head.4 = (f32[56,16,128]{2,1,0:T(8,128)}, f32[56,16,128]{2,1,0:T(8,128)}, f32[56,16,128]{2,1,0:T(8,128)}, f32[56,16,128]{2,1,0:T(8,128)}) custom-call(f32[128,128,128]{2,1,0:T(8,128)} %bitcast.35, f32[128,56,128]{2,1,0:T(8,128)} %bitcast.12.product_ref, bf16[128,384]{1,0:T(8,128)(2,1)} %get-tuple-element.83.gate_ref, ...), custom_call_target="tpu_custom_call" | custom-call | flops 1277165568 | bytes 1146880 | tf_op jit(solution)/shard_map/head/pallas_call | solution.py:243
  552.6 1.5 collective-permute-start.14
  554.0 10.2 %collective-permute-start.16 = (f32[56,16,128]{2,1,0:T(8,128)}, f32[56,16,128]{2,1,0:T(8,128)}, u32[]{:S(2)}, u32[]{:S(2)}) collective-permute-start(f32[56,16,128]{2,1,0:T(8,128)} %get-tuple-element.59.refs_7_), channel_id=1, source_target_pairs={{0,2},{1,3},{2,0},{3,1},{4,6},{5,7},{6,4},{7,5},{8,10},{9,11},{10,... | collective-permute-start | bytes 1376264 | tf_op jit(solution)/shard_map/ppermute | solution.py:325
  564.3 4.4 collective-permute-start.18
  570.7 16.0 %head.5 = (f32[32,16,128]{2,1,0:T(8,128)}, f32[32,16,128]{2,1,0:T(8,128)}, f32[32,16,128]{2,1,0:T(8,128)}, f32[32,16,128]{2,1,0:T(8,128)}) custom-call(f32[128,128,128]{2,1,0:T(8,128)} %bitcast.36, f32[128,32,128]{2,1,0:T(8,128)} %bitcast.41, bf16[128,384]{1,0:T(8,128)(2,1)} %get-tuple-element.83.gate_ref, bf16[128,384]{1,0:T(8,128)(2,1)} %get-tuple-element.84.output_ref, ...), custom_call_target="tpu_custom_call" | custom-call | flops 729808896 | bytes 655360 | tf_op jit(solution)/shard_map/head/pallas_call | solution.py:243
  586.7 7.2 %collective-permute-start.13 = (f32[56,16,128]{2,1,0:T(8,128)S(1)}, f32[56,16,128]{2,1,0:T(8,128)S(1)}, u32[]{:S(2)}, u32[]{:S(2)}) collective-permute-start(f32[56,16,128]{2,1,0:T(8,128)S(1)} %copy-done.3), channel_id=1, source_target_pairs={{0,0},{1,4},{2,8},{3,12},{4,1},{5,5},{6,9},{7,13},{8,2},{9,6},{10,... | collective-permute-start | bytes 1376264 | tf_op jit(solution)/shard_map/ppermute | solution.py:325
  594.1 2.2 collective-permute-start.15
  596.2 3.7 collective-permute-start.17
  599.9 9.3 %collective-permute-start.12 = (f32[32,16,128]{2,1,0:T(8,128)}, f32[32,16,128]{2,1,0:T(8,128)}, u32[]{:S(2)}, u32[]{:S(2)}) collective-permute-start(f32[32,16,128]{2,1,0:T(8,128)} %get-tuple-element.62.refs_11_), channel_id=1, source_target_pairs={{0,3},{1,2},{2,1},{3,0},{4,7},{5,6},{6,5},{7,4},{8,11},{9,10},{10,... | collective-permute-start | bytes 786440 | tf_op jit(solution)/shard_map/ppermute | solution.py:325
  609.2 15.4 %collective-permute-start.19 = (f32[56,16,128]{2,1,0:T(8,128)}, f32[56,16,128]{2,1,0:T(8,128)S(1)}, u32[]{:S(2)}, u32[]{:S(2)}) collective-permute-start(f32[56,16,128]{2,1,0:T(8,128)} %collective-permute-done.18), channel_id=1, source_target_pairs={{0,12},{1,8},{2,4},{3,0},{4,13},{5,9},{6,5},{7,1},{8,14},{9,10},{1... | collective-permute-start | bytes 1376264 | tf_op jit(solution)/shard_map/ppermute | solution.py:325
  625.4 6.3 turned.1.base_ref
  631.8 4.3 joined.3.base_ref
  636.0 3.2 collective-permute-start.20
  639.3 5.0 collective-permute-start.21
  644.3 3.1 collective-permute-start.23
  648.2 5.4 joined.4.base_ref
  653.6 7.9 %collective-permute-done.20.refs_0_ = f32[32,16,128]{2,1,0:T(8,128)S(1)} collective-permute-done((f32[32,16,128]{2,1,0:T(8,128)S(1)}, f32[32,16,128]{2,1,0:T(8,128)S(1)}, u32[]{:S(2)}, u32[]{:S(2)}) %collective-permute-start.20) | collective-permute-done | bytes 262176 | tf_op jit(solution)/shard_map/ppermute | solution.py:325
  662.4 3.2 collective-permute-done.22.refs_2_
  665.6 4.8 collective-permute-done.23.refs_3_
  671.1 3.5 joined.5
  (93 shorter events, 15.7 us)
Async XLA Ops:
  9.0 36.0 %all-to-all-start.1 = ((f32[8,16,40,128]{3,2,1,0:T(8,128)}), f32[8,16,40,128]{3,2,1,0:T(8,128)S(1)}, u32[]{:S(2)}, u32[]{:S(2)}) async-start(f32[8,16,40,128]{3,2,1,0:T(8,128)} %bitcast.40), calls=%async_computation.1 | async-start | bytes 5242880 | tf_op jit(solution)/shard_map/all_to_all | solution.py:368
  45.0 7.2 %copy-start = (f32[8,16,40,128]{3,2,1,0:T(8,128)}, f32[8,16,40,128]{3,2,1,0:T(8,128)S(1)}, u32[]{:S(2)}) copy-start(f32[8,16,40,128]{3,2,1,0:T(8,128)S(1)} %all-to-all-done.1.own_ref) | copy-start | bytes 7864324
  45.0 132.9 %all-to-all-start = ((f32[8,16,96,128]{3,2,1,0:T(8,128)}), f32[8,16,96,128]{3,2,1,0:T(8,128)}, u32[]{:S(2)}, u32[]{:S(2)}) async-start(f32[8,16,96,128]{3,2,1,0:T(8,128)} %bitcast.38), calls=%async_computation | async-start | bytes 12582912 | tf_op jit(solution)/shard_map/all_to_all | solution.py:368
  52.1 125.7 %collective-permute-start = (f32[8,16,40,128]{3,2,1,0:T(8,128)S(1)}, f32[8,16,40,128]{3,2,1,0:T(8,128)}, u32[]{:S(2)}, u32[]{:S(2)}) collective-permute-start(f32[8,16,40,128]{3,2,1,0:T(8,128)S(1)} %all-to-all-done.1.own_ref), channel_id=1, source_target_pairs={{0,8},{8,0},{1,9},{9,1},{2,10},{10,2},{3,11},{11,3},{4,12},{12,4},... | collective-permute-start | bytes 7864328 | tf_op jit(solution)/shard_map/ppermute | solution.py:376
  177.9 175.5 %all-to-all-start.2 = ((f32[8,16,120,128]{3,2,1,0:T(8,128)}), f32[8,16,120,128]{3,2,1,0:T(8,128)}, u32[]{:S(2)}, u32[]{:S(2)}) async-start(f32[8,16,120,128]{3,2,1,0:T(8,128)} %bitcast.37), calls=%async_computation.2 | async-start | bytes 15728640 | tf_op jit(solution)/shard_map/all_to_all | solution.py:368
  196.6 167.3 %collective-permute-start.1 = (f32[8,16,56,128]{3,2,1,0:T(8,128)}, f32[8,16,56,128]{3,2,1,0:T(8,128)}, u32[]{:S(2)}, u32[]{:S(2)}) collective-permute-start(f32[8,16,56,128]{3,2,1,0:T(8,128)} %slice.8.own_ref), channel_id=1, source_target_pairs={{0,8},{8,0},{1,9},{9,1},{2,10},{10,2},{3,11},{11,3},{4,12},{12,4},... | collective-permute-start | bytes 11010056 | tf_op jit(solution)/shard_map/ppermute | solution.py:376
  363.8 6.7 copy-start.17
  363.8 6.8 %copy-start.18 = (f32[128,128]{1,0:T(8,128)S(1)}, f32[128,128]{1,0:T(8,128)}, u32[]{:S(2)}) copy-start(f32[128,128]{1,0:T(8,128)} %param.14) | copy-start | bytes 196612
  363.8 54.4 %all-to-all-start.3 = ((f32[8,16,40,128]{3,2,1,0:T(8,128)}), f32[8,16,40,128]{3,2,1,0:T(8,128)S(1)}, u32[]{:S(2)}, u32[]{:S(2)}) async-start(f32[8,16,40,128]{3,2,1,0:T(8,128)} %product.3), calls=%async_computation.3 | async-start | bytes 5242880 | tf_op jit(solution)/shard_map/all_to_all | solution.py:379
  372.0 6.8 %copy-start.20 = (f32[128]{0:T(128)S(1)}, f32[128]{0:T(128)}, u32[]{:S(2)}) copy-start(f32[128]{0:T(128)} %param.12) | copy-start | bytes 1540
  372.0 6.8 %copy-start.21 = (f32[128]{0:T(128)S(1)}, f32[128]{0:T(128)}, u32[]{:S(2)}) copy-start(f32[128]{0:T(128)} %param.16) | copy-start | bytes 1540
  372.0 7.5 %copy-start.22 = (f32[128]{0:T(128)S(1)}, f32[128]{0:T(128)}, u32[]{:S(2)}) copy-start(f32[128]{0:T(128)} %param.17) | copy-start | bytes 1540
  373.1 5.0 copy-start.19
  376.3 88.3 %collective-permute-start.2 = (f32[8,16,32,128]{3,2,1,0:T(8,128)}, f32[8,16,32,128]{3,2,1,0:T(8,128)}, u32[]{:S(2)}, u32[]{:S(2)}) collective-permute-start(f32[8,16,32,128]{3,2,1,0:T(8,128)} %slice.9.own_ref), channel_id=1, source_target_pairs={{0,8},{8,0},{1,9},{9,1},{2,10},{10,2},{3,11},{11,3},{4,12},{12,4},... | collective-permute-start | bytes 6291464 | tf_op jit(solution)/shard_map/ppermute | solution.py:376
  438.9 25.7 %collective-permute-start.3 = (f32[40,16,128]{2,1,0:T(8,128)}, f32[40,16,128]{2,1,0:T(8,128)}, u32[]{:S(2)}, u32[]{:S(2)}) collective-permute-start(f32[40,16,128]{2,1,0:T(8,128)} %get-tuple-element.43.refs_3_), channel_id=1, source_target_pairs={{0,1},{1,0},{2,3},{3,2},{4,5},{5,4},{6,7},{7,6},{8,9},{9,8},{10,11... | collective-permute-start | bytes 983048 | tf_op jit(solution)/shard_map/ppermute | solution.py:325
  440.5 24.1 %collective-permute-start.4 = (f32[40,16,128]{2,1,0:T(8,128)}, f32[40,16,128]{2,1,0:T(8,128)}, u32[]{:S(2)}, u32[]{:S(2)}) collective-permute-start(f32[40,16,128]{2,1,0:T(8,128)} %get-tuple-element.44.refs_6_), channel_id=1, source_target_pairs={{0,2},{1,3},{2,0},{3,1},{4,6},{5,7},{6,4},{7,5},{8,10},{9,11},{10,... | collective-permute-start | bytes 983048 | tf_op jit(solution)/shard_map/ppermute | solution.py:325
  441.0 23.6 %collective-permute-start.5 = (f32[40,16,128]{2,1,0:T(8,128)}, f32[40,16,128]{2,1,0:T(8,128)}, u32[]{:S(2)}, u32[]{:S(2)}) collective-permute-start(f32[40,16,128]{2,1,0:T(8,128)} %get-tuple-element.45.refs_9_), channel_id=1, source_target_pairs={{0,3},{1,2},{2,1},{3,0},{4,7},{5,6},{6,5},{7,4},{8,11},{9,10},{10,... | collective-permute-start | bytes 983048 | tf_op jit(solution)/shard_map/ppermute | solution.py:325
  464.6 46.2 %all-to-all-start.4 = ((f32[8,16,56,128]{3,2,1,0:T(8,128)}), f32[8,16,56,128]{3,2,1,0:T(8,128)}, u32[]{:S(2)}, u32[]{:S(2)}) async-start(f32[8,16,56,128]{3,2,1,0:T(8,128)} %product.4), calls=%async_computation.4 | async-start | bytes 7340032 | tf_op jit(solution)/shard_map/all_to_all | solution.py:379
  481.2 35.7 %copy-start.8 = (f32[40,16,128]{2,1,0:T(8,128)S(1)}, f32[40,16,128]{2,1,0:T(8,128)}, u32[]{:S(2)}) copy-start(f32[40,16,128]{2,1,0:T(8,128)} %get-tuple-element.51.refs_0_) | copy-start | bytes 983044
  510.8 57.9 %all-to-all-start.5 = ((f32[8,16,32,128]{3,2,1,0:T(8,128)}), f32[8,16,32,128]{3,2,1,0:T(8,128)S(1)}, u32[]{:S(2)}, u32[]{:S(2)}) async-start(f32[8,16,32,128]{3,2,1,0:T(8,128)} %product.5), calls=%async_computation.5 | async-start | bytes 4194304 | tf_op jit(solution)/shard_map/all_to_all | solution.py:379
  516.9 37.1 %collective-permute-start.6 = (f32[40,16,128]{2,1,0:T(8,128)S(1)}, f32[40,16,128]{2,1,0:T(8,128)S(1)}, u32[]{:S(2)}, u32[]{:S(2)}) collective-permute-start(f32[40,16,128]{2,1,0:T(8,128)S(1)} %copy-done.8), channel_id=1, source_target_pairs={{0,0},{1,4},{2,8},{3,12},{4,1},{5,5},{6,9},{7,13},{8,2},{9,6},{10,... | collective-permute-start | bytes 983048 | tf_op jit(solution)/shard_map/ppermute | solution.py:325
  520.2 44.1 %collective-permute-start.7 = (f32[40,16,128]{2,1,0:T(8,128)}, f32[40,16,128]{2,1,0:T(8,128)S(1)}, u32[]{:S(2)}, u32[]{:S(2)}) collective-permute-start(f32[40,16,128]{2,1,0:T(8,128)} %collective-permute-done.3), channel_id=1, source_target_pairs={{0,4},{1,0},{2,12},{3,8},{4,5},{5,1},{6,13},{7,9},{8,6},{9,2},{10,... | collective-permute-start | bytes 983048 | tf_op jit(solution)/shard_map/ppermute | solution.py:325
  523.6 45.0 %collective-permute-start.8 = (f32[40,16,128]{2,1,0:T(8,128)}, f32[40,16,128]{2,1,0:T(8,128)S(1)}, u32[]{:S(2)}, u32[]{:S(2)}) collective-permute-start(f32[40,16,128]{2,1,0:T(8,128)} %collective-permute-done.4), channel_id=1, source_target_pairs={{0,8},{1,12},{2,0},{3,4},{4,9},{5,13},{6,1},{7,5},{8,10},{9,14},{1... | collective-permute-start | bytes 983048 | tf_op jit(solution)/shard_map/ppermute | solution.py:325
  523.6 45.0 %collective-permute-start.9 = (f32[40,16,128]{2,1,0:T(8,128)}, f32[40,16,128]{2,1,0:T(8,128)}, u32[]{:S(2)}, u32[]{:S(2)}) collective-permute-start(f32[40,16,128]{2,1,0:T(8,128)} %collective-permute-done.5), channel_id=1, source_target_pairs={{0,12},{1,8},{2,4},{3,0},{4,13},{5,9},{6,5},{7,1},{8,14},{9,10},{1... | collective-permute-start | bytes 983048 | tf_op jit(solution)/shard_map/ppermute | solution.py:325
  552.6 41.4 %collective-permute-start.14 = (f32[56,16,128]{2,1,0:T(8,128)}, f32[56,16,128]{2,1,0:T(8,128)}, u32[]{:S(2)}, u32[]{:S(2)}) collective-permute-start(f32[56,16,128]{2,1,0:T(8,128)} %get-tuple-element.57.refs_4_), channel_id=1, source_target_pairs={{0,1},{1,0},{2,3},{3,2},{4,5},{5,4},{6,7},{7,6},{8,9},{9,8},{10,11... | collective-permute-start | bytes 1376264 | tf_op jit(solution)/shard_map/ppermute | solution.py:325
  554.0 77.7 %copy-start.9 = (f32[40,16,128]{2,1,0:T(8,128)}, f32[40,16,128]{2,1,0:T(8,128)S(1)}, u32[]{:S(2)}) copy-start(f32[40,16,128]{2,1,0:T(8,128)S(1)} %collective-permute-done.6.refs_0_) | copy-start | bytes 983044
  554.0 40.0 %collective-permute-start.16 = (f32[56,16,128]{2,1,0:T(8,128)}, f32[56,16,128]{2,1,0:T(8,128)}, u32[]{:S(2)}, u32[]{:S(2)}) collective-permute-start(f32[56,16,128]{2,1,0:T(8,128)} %get-tuple-element.59.refs_7_), channel_id=1, source_target_pairs={{0,2},{1,3},{2,0},{3,1},{4,6},{5,7},{6,4},{7,5},{8,10},{9,11},{10,... | collective-permute-start | bytes 1376264 | tf_op jit(solution)/shard_map/ppermute | solution.py:325
  564.2 67.5 %copy-start.10 = (f32[40,16,128]{2,1,0:T(8,128)}, f32[40,16,128]{2,1,0:T(8,128)S(1)}, u32[]{:S(2)}) copy-start(f32[40,16,128]{2,1,0:T(8,128)S(1)} %collective-permute-done.7.refs_1_) | copy-start | bytes 983044
  564.3 32.0 %collective-permute-start.18 = (f32[56,16,128]{2,1,0:T(8,128)}, f32[56,16,128]{2,1,0:T(8,128)}, u32[]{:S(2)}, u32[]{:S(2)}) collective-permute-start(f32[56,16,128]{2,1,0:T(8,128)} %get-tuple-element.61.refs_10_), channel_id=1, source_target_pairs={{0,3},{1,2},{2,1},{3,0},{4,7},{5,6},{6,5},{7,4},{8,11},{9,10},{10,... | collective-permute-start | bytes 1376264 | tf_op jit(solution)/shard_map/ppermute | solution.py:325
  570.7 16.0 %copy-start.3 = (f32[56,16,128]{2,1,0:T(8,128)S(1)}, f32[56,16,128]{2,1,0:T(8,128)}, u32[]{:S(2)}) copy-start(f32[56,16,128]{2,1,0:T(8,128)} %get-tuple-element.49.refs_1_) | copy-start | bytes 1376260
  570.7 54.0 %copy-start.23 = (f32[64]{0:T(128)S(1)}, f32[64]{0:T(128)}, u32[]{:S(2)}) copy-start(f32[64]{0:T(128)} %param.21) | copy-start | bytes 772
  586.7 13.2 %collective-permute-start.10 = (f32[32,16,128]{2,1,0:T(8,128)}, f32[32,16,128]{2,1,0:T(8,128)S(1)}, u32[]{:S(2)}, u32[]{:S(2)}) collective-permute-start(f32[32,16,128]{2,1,0:T(8,128)} %get-tuple-element.58.refs_5_), channel_id=1, source_target_pairs={{0,1},{1,0},{2,3},{3,2},{4,5},{5,4},{6,7},{7,6},{8,9},{9,8},{10,11... | collective-permute-start | bytes 786440 | tf_op jit(solution)/shard_map/ppermute | solution.py:325
  586.7 52.5 %collective-permute-start.13 = (f32[56,16,128]{2,1,0:T(8,128)S(1)}, f32[56,16,128]{2,1,0:T(8,128)S(1)}, u32[]{:S(2)}, u32[]{:S(2)}) collective-permute-start(f32[56,16,128]{2,1,0:T(8,128)S(1)} %copy-done.3), channel_id=1, source_target_pairs={{0,0},{1,4},{2,8},{3,12},{4,1},{5,5},{6,9},{7,13},{8,2},{9,6},{10,... | collective-permute-start | bytes 1376264 | tf_op jit(solution)/shard_map/ppermute | solution.py:325
  594.0 15.2 %collective-permute-start.11 = (f32[32,16,128]{2,1,0:T(8,128)}, f32[32,16,128]{2,1,0:T(8,128)}, u32[]{:S(2)}, u32[]{:S(2)}) collective-permute-start(f32[32,16,128]{2,1,0:T(8,128)} %get-tuple-element.60.refs_8_), channel_id=1, source_target_pairs={{0,2},{1,3},{2,0},{3,1},{4,6},{5,7},{6,4},{7,5},{8,10},{9,11},{10,... | collective-permute-start | bytes 786440 | tf_op jit(solution)/shard_map/ppermute | solution.py:325
  594.1 50.2 %collective-permute-start.15 = (f32[56,16,128]{2,1,0:T(8,128)}, f32[56,16,128]{2,1,0:T(8,128)S(1)}, u32[]{:S(2)}, u32[]{:S(2)}) collective-permute-start(f32[56,16,128]{2,1,0:T(8,128)} %collective-permute-done.14), channel_id=1, source_target_pairs={{0,4},{1,0},{2,12},{3,8},{4,5},{5,1},{6,13},{7,9},{8,6},{9,2},{10,... | collective-permute-start | bytes 1376264 | tf_op jit(solution)/shard_map/ppermute | solution.py:325
  596.2 48.0 %collective-permute-start.17 = (f32[56,16,128]{2,1,0:T(8,128)}, f32[56,16,128]{2,1,0:T(8,128)S(1)}, u32[]{:S(2)}, u32[]{:S(2)}) collective-permute-start(f32[56,16,128]{2,1,0:T(8,128)} %collective-permute-done.16), channel_id=1, source_target_pairs={{0,8},{1,12},{2,0},{3,4},{4,9},{5,13},{6,1},{7,5},{8,10},{9,14},{1... | collective-permute-start | bytes 1376264 | tf_op jit(solution)/shard_map/ppermute | solution.py:325
  599.9 36.1 %collective-permute-start.12 = (f32[32,16,128]{2,1,0:T(8,128)}, f32[32,16,128]{2,1,0:T(8,128)}, u32[]{:S(2)}, u32[]{:S(2)}) collective-permute-start(f32[32,16,128]{2,1,0:T(8,128)} %get-tuple-element.62.refs_11_), channel_id=1, source_target_pairs={{0,3},{1,2},{2,1},{3,0},{4,7},{5,6},{6,5},{7,4},{8,11},{9,10},{10,... | collective-permute-start | bytes 786440 | tf_op jit(solution)/shard_map/ppermute | solution.py:325
  609.2 38.2 %collective-permute-start.19 = (f32[56,16,128]{2,1,0:T(8,128)}, f32[56,16,128]{2,1,0:T(8,128)S(1)}, u32[]{:S(2)}, u32[]{:S(2)}) collective-permute-start(f32[56,16,128]{2,1,0:T(8,128)} %collective-permute-done.18), channel_id=1, source_target_pairs={{0,12},{1,8},{2,4},{3,0},{4,13},{5,9},{6,5},{7,1},{8,14},{9,10},{1... | collective-permute-start | bytes 1376264 | tf_op jit(solution)/shard_map/ppermute | solution.py:325
  631.8 4.3 copy-start.12
  636.0 25.5 %collective-permute-start.20 = (f32[32,16,128]{2,1,0:T(8,128)S(1)}, f32[32,16,128]{2,1,0:T(8,128)S(1)}, u32[]{:S(2)}, u32[]{:S(2)}) collective-permute-start(f32[32,16,128]{2,1,0:T(8,128)S(1)} %copy-done.12), channel_id=1, source_target_pairs={{0,0},{1,4},{2,8},{3,12},{4,1},{5,5},{6,9},{7,13},{8,2},{9,6},{10,... | collective-permute-start | bytes 786440 | tf_op jit(solution)/shard_map/ppermute | solution.py:325
  639.3 8.2 %copy-start.4 = (f32[56,16,128]{2,1,0:T(8,128)}, f32[56,16,128]{2,1,0:T(8,128)S(1)}, u32[]{:S(2)}) copy-start(f32[56,16,128]{2,1,0:T(8,128)S(1)} %collective-permute-done.13.refs_0_) | copy-start | bytes 1376260
  639.3 23.1 %collective-permute-start.21 = (f32[32,16,128]{2,1,0:T(8,128)S(1)}, f32[32,16,128]{2,1,0:T(8,128)S(1)}, u32[]{:S(2)}, u32[]{:S(2)}) collective-permute-start(f32[32,16,128]{2,1,0:T(8,128)S(1)} %collective-permute-done.10), channel_id=1, source_target_pairs={{0,4},{1,0},{2,12},{3,8},{4,5},{5,1},{6,13},{7,9},{8,6},{9,2},{10,... | collective-permute-start | bytes 786440 | tf_op jit(solution)/shard_map/ppermute | solution.py:325
  644.3 3.2 copy-start.5
  644.3 21.3 %collective-permute-start.22 = (f32[32,16,128]{2,1,0:T(8,128)}, f32[32,16,128]{2,1,0:T(8,128)S(1)}, u32[]{:S(2)}, u32[]{:S(2)}) collective-permute-start(f32[32,16,128]{2,1,0:T(8,128)} %collective-permute-done.11), channel_id=1, source_target_pairs={{0,8},{1,12},{2,0},{3,4},{4,9},{5,13},{6,1},{7,5},{8,10},{9,14},{1... | collective-permute-start | bytes 786440 | tf_op jit(solution)/shard_map/ppermute | solution.py:325
  644.3 26.1 %collective-permute-start.23 = (f32[32,16,128]{2,1,0:T(8,128)}, f32[32,16,128]{2,1,0:T(8,128)S(1)}, u32[]{:S(2)}, u32[]{:S(2)}) collective-permute-start(f32[32,16,128]{2,1,0:T(8,128)} %collective-permute-done.12), channel_id=1, source_target_pairs={{0,12},{1,8},{2,4},{3,0},{4,13},{5,9},{6,5},{7,1},{8,14},{9,10},{1... | collective-permute-start | bytes 786440 | tf_op jit(solution)/shard_map/ppermute | solution.py:325
  661.5 8.9 %copy-start.13 = (f32[32,16,128]{2,1,0:T(8,128)}, f32[32,16,128]{2,1,0:T(8,128)S(1)}, u32[]{:S(2)}) copy-start(f32[32,16,128]{2,1,0:T(8,128)S(1)} %collective-permute-done.20.refs_0_) | copy-start | bytes 786436
  662.4 8.0 %copy-start.14 = (f32[32,16,128]{2,1,0:T(8,128)}, f32[32,16,128]{2,1,0:T(8,128)S(1)}, u32[]{:S(2)}) copy-start(f32[32,16,128]{2,1,0:T(8,128)S(1)} %collective-permute-done.21.refs_1_) | copy-start | bytes 786436
  665.6 4.8 copy-start.15
  (6 other events, 8.2 us)

commit v12 on v11

--- a/solution.py
+++ b/solution.py
@@ -11,7 +11,7 @@
 LANES = 128
 GROUP = 8
 STEP = 2
-CHUNKS = (40, 56, 32)
+CHUNKS = (48, 56, 24)
 LOWER = 40
 PARTS = 4
 VMEM = 56 * 1024 * 1024

time: 677 us -> 691 us (1.021)
  waiting for transfers between devices: 376 us -> 420 us
  starting transfers between devices: 129 us -> 96.1 us
    ppermute x21, waiting for transfers between devices: 16.8 us -> 56.1 us  [move(): return lax.ppermute(values, ('half', 'lo', 'col'), pairs)]
    ppermute x21, starting transfers between devices: 78.3 us -> 40 us  [move(): return lax.ppermute(values, ('half', 'lo', 'col'), pairs)]
    all_to_all x3, waiting for transfers between devices: 66.4 us -> 75.4 us  [delivered(): lax.all_to_all(values, ('lo', 'col'), split_axis=0, concat_axis=0, tiled=...]
  transfers between devices with their start and end apart: 30 -> 30, of which waited for: 10 -> 14; matrix products, arithmetic and copies ran while one was open for 2% -> 2% of each run, Pallas kernels for 20% -> 20%
where the time goes in v12:
time: 691 us; the launch traced here: 688 us
  waiting for transfers between devices  420 us (61%)
  Pallas kernels  148 us (21%)
  starting transfers between devices  96.1 us (14%)
  local copies, waits for them, and re-layouts  18.1 us (3%)
    all_to_all x3, waiting for transfers between devices, spread(): lax.all_to_all(values, ('lo', 'col'), split_axis=0, concat_axis=0, tiled=...  170 us
    ppermute x3, waiting for transfers between devices, exchange(): return lax.ppermute(values, 'half', [(0, 1), (1, 0)])  119 us
    all_to_all x3, waiting for transfers between devices, delivered(): lax.all_to_all(values, ('lo', 'col'), split_axis=0, concat_axis=0, tiled=...  75.4 us
    pallas_call x3, Pallas kernels, head(): pl.pallas_call(head_kernel, grid=(steps,), in_specs=[pl.BlockSpec((tile_r...  61.3 us
    ppermute x21, waiting for transfers between devices, move(): return lax.ppermute(values, ('half', 'lo', 'col'), pairs)  56.1 us
    ppermute x21, starting transfers between devices, move(): return lax.ppermute(values, ('half', 'lo', 'col'), pairs)  40 us
    pallas_call x3, Pallas kernels, hands(): pl.pallas_call(hands_kernel, grid=(rows // GROUP,), in_specs=[pl.BlockSpe...  35.3 us
    pallas_call x3, Pallas kernels, product(): pl.pallas_call(product_kernel, grid_spec=pltpu.PrefetchScalarGridSpec(num...  31.5 us
  transfers between devices with their start and end apart: 30, of which 14 were waited for; matrix products, arithmetic and copies ran while one was open for 2% of the time, Pallas kernels for 20%

profile of v12, /device:TPU:12, one launch (start us, length us, event | category | flops | bytes accessed | tf_op | source)
XLA Modules:
  0.0 688.2 jit_solution(5818704990497679539)
XLA Ops:
  2.6 7.1 %hands.5 = f32[128,48,128]{2,1,0:T(8,128)} custom-call(f32[128,128,128]{2,1,0:T(8,128)} %bitcast.31, bf16[512,384]{1,0:T(8,128)(2,1)} %pad_maximum_fusion.1.weights_ref), custom_call_target="tpu_custom_call" | custom-call | flops 150994944 | bytes 786432 | tf_op jit(solution)/shard_map/hands/pallas_call | solution.py:132
  9.7 5.1 all-to-all-start.1
  14.9 13.1 %hands.3 = f32[128,96,128]{2,1,0:T(8,128)} custom-call(f32[128,128,128]{2,1,0:T(8,128)} %bitcast.32, bf16[512,384]{1,0:T(8,128)(2,1)} %pad_maximum_fusion.1.weights_ref), custom_call_target="tpu_custom_call" | custom-call | flops 301989888 | bytes 1572864 | tf_op jit(solution)/shard_map/hands/pallas_call | solution.py:132
  28.0 24.1 %all-to-all-done.1.own_ref = f32[8,16,48,128]{3,2,1,0:T(8,128)S(1)} async-done(((f32[8,16,48,128]{3,2,1,0:T(8,128)}), f32[8,16,48,128]{3,2,1,0:T(8,128)S(1)}, u32[]{:S(2)}, u32[]{:S(2)}) %all-to-all-start.1) | async-done | bytes 3145760 | tf_op jit(solution)/shard_map/all_to_all | solution.py:368
  52.1 7.6 %all-to-all-start = ((f32[8,16,96,128]{3,2,1,0:T(8,128)}), f32[8,16,96,128]{3,2,1,0:T(8,128)}, u32[]{:S(2)}, u32[]{:S(2)}) async-start(f32[8,16,96,128]{3,2,1,0:T(8,128)} %bitcast.38), calls=%async_computation | async-start | bytes 12582912 | tf_op jit(solution)/shard_map/all_to_all | solution.py:368
  59.7 2.5 collective-permute-start
  62.2 15.0 %hands.4 = f32[128,112,128]{2,1,0:T(8,128)} custom-call(f32[128,128,128]{2,1,0:T(8,128)} %bitcast.33, bf16[512,384]{1,0:T(8,128)(2,1)} %pad_maximum_fusion.1.weights_ref), custom_call_target="tpu_custom_call" | custom-call | flops 352321536 | bytes 1835008 | tf_op jit(solution)/shard_map/hands/pallas_call | solution.py:132
  77.2 119.2 %collective-permute-done.other_ref = f32[8,16,48,128]{3,2,1,0:T(8,128)} collective-permute-done((f32[8,16,48,128]{3,2,1,0:T(8,128)S(1)}, f32[8,16,48,128]{3,2,1,0:T(8,128)}, u32[]{:S(2)}, u32[]{:S(2)}) %collective-permute-start) | collective-permute-done | bytes 3145760 | tf_op jit(solution)/shard_map/ppermute | solution.py:376
  196.4 14.5 %all-to-all-start.2 = ((f32[8,16,112,128]{3,2,1,0:T(8,128)}), f32[8,16,112,128]{3,2,1,0:T(8,128)}, u32[]{:S(2)}, u32[]{:S(2)}) async-start(f32[8,16,112,128]{3,2,1,0:T(8,128)} %bitcast.37), calls=%async_computation.2 | async-start | bytes 14680064 | tf_op jit(solution)/shard_map/all_to_all | solution.py:368
  210.9 4.2 slice.8.own_ref
  215.3 145.7 %all-to-all-done.2.high_ref = f32[8,16,112,128]{3,2,1,0:T(8,128)} async-done(((f32[8,16,112,128]{3,2,1,0:T(8,128)}), f32[8,16,112,128]{3,2,1,0:T(8,128)}, u32[]{:S(2)}, u32[]{:S(2)}) %all-to-all-start.2) | async-done | bytes 7340064 | tf_op jit(solution)/shard_map/all_to_all | solution.py:368
  361.0 10.9 %product.3 = f32[8,16,48,128]{3,2,1,0:T(8,128)} custom-call(s32[1]{0:T(128)} %bitcast.1.half_ref, f32[8,16,96,128]{3,2,1,0:T(8,128)} %all-to-all-done.low_ref, f32[8,16,112,128]{3,2,1,0:T(8,128)} %all-to-all-done.2.high_ref, f32[8,16,48,128]{3,2,1,0:T(8,128)} %copy-done, f32[8,16,48,128]{3,2,1,0:T(8,128)} %collective-permute-done.other_ref), custom_call_target="tpu_custom_call" | custom-call | flops 301989888 | bytes 1835008 | tf_op jit(solution)/shard_map/product/pallas_call | solution.py:189
  371.9 11.5 %all-to-all-start.3 = ((f32[8,16,48,128]{3,2,1,0:T(8,128)}), f32[8,16,48,128]{3,2,1,0:T(8,128)S(1)}, u32[]{:S(2)}, u32[]{:S(2)}) async-start(f32[8,16,48,128]{3,2,1,0:T(8,128)} %product.3), calls=%async_computation.3 | async-start | bytes 6291456 | tf_op jit(solution)/shard_map/all_to_all | solution.py:379
  383.5 2.0 copy.18
  387.6 2.7 slice.9.own_ref
  390.3 1.6 collective-permute-start.2
  395.1 46.5 %all-to-all-done.3 = f32[8,16,48,128]{3,2,1,0:T(8,128)S(1)} async-done(((f32[8,16,48,128]{3,2,1,0:T(8,128)}), f32[8,16,48,128]{3,2,1,0:T(8,128)S(1)}, u32[]{:S(2)}, u32[]{:S(2)}) %all-to-all-start.3) | async-done | bytes 3145760 | tf_op jit(solution)/shard_map/all_to_all | solution.py:379
  441.6 1.7 copy-done.1
  443.3 22.7 %head.3 = (f32[48,16,128]{2,1,0:T(8,128)}, f32[48,16,128]{2,1,0:T(8,128)}, f32[48,16,128]{2,1,0:T(8,128)}, f32[48,16,128]{2,1,0:T(8,128)}) custom-call(f32[128,128,128]{2,1,0:T(8,128)} %bitcast.34, f32[128,48,128]{2,1,0:T(8,128)} %bitcast.39, bf16[128,384]{1,0:T(8,128)(2,1)} %get-tuple-element.83.gate_ref, bf16[128,384]{1,0:T(8,128)(2,1)} %get-tuple-element.84.output_ref, ...), custom_call_target="tpu_custom_call" | custom-call | flops 1094713344 | bytes 983040 | tf_op jit(solution)/shard_map/head/pallas_call | solution.py:243
  466.0 2.3 collective-permute-start.3
  469.8 11.1 %product.4 = f32[8,16,56,128]{3,2,1,0:T(8,128)} custom-call(s32[1]{0:T(128)} %bitcast.1.half_ref, f32[8,16,96,128]{3,2,1,0:T(8,128)} %all-to-all-done.low_ref, f32[8,16,112,128]{3,2,1,0:T(8,128)} %all-to-all-done.2.high_ref, f32[8,16,56,128]{3,2,1,0:T(8,128)} %slice.8.own_ref, f32[8,16,56,128]{3,2,1,0:T(8,128)} %collective-permute-done.1.other_ref), custom_call_target="tpu_custom_call" | custom-call | flops 352321536 | bytes 1966080 | tf_op jit(solution)/shard_map/product/pallas_call | solution.py:189
  480.9 2.3 collective-permute-done.4
  483.3 6.9 %all-to-all-start.4 = ((f32[8,16,56,128]{3,2,1,0:T(8,128)}), f32[8,16,56,128]{3,2,1,0:T(8,128)}, u32[]{:S(2)}, u32[]{:S(2)}) async-start(f32[8,16,56,128]{3,2,1,0:T(8,128)} %product.4), calls=%async_computation.4 | async-start | bytes 7340032 | tf_op jit(solution)/shard_map/all_to_all | solution.py:379
  490.2 9.6 %product.5 = f32[8,16,24,128]{3,2,1,0:T(8,128)} custom-call(s32[1]{0:T(128)} %bitcast.1.half_ref, f32[8,16,96,128]{3,2,1,0:T(8,128)} %all-to-all-done.low_ref, f32[8,16,112,128]{3,2,1,0:T(8,128)} %all-to-all-done.2.high_ref, f32[8,16,24,128]{3,2,1,0:T(8,128)} %slice.9.own_ref, f32[8,16,24,128]{3,2,1,0:T(8,128)} %collective-permute-done.2.other_ref), custom_call_target="tpu_custom_call" | custom-call | flops 150994944 | bytes 1441792 | tf_op jit(solution)/shard_map/product/pallas_call | solution.py:189
  499.8 28.8 %all-to-all-done.4 = f32[8,16,56,128]{3,2,1,0:T(8,128)} async-done(((f32[8,16,56,128]{3,2,1,0:T(8,128)}), f32[8,16,56,128]{3,2,1,0:T(8,128)}, u32[]{:S(2)}, u32[]{:S(2)}) %all-to-all-start.4) | async-done | bytes 3670048 | tf_op jit(solution)/shard_map/all_to_all | solution.py:379
  528.6 6.1 all-to-all-start.5
  534.7 1.9 collective-permute-start.6
  536.7 4.8 collective-permute-start.7
  541.4 26.1 %head.4 = (f32[56,16,128]{2,1,0:T(8,128)}, f32[56,16,128]{2,1,0:T(8,128)}, f32[56,16,128]{2,1,0:T(8,128)}, f32[56,16,128]{2,1,0:T(8,128)}) custom-call(f32[128,128,128]{2,1,0:T(8,128)} %bitcast.35, f32[128,56,128]{2,1,0:T(8,128)} %bitcast.12.product_ref, bf16[128,384]{1,0:T(8,128)(2,1)} %get-tuple-element.83.gate_ref, ...), custom_call_target="tpu_custom_call" | custom-call | flops 1277165568 | bytes 1146880 | tf_op jit(solution)/shard_map/head/pallas_call | solution.py:243
  567.7 4.3 collective-permute-start.8
  573.5 5.6 collective-permute-done.7.refs_1_
  579.1 16.3 %collective-permute-done.8.refs_2_ = f32[48,16,128]{2,1,0:T(8,128)S(1)} collective-permute-done((f32[48,16,128]{2,1,0:T(8,128)}, f32[48,16,128]{2,1,0:T(8,128)S(1)}, u32[]{:S(2)}, u32[]{:S(2)}) %collective-permute-start.8) | collective-permute-done | bytes 393248 | tf_op jit(solution)/shard_map/ppermute | solution.py:325
  596.2 3.2 collective-permute-start.13
  599.4 3.3 collective-permute-done.9.refs_3_
  603.9 12.5 %head.5 = (f32[24,16,128]{2,1,0:T(8,128)}, f32[24,16,128]{2,1,0:T(8,128)}, f32[24,16,128]{2,1,0:T(8,128)}, f32[24,16,128]{2,1,0:T(8,128)}) custom-call(f32[128,128,128]{2,1,0:T(8,128)} %bitcast.36, f32[128,24,128]{2,1,0:T(8,128)} %bitcast.41, bf16[128,384]{1,0:T(8,128)(2,1)} %get-tuple-element.83.gate_ref, bf16[128,384]{1,0:T(8,128)(2,1)} %get-tuple-element.84.output_ref, ...), custom_call_target="tpu_custom_call" | custom-call | flops 547356672 | bytes 491520 | tf_op jit(solution)/shard_map/head/pallas_call | solution.py:243
  616.4 4.4 collective-permute-start.10
  620.8 5.3 collective-permute-start.17
  626.1 8.0 %collective-permute-done.10 = f32[24,16,128]{2,1,0:T(8,128)S(1)} collective-permute-done((f32[24,16,128]{2,1,0:T(8,128)}, f32[24,16,128]{2,1,0:T(8,128)S(1)}, u32[]{:S(2)}, u32[]{:S(2)}) %collective-permute-start.10) | collective-permute-done | bytes 196640 | tf_op jit(solution)/shard_map/ppermute | solution.py:325
  634.1 2.6 collective-permute-start.19
  636.7 13.7 %collective-permute-done.11 = f32[24,16,128]{2,1,0:T(8,128)S(1)} collective-permute-done((f32[24,16,128]{2,1,0:T(8,128)}, f32[24,16,128]{2,1,0:T(8,128)S(1)}, u32[]{:S(2)}, u32[]{:S(2)}) %collective-permute-start.11) | collective-permute-done | bytes 196640 | tf_op jit(solution)/shard_map/ppermute | solution.py:325
  651.9 6.3 turned.1.base_ref
  658.2 4.9 joined.3.base_ref
  663.1 3.5 collective-permute-start.20
  666.6 5.6 collective-permute-start.21
  673.9 5.4 joined.4.base_ref
  679.3 2.6 collective-permute-done.22.refs_2_
  681.9 2.6 collective-permute-done.23.refs_3_
  685.2 3.0 joined.5
  (97 shorter events, 17.1 us)
Async XLA Ops:
  9.7 42.4 %all-to-all-start.1 = ((f32[8,16,48,128]{3,2,1,0:T(8,128)}), f32[8,16,48,128]{3,2,1,0:T(8,128)S(1)}, u32[]{:S(2)}, u32[]{:S(2)}) async-start(f32[8,16,48,128]{3,2,1,0:T(8,128)} %bitcast.40), calls=%async_computation.1 | async-start | bytes 6291456 | tf_op jit(solution)/shard_map/all_to_all | solution.py:368
  52.1 7.6 %copy-start = (f32[8,16,48,128]{3,2,1,0:T(8,128)}, f32[8,16,48,128]{3,2,1,0:T(8,128)S(1)}, u32[]{:S(2)}) copy-start(f32[8,16,48,128]{3,2,1,0:T(8,128)S(1)} %all-to-all-done.1.own_ref) | copy-start | bytes 9437188
  52.1 144.3 %all-to-all-start = ((f32[8,16,96,128]{3,2,1,0:T(8,128)}), f32[8,16,96,128]{3,2,1,0:T(8,128)}, u32[]{:S(2)}, u32[]{:S(2)}) async-start(f32[8,16,96,128]{3,2,1,0:T(8,128)} %bitcast.38), calls=%async_computation | async-start | bytes 12582912 | tf_op jit(solution)/shard_map/all_to_all | solution.py:368
  59.7 136.7 %collective-permute-start = (f32[8,16,48,128]{3,2,1,0:T(8,128)S(1)}, f32[8,16,48,128]{3,2,1,0:T(8,128)}, u32[]{:S(2)}, u32[]{:S(2)}) collective-permute-start(f32[8,16,48,128]{3,2,1,0:T(8,128)S(1)} %all-to-all-done.1.own_ref), channel_id=1, source_target_pairs={{0,8},{8,0},{1,9},{9,1},{2,10},{10,2},{3,11},{11,3},{4,12},{12,4},... | collective-permute-start | bytes 9437192 | tf_op jit(solution)/shard_map/ppermute | solution.py:376
  196.4 164.5 %all-to-all-start.2 = ((f32[8,16,112,128]{3,2,1,0:T(8,128)}), f32[8,16,112,128]{3,2,1,0:T(8,128)}, u32[]{:S(2)}, u32[]{:S(2)}) async-start(f32[8,16,112,128]{3,2,1,0:T(8,128)} %bitcast.37), calls=%async_computation.2 | async-start | bytes 14680064 | tf_op jit(solution)/shard_map/all_to_all | solution.py:368
  215.1 156.8 %collective-permute-start.1 = (f32[8,16,56,128]{3,2,1,0:T(8,128)}, f32[8,16,56,128]{3,2,1,0:T(8,128)}, u32[]{:S(2)}, u32[]{:S(2)}) collective-permute-start(f32[8,16,56,128]{3,2,1,0:T(8,128)} %slice.8.own_ref), channel_id=1, source_target_pairs={{0,8},{8,0},{1,9},{9,1},{2,10},{10,2},{3,11},{11,3},{4,12},{12,4},... | collective-permute-start | bytes 11010056 | tf_op jit(solution)/shard_map/ppermute | solution.py:376
  371.8 11.5 %copy-start.18 = (f32[128,128]{1,0:T(8,128)S(1)}, f32[128,128]{1,0:T(8,128)}, u32[]{:S(2)}) copy-start(f32[128,128]{1,0:T(8,128)} %param.15) | copy-start | bytes 196612
  371.8 11.6 %copy-start.19 = (f32[128,128]{1,0:T(8,128)S(1)}, f32[128,128]{1,0:T(8,128)}, u32[]{:S(2)}) copy-start(f32[128,128]{1,0:T(8,128)} %param.14) | copy-start | bytes 196612
  371.8 15.7 %copy-start.20 = (f32[128]{0:T(128)S(1)}, f32[128]{0:T(128)}, u32[]{:S(2)}) copy-start(f32[128]{0:T(128)} %param.12) | copy-start | bytes 1540
  371.8 15.7 %copy-start.21 = (f32[128]{0:T(128)S(1)}, f32[128]{0:T(128)}, u32[]{:S(2)}) copy-start(f32[128]{0:T(128)} %param.16) | copy-start | bytes 1540
  371.9 69.7 %all-to-all-start.3 = ((f32[8,16,48,128]{3,2,1,0:T(8,128)}), f32[8,16,48,128]{3,2,1,0:T(8,128)S(1)}, u32[]{:S(2)}, u32[]{:S(2)}) async-start(f32[8,16,48,128]{3,2,1,0:T(8,128)} %product.3), calls=%async_computation.3 | async-start | bytes 6291456 | tf_op jit(solution)/shard_map/all_to_all | solution.py:379
  383.3 9.8 %copy-start.22 = (f32[128]{0:T(128)S(1)}, f32[128]{0:T(128)}, u32[]{:S(2)}) copy-start(f32[128]{0:T(128)} %param.17) | copy-start | bytes 1540
  386.7 6.5 copy-start.3
  390.3 90.7 %collective-permute-start.2 = (f32[8,16,24,128]{3,2,1,0:T(8,128)}, f32[8,16,24,128]{3,2,1,0:T(8,128)}, u32[]{:S(2)}, u32[]{:S(2)}) collective-permute-start(f32[8,16,24,128]{3,2,1,0:T(8,128)} %slice.9.own_ref), channel_id=1, source_target_pairs={{0,8},{8,0},{1,9},{9,1},{2,10},{10,2},{3,11},{11,3},{4,12},{12,4},... | collective-permute-start | bytes 4718600 | tf_op jit(solution)/shard_map/ppermute | solution.py:376
  466.0 14.9 %collective-permute-start.3 = (f32[48,16,128]{2,1,0:T(8,128)}, f32[48,16,128]{2,1,0:T(8,128)}, u32[]{:S(2)}, u32[]{:S(2)}) collective-permute-start(f32[48,16,128]{2,1,0:T(8,128)} %get-tuple-element.43.refs_3_), channel_id=1, source_target_pairs={{0,1},{1,0},{2,3},{3,2},{4,5},{5,4},{6,7},{7,6},{8,9},{9,8},{10,11... | collective-permute-start | bytes 1179656 | tf_op jit(solution)/shard_map/ppermute | solution.py:325
  468.3 15.0 %collective-permute-start.4 = (f32[48,16,128]{2,1,0:T(8,128)}, f32[48,16,128]{2,1,0:T(8,128)}, u32[]{:S(2)}, u32[]{:S(2)}) collective-permute-start(f32[48,16,128]{2,1,0:T(8,128)} %get-tuple-element.44.refs_6_), channel_id=1, source_target_pairs={{0,2},{1,3},{2,0},{3,1},{4,6},{5,7},{6,4},{7,5},{8,10},{9,11},{10,... | collective-permute-start | bytes 1179656 | tf_op jit(solution)/shard_map/ppermute | solution.py:325
  468.9 14.4 %collective-permute-start.5 = (f32[48,16,128]{2,1,0:T(8,128)}, f32[48,16,128]{2,1,0:T(8,128)}, u32[]{:S(2)}, u32[]{:S(2)}) collective-permute-start(f32[48,16,128]{2,1,0:T(8,128)} %get-tuple-element.45.refs_9_), channel_id=1, source_target_pairs={{0,3},{1,2},{2,1},{3,0},{4,7},{5,6},{6,5},{7,4},{8,11},{9,10},{10,... | collective-permute-start | bytes 1179656 | tf_op jit(solution)/shard_map/ppermute | solution.py:325
  483.3 45.4 %all-to-all-start.4 = ((f32[8,16,56,128]{3,2,1,0:T(8,128)}), f32[8,16,56,128]{3,2,1,0:T(8,128)}, u32[]{:S(2)}, u32[]{:S(2)}) async-start(f32[8,16,56,128]{3,2,1,0:T(8,128)} %product.4), calls=%async_computation.4 | async-start | bytes 7340032 | tf_op jit(solution)/shard_map/all_to_all | solution.py:379
  499.8 35.0 %copy-start.8 = (f32[48,16,128]{2,1,0:T(8,128)S(1)}, f32[48,16,128]{2,1,0:T(8,128)}, u32[]{:S(2)}) copy-start(f32[48,16,128]{2,1,0:T(8,128)} %get-tuple-element.51.refs_0_) | copy-start | bytes 1179652
  528.6 74.1 %all-to-all-start.5 = ((f32[8,16,24,128]{3,2,1,0:T(8,128)}), f32[8,16,24,128]{3,2,1,0:T(8,128)S(1)}, u32[]{:S(2)}, u32[]{:S(2)}) async-start(f32[8,16,24,128]{3,2,1,0:T(8,128)} %product.5), calls=%async_computation.5 | async-start | bytes 3145728 | tf_op jit(solution)/shard_map/all_to_all | solution.py:379
  534.7 38.8 %collective-permute-start.6 = (f32[48,16,128]{2,1,0:T(8,128)S(1)}, f32[48,16,128]{2,1,0:T(8,128)S(1)}, u32[]{:S(2)}, u32[]{:S(2)}) collective-permute-start(f32[48,16,128]{2,1,0:T(8,128)S(1)} %copy-done.8), channel_id=1, source_target_pairs={{0,0},{1,4},{2,8},{3,12},{4,1},{5,5},{6,9},{7,13},{8,2},{9,6},{10,... | collective-permute-start | bytes 1179656 | tf_op jit(solution)/shard_map/ppermute | solution.py:325
  536.7 42.4 %collective-permute-start.7 = (f32[48,16,128]{2,1,0:T(8,128)}, f32[48,16,128]{2,1,0:T(8,128)S(1)}, u32[]{:S(2)}, u32[]{:S(2)}) collective-permute-start(f32[48,16,128]{2,1,0:T(8,128)} %collective-permute-done.3), channel_id=1, source_target_pairs={{0,4},{1,0},{2,12},{3,8},{4,5},{5,1},{6,13},{7,9},{8,6},{9,2},{10,... | collective-permute-start | bytes 1179656 | tf_op jit(solution)/shard_map/ppermute | solution.py:325
  567.5 53.3 %collective-permute-start.14 = (f32[56,16,128]{2,1,0:T(8,128)}, f32[56,16,128]{2,1,0:T(8,128)}, u32[]{:S(2)}, u32[]{:S(2)}) collective-permute-start(f32[56,16,128]{2,1,0:T(8,128)} %get-tuple-element.57.refs_4_), channel_id=1, source_target_pairs={{0,1},{1,0},{2,3},{3,2},{4,5},{5,4},{6,7},{7,6},{8,9},{9,8},{10,11... | collective-permute-start | bytes 1376264 | tf_op jit(solution)/shard_map/ppermute | solution.py:325
  567.6 53.2 %collective-permute-start.16 = (f32[56,16,128]{2,1,0:T(8,128)}, f32[56,16,128]{2,1,0:T(8,128)}, u32[]{:S(2)}, u32[]{:S(2)}) collective-permute-start(f32[56,16,128]{2,1,0:T(8,128)} %get-tuple-element.59.refs_7_), channel_id=1, source_target_pairs={{0,2},{1,3},{2,0},{3,1},{4,6},{5,7},{6,4},{7,5},{8,10},{9,11},{10,... | collective-permute-start | bytes 1376264 | tf_op jit(solution)/shard_map/ppermute | solution.py:325
  567.7 27.8 %collective-permute-start.8 = (f32[48,16,128]{2,1,0:T(8,128)}, f32[48,16,128]{2,1,0:T(8,128)S(1)}, u32[]{:S(2)}, u32[]{:S(2)}) collective-permute-start(f32[48,16,128]{2,1,0:T(8,128)} %collective-permute-done.4), channel_id=1, source_target_pairs={{0,8},{1,12},{2,0},{3,4},{4,9},{5,13},{6,1},{7,5},{8,10},{9,14},{1... | collective-permute-start | bytes 1179656 | tf_op jit(solution)/shard_map/ppermute | solution.py:325
  573.5 84.7 %copy-start.9 = (f32[48,16,128]{2,1,0:T(8,128)}, f32[48,16,128]{2,1,0:T(8,128)S(1)}, u32[]{:S(2)}) copy-start(f32[48,16,128]{2,1,0:T(8,128)S(1)} %collective-permute-done.6.refs_0_) | copy-start | bytes 1179652
  573.5 29.2 %collective-permute-start.9 = (f32[48,16,128]{2,1,0:T(8,128)}, f32[48,16,128]{2,1,0:T(8,128)S(1)}, u32[]{:S(2)}, u32[]{:S(2)}) collective-permute-start(f32[48,16,128]{2,1,0:T(8,128)} %collective-permute-done.5), channel_id=1, source_target_pairs={{0,12},{1,8},{2,4},{3,0},{4,13},{5,9},{6,5},{7,1},{8,14},{9,10},{1... | collective-permute-start | bytes 1179656 | tf_op jit(solution)/shard_map/ppermute | solution.py:325
  579.1 79.1 %copy-start.10 = (f32[48,16,128]{2,1,0:T(8,128)}, f32[48,16,128]{2,1,0:T(8,128)S(1)}, u32[]{:S(2)}) copy-start(f32[48,16,128]{2,1,0:T(8,128)S(1)} %collective-permute-done.7.refs_1_) | copy-start | bytes 1179652
  579.1 47.0 %collective-permute-start.18 = (f32[56,16,128]{2,1,0:T(8,128)}, f32[56,16,128]{2,1,0:T(8,128)}, u32[]{:S(2)}, u32[]{:S(2)}) collective-permute-start(f32[56,16,128]{2,1,0:T(8,128)} %get-tuple-element.61.refs_10_), channel_id=1, source_target_pairs={{0,3},{1,2},{2,1},{3,0},{4,7},{5,6},{6,5},{7,4},{8,11},{9,10},{10,... | collective-permute-start | bytes 1376264 | tf_op jit(solution)/shard_map/ppermute | solution.py:325
  596.2 70.4 %collective-permute-start.13 = (f32[56,16,128]{2,1,0:T(8,128)}, f32[56,16,128]{2,1,0:T(8,128)S(1)}, u32[]{:S(2)}, u32[]{:S(2)}) collective-permute-start(f32[56,16,128]{2,1,0:T(8,128)} %get-tuple-element.49.refs_1_), channel_id=1, source_target_pairs={{0,0},{1,4},{2,8},{3,12},{4,1},{5,5},{6,9},{7,13},{8,2},{9,6},{10,... | collective-permute-start | bytes 1376264 | tf_op jit(solution)/shard_map/ppermute | solution.py:325
  602.7 55.5 %copy-start.12 = (f32[48,16,128]{2,1,0:T(8,128)}, f32[48,16,128]{2,1,0:T(8,128)S(1)}, u32[]{:S(2)}) copy-start(f32[48,16,128]{2,1,0:T(8,128)S(1)} %collective-permute-done.9.refs_3_) | copy-start | bytes 1179652
  603.9 47.2 %copy-start.23 = (f32[64]{0:T(128)S(1)}, f32[64]{0:T(128)}, u32[]{:S(2)}) copy-start(f32[64]{0:T(128)} %param.21) | copy-start | bytes 772
  616.4 17.7 %collective-permute-start.10 = (f32[24,16,128]{2,1,0:T(8,128)}, f32[24,16,128]{2,1,0:T(8,128)S(1)}, u32[]{:S(2)}, u32[]{:S(2)}) collective-permute-start(f32[24,16,128]{2,1,0:T(8,128)} %get-tuple-element.58.refs_5_), channel_id=1, source_target_pairs={{0,1},{1,0},{2,3},{3,2},{4,5},{5,4},{6,7},{7,6},{8,9},{9,8},{10,11... | collective-permute-start | bytes 589832 | tf_op jit(solution)/shard_map/ppermute | solution.py:325
  620.8 51.4 %collective-permute-start.15 = (f32[56,16,128]{2,1,0:T(8,128)}, f32[56,16,128]{2,1,0:T(8,128)S(1)}, u32[]{:S(2)}, u32[]{:S(2)}) collective-permute-start(f32[56,16,128]{2,1,0:T(8,128)} %collective-permute-done.14), channel_id=1, source_target_pairs={{0,4},{1,0},{2,12},{3,8},{4,5},{5,1},{6,13},{7,9},{8,6},{9,2},{10,... | collective-permute-start | bytes 1376264 | tf_op jit(solution)/shard_map/ppermute | solution.py:325
  620.8 51.4 %collective-permute-start.17 = (f32[56,16,128]{2,1,0:T(8,128)}, f32[56,16,128]{2,1,0:T(8,128)S(1)}, u32[]{:S(2)}, u32[]{:S(2)}) collective-permute-start(f32[56,16,128]{2,1,0:T(8,128)} %collective-permute-done.16), channel_id=1, source_target_pairs={{0,8},{1,12},{2,0},{3,4},{4,9},{5,13},{6,1},{7,5},{8,10},{9,14},{1... | collective-permute-start | bytes 1376264 | tf_op jit(solution)/shard_map/ppermute | solution.py:325
  626.1 24.3 %collective-permute-start.11 = (f32[24,16,128]{2,1,0:T(8,128)}, f32[24,16,128]{2,1,0:T(8,128)S(1)}, u32[]{:S(2)}, u32[]{:S(2)}) collective-permute-start(f32[24,16,128]{2,1,0:T(8,128)} %get-tuple-element.60.refs_8_), channel_id=1, source_target_pairs={{0,2},{1,3},{2,0},{3,1},{4,6},{5,7},{6,4},{7,5},{8,10},{9,11},{10,... | collective-permute-start | bytes 589832 | tf_op jit(solution)/shard_map/ppermute | solution.py:325
  634.1 38.8 %collective-permute-start.19 = (f32[56,16,128]{2,1,0:T(8,128)}, f32[56,16,128]{2,1,0:T(8,128)S(1)}, u32[]{:S(2)}, u32[]{:S(2)}) collective-permute-start(f32[56,16,128]{2,1,0:T(8,128)} %collective-permute-done.18), channel_id=1, source_target_pairs={{0,12},{1,8},{2,4},{3,0},{4,13},{5,9},{6,5},{7,1},{8,14},{9,10},{1... | collective-permute-start | bytes 1376264 | tf_op jit(solution)/shard_map/ppermute | solution.py:325
  651.1 12.0 %collective-permute-start.12 = (f32[24,16,128]{2,1,0:T(8,128)}, f32[24,16,128]{2,1,0:T(8,128)}, u32[]{:S(2)}, u32[]{:S(2)}) collective-permute-start(f32[24,16,128]{2,1,0:T(8,128)} %get-tuple-element.62.refs_11_), channel_id=1, source_target_pairs={{0,3},{1,2},{2,1},{3,0},{4,7},{5,6},{6,5},{7,4},{8,11},{9,10},{10,... | collective-permute-start | bytes 589832 | tf_op jit(solution)/shard_map/ppermute | solution.py:325
  658.2 4.9 copy-start.13
  658.2 14.0 %copy-start.25 = (f32[24,16,128]{2,1,0:T(8,128)S(1)}, f32[24,16,128]{2,1,0:T(8,128)}, u32[]{:S(2)}) copy-start(f32[24,16,128]{2,1,0:T(8,128)} %copy-done.24) | copy-start | bytes 589828
  663.1 16.2 %collective-permute-start.20 = (f32[24,16,128]{2,1,0:T(8,128)S(1)}, f32[24,16,128]{2,1,0:T(8,128)S(1)}, u32[]{:S(2)}, u32[]{:S(2)}) collective-permute-start(f32[24,16,128]{2,1,0:T(8,128)S(1)} %copy-done.13), channel_id=1, source_target_pairs={{0,0},{1,4},{2,8},{3,12},{4,1},{5,5},{6,9},{7,13},{8,2},{9,6},{10,... | collective-permute-start | bytes 589832 | tf_op jit(solution)/shard_map/ppermute | solution.py:325
  666.6 6.3 copy-start.4
  666.6 12.7 %collective-permute-start.21 = (f32[24,16,128]{2,1,0:T(8,128)S(1)}, f32[24,16,128]{2,1,0:T(8,128)S(1)}, u32[]{:S(2)}, u32[]{:S(2)}) collective-permute-start(f32[24,16,128]{2,1,0:T(8,128)S(1)} %collective-permute-done.10), channel_id=1, source_target_pairs={{0,4},{1,0},{2,12},{3,8},{4,5},{5,1},{6,13},{7,9},{8,6},{9,2},{10,... | collective-permute-start | bytes 589832 | tf_op jit(solution)/shard_map/ppermute | solution.py:325
  672.2 9.7 %collective-permute-start.22 = (f32[24,16,128]{2,1,0:T(8,128)S(1)}, f32[24,16,128]{2,1,0:T(8,128)S(1)}, u32[]{:S(2)}, u32[]{:S(2)}) collective-permute-start(f32[24,16,128]{2,1,0:T(8,128)S(1)} %copy-done.25), channel_id=1, source_target_pairs={{0,8},{1,12},{2,0},{3,4},{4,9},{5,13},{6,1},{7,5},{8,10},{9,14},{1... | collective-permute-start | bytes 589832 | tf_op jit(solution)/shard_map/ppermute | solution.py:325
  672.3 12.2 %collective-permute-start.23 = (f32[24,16,128]{2,1,0:T(8,128)}, f32[24,16,128]{2,1,0:T(8,128)S(1)}, u32[]{:S(2)}, u32[]{:S(2)}) collective-permute-start(f32[24,16,128]{2,1,0:T(8,128)} %collective-permute-done.12), channel_id=1, source_target_pairs={{0,12},{1,8},{2,4},{3,0},{4,13},{5,9},{6,5},{7,1},{8,14},{9,10},{1... | collective-permute-start | bytes 589832 | tf_op jit(solution)/shard_map/ppermute | solution.py:325
  679.3 5.2 copy-start.14
  679.3 5.2 copy-start.15
  681.9 2.7 copy-start.16
  (8 other events, 7.4 us)

commit v13 on v11

--- a/solution.py
+++ b/solution.py
@@ -403,16 +403,14 @@
     mirror = [across(shifted, row_count)]
     values, after = tie((delivered(values), blocks(2)))
     own.append(run_head(values, 1))
-    values, mirror[0] = tie((delivered(after), mirror[0]))
-    own.append(run_head(values, 2))
-    mirror.append(across(aside(own[1], row_count), row_count))
-    shifted = aside(own[2], row_count)
+    shifted, mirror[0] = tie((aside(own[1], row_count), mirror[0]))
+    own.append(run_head(delivered(after), 2))
+    mirror.append(across(shifted, row_count))
+    mirror.append(across(aside(own[2], row_count), row_count))
     bins = distogram_bias.shape[0] // PARTS
     bias = jnp.broadcast_to(distogram_bias.reshape(PARTS, bins, 1), (PARTS, bins, tile_cols))
-    logits = joined(turned(bias, own), mirror[0], firsts[0])
-    logits, shifted[1:] = tie((logits, shifted[1:]))
-    mirror.append(across(shifted, row_count))
-    for first, block in zip(firsts[1:], mirror[1:]):
+    logits = turned(bias, own)
+    for first, block in zip(firsts, mirror):
         logits = joined(logits, block, first)
     logits = logits.reshape(tile_rows, PARTS * bins, tile_cols)
     return jnp.swapaxes(logits, 1, 2)[None]

time: 677 us -> 686 us (1.013)
  waiting for transfers between devices: 376 us -> 402 us
  starting transfers between devices: 129 us -> 108 us
    ppermute x21, waiting for transfers between devices: 16.8 us -> 43.5 us  [move(): return lax.ppermute(values, ('half', 'lo', 'col'), pairs)]
    ppermute x21, starting transfers between devices: 78.3 us -> 57.8 us  [move(): return lax.ppermute(values, ('half', 'lo', 'col'), pairs)]
where the time goes in v13:
time: 686 us; the launch traced here: 681 us
  waiting for transfers between devices  402 us (59%)
  Pallas kernels  148 us (22%)
  starting transfers between devices  108 us (16%)
  local copies, waits for them, and re-layouts  16.9 us (2%)
    all_to_all x3, waiting for transfers between devices, spread(): lax.all_to_all(values, ('lo', 'col'), split_axis=0, concat_axis=0, tiled=...  175 us
    ppermute x3, waiting for transfers between devices, exchange(): return lax.ppermute(values, 'half', [(0, 1), (1, 0)])  118 us
    all_to_all x3, waiting for transfers between devices, delivered(): lax.all_to_all(values, ('lo', 'col'), split_axis=0, concat_axis=0, tiled=...  66.4 us
    pallas_call x3, Pallas kernels, head(): pl.pallas_call(head_kernel, grid=(steps,), in_specs=[pl.BlockSpec((tile_r...  61.3 us
    ppermute x21, starting transfers between devices, move(): return lax.ppermute(values, ('half', 'lo', 'col'), pairs)  57.8 us
    ppermute x21, waiting for transfers between devices, move(): return lax.ppermute(values, ('half', 'lo', 'col'), pairs)  43.5 us
    pallas_call x3, Pallas kernels, hands(): pl.pallas_call(hands_kernel, grid=(rows // GROUP,), in_specs=[pl.BlockSpe...  35.6 us
    pallas_call x3, Pallas kernels, product(): pl.pallas_call(product_kernel, grid_spec=pltpu.PrefetchScalarGridSpec(num...  31.7 us
  transfers between devices with their start and end apart: 30, of which 10 were waited for; matrix products, arithmetic and copies ran while one was open for 2% of the time, Pallas kernels for 20%

profile of v13, /device:TPU:12, one launch (start us, length us, event | category | flops | bytes accessed | tf_op | source)
XLA Modules:
  0.0 680.9 jit_solution(16447740498282742072)
XLA Ops:
  2.6 6.4 hands.5
  8.9 5.1 all-to-all-start.1
  14.1 13.1 %hands.3 = f32[128,96,128]{2,1,0:T(8,128)} custom-call(f32[128,128,128]{2,1,0:T(8,128)} %bitcast.32, bf16[512,384]{1,0:T(8,128)(2,1)} %pad_maximum_fusion.1.weights_ref), custom_call_target="tpu_custom_call" | custom-call | flops 301989888 | bytes 1572864 | tf_op jit(solution)/shard_map/hands/pallas_call | solution.py:132
  27.2 17.8 %all-to-all-done.1.own_ref = f32[8,16,40,128]{3,2,1,0:T(8,128)S(1)} async-done(((f32[8,16,40,128]{3,2,1,0:T(8,128)}), f32[8,16,40,128]{3,2,1,0:T(8,128)S(1)}, u32[]{:S(2)}, u32[]{:S(2)}) %all-to-all-start.1) | async-done | bytes 2621472 | tf_op jit(solution)/shard_map/all_to_all | solution.py:368
  44.9 7.2 %all-to-all-start = ((f32[8,16,96,128]{3,2,1,0:T(8,128)}), f32[8,16,96,128]{3,2,1,0:T(8,128)}, u32[]{:S(2)}, u32[]{:S(2)}) async-start(f32[8,16,96,128]{3,2,1,0:T(8,128)} %bitcast.38), calls=%async_computation | async-start | bytes 12582912 | tf_op jit(solution)/shard_map/all_to_all | solution.py:368
  52.1 2.6 collective-permute-start
  54.7 16.2 %hands.4 = f32[128,120,128]{2,1,0:T(8,128)} custom-call(f32[128,128,128]{2,1,0:T(8,128)} %bitcast.33, bf16[512,384]{1,0:T(8,128)(2,1)} %pad_maximum_fusion.1.weights_ref), custom_call_target="tpu_custom_call" | custom-call | flops 377487360 | bytes 1966080 | tf_op jit(solution)/shard_map/hands/pallas_call | solution.py:132
  70.9 107.0 %collective-permute-done.other_ref = f32[8,16,40,128]{3,2,1,0:T(8,128)} collective-permute-done((f32[8,16,40,128]{3,2,1,0:T(8,128)S(1)}, f32[8,16,40,128]{3,2,1,0:T(8,128)}, u32[]{:S(2)}, u32[]{:S(2)}) %collective-permute-start) | collective-permute-done | bytes 2621472 | tf_op jit(solution)/shard_map/ppermute | solution.py:376
  177.8 14.5 %all-to-all-start.2 = ((f32[8,16,120,128]{3,2,1,0:T(8,128)}), f32[8,16,120,128]{3,2,1,0:T(8,128)}, u32[]{:S(2)}, u32[]{:S(2)}) async-start(f32[8,16,120,128]{3,2,1,0:T(8,128)} %bitcast.37), calls=%async_computation.2 | async-start | bytes 15728640 | tf_op jit(solution)/shard_map/all_to_all | solution.py:368
  192.4 4.2 slice.8.own_ref
  196.6 156.8 %all-to-all-done.2.high_ref = f32[8,16,120,128]{3,2,1,0:T(8,128)} async-done(((f32[8,16,120,128]{3,2,1,0:T(8,128)}), f32[8,16,120,128]{3,2,1,0:T(8,128)}, u32[]{:S(2)}, u32[]{:S(2)}) %all-to-all-start.2) | async-done | bytes 7864352 | tf_op jit(solution)/shard_map/all_to_all | solution.py:368
  353.3 10.5 %product.3 = f32[8,16,40,128]{3,2,1,0:T(8,128)} custom-call(s32[1]{0:T(128)} %bitcast.1.half_ref, f32[8,16,96,128]{3,2,1,0:T(8,128)} %all-to-all-done.low_ref, f32[8,16,120,128]{3,2,1,0:T(8,128)} %all-to-all-done.2.high_ref, f32[8,16,40,128]{3,2,1,0:T(8,128)} %copy-done, f32[8,16,40,128]{3,2,1,0:T(8,128)} %collective-permute-done.other_ref), custom_call_target="tpu_custom_call" | custom-call | flops 251658240 | bytes 1703936 | tf_op jit(solution)/shard_map/product/pallas_call | solution.py:189
  363.9 6.6 all-to-all-start.3
  370.7 1.2 copy.18
  373.1 3.1 slice.9.own_ref
  376.2 1.9 collective-permute-start.2
  381.4 36.8 %all-to-all-done.3 = f32[8,16,40,128]{3,2,1,0:T(8,128)S(1)} async-done(((f32[8,16,40,128]{3,2,1,0:T(8,128)}), f32[8,16,40,128]{3,2,1,0:T(8,128)S(1)}, u32[]{:S(2)}, u32[]{:S(2)}) %all-to-all-start.3) | async-done | bytes 2621472 | tf_op jit(solution)/shard_map/all_to_all | solution.py:379
  418.2 1.5 copy-done.1
  419.8 19.2 %head.3 = (f32[40,16,128]{2,1,0:T(8,128)}, f32[40,16,128]{2,1,0:T(8,128)}, f32[40,16,128]{2,1,0:T(8,128)}, f32[40,16,128]{2,1,0:T(8,128)}) custom-call(f32[128,128,128]{2,1,0:T(8,128)} %bitcast.34, f32[128,40,128]{2,1,0:T(8,128)} %bitcast.39, bf16[128,384]{1,0:T(8,128)(2,1)} %get-tuple-element.81.gate_ref, bf16[128,384]{1,0:T(8,128)(2,1)} %get-tuple-element.82.output_ref, ...), custom_call_target="tpu_custom_call" | custom-call | flops 912261120 | bytes 819200 | tf_op jit(solution)/shard_map/head/pallas_call | solution.py:243
  439.0 1.6 collective-permute-start.3
  441.2 1.4 collective-permute-start.5
  442.5 11.1 %product.4 = f32[8,16,56,128]{3,2,1,0:T(8,128)} custom-call(s32[1]{0:T(128)} %bitcast.1.half_ref, f32[8,16,96,128]{3,2,1,0:T(8,128)} %all-to-all-done.low_ref, f32[8,16,120,128]{3,2,1,0:T(8,128)} %all-to-all-done.2.high_ref, f32[8,16,56,128]{3,2,1,0:T(8,128)} %slice.8.own_ref, f32[8,16,56,128]{3,2,1,0:T(8,128)} %collective-permute-done.1.other_ref), custom_call_target="tpu_custom_call" | custom-call | flops 352321536 | bytes 1966080 | tf_op jit(solution)/shard_map/product/pallas_call | solution.py:189
  453.6 10.9 %collective-permute-done.2.other_ref = f32[8,16,32,128]{3,2,1,0:T(8,128)} collective-permute-done((f32[8,16,32,128]{3,2,1,0:T(8,128)}, f32[8,16,32,128]{3,2,1,0:T(8,128)}, u32[]{:S(2)}, u32[]{:S(2)}) %collective-permute-start.2) | collective-permute-done | bytes 2097184 | tf_op jit(solution)/shard_map/ppermute | solution.py:376
  464.5 6.6 all-to-all-start.4
  471.1 10.1 %product.5 = f32[8,16,32,128]{3,2,1,0:T(8,128)} custom-call(s32[1]{0:T(128)} %bitcast.1.half_ref, f32[8,16,96,128]{3,2,1,0:T(8,128)} %all-to-all-done.low_ref, f32[8,16,120,128]{3,2,1,0:T(8,128)} %all-to-all-done.2.high_ref, f32[8,16,32,128]{3,2,1,0:T(8,128)} %slice.9.own_ref, f32[8,16,32,128]{3,2,1,0:T(8,128)} %collective-permute-done.2.other_ref), custom_call_target="tpu_custom_call" | custom-call | flops 201326592 | bytes 1572864 | tf_op jit(solution)/shard_map/product/pallas_call | solution.py:189
  481.2 29.6 %all-to-all-done.4 = f32[8,16,56,128]{3,2,1,0:T(8,128)} async-done(((f32[8,16,56,128]{3,2,1,0:T(8,128)}), f32[8,16,56,128]{3,2,1,0:T(8,128)}, u32[]{:S(2)}, u32[]{:S(2)}) %all-to-all-start.4) | async-done | bytes 3670048 | tf_op jit(solution)/shard_map/all_to_all | solution.py:379
  510.8 6.1 all-to-all-start.5
  516.9 2.2 collective-permute-start.10
  519.1 26.2 %head.4 = (f32[56,16,128]{2,1,0:T(8,128)}, f32[56,16,128]{2,1,0:T(8,128)}, f32[56,16,128]{2,1,0:T(8,128)}, f32[56,16,128]{2,1,0:T(8,128)}) custom-call(f32[128,128,128]{2,1,0:T(8,128)} %bitcast.35, f32[128,56,128]{2,1,0:T(8,128)} %bitcast.12.product_ref, bf16[128,384]{1,0:T(8,128)(2,1)} %get-tuple-element.81.gate_ref, ...), custom_call_target="tpu_custom_call" | custom-call | flops 1277165568 | bytes 1146880 | tf_op jit(solution)/shard_map/head/pallas_call | solution.py:243
  545.6 3.3 collective-permute-start.7
  548.9 16.0 %collective-permute-start.12 = (f32[40,16,128]{2,1,0:T(8,128)S(1)}, f32[40,16,128]{2,1,0:T(8,128)S(1)}, u32[]{:S(2)}, u32[]{:S(2)}) collective-permute-start(f32[40,16,128]{2,1,0:T(8,128)S(1)} %collective-permute-done.5), channel_id=1, source_target_pairs={{0,12},{1,8},{2,4},{3,0},{4,13},{5,9},{6,5},{7,1},{8,14},{9,10},{1... | collective-permute-start | bytes 983048 | tf_op jit(solution)/shard_map/ppermute | solution.py:325
  564.9 9.1 %collective-permute-start.9 = (f32[40,16,128]{2,1,0:T(8,128)S(1)}, f32[40,16,128]{2,1,0:T(8,128)S(1)}, u32[]{:S(2)}, u32[]{:S(2)}) collective-permute-start(f32[40,16,128]{2,1,0:T(8,128)S(1)} %copy-done.7), channel_id=1, source_target_pairs={{0,0},{1,4},{2,8},{3,12},{4,1},{5,5},{6,9},{7,13},{8,2},{9,6},{10,... | collective-permute-start | bytes 983048 | tf_op jit(solution)/shard_map/ppermute | solution.py:325
  573.9 8.3 %collective-permute-done.12.refs_3_ = f32[40,16,128]{2,1,0:T(8,128)S(1)} collective-permute-done((f32[40,16,128]{2,1,0:T(8,128)S(1)}, f32[40,16,128]{2,1,0:T(8,128)S(1)}, u32[]{:S(2)}, u32[]{:S(2)}) %collective-permute-start.12) | collective-permute-done | bytes 327712 | tf_op jit(solution)/shard_map/ppermute | solution.py:325
  582.2 27.6 %collective-permute-done.9.refs_0_ = f32[40,16,128]{2,1,0:T(8,128)S(1)} collective-permute-done((f32[40,16,128]{2,1,0:T(8,128)S(1)}, f32[40,16,128]{2,1,0:T(8,128)S(1)}, u32[]{:S(2)}, u32[]{:S(2)}) %collective-permute-start.9) | collective-permute-done | bytes 327712 | tf_op jit(solution)/shard_map/ppermute | solution.py:325
  609.9 7.2 %collective-permute-start.13 = (f32[56,16,128]{2,1,0:T(8,128)}, f32[56,16,128]{2,1,0:T(8,128)S(1)}, u32[]{:S(2)}, u32[]{:S(2)}) collective-permute-start(f32[56,16,128]{2,1,0:T(8,128)} %get-tuple-element.65.refs_1_), channel_id=1, source_target_pairs={{0,0},{1,4},{2,8},{3,12},{4,1},{5,5},{6,9},{7,13},{8,2},{9,6},{10,... | collective-permute-start | bytes 1376264 | tf_op jit(solution)/shard_map/ppermute | solution.py:325
  617.3 1.3 copy-done.2
  618.6 15.9 %head.5 = (f32[32,16,128]{2,1,0:T(8,128)}, f32[32,16,128]{2,1,0:T(8,128)}, f32[32,16,128]{2,1,0:T(8,128)}, f32[32,16,128]{2,1,0:T(8,128)}) custom-call(f32[128,128,128]{2,1,0:T(8,128)} %bitcast.36, f32[128,32,128]{2,1,0:T(8,128)} %bitcast.41, bf16[128,384]{1,0:T(8,128)(2,1)} %get-tuple-element.81.gate_ref, bf16[128,384]{1,0:T(8,128)(2,1)} %get-tuple-element.82.output_ref, ...), custom_call_target="tpu_custom_call" | custom-call | flops 729808896 | bytes 655360 | tf_op jit(solution)/shard_map/head/pallas_call | solution.py:243
  635.2 2.9 collective-permute-start.22
  638.1 6.1 collective-permute-done.15.refs_2_
  644.2 1.9 collective-permute-start.17
  646.2 1.5 collective-permute-start.19
  647.7 1.4 collective-permute-done.20
  649.1 5.2 collective-permute-start.21
  654.3 3.9 collective-permute-start.23
  659.0 6.3 turned.1.base_ref
  665.3 4.2 joined.3.base_ref
  670.3 5.4 joined.4.base_ref
  677.4 3.5 joined.5
  (91 shorter events, 12.2 us)
Async XLA Ops:
  8.9 36.0 %all-to-all-start.1 = ((f32[8,16,40,128]{3,2,1,0:T(8,128)}), f32[8,16,40,128]{3,2,1,0:T(8,128)S(1)}, u32[]{:S(2)}, u32[]{:S(2)}) async-start(f32[8,16,40,128]{3,2,1,0:T(8,128)} %bitcast.40), calls=%async_computation.1 | async-start | bytes 5242880 | tf_op jit(solution)/shard_map/all_to_all | solution.py:368
  44.9 7.2 %copy-start = (f32[8,16,40,128]{3,2,1,0:T(8,128)}, f32[8,16,40,128]{3,2,1,0:T(8,128)S(1)}, u32[]{:S(2)}) copy-start(f32[8,16,40,128]{3,2,1,0:T(8,128)S(1)} %all-to-all-done.1.own_ref) | copy-start | bytes 7864324
  44.9 132.9 %all-to-all-start = ((f32[8,16,96,128]{3,2,1,0:T(8,128)}), f32[8,16,96,128]{3,2,1,0:T(8,128)}, u32[]{:S(2)}, u32[]{:S(2)}) async-start(f32[8,16,96,128]{3,2,1,0:T(8,128)} %bitcast.38), calls=%async_computation | async-start | bytes 12582912 | tf_op jit(solution)/shard_map/all_to_all | solution.py:368
  52.1 125.7 %collective-permute-start = (f32[8,16,40,128]{3,2,1,0:T(8,128)S(1)}, f32[8,16,40,128]{3,2,1,0:T(8,128)}, u32[]{:S(2)}, u32[]{:S(2)}) collective-permute-start(f32[8,16,40,128]{3,2,1,0:T(8,128)S(1)} %all-to-all-done.1.own_ref), channel_id=1, source_target_pairs={{0,8},{8,0},{1,9},{9,1},{2,10},{10,2},{3,11},{11,3},{4,12},{12,4},... | collective-permute-start | bytes 7864328 | tf_op jit(solution)/shard_map/ppermute | solution.py:376
  177.8 175.5 %all-to-all-start.2 = ((f32[8,16,120,128]{3,2,1,0:T(8,128)}), f32[8,16,120,128]{3,2,1,0:T(8,128)}, u32[]{:S(2)}, u32[]{:S(2)}) async-start(f32[8,16,120,128]{3,2,1,0:T(8,128)} %bitcast.37), calls=%async_computation.2 | async-start | bytes 15728640 | tf_op jit(solution)/shard_map/all_to_all | solution.py:368
  196.6 167.3 %collective-permute-start.1 = (f32[8,16,56,128]{3,2,1,0:T(8,128)}, f32[8,16,56,128]{3,2,1,0:T(8,128)}, u32[]{:S(2)}, u32[]{:S(2)}) collective-permute-start(f32[8,16,56,128]{3,2,1,0:T(8,128)} %slice.8.own_ref), channel_id=1, source_target_pairs={{0,8},{8,0},{1,9},{9,1},{2,10},{10,2},{3,11},{11,3},{4,12},{12,4},... | collective-permute-start | bytes 11010056 | tf_op jit(solution)/shard_map/ppermute | solution.py:376
  363.9 6.7 copy-start.16
  363.9 6.8 copy-start.17
  363.9 54.3 %all-to-all-start.3 = ((f32[8,16,40,128]{3,2,1,0:T(8,128)}), f32[8,16,40,128]{3,2,1,0:T(8,128)S(1)}, u32[]{:S(2)}, u32[]{:S(2)}) async-start(f32[8,16,40,128]{3,2,1,0:T(8,128)} %product.3), calls=%async_computation.3 | async-start | bytes 5242880 | tf_op jit(solution)/shard_map/all_to_all | solution.py:379
  372.0 6.8 copy-start.19
  372.0 6.8 copy-start.20
  372.0 7.5 %copy-start.21 = (f32[128]{0:T(128)S(1)}, f32[128]{0:T(128)}, u32[]{:S(2)}) copy-start(f32[128]{0:T(128)} %param.17) | copy-start | bytes 1540
  373.1 5.0 copy-start.18
  376.2 88.3 %collective-permute-start.2 = (f32[8,16,32,128]{3,2,1,0:T(8,128)}, f32[8,16,32,128]{3,2,1,0:T(8,128)}, u32[]{:S(2)}, u32[]{:S(2)}) collective-permute-start(f32[8,16,32,128]{3,2,1,0:T(8,128)} %slice.9.own_ref), channel_id=1, source_target_pairs={{0,8},{8,0},{1,9},{9,1},{2,10},{10,2},{3,11},{11,3},{4,12},{12,4},... | collective-permute-start | bytes 6291464 | tf_op jit(solution)/shard_map/ppermute | solution.py:376
  418.2 1.5 copy-start.1
  439.0 25.5 %collective-permute-start.3 = (f32[40,16,128]{2,1,0:T(8,128)}, f32[40,16,128]{2,1,0:T(8,128)S(1)}, u32[]{:S(2)}, u32[]{:S(2)}) collective-permute-start(f32[40,16,128]{2,1,0:T(8,128)} %get-tuple-element.42.refs_3_), channel_id=1, source_target_pairs={{0,1},{1,0},{2,3},{3,2},{4,5},{5,4},{6,7},{7,6},{8,9},{9,8},{10,11... | collective-permute-start | bytes 983048 | tf_op jit(solution)/shard_map/ppermute | solution.py:325
  440.6 23.9 %collective-permute-start.4 = (f32[40,16,128]{2,1,0:T(8,128)}, f32[40,16,128]{2,1,0:T(8,128)S(1)}, u32[]{:S(2)}, u32[]{:S(2)}) collective-permute-start(f32[40,16,128]{2,1,0:T(8,128)} %get-tuple-element.43.refs_6_), channel_id=1, source_target_pairs={{0,2},{1,3},{2,0},{3,1},{4,6},{5,7},{6,4},{7,5},{8,10},{9,11},{10,... | collective-permute-start | bytes 983048 | tf_op jit(solution)/shard_map/ppermute | solution.py:325
  441.2 23.4 %collective-permute-start.5 = (f32[40,16,128]{2,1,0:T(8,128)}, f32[40,16,128]{2,1,0:T(8,128)S(1)}, u32[]{:S(2)}, u32[]{:S(2)}) collective-permute-start(f32[40,16,128]{2,1,0:T(8,128)} %get-tuple-element.44.refs_9_), channel_id=1, source_target_pairs={{0,3},{1,2},{2,1},{3,0},{4,7},{5,6},{6,5},{7,4},{8,11},{9,10},{10,... | collective-permute-start | bytes 983048 | tf_op jit(solution)/shard_map/ppermute | solution.py:325
  464.5 46.2 %all-to-all-start.4 = ((f32[8,16,56,128]{3,2,1,0:T(8,128)}), f32[8,16,56,128]{3,2,1,0:T(8,128)}, u32[]{:S(2)}, u32[]{:S(2)}) async-start(f32[8,16,56,128]{3,2,1,0:T(8,128)} %product.4), calls=%async_computation.4 | async-start | bytes 7340032 | tf_op jit(solution)/shard_map/all_to_all | solution.py:379
  510.8 106.5 %all-to-all-start.5 = ((f32[8,16,32,128]{3,2,1,0:T(8,128)}), f32[8,16,32,128]{3,2,1,0:T(8,128)S(1)}, u32[]{:S(2)}, u32[]{:S(2)}) async-start(f32[8,16,32,128]{3,2,1,0:T(8,128)} %product.5), calls=%async_computation.5 | async-start | bytes 4194304 | tf_op jit(solution)/shard_map/all_to_all | solution.py:379
  516.9 48.0 %copy-start.7 = (f32[40,16,128]{2,1,0:T(8,128)S(1)}, f32[40,16,128]{2,1,0:T(8,128)}, u32[]{:S(2)}) copy-start(f32[40,16,128]{2,1,0:T(8,128)} %get-tuple-element.57.refs_0_) | copy-start | bytes 983044
  516.9 32.0 %collective-permute-start.10 = (f32[40,16,128]{2,1,0:T(8,128)S(1)}, f32[40,16,128]{2,1,0:T(8,128)S(1)}, u32[]{:S(2)}, u32[]{:S(2)}) collective-permute-start(f32[40,16,128]{2,1,0:T(8,128)S(1)} %collective-permute-done.3), channel_id=1, source_target_pairs={{0,4},{1,0},{2,12},{3,8},{4,5},{5,1},{6,13},{7,9},{8,6},{9,2},{10,... | collective-permute-start | bytes 983048 | tf_op jit(solution)/shard_map/ppermute | solution.py:325
  519.1 45.8 %collective-permute-start.11 = (f32[40,16,128]{2,1,0:T(8,128)S(1)}, f32[40,16,128]{2,1,0:T(8,128)S(1)}, u32[]{:S(2)}, u32[]{:S(2)}) collective-permute-start(f32[40,16,128]{2,1,0:T(8,128)S(1)} %collective-permute-done.4), channel_id=1, source_target_pairs={{0,8},{1,12},{2,0},{3,4},{4,9},{5,13},{6,1},{7,5},{8,10},{9,14},{1... | collective-permute-start | bytes 983048 | tf_op jit(solution)/shard_map/ppermute | solution.py:325
  545.2 64.6 %collective-permute-start.6 = (f32[56,16,128]{2,1,0:T(8,128)}, f32[56,16,128]{2,1,0:T(8,128)}, u32[]{:S(2)}, u32[]{:S(2)}) collective-permute-start(f32[56,16,128]{2,1,0:T(8,128)} %get-tuple-element.51.refs_4_), channel_id=1, source_target_pairs={{0,1},{1,0},{2,3},{3,2},{4,5},{5,4},{6,7},{7,6},{8,9},{9,8},{10,11... | collective-permute-start | bytes 1376264 | tf_op jit(solution)/shard_map/ppermute | solution.py:325
  545.6 64.3 %collective-permute-start.7 = (f32[56,16,128]{2,1,0:T(8,128)}, f32[56,16,128]{2,1,0:T(8,128)}, u32[]{:S(2)}, u32[]{:S(2)}) collective-permute-start(f32[56,16,128]{2,1,0:T(8,128)} %get-tuple-element.53.refs_7_), channel_id=1, source_target_pairs={{0,2},{1,3},{2,0},{3,1},{4,6},{5,7},{6,4},{7,5},{8,10},{9,11},{10,... | collective-permute-start | bytes 1376264 | tf_op jit(solution)/shard_map/ppermute | solution.py:325
  548.9 61.0 %collective-permute-start.8 = (f32[56,16,128]{2,1,0:T(8,128)}, f32[56,16,128]{2,1,0:T(8,128)}, u32[]{:S(2)}, u32[]{:S(2)}) collective-permute-start(f32[56,16,128]{2,1,0:T(8,128)} %get-tuple-element.55.refs_10_), channel_id=1, source_target_pairs={{0,3},{1,2},{2,1},{3,0},{4,7},{5,6},{6,5},{7,4},{8,11},{9,10},{10,... | collective-permute-start | bytes 1376264 | tf_op jit(solution)/shard_map/ppermute | solution.py:325
  548.9 68.3 %copy-start.8 = (f32[40,16,128]{2,1,0:T(8,128)}, f32[40,16,128]{2,1,0:T(8,128)S(1)}, u32[]{:S(2)}) copy-start(f32[40,16,128]{2,1,0:T(8,128)S(1)} %collective-permute-done.10.refs_1_) | copy-start | bytes 983044
  548.9 33.3 %collective-permute-start.12 = (f32[40,16,128]{2,1,0:T(8,128)S(1)}, f32[40,16,128]{2,1,0:T(8,128)S(1)}, u32[]{:S(2)}, u32[]{:S(2)}) collective-permute-start(f32[40,16,128]{2,1,0:T(8,128)S(1)} %collective-permute-done.5), channel_id=1, source_target_pairs={{0,12},{1,8},{2,4},{3,0},{4,13},{5,9},{6,5},{7,1},{8,14},{9,10},{1... | collective-permute-start | bytes 983048 | tf_op jit(solution)/shard_map/ppermute | solution.py:325
  564.9 52.3 %copy-start.9 = (f32[40,16,128]{2,1,0:T(8,128)}, f32[40,16,128]{2,1,0:T(8,128)S(1)}, u32[]{:S(2)}) copy-start(f32[40,16,128]{2,1,0:T(8,128)S(1)} %collective-permute-done.11.refs_2_) | copy-start | bytes 983044
  564.9 45.0 %collective-permute-start.9 = (f32[40,16,128]{2,1,0:T(8,128)S(1)}, f32[40,16,128]{2,1,0:T(8,128)S(1)}, u32[]{:S(2)}, u32[]{:S(2)}) collective-permute-start(f32[40,16,128]{2,1,0:T(8,128)S(1)} %copy-done.7), channel_id=1, source_target_pairs={{0,0},{1,4},{2,8},{3,12},{4,1},{5,5},{6,9},{7,13},{8,2},{9,6},{10,... | collective-permute-start | bytes 983048 | tf_op jit(solution)/shard_map/ppermute | solution.py:325
  582.2 34.9 %copy-start.10 = (f32[40,16,128]{2,1,0:T(8,128)}, f32[40,16,128]{2,1,0:T(8,128)S(1)}, u32[]{:S(2)}) copy-start(f32[40,16,128]{2,1,0:T(8,128)S(1)} %collective-permute-done.12.refs_3_) | copy-start | bytes 983044
  609.9 7.3 %copy-start.11 = (f32[40,16,128]{2,1,0:T(8,128)}, f32[40,16,128]{2,1,0:T(8,128)S(1)}, u32[]{:S(2)}) copy-start(f32[40,16,128]{2,1,0:T(8,128)S(1)} %collective-permute-done.9.refs_0_) | copy-start | bytes 983044
  609.9 25.3 %collective-permute-start.13 = (f32[56,16,128]{2,1,0:T(8,128)}, f32[56,16,128]{2,1,0:T(8,128)S(1)}, u32[]{:S(2)}, u32[]{:S(2)}) collective-permute-start(f32[56,16,128]{2,1,0:T(8,128)} %get-tuple-element.65.refs_1_), channel_id=1, source_target_pairs={{0,0},{1,4},{2,8},{3,12},{4,1},{5,5},{6,9},{7,13},{8,2},{9,6},{10,... | collective-permute-start | bytes 1376264 | tf_op jit(solution)/shard_map/ppermute | solution.py:325
  617.1 21.0 %collective-permute-start.14 = (f32[56,16,128]{2,1,0:T(8,128)}, f32[56,16,128]{2,1,0:T(8,128)S(1)}, u32[]{:S(2)}, u32[]{:S(2)}) collective-permute-start(f32[56,16,128]{2,1,0:T(8,128)} %collective-permute-done.6), channel_id=1, source_target_pairs={{0,4},{1,0},{2,12},{3,8},{4,5},{5,1},{6,13},{7,9},{8,6},{9,2},{10,... | collective-permute-start | bytes 1376264 | tf_op jit(solution)/shard_map/ppermute | solution.py:325
  617.2 27.0 %collective-permute-start.15 = (f32[56,16,128]{2,1,0:T(8,128)}, f32[56,16,128]{2,1,0:T(8,128)S(1)}, u32[]{:S(2)}, u32[]{:S(2)}) collective-permute-start(f32[56,16,128]{2,1,0:T(8,128)} %collective-permute-done.7), channel_id=1, source_target_pairs={{0,8},{1,12},{2,0},{3,4},{4,9},{5,13},{6,1},{7,5},{8,10},{9,14},{1... | collective-permute-start | bytes 1376264 | tf_op jit(solution)/shard_map/ppermute | solution.py:325
  617.3 1.3 copy-start.2
  618.6 39.6 %copy-start.22 = (f32[64]{0:T(128)S(1)}, f32[64]{0:T(128)}, u32[]{:S(2)}) copy-start(f32[64]{0:T(128)} %param.21) | copy-start | bytes 772
  634.5 11.6 %collective-permute-start.18 = (f32[32,16,128]{2,1,0:T(8,128)}, f32[32,16,128]{2,1,0:T(8,128)S(1)}, u32[]{:S(2)}, u32[]{:S(2)}) collective-permute-start(f32[32,16,128]{2,1,0:T(8,128)} %get-tuple-element.52.refs_5_), channel_id=1, source_target_pairs={{0,1},{1,0},{2,3},{3,2},{4,5},{5,4},{6,7},{7,6},{8,9},{9,8},{10,11... | collective-permute-start | bytes 786440 | tf_op jit(solution)/shard_map/ppermute | solution.py:325
  635.1 14.0 %collective-permute-start.20 = (f32[32,16,128]{2,1,0:T(8,128)}, f32[32,16,128]{2,1,0:T(8,128)S(1)}, u32[]{:S(2)}, u32[]{:S(2)}) collective-permute-start(f32[32,16,128]{2,1,0:T(8,128)} %get-tuple-element.54.refs_8_), channel_id=1, source_target_pairs={{0,2},{1,3},{2,0},{3,1},{4,6},{5,7},{6,4},{7,5},{8,10},{9,11},{10,... | collective-permute-start | bytes 786440 | tf_op jit(solution)/shard_map/ppermute | solution.py:325
  635.2 30.1 %copy-start.3 = (f32[56,16,128]{2,1,0:T(8,128)}, f32[56,16,128]{2,1,0:T(8,128)S(1)}, u32[]{:S(2)}) copy-start(f32[56,16,128]{2,1,0:T(8,128)S(1)} %collective-permute-done.13.refs_0_) | copy-start | bytes 1376260
  635.2 19.2 %collective-permute-start.22 = (f32[32,16,128]{2,1,0:T(8,128)}, f32[32,16,128]{2,1,0:T(8,128)}, u32[]{:S(2)}, u32[]{:S(2)}) collective-permute-start(f32[32,16,128]{2,1,0:T(8,128)} %get-tuple-element.56.refs_11_), channel_id=1, source_target_pairs={{0,3},{1,2},{2,1},{3,0},{4,7},{5,6},{6,5},{7,4},{8,11},{9,10},{10,... | collective-permute-start | bytes 786440 | tf_op jit(solution)/shard_map/ppermute | solution.py:325
  638.1 27.2 %copy-start.4 = (f32[56,16,128]{2,1,0:T(8,128)}, f32[56,16,128]{2,1,0:T(8,128)S(1)}, u32[]{:S(2)}) copy-start(f32[56,16,128]{2,1,0:T(8,128)S(1)} %collective-permute-done.14.refs_1_) | copy-start | bytes 1376260
  638.1 31.5 %collective-permute-start.16 = (f32[56,16,128]{2,1,0:T(8,128)}, f32[56,16,128]{2,1,0:T(8,128)S(1)}, u32[]{:S(2)}, u32[]{:S(2)}) collective-permute-start(f32[56,16,128]{2,1,0:T(8,128)} %collective-permute-done.8), channel_id=1, source_target_pairs={{0,12},{1,8},{2,4},{3,0},{4,13},{5,9},{6,5},{7,1},{8,14},{9,10},{1... | collective-permute-start | bytes 1376264 | tf_op jit(solution)/shard_map/ppermute | solution.py:325
  644.2 21.1 %copy-start.5 = (f32[56,16,128]{2,1,0:T(8,128)}, f32[56,16,128]{2,1,0:T(8,128)S(1)}, u32[]{:S(2)}) copy-start(f32[56,16,128]{2,1,0:T(8,128)S(1)} %collective-permute-done.15.refs_2_) | copy-start | bytes 1376260
  644.2 31.5 %collective-permute-start.17 = (f32[32,16,128]{2,1,0:T(8,128)}, f32[32,16,128]{2,1,0:T(8,128)S(1)}, u32[]{:S(2)}, u32[]{:S(2)}) collective-permute-start(f32[32,16,128]{2,1,0:T(8,128)} %get-tuple-element.50.refs_2_), channel_id=1, source_target_pairs={{0,0},{1,4},{2,8},{3,12},{4,1},{5,5},{6,9},{7,13},{8,2},{9,6},{10,... | collective-permute-start | bytes 786440 | tf_op jit(solution)/shard_map/ppermute | solution.py:325
  646.2 29.6 %collective-permute-start.19 = (f32[32,16,128]{2,1,0:T(8,128)S(1)}, f32[32,16,128]{2,1,0:T(8,128)S(1)}, u32[]{:S(2)}, u32[]{:S(2)}) collective-permute-start(f32[32,16,128]{2,1,0:T(8,128)S(1)} %collective-permute-done.18), channel_id=1, source_target_pairs={{0,4},{1,0},{2,12},{3,8},{4,5},{5,1},{6,13},{7,9},{8,6},{9,2},{10,... | collective-permute-start | bytes 786440 | tf_op jit(solution)/shard_map/ppermute | solution.py:325
  649.1 26.6 %collective-permute-start.21 = (f32[32,16,128]{2,1,0:T(8,128)S(1)}, f32[32,16,128]{2,1,0:T(8,128)S(1)}, u32[]{:S(2)}, u32[]{:S(2)}) collective-permute-start(f32[32,16,128]{2,1,0:T(8,128)S(1)} %collective-permute-done.20), channel_id=1, source_target_pairs={{0,8},{1,12},{2,0},{3,4},{4,9},{5,13},{6,1},{7,5},{8,10},{9,14},{1... | collective-permute-start | bytes 786440 | tf_op jit(solution)/shard_map/ppermute | solution.py:325
  654.3 21.4 %collective-permute-start.23 = (f32[32,16,128]{2,1,0:T(8,128)}, f32[32,16,128]{2,1,0:T(8,128)S(1)}, u32[]{:S(2)}, u32[]{:S(2)}) collective-permute-start(f32[32,16,128]{2,1,0:T(8,128)} %collective-permute-done.22), channel_id=1, source_target_pairs={{0,12},{1,8},{2,4},{3,0},{4,13},{5,9},{6,5},{7,1},{8,14},{9,10},{1... | collective-permute-start | bytes 786440 | tf_op jit(solution)/shard_map/ppermute | solution.py:325
  (5 other events, 3.9 us)

commit v14 on v13

--- a/solution.py
+++ b/solution.py
@@ -403,10 +403,12 @@
     mirror = [across(shifted, row_count)]
     values, after = tie((delivered(values), blocks(2)))
     own.append(run_head(values, 1))
-    shifted, mirror[0] = tie((aside(own[1], row_count), mirror[0]))
-    own.append(run_head(delivered(after), 2))
+    shifted, mirror[0], late = tie(
+        (aside(own[1], row_count), mirror[0], run_head(delivered(after), 2))
+    )
+    own.append(late)
     mirror.append(across(shifted, row_count))
-    mirror.append(across(aside(own[2], row_count), row_count))
+    mirror.append(across(aside(late, row_count), row_count))
     bins = distogram_bias.shape[0] // PARTS
     bias = jnp.broadcast_to(distogram_bias.reshape(PARTS, bins, 1), (PARTS, bins, tile_cols))
     logits = turned(bias, own)

time: 686 us -> 678 us (0.988)
  waiting for transfers between devices: 402 us -> 370 us
  starting transfers between devices: 108 us -> 136 us
    ppermute x21, waiting for transfers between devices: 43.5 us -> 10.7 us  [move(): return lax.ppermute(values, ('half', 'lo', 'col'), pairs)]
    ppermute x21, starting transfers between devices: 57.8 us -> 85.1 us  [move(): return lax.ppermute(values, ('half', 'lo', 'col'), pairs)]
  transfers between devices with their start and end apart: 30 -> 30, of which waited for: 10 -> 8; matrix products, arithmetic and copies ran while one was open for 2% -> 2% of each run, Pallas kernels for 20% -> 20%
where the time goes in v14:
time: 678 us; the launch traced here: 675 us
  waiting for transfers between devices  370 us (55%)
  Pallas kernels  148 us (22%)
  starting transfers between devices  136 us (20%)
  local copies, waits for them, and re-layouts  16.9 us (2%)
    all_to_all x3, waiting for transfers between devices, spread(): lax.all_to_all(values, ('lo', 'col'), split_axis=0, concat_axis=0, tiled=...  175 us
    ppermute x3, waiting for transfers between devices, exchange(): return lax.ppermute(values, 'half', [(0, 1), (1, 0)])  118 us
    ppermute x21, starting transfers between devices, move(): return lax.ppermute(values, ('half', 'lo', 'col'), pairs)  85.1 us
    all_to_all x3, waiting for transfers between devices, delivered(): lax.all_to_all(values, ('lo', 'col'), split_axis=0, concat_axis=0, tiled=...  66.5 us
    pallas_call x3, Pallas kernels, head(): pl.pallas_call(head_kernel, grid=(steps,), in_specs=[pl.BlockSpec((tile_r...  61.3 us
    pallas_call x3, Pallas kernels, hands(): pl.pallas_call(hands_kernel, grid=(rows // GROUP,), in_specs=[pl.BlockSpe...  35.6 us
    pallas_call x3, Pallas kernels, product(): pl.pallas_call(product_kernel, grid_spec=pltpu.PrefetchScalarGridSpec(num...  31.7 us
    all_to_all x3, starting transfers between devices, spread(): lax.all_to_all(values, ('lo', 'col'), split_axis=0, concat_axis=0, tiled=...  26.8 us
  transfers between devices with their start and end apart: 30, of which 8 were waited for; matrix products, arithmetic and copies ran while one was open for 2% of the time, Pallas kernels for 20%

profile of v14, /device:TPU:12, one launch (start us, length us, event | category | flops | bytes accessed | tf_op | source)
XLA Modules:
  0.0 675.4 jit_solution(9820418376869914319)
XLA Ops:
  2.6 6.4 hands.5
  9.0 5.1 all-to-all-start.1
  14.1 13.1 %hands.3 = f32[128,96,128]{2,1,0:T(8,128)} custom-call(f32[128,128,128]{2,1,0:T(8,128)} %bitcast.32, bf16[512,384]{1,0:T(8,128)(2,1)} %pad_maximum_fusion.1.weights_ref), custom_call_target="tpu_custom_call" | custom-call | flops 301989888 | bytes 1572864 | tf_op jit(solution)/shard_map/hands/pallas_call | solution.py:132
  27.2 17.8 %all-to-all-done.1.own_ref = f32[8,16,40,128]{3,2,1,0:T(8,128)S(1)} async-done(((f32[8,16,40,128]{3,2,1,0:T(8,128)}), f32[8,16,40,128]{3,2,1,0:T(8,128)S(1)}, u32[]{:S(2)}, u32[]{:S(2)}) %all-to-all-start.1) | async-done | bytes 2621472 | tf_op jit(solution)/shard_map/all_to_all | solution.py:368
  45.0 7.2 %all-to-all-start = ((f32[8,16,96,128]{3,2,1,0:T(8,128)}), f32[8,16,96,128]{3,2,1,0:T(8,128)}, u32[]{:S(2)}, u32[]{:S(2)}) async-start(f32[8,16,96,128]{3,2,1,0:T(8,128)} %bitcast.38), calls=%async_computation | async-start | bytes 12582912 | tf_op jit(solution)/shard_map/all_to_all | solution.py:368
  52.1 2.6 collective-permute-start
  54.7 16.2 %hands.4 = f32[128,120,128]{2,1,0:T(8,128)} custom-call(f32[128,128,128]{2,1,0:T(8,128)} %bitcast.33, bf16[512,384]{1,0:T(8,128)(2,1)} %pad_maximum_fusion.1.weights_ref), custom_call_target="tpu_custom_call" | custom-call | flops 377487360 | bytes 1966080 | tf_op jit(solution)/shard_map/hands/pallas_call | solution.py:132
  70.9 106.9 %collective-permute-done.other_ref = f32[8,16,40,128]{3,2,1,0:T(8,128)} collective-permute-done((f32[8,16,40,128]{3,2,1,0:T(8,128)S(1)}, f32[8,16,40,128]{3,2,1,0:T(8,128)}, u32[]{:S(2)}, u32[]{:S(2)}) %collective-permute-start) | collective-permute-done | bytes 2621472 | tf_op jit(solution)/shard_map/ppermute | solution.py:376
  177.9 14.5 %all-to-all-start.2 = ((f32[8,16,120,128]{3,2,1,0:T(8,128)}), f32[8,16,120,128]{3,2,1,0:T(8,128)}, u32[]{:S(2)}, u32[]{:S(2)}) async-start(f32[8,16,120,128]{3,2,1,0:T(8,128)} %bitcast.37), calls=%async_computation.2 | async-start | bytes 15728640 | tf_op jit(solution)/shard_map/all_to_all | solution.py:368
  192.4 4.2 slice.8.own_ref
  196.6 156.8 %all-to-all-done.2.high_ref = f32[8,16,120,128]{3,2,1,0:T(8,128)} async-done(((f32[8,16,120,128]{3,2,1,0:T(8,128)}), f32[8,16,120,128]{3,2,1,0:T(8,128)}, u32[]{:S(2)}, u32[]{:S(2)}) %all-to-all-start.2) | async-done | bytes 7864352 | tf_op jit(solution)/shard_map/all_to_all | solution.py:368
  353.4 10.5 %product.3 = f32[8,16,40,128]{3,2,1,0:T(8,128)} custom-call(s32[1]{0:T(128)} %bitcast.1.half_ref, f32[8,16,96,128]{3,2,1,0:T(8,128)} %all-to-all-done.low_ref, f32[8,16,120,128]{3,2,1,0:T(8,128)} %all-to-all-done.2.high_ref, f32[8,16,40,128]{3,2,1,0:T(8,128)} %copy-done, f32[8,16,40,128]{3,2,1,0:T(8,128)} %collective-permute-done.other_ref), custom_call_target="tpu_custom_call" | custom-call | flops 251658240 | bytes 1703936 | tf_op jit(solution)/shard_map/product/pallas_call | solution.py:189
  363.9 6.7 all-to-all-start.3
  370.7 1.2 copy.18
  372.0 1.1 copy.19
  373.1 3.1 slice.9.own_ref
  376.2 1.9 collective-permute-start.2
  381.3 36.9 %all-to-all-done.3 = f32[8,16,40,128]{3,2,1,0:T(8,128)S(1)} async-done(((f32[8,16,40,128]{3,2,1,0:T(8,128)}), f32[8,16,40,128]{3,2,1,0:T(8,128)S(1)}, u32[]{:S(2)}, u32[]{:S(2)}) %all-to-all-start.3) | async-done | bytes 2621472 | tf_op jit(solution)/shard_map/all_to_all | solution.py:379
  418.2 1.6 copy-done.1
  419.8 19.2 %head.3 = (f32[40,16,128]{2,1,0:T(8,128)}, f32[40,16,128]{2,1,0:T(8,128)}, f32[40,16,128]{2,1,0:T(8,128)}, f32[40,16,128]{2,1,0:T(8,128)}) custom-call(f32[128,128,128]{2,1,0:T(8,128)} %bitcast.34, f32[128,40,128]{2,1,0:T(8,128)} %bitcast.39, bf16[128,384]{1,0:T(8,128)(2,1)} %get-tuple-element.89.gate_ref, bf16[128,384]{1,0:T(8,128)(2,1)} %get-tuple-element.90.output_ref, ...), custom_call_target="tpu_custom_call" | custom-call | flops 912261120 | bytes 819200 | tf_op jit(solution)/shard_map/head/pallas_call | solution.py:243
  439.1 1.6 collective-permute-start.3
  441.2 1.4 collective-permute-start.5
  442.6 11.1 %product.4 = f32[8,16,56,128]{3,2,1,0:T(8,128)} custom-call(s32[1]{0:T(128)} %bitcast.1.half_ref, f32[8,16,96,128]{3,2,1,0:T(8,128)} %all-to-all-done.low_ref, f32[8,16,120,128]{3,2,1,0:T(8,128)} %all-to-all-done.2.high_ref, f32[8,16,56,128]{3,2,1,0:T(8,128)} %slice.8.own_ref, f32[8,16,56,128]{3,2,1,0:T(8,128)} %collective-permute-done.1.other_ref), custom_call_target="tpu_custom_call" | custom-call | flops 352321536 | bytes 1966080 | tf_op jit(solution)/shard_map/product/pallas_call | solution.py:189
  453.7 10.8 %collective-permute-done.2.other_ref = f32[8,16,32,128]{3,2,1,0:T(8,128)} collective-permute-done((f32[8,16,32,128]{3,2,1,0:T(8,128)}, f32[8,16,32,128]{3,2,1,0:T(8,128)}, u32[]{:S(2)}, u32[]{:S(2)}) %collective-permute-start.2) | collective-permute-done | bytes 2097184 | tf_op jit(solution)/shard_map/ppermute | solution.py:376
  464.5 6.5 all-to-all-start.4
  471.1 10.1 %product.5 = f32[8,16,32,128]{3,2,1,0:T(8,128)} custom-call(s32[1]{0:T(128)} %bitcast.1.half_ref, f32[8,16,96,128]{3,2,1,0:T(8,128)} %all-to-all-done.low_ref, f32[8,16,120,128]{3,2,1,0:T(8,128)} %all-to-all-done.2.high_ref, f32[8,16,32,128]{3,2,1,0:T(8,128)} %slice.9.own_ref, f32[8,16,32,128]{3,2,1,0:T(8,128)} %collective-permute-done.2.other_ref), custom_call_target="tpu_custom_call" | custom-call | flops 201326592 | bytes 1572864 | tf_op jit(solution)/shard_map/product/pallas_call | solution.py:189
  481.1 29.6 %all-to-all-done.4 = f32[8,16,56,128]{3,2,1,0:T(8,128)} async-done(((f32[8,16,56,128]{3,2,1,0:T(8,128)}), f32[8,16,56,128]{3,2,1,0:T(8,128)}, u32[]{:S(2)}, u32[]{:S(2)}) %all-to-all-start.4) | async-done | bytes 3670048 | tf_op jit(solution)/shard_map/all_to_all | solution.py:379
  510.7 6.1 all-to-all-start.5
  516.8 2.2 collective-permute-start.10
  519.1 26.1 %head.4 = (f32[56,16,128]{2,1,0:T(8,128)}, f32[56,16,128]{2,1,0:T(8,128)}, f32[56,16,128]{2,1,0:T(8,128)}, f32[56,16,128]{2,1,0:T(8,128)}) custom-call(f32[128,128,128]{2,1,0:T(8,128)} %bitcast.35, f32[128,56,128]{2,1,0:T(8,128)} %bitcast.12.product_ref, bf16[128,384]{1,0:T(8,128)(2,1)} %get-tuple-element.89.gate_ref, ...), custom_call_target="tpu_custom_call" | custom-call | flops 1277165568 | bytes 1146880 | tf_op jit(solution)/shard_map/head/pallas_call | solution.py:243
  545.6 3.3 collective-permute-start.7
  548.9 16.2 %collective-permute-start.12 = (f32[40,16,128]{2,1,0:T(8,128)}, f32[40,16,128]{2,1,0:T(8,128)}, u32[]{:S(2)}, u32[]{:S(2)}) collective-permute-start(f32[40,16,128]{2,1,0:T(8,128)} %collective-permute-done.5), channel_id=1, source_target_pairs={{0,12},{1,8},{2,4},{3,0},{4,13},{5,9},{6,5},{7,1},{8,14},{9,10},{1... | collective-permute-start | bytes 983048 | tf_op jit(solution)/shard_map/ppermute | solution.py:325
  565.1 9.0 %collective-permute-start.9 = (f32[40,16,128]{2,1,0:T(8,128)S(1)}, f32[40,16,128]{2,1,0:T(8,128)}, u32[]{:S(2)}, u32[]{:S(2)}) collective-permute-start(f32[40,16,128]{2,1,0:T(8,128)S(1)} %copy-done.8), channel_id=1, source_target_pairs={{0,0},{1,4},{2,8},{3,12},{4,1},{5,5},{6,9},{7,13},{8,2},{9,6},{10,... | collective-permute-start | bytes 983048 | tf_op jit(solution)/shard_map/ppermute | solution.py:325
  574.1 1.3 copy-done.2
  575.4 16.0 %head.5 = (f32[32,16,128]{2,1,0:T(8,128)}, f32[32,16,128]{2,1,0:T(8,128)}, f32[32,16,128]{2,1,0:T(8,128)}, f32[32,16,128]{2,1,0:T(8,128)}) custom-call(f32[128,128,128]{2,1,0:T(8,128)} %bitcast.36, f32[128,32,128]{2,1,0:T(8,128)} %bitcast.41, bf16[128,384]{1,0:T(8,128)(2,1)} %get-tuple-element.89.gate_ref, bf16[128,384]{1,0:T(8,128)(2,1)} %get-tuple-element.90.output_ref, ...), custom_call_target="tpu_custom_call" | custom-call | flops 729808896 | bytes 655360 | tf_op jit(solution)/shard_map/head/pallas_call | solution.py:243
  591.6 4.3 collective-permute-start.13
  595.9 2.8 collective-permute-start.14
  598.8 2.3 collective-permute-start.22
  601.1 18.9 %collective-permute-start.16 = (f32[56,16,128]{2,1,0:T(8,128)}, f32[56,16,128]{2,1,0:T(8,128)S(1)}, u32[]{:S(2)}, u32[]{:S(2)}) collective-permute-start(f32[56,16,128]{2,1,0:T(8,128)} %collective-permute-done.8), channel_id=1, source_target_pairs={{0,12},{1,8},{2,4},{3,0},{4,13},{5,9},{6,5},{7,1},{8,14},{9,10},{1... | collective-permute-start | bytes 1376264 | tf_op jit(solution)/shard_map/ppermute | solution.py:325
  620.1 1.9 collective-permute-start.17
  622.0 5.6 collective-permute-done.13.refs_0_
  627.5 13.8 %collective-permute-start.19 = (f32[32,16,128]{2,1,0:T(8,128)}, f32[32,16,128]{2,1,0:T(8,128)S(1)}, u32[]{:S(2)}, u32[]{:S(2)}) collective-permute-start(f32[32,16,128]{2,1,0:T(8,128)} %collective-permute-done.18), channel_id=1, source_target_pairs={{0,4},{1,0},{2,12},{3,8},{4,5},{5,1},{6,13},{7,9},{8,6},{9,2},{10,... | collective-permute-start | bytes 786440 | tf_op jit(solution)/shard_map/ppermute | solution.py:325
  641.3 5.1 collective-permute-done.14.refs_1_
  646.4 6.2 collective-permute-start.23
  653.4 6.3 turned.1.base_ref
  659.8 4.2 joined.3.base_ref
  664.8 5.4 joined.4.base_ref
  671.8 3.5 joined.5
  (89 shorter events, 10.4 us)
Async XLA Ops:
  9.0 36.0 %all-to-all-start.1 = ((f32[8,16,40,128]{3,2,1,0:T(8,128)}), f32[8,16,40,128]{3,2,1,0:T(8,128)S(1)}, u32[]{:S(2)}, u32[]{:S(2)}) async-start(f32[8,16,40,128]{3,2,1,0:T(8,128)} %bitcast.40), calls=%async_computation.1 | async-start | bytes 5242880 | tf_op jit(solution)/shard_map/all_to_all | solution.py:368
  45.0 7.2 %copy-start = (f32[8,16,40,128]{3,2,1,0:T(8,128)}, f32[8,16,40,128]{3,2,1,0:T(8,128)S(1)}, u32[]{:S(2)}) copy-start(f32[8,16,40,128]{3,2,1,0:T(8,128)S(1)} %all-to-all-done.1.own_ref) | copy-start | bytes 7864324
  45.0 132.9 %all-to-all-start = ((f32[8,16,96,128]{3,2,1,0:T(8,128)}), f32[8,16,96,128]{3,2,1,0:T(8,128)}, u32[]{:S(2)}, u32[]{:S(2)}) async-start(f32[8,16,96,128]{3,2,1,0:T(8,128)} %bitcast.38), calls=%async_computation | async-start | bytes 12582912 | tf_op jit(solution)/shard_map/all_to_all | solution.py:368
  52.1 125.7 %collective-permute-start = (f32[8,16,40,128]{3,2,1,0:T(8,128)S(1)}, f32[8,16,40,128]{3,2,1,0:T(8,128)}, u32[]{:S(2)}, u32[]{:S(2)}) collective-permute-start(f32[8,16,40,128]{3,2,1,0:T(8,128)S(1)} %all-to-all-done.1.own_ref), channel_id=1, source_target_pairs={{0,8},{8,0},{1,9},{9,1},{2,10},{10,2},{3,11},{11,3},{4,12},{12,4},... | collective-permute-start | bytes 7864328 | tf_op jit(solution)/shard_map/ppermute | solution.py:376
  177.9 175.5 %all-to-all-start.2 = ((f32[8,16,120,128]{3,2,1,0:T(8,128)}), f32[8,16,120,128]{3,2,1,0:T(8,128)}, u32[]{:S(2)}, u32[]{:S(2)}) async-start(f32[8,16,120,128]{3,2,1,0:T(8,128)} %bitcast.37), calls=%async_computation.2 | async-start | bytes 15728640 | tf_op jit(solution)/shard_map/all_to_all | solution.py:368
  196.6 167.3 %collective-permute-start.1 = (f32[8,16,56,128]{3,2,1,0:T(8,128)}, f32[8,16,56,128]{3,2,1,0:T(8,128)}, u32[]{:S(2)}, u32[]{:S(2)}) collective-permute-start(f32[8,16,56,128]{3,2,1,0:T(8,128)} %slice.8.own_ref), channel_id=1, source_target_pairs={{0,8},{8,0},{1,9},{9,1},{2,10},{10,2},{3,11},{11,3},{4,12},{12,4},... | collective-permute-start | bytes 11010056 | tf_op jit(solution)/shard_map/ppermute | solution.py:376
  363.9 6.7 copy-start.15
  363.9 6.8 %copy-start.16 = (f32[128,128]{1,0:T(8,128)S(1)}, f32[128,128]{1,0:T(8,128)}, u32[]{:S(2)}) copy-start(f32[128,128]{1,0:T(8,128)} %param.14) | copy-start | bytes 196612
  363.9 54.3 %all-to-all-start.3 = ((f32[8,16,40,128]{3,2,1,0:T(8,128)}), f32[8,16,40,128]{3,2,1,0:T(8,128)S(1)}, u32[]{:S(2)}, u32[]{:S(2)}) async-start(f32[8,16,40,128]{3,2,1,0:T(8,128)} %product.3), calls=%async_computation.3 | async-start | bytes 5242880 | tf_op jit(solution)/shard_map/all_to_all | solution.py:379
  372.0 6.7 copy-start.18
  372.0 6.7 copy-start.19
  372.0 7.5 %copy-start.20 = (f32[128]{0:T(128)S(1)}, f32[128]{0:T(128)}, u32[]{:S(2)}) copy-start(f32[128]{0:T(128)} %param.17) | copy-start | bytes 1540
  373.1 5.0 copy-start.17
  376.2 88.3 %collective-permute-start.2 = (f32[8,16,32,128]{3,2,1,0:T(8,128)}, f32[8,16,32,128]{3,2,1,0:T(8,128)}, u32[]{:S(2)}, u32[]{:S(2)}) collective-permute-start(f32[8,16,32,128]{3,2,1,0:T(8,128)} %slice.9.own_ref), channel_id=1, source_target_pairs={{0,8},{8,0},{1,9},{9,1},{2,10},{10,2},{3,11},{11,3},{4,12},{12,4},... | collective-permute-start | bytes 6291464 | tf_op jit(solution)/shard_map/ppermute | solution.py:376
  418.2 1.6 copy-start.1
  439.1 25.4 %collective-permute-start.3 = (f32[40,16,128]{2,1,0:T(8,128)}, f32[40,16,128]{2,1,0:T(8,128)}, u32[]{:S(2)}, u32[]{:S(2)}) collective-permute-start(f32[40,16,128]{2,1,0:T(8,128)} %get-tuple-element.46.refs_3_), channel_id=1, source_target_pairs={{0,1},{1,0},{2,3},{3,2},{4,5},{5,4},{6,7},{7,6},{8,9},{9,8},{10,11... | collective-permute-start | bytes 983048 | tf_op jit(solution)/shard_map/ppermute | solution.py:325
  440.7 23.9 %collective-permute-start.4 = (f32[40,16,128]{2,1,0:T(8,128)}, f32[40,16,128]{2,1,0:T(8,128)S(1)}, u32[]{:S(2)}, u32[]{:S(2)}) collective-permute-start(f32[40,16,128]{2,1,0:T(8,128)} %get-tuple-element.47.refs_6_), channel_id=1, source_target_pairs={{0,2},{1,3},{2,0},{3,1},{4,6},{5,7},{6,4},{7,5},{8,10},{9,11},{10,... | collective-permute-start | bytes 983048 | tf_op jit(solution)/shard_map/ppermute | solution.py:325
  441.2 23.3 %collective-permute-start.5 = (f32[40,16,128]{2,1,0:T(8,128)}, f32[40,16,128]{2,1,0:T(8,128)}, u32[]{:S(2)}, u32[]{:S(2)}) collective-permute-start(f32[40,16,128]{2,1,0:T(8,128)} %get-tuple-element.48.refs_9_), channel_id=1, source_target_pairs={{0,3},{1,2},{2,1},{3,0},{4,7},{5,6},{6,5},{7,4},{8,11},{9,10},{10,... | collective-permute-start | bytes 983048 | tf_op jit(solution)/shard_map/ppermute | solution.py:325
  464.5 46.2 %all-to-all-start.4 = ((f32[8,16,56,128]{3,2,1,0:T(8,128)}), f32[8,16,56,128]{3,2,1,0:T(8,128)}, u32[]{:S(2)}, u32[]{:S(2)}) async-start(f32[8,16,56,128]{3,2,1,0:T(8,128)} %product.4), calls=%async_computation.4 | async-start | bytes 7340032 | tf_op jit(solution)/shard_map/all_to_all | solution.py:379
  510.7 63.4 %all-to-all-start.5 = ((f32[8,16,32,128]{3,2,1,0:T(8,128)}), f32[8,16,32,128]{3,2,1,0:T(8,128)S(1)}, u32[]{:S(2)}, u32[]{:S(2)}) async-start(f32[8,16,32,128]{3,2,1,0:T(8,128)} %product.5), calls=%async_computation.5 | async-start | bytes 4194304 | tf_op jit(solution)/shard_map/all_to_all | solution.py:379
  516.8 48.2 %copy-start.8 = (f32[40,16,128]{2,1,0:T(8,128)S(1)}, f32[40,16,128]{2,1,0:T(8,128)}, u32[]{:S(2)}) copy-start(f32[40,16,128]{2,1,0:T(8,128)} %get-tuple-element.56.refs_0_) | copy-start | bytes 983044
  516.8 32.0 %collective-permute-start.10 = (f32[40,16,128]{2,1,0:T(8,128)}, f32[40,16,128]{2,1,0:T(8,128)S(1)}, u32[]{:S(2)}, u32[]{:S(2)}) collective-permute-start(f32[40,16,128]{2,1,0:T(8,128)} %collective-permute-done.3), channel_id=1, source_target_pairs={{0,4},{1,0},{2,12},{3,8},{4,5},{5,1},{6,13},{7,9},{8,6},{9,2},{10,... | collective-permute-start | bytes 983048 | tf_op jit(solution)/shard_map/ppermute | solution.py:325
  519.1 46.0 %collective-permute-start.11 = (f32[40,16,128]{2,1,0:T(8,128)S(1)}, f32[40,16,128]{2,1,0:T(8,128)S(1)}, u32[]{:S(2)}, u32[]{:S(2)}) collective-permute-start(f32[40,16,128]{2,1,0:T(8,128)S(1)} %collective-permute-done.4), channel_id=1, source_target_pairs={{0,8},{1,12},{2,0},{3,4},{4,9},{5,13},{6,1},{7,5},{8,10},{9,14},{1... | collective-permute-start | bytes 983048 | tf_op jit(solution)/shard_map/ppermute | solution.py:325
  545.2 46.2 %collective-permute-start.6 = (f32[56,16,128]{2,1,0:T(8,128)}, f32[56,16,128]{2,1,0:T(8,128)}, u32[]{:S(2)}, u32[]{:S(2)}) collective-permute-start(f32[56,16,128]{2,1,0:T(8,128)} %get-tuple-element.53.refs_4_), channel_id=1, source_target_pairs={{0,1},{1,0},{2,3},{3,2},{4,5},{5,4},{6,7},{7,6},{8,9},{9,8},{10,11... | collective-permute-start | bytes 1376264 | tf_op jit(solution)/shard_map/ppermute | solution.py:325
  545.6 45.8 %collective-permute-start.7 = (f32[56,16,128]{2,1,0:T(8,128)}, f32[56,16,128]{2,1,0:T(8,128)}, u32[]{:S(2)}, u32[]{:S(2)}) collective-permute-start(f32[56,16,128]{2,1,0:T(8,128)} %get-tuple-element.54.refs_7_), channel_id=1, source_target_pairs={{0,2},{1,3},{2,0},{3,1},{4,6},{5,7},{6,4},{7,5},{8,10},{9,11},{10,... | collective-permute-start | bytes 1376264 | tf_op jit(solution)/shard_map/ppermute | solution.py:325
  548.9 42.6 %collective-permute-start.8 = (f32[56,16,128]{2,1,0:T(8,128)}, f32[56,16,128]{2,1,0:T(8,128)}, u32[]{:S(2)}, u32[]{:S(2)}) collective-permute-start(f32[56,16,128]{2,1,0:T(8,128)} %get-tuple-element.55.refs_10_), channel_id=1, source_target_pairs={{0,3},{1,2},{2,1},{3,0},{4,7},{5,6},{6,5},{7,4},{8,11},{9,10},{10,... | collective-permute-start | bytes 1376264 | tf_op jit(solution)/shard_map/ppermute | solution.py:325
  548.9 110.9 %copy-start.9 = (f32[40,16,128]{2,1,0:T(8,128)}, f32[40,16,128]{2,1,0:T(8,128)S(1)}, u32[]{:S(2)}) copy-start(f32[40,16,128]{2,1,0:T(8,128)S(1)} %collective-permute-done.10.refs_1_) | copy-start | bytes 983044
  548.9 42.5 %collective-permute-start.12 = (f32[40,16,128]{2,1,0:T(8,128)}, f32[40,16,128]{2,1,0:T(8,128)}, u32[]{:S(2)}, u32[]{:S(2)}) collective-permute-start(f32[40,16,128]{2,1,0:T(8,128)} %collective-permute-done.5), channel_id=1, source_target_pairs={{0,12},{1,8},{2,4},{3,0},{4,13},{5,9},{6,5},{7,1},{8,14},{9,10},{1... | collective-permute-start | bytes 983048 | tf_op jit(solution)/shard_map/ppermute | solution.py:325
  565.1 94.7 %copy-start.10 = (f32[40,16,128]{2,1,0:T(8,128)}, f32[40,16,128]{2,1,0:T(8,128)S(1)}, u32[]{:S(2)}) copy-start(f32[40,16,128]{2,1,0:T(8,128)S(1)} %collective-permute-done.11.refs_2_) | copy-start | bytes 983044
  565.1 26.3 %collective-permute-start.9 = (f32[40,16,128]{2,1,0:T(8,128)S(1)}, f32[40,16,128]{2,1,0:T(8,128)}, u32[]{:S(2)}, u32[]{:S(2)}) collective-permute-start(f32[40,16,128]{2,1,0:T(8,128)S(1)} %copy-done.8), channel_id=1, source_target_pairs={{0,0},{1,4},{2,8},{3,12},{4,1},{5,5},{6,9},{7,13},{8,2},{9,6},{10,... | collective-permute-start | bytes 983048 | tf_op jit(solution)/shard_map/ppermute | solution.py:325
  574.1 1.3 copy-start.2
  575.4 16.2 %copy-start.3 = (f32[56,16,128]{2,1,0:T(8,128)S(1)}, f32[56,16,128]{2,1,0:T(8,128)}, u32[]{:S(2)}) copy-start(f32[56,16,128]{2,1,0:T(8,128)} %get-tuple-element.73.refs_1_) | copy-start | bytes 1376260
  575.4 77.3 %copy-start.21 = (f32[64]{0:T(128)S(1)}, f32[64]{0:T(128)}, u32[]{:S(2)}) copy-start(f32[64]{0:T(128)} %param.21) | copy-start | bytes 772
  591.4 7.4 %collective-permute-start.18 = (f32[32,16,128]{2,1,0:T(8,128)}, f32[32,16,128]{2,1,0:T(8,128)}, u32[]{:S(2)}, u32[]{:S(2)}) collective-permute-start(f32[32,16,128]{2,1,0:T(8,128)} %get-tuple-element.66.refs_5_), channel_id=1, source_target_pairs={{0,1},{1,0},{2,3},{3,2},{4,5},{5,4},{6,7},{7,6},{8,9},{9,8},{10,11... | collective-permute-start | bytes 786440 | tf_op jit(solution)/shard_map/ppermute | solution.py:325
  591.5 9.7 %collective-permute-start.20 = (f32[32,16,128]{2,1,0:T(8,128)}, f32[32,16,128]{2,1,0:T(8,128)}, u32[]{:S(2)}, u32[]{:S(2)}) collective-permute-start(f32[32,16,128]{2,1,0:T(8,128)} %get-tuple-element.67.refs_8_), channel_id=1, source_target_pairs={{0,2},{1,3},{2,0},{3,1},{4,6},{5,7},{6,4},{7,5},{8,10},{9,11},{10,... | collective-permute-start | bytes 786440 | tf_op jit(solution)/shard_map/ppermute | solution.py:325
  591.6 36.0 %collective-permute-start.13 = (f32[56,16,128]{2,1,0:T(8,128)S(1)}, f32[56,16,128]{2,1,0:T(8,128)S(1)}, u32[]{:S(2)}, u32[]{:S(2)}) collective-permute-start(f32[56,16,128]{2,1,0:T(8,128)S(1)} %copy-done.3), channel_id=1, source_target_pairs={{0,0},{1,4},{2,8},{3,12},{4,1},{5,5},{6,9},{7,13},{8,2},{9,6},{10,... | collective-permute-start | bytes 1376264 | tf_op jit(solution)/shard_map/ppermute | solution.py:325
  595.9 50.5 %collective-permute-start.14 = (f32[56,16,128]{2,1,0:T(8,128)}, f32[56,16,128]{2,1,0:T(8,128)S(1)}, u32[]{:S(2)}, u32[]{:S(2)}) collective-permute-start(f32[56,16,128]{2,1,0:T(8,128)} %collective-permute-done.6), channel_id=1, source_target_pairs={{0,4},{1,0},{2,12},{3,8},{4,5},{5,1},{6,13},{7,9},{8,6},{9,2},{10,... | collective-permute-start | bytes 1376264 | tf_op jit(solution)/shard_map/ppermute | solution.py:325
  598.7 47.7 %collective-permute-start.15 = (f32[56,16,128]{2,1,0:T(8,128)}, f32[56,16,128]{2,1,0:T(8,128)S(1)}, u32[]{:S(2)}, u32[]{:S(2)}) collective-permute-start(f32[56,16,128]{2,1,0:T(8,128)} %collective-permute-done.7), channel_id=1, source_target_pairs={{0,8},{1,12},{2,0},{3,4},{4,9},{5,13},{6,1},{7,5},{8,10},{9,14},{1... | collective-permute-start | bytes 1376264 | tf_op jit(solution)/shard_map/ppermute | solution.py:325
  598.8 21.2 %collective-permute-start.22 = (f32[32,16,128]{2,1,0:T(8,128)}, f32[32,16,128]{2,1,0:T(8,128)}, u32[]{:S(2)}, u32[]{:S(2)}) collective-permute-start(f32[32,16,128]{2,1,0:T(8,128)} %get-tuple-element.68.refs_11_), channel_id=1, source_target_pairs={{0,3},{1,2},{2,1},{3,0},{4,7},{5,6},{6,5},{7,4},{8,11},{9,10},{10,... | collective-permute-start | bytes 786440 | tf_op jit(solution)/shard_map/ppermute | solution.py:325
  601.1 62.9 %collective-permute-start.16 = (f32[56,16,128]{2,1,0:T(8,128)}, f32[56,16,128]{2,1,0:T(8,128)S(1)}, u32[]{:S(2)}, u32[]{:S(2)}) collective-permute-start(f32[56,16,128]{2,1,0:T(8,128)} %collective-permute-done.8), channel_id=1, source_target_pairs={{0,12},{1,8},{2,4},{3,0},{4,13},{5,9},{6,5},{7,1},{8,14},{9,10},{1... | collective-permute-start | bytes 1376264 | tf_op jit(solution)/shard_map/ppermute | solution.py:325
  620.1 50.2 %collective-permute-start.17 = (f32[32,16,128]{2,1,0:T(8,128)}, f32[32,16,128]{2,1,0:T(8,128)S(1)}, u32[]{:S(2)}, u32[]{:S(2)}) collective-permute-start(f32[32,16,128]{2,1,0:T(8,128)} %get-tuple-element.65.refs_2_), channel_id=1, source_target_pairs={{0,0},{1,4},{2,8},{3,12},{4,1},{5,5},{6,9},{7,13},{8,2},{9,6},{10,... | collective-permute-start | bytes 786440 | tf_op jit(solution)/shard_map/ppermute | solution.py:325
  627.5 32.2 %copy-start.4 = (f32[56,16,128]{2,1,0:T(8,128)}, f32[56,16,128]{2,1,0:T(8,128)S(1)}, u32[]{:S(2)}) copy-start(f32[56,16,128]{2,1,0:T(8,128)S(1)} %collective-permute-done.13.refs_0_) | copy-start | bytes 1376260
  627.5 42.7 %collective-permute-start.19 = (f32[32,16,128]{2,1,0:T(8,128)}, f32[32,16,128]{2,1,0:T(8,128)S(1)}, u32[]{:S(2)}, u32[]{:S(2)}) collective-permute-start(f32[32,16,128]{2,1,0:T(8,128)} %collective-permute-done.18), channel_id=1, source_target_pairs={{0,4},{1,0},{2,12},{3,8},{4,5},{5,1},{6,13},{7,9},{8,6},{9,2},{10,... | collective-permute-start | bytes 786440 | tf_op jit(solution)/shard_map/ppermute | solution.py:325
  646.4 13.3 %copy-start.5 = (f32[56,16,128]{2,1,0:T(8,128)}, f32[56,16,128]{2,1,0:T(8,128)S(1)}, u32[]{:S(2)}) copy-start(f32[56,16,128]{2,1,0:T(8,128)S(1)} %collective-permute-done.14.refs_1_) | copy-start | bytes 1376260
  646.4 23.8 %collective-permute-start.21 = (f32[32,16,128]{2,1,0:T(8,128)}, f32[32,16,128]{2,1,0:T(8,128)S(1)}, u32[]{:S(2)}, u32[]{:S(2)}) collective-permute-start(f32[32,16,128]{2,1,0:T(8,128)} %collective-permute-done.20), channel_id=1, source_target_pairs={{0,8},{1,12},{2,0},{3,4},{4,9},{5,13},{6,1},{7,5},{8,10},{9,14},{1... | collective-permute-start | bytes 786440 | tf_op jit(solution)/shard_map/ppermute | solution.py:325
  646.4 13.3 %copy-start.6 = (f32[56,16,128]{2,1,0:T(8,128)}, f32[56,16,128]{2,1,0:T(8,128)S(1)}, u32[]{:S(2)}) copy-start(f32[56,16,128]{2,1,0:T(8,128)S(1)} %collective-permute-done.15.refs_2_) | copy-start | bytes 1376260
  646.4 23.8 %collective-permute-start.23 = (f32[32,16,128]{2,1,0:T(8,128)}, f32[32,16,128]{2,1,0:T(8,128)S(1)}, u32[]{:S(2)}, u32[]{:S(2)}) collective-permute-start(f32[32,16,128]{2,1,0:T(8,128)} %collective-permute-done.22), channel_id=1, source_target_pairs={{0,12},{1,8},{2,4},{3,0},{4,13},{5,9},{6,5},{7,1},{8,14},{9,10},{1... | collective-permute-start | bytes 786440 | tf_op jit(solution)/shard_map/ppermute | solution.py:325
  670.2 0.9 copy-start.13
  (4 other events, 3.0 us)
